TPU v7x, 128 devices: a whole 4x4x4 slice. The times are simulated.
128 devices in a mesh: tm: 16 (over x_hi, z, core), space: 8 (over y, x_lo).
Axes of the slice: x: 4 (x_hi: 2, x_lo: 2; x = x_hi * 2 + x_lo), y: 4, z: 4, core: 2. Of those that a mesh axis runs over, the one named last changes fastest.
Arguments:
- startup_condition: float32 [2, 32, 128, 128], P(None, 'space'), may hold values from -3 to 3
- slab_final_guess: float32 [16, 2, 32, 128, 128], P('tm', None, 'space'), may hold values from -4 to 4
- thermal_diffusivity_pair: float32 [2, 32, 128, 128], P(None, 'space'), may hold values from 0.25 to 2
- interphase_exchange_rate: float32 [32, 128, 128], P('space'), may hold values from 0.1 to 1
- inlet_stream_warmth: float32 [128, 128], replicated, may hold values from 1 to 3
Outputs:
- updated_c_points: float32 [16, 2, 32, 128, 128], P('tm', None, 'space')
All inputs are finite; a program needn't handle non-finite values.
Results may differ from a plain program's by a relative error of at most 0.00002.
Values sent between devices are 32-bit elements; how exact they have to be, the bound alone decides.
No kernel may reach another device: no remote copies, remote signals or barrier semaphores. Data moves between devices by JAX's collectives and lax.ppermute only.
A program may use at most 64 MiB of HBM per device.

v0:
```python
import jax
import jax.numpy as jnp
from jax import lax
from jax.sharding import PartitionSpec as P

FINE_STEP_COUNT = 4
SWEEPS = 2


rate_along = 4.0
rate_across = 0.5
advection = 1.0
damping = 0.8


def extended(cells, sides, width):
    for axis, dim in sides:
        count = lax.axis_size(axis)
        ends = count - 1
        head = lax.slice_in_dim(cells, 0, width, axis=dim)
        tail = lax.slice_in_dim(cells, cells.shape[dim] - width, cells.shape[dim], axis=dim)
        cells = jnp.concatenate(
            [
                lax.ppermute(tail, axis, [(i, (i + 1) % count) for i in range(ends)]),
                cells,
                lax.ppermute(head, axis, [((i + 1) % count, i) for i in range(ends)]),
            ],
            axis=dim,
        )
    return cells


def passed_along(value, axis, steps):
    count = lax.axis_size(axis)
    first, last = (max(0, -steps), min(count, count - steps))
    return lax.ppermute(value, axis, [(source, source + steps) for source in range(first, last)])


def face_weights(conductance, coupling_field):
    centre = conductance[:, 1:-1]
    padded = jnp.pad(centre, ((0, 0), (0, 0), (1, 1), (1, 1)))
    upwind = jnp.array([0.0, advection], jnp.float32)[:, None, None, None]
    to_west = rate_along * 0.5 * (centre + conductance[:, :-2]) + upwind
    to_east = rate_along * 0.5 * (centre + conductance[:, 2:])
    to_south = rate_across * 0.5 * (centre + padded[:, :, :-2, 1:-1])
    to_north = rate_across * 0.5 * (centre + padded[:, :, 2:, 1:-1])
    to_below = rate_across * 0.5 * (centre + padded[:, :, 1:-1, :-2])
    to_above = rate_across * 0.5 * (centre + padded[:, :, 1:-1, 2:])
    weights = (to_west, to_east, to_south, to_north, to_below, to_above)
    outflow = to_west + to_east + to_south + to_north + to_below + to_above + coupling_field[None]
    return (weights, outflow)


def jacobi_sweep(weights, outflow, coupling_field, factor, widened, earlier):
    current = widened[:, 1:-1]
    padded = jnp.pad(widened, ((0, 0), (0, 0), (1, 1), (1, 1)))
    to_west, to_east, to_south, to_north, to_below, to_above = weights
    inflow = (
        to_west * padded[:, :-2, 1:-1, 1:-1]
        + to_east * padded[:, 2:, 1:-1, 1:-1]
        + to_south * padded[:, 1:-1, :-2, 1:-1]
        + to_north * padded[:, 1:-1, 2:, 1:-1]
        + to_below * padded[:, 1:-1, 1:-1, :-2]
        + to_above * padded[:, 1:-1, 1:-1, 2:]
    )
    inflow = inflow + coupling_field[None] * current[::-1]
    pivot_value = 1.0 + factor * outflow
    defect = earlier + factor * inflow - pivot_value * current
    return current + damping * defect / pivot_value


def shards(
    startup_condition,
    slab_final_guess,
    thermal_diffusivity_pair,
    interphase_exchange_rate,
    inlet_stream_warmth,
):
    brick_index = lax.axis_index("space")
    brick_count = lax.axis_size("space")
    slab_index = lax.axis_index("tm")
    cells_x = thermal_diffusivity_pair.shape[1]
    upstream_neighbour_data = jnp.stack([jnp.zeros_like(inlet_stream_warmth), inlet_stream_warmth])
    coarse_factor = float(FINE_STEP_COUNT)
    margin = SWEEPS
    stacked = jnp.concatenate([thermal_diffusivity_pair, interphase_exchange_rate[None]], axis=0)
    widened_coefficients = extended(stacked, (("space", 1),), SWEEPS)
    conductance = jnp.pad(widened_coefficients[:2], ((0, 0), (1, 1), (0, 0), (0, 0)))
    coupling_region = widened_coefficients[2]
    weights, outflow = face_weights(conductance, coupling_region)
    position = brick_index * cells_x - margin + jnp.arange(cells_x + 2 * margin, dtype=jnp.int32)
    outside_left = (position < 0)[None, :, None, None]
    outside_right = (position >= brick_count * cells_x)[None, :, None, None]

    def impose(field):
        field = jnp.where(outside_left, upstream_neighbour_data[:, None], field)
        return jnp.where(outside_right, 0.0, field)

    def advance(state_now, factor):
        earlier = impose(extended(state_now, (("space", 1),), SWEEPS))
        current = earlier
        for sweep_index in range(SWEEPS):
            widened = jnp.pad(current, ((0, 0), (1, 1), (0, 0), (0, 0)))
            current = impose(
                jacobi_sweep(weights, outflow, coupling_region, factor, widened, earlier)
            )
        return current[:, margin:-margin]

    received = passed_along(slab_final_guess[0], "tm", 1)
    slab_begin = jnp.where(slab_index == 0, startup_condition, received)
    fine_state = slab_begin
    for step_index in range(FINE_STEP_COUNT):
        fine_state = advance(fine_state, 1.0)
    correction = fine_state - advance(slab_begin, coarse_factor)

    def relay_round(relay_round_index, current):
        arrived = passed_along(current, "tm", 1)
        chain_start = jnp.where(slab_index == 0, startup_condition, arrived)
        return advance(chain_start, coarse_factor) + correction

    result = lax.fori_loop(0, lax.axis_size("tm"), relay_round, correction)
    return result[None]


def solution(mesh):
    return jax.shard_map(
        shards,
        mesh=mesh,
        in_specs=(
            P(None, "space", None, None),
            P("tm", None, "space", None, None),
            P(None, "space", None, None),
            P("space", None, None),
            P(),
        ),
        out_specs=P("tm", None, "space", None, None),
        check_vma=False,
    )
```

profile of v0, /device:TPU:4, one launch (start us, length us, event | category | flops | bytes accessed | tf_op | source)
XLA Modules:
  0.0 734.1 jit_solution(7438113510541745341)
XLA Ops:
  2.6 4.6 collective-permute-start.6
  7.1 1.9 collective-permute-start.3
  9.1 6.0 collective-permute-done.7
  16.5 8.7 %collective-permute-done.3 = f32[2,4,128,128]{3,2,1,0:T(8,128)S(1)} collective-permute-done((f32[2,4,128,128]{3,2,1,0:T(8,128)}, f32[2,4,128,128]{3,2,1,0:T(8,128)S(1)}, u32[]{:S(2)}, u32[]{:S(2)}) %collective-permute-start.3) | collective-permute-done | bytes 524320 | tf_op jit(solution)/shard_map/ppermute | solution.py:36
  26.8 9.9 %collective-permute-start.4 = (f32[2,2,128,128]{3,2,1,0:T(8,128)S(1)}, f32[2,2,128,128]{3,2,1,0:T(8,128)S(1)}, u32[]{:S(2)}, u32[]{:S(2)}) collective-permute-start(f32[2,2,128,128]{3,2,1,0:T(8,128)S(1)} %get-tuple-element.340), channel_id=1, source_target_pairs={{0,1},{1,2},{2,3},{3,4},{4,5},{5,6},{6,7},{8,9},{9,10},{10,11},{11... | collective-permute-start | bytes 786440 | tf_op jit(solution)/shard_map/ppermute | solution.py:24
  42.6 2.2 fusion.178
  46.1 8.0 %collective-permute-start.8 = (f32[2,2,128,128]{3,2,1,0:T(8,128)S(1)}, f32[2,2,128,128]{3,2,1,0:T(8,128)S(1)}, u32[]{:S(2)}, u32[]{:S(2)}) collective-permute-start(f32[2,2,128,128]{3,2,1,0:T(8,128)S(1)} %get-tuple-element.336), channel_id=1, source_target_pairs={{0,1},{1,2},{2,3},{3,4},{4,5},{5,6},{6,7},{8,9},{9,10},{10,11},{11... | collective-permute-start | bytes 786440 | tf_op jit(solution)/shard_map/ppermute | solution.py:24
  54.2 4.3 collective-permute-done.9
  65.3 6.7 collective-permute-start.10
  72.0 5.0 collective-permute-done.11
  82.9 6.5 collective-permute-start.12
  89.8 2.1 collective-permute-done.13
  93.6 2.9 fusion.174
  96.7 2.5 fusion.148
  100.7 633.4 %while.14 = (s32[]{:T(128)}, f32[2,4,128,128]{3,2,1,0:T(8,128)}, f32[2,128,128]{2,1,0:T(8,128)S(1)}, pred[]{:T(512)}, f32[2,4,128,128]{3,2,1,0:T(8,128)}, /*inde...) while((s32[]{:T(128)}, f32[2,4,128,128]{3,2,1,0:T(8,128)}, ...), condition=%wide.region_1.2_spmd.clone.clone, body=%wide.region_0.1_spmd.clone.clone.sunk | while | flops 12582938 | bytes 64882176 | solution.py:121
  100.7 1.9 collective-permute-start
  102.6 12.4 %collective-permute-done = f32[2,4,128,128]{3,2,1,0:T(8,128)S(1)} collective-permute-done((f32[2,4,128,128]{3,2,1,0:T(8,128)}, f32[2,4,128,128]{3,2,1,0:T(8,128)S(1)}, u32[]{:S(2)}, u32[]{:S(2)}) %collective-permute-start) | collective-permute-done | bytes 524320 | tf_op jit(solution)/shard_map/while/body/eval_jaxpr/ppermute | solution.py:36
  117.9 6.6 collective-permute-start.2
  130.8 2.9 fusion.198
  138.0 12.4 %collective-permute-done = f32[2,4,128,128]{3,2,1,0:T(8,128)S(1)} collective-permute-done((f32[2,4,128,128]{3,2,1,0:T(8,128)}, f32[2,4,128,128]{3,2,1,0:T(8,128)S(1)}, u32[]{:S(2)}, u32[]{:S(2)}) %collective-permute-start) | collective-permute-done | bytes 524320 | tf_op jit(solution)/shard_map/while/body/eval_jaxpr/ppermute | solution.py:36
  153.4 8.0 %collective-permute-start.2 = (f32[2,2,128,128]{3,2,1,0:T(8,128)S(1)}, f32[2,2,128,128]{3,2,1,0:T(8,128)}, u32[]{:S(2)}, u32[]{:S(2)}) collective-permute-start(f32[2,2,128,128]{3,2,1,0:T(8,128)S(1)} %get-tuple-element.443), channel_id=1, source_target_pairs={{0,1},{1,2},{2,3},{3,4},{4,5},{5,6},{6,7},{8,9},{9,10},{10,11},{11... | collective-permute-start | bytes 786440 | tf_op jit(solution)/shard_map/while/body/eval_jaxpr/ppermute | solution.py:24
  167.6 2.9 fusion.198
  174.8 13.0 %collective-permute-done = f32[2,4,128,128]{3,2,1,0:T(8,128)S(1)} collective-permute-done((f32[2,4,128,128]{3,2,1,0:T(8,128)}, f32[2,4,128,128]{3,2,1,0:T(8,128)S(1)}, u32[]{:S(2)}, u32[]{:S(2)}) %collective-permute-start) | collective-permute-done | bytes 524320 | tf_op jit(solution)/shard_map/while/body/eval_jaxpr/ppermute | solution.py:36
  190.8 12.1 %collective-permute-start.2 = (f32[2,2,128,128]{3,2,1,0:T(8,128)S(1)}, f32[2,2,128,128]{3,2,1,0:T(8,128)}, u32[]{:S(2)}, u32[]{:S(2)}) collective-permute-start(f32[2,2,128,128]{3,2,1,0:T(8,128)S(1)} %get-tuple-element.443), channel_id=1, source_target_pairs={{0,1},{1,2},{2,3},{3,4},{4,5},{5,6},{6,7},{8,9},{9,10},{10,11},{11... | collective-permute-start | bytes 786440 | tf_op jit(solution)/shard_map/while/body/eval_jaxpr/ppermute | solution.py:24
  209.0 2.9 fusion.198
  216.3 14.5 %collective-permute-done = f32[2,4,128,128]{3,2,1,0:T(8,128)S(1)} collective-permute-done((f32[2,4,128,128]{3,2,1,0:T(8,128)}, f32[2,4,128,128]{3,2,1,0:T(8,128)S(1)}, u32[]{:S(2)}, u32[]{:S(2)}) %collective-permute-start) | collective-permute-done | bytes 524320 | tf_op jit(solution)/shard_map/while/body/eval_jaxpr/ppermute | solution.py:36
  233.7 9.2 %collective-permute-start.2 = (f32[2,2,128,128]{3,2,1,0:T(8,128)S(1)}, f32[2,2,128,128]{3,2,1,0:T(8,128)}, u32[]{:S(2)}, u32[]{:S(2)}) collective-permute-start(f32[2,2,128,128]{3,2,1,0:T(8,128)S(1)} %get-tuple-element.443), channel_id=1, source_target_pairs={{0,1},{1,2},{2,3},{3,4},{4,5},{5,6},{6,7},{8,9},{9,10},{10,11},{11... | collective-permute-start | bytes 786440 | tf_op jit(solution)/shard_map/while/body/eval_jaxpr/ppermute | solution.py:24
  249.1 2.9 fusion.198
  256.3 14.5 %collective-permute-done = f32[2,4,128,128]{3,2,1,0:T(8,128)S(1)} collective-permute-done((f32[2,4,128,128]{3,2,1,0:T(8,128)}, f32[2,4,128,128]{3,2,1,0:T(8,128)S(1)}, u32[]{:S(2)}, u32[]{:S(2)}) %collective-permute-start) | collective-permute-done | bytes 524320 | tf_op jit(solution)/shard_map/while/body/eval_jaxpr/ppermute | solution.py:36
  273.8 9.0 %collective-permute-start.2 = (f32[2,2,128,128]{3,2,1,0:T(8,128)S(1)}, f32[2,2,128,128]{3,2,1,0:T(8,128)}, u32[]{:S(2)}, u32[]{:S(2)}) collective-permute-start(f32[2,2,128,128]{3,2,1,0:T(8,128)S(1)} %get-tuple-element.443), channel_id=1, source_target_pairs={{0,1},{1,2},{2,3},{3,4},{4,5},{5,6},{6,7},{8,9},{9,10},{10,11},{11... | collective-permute-start | bytes 786440 | tf_op jit(solution)/shard_map/while/body/eval_jaxpr/ppermute | solution.py:24
  289.1 2.9 fusion.198
  296.3 14.5 %collective-permute-done = f32[2,4,128,128]{3,2,1,0:T(8,128)S(1)} collective-permute-done((f32[2,4,128,128]{3,2,1,0:T(8,128)}, f32[2,4,128,128]{3,2,1,0:T(8,128)S(1)}, u32[]{:S(2)}, u32[]{:S(2)}) %collective-permute-start) | collective-permute-done | bytes 524320 | tf_op jit(solution)/shard_map/while/body/eval_jaxpr/ppermute | solution.py:36
  313.8 9.0 %collective-permute-start.2 = (f32[2,2,128,128]{3,2,1,0:T(8,128)S(1)}, f32[2,2,128,128]{3,2,1,0:T(8,128)}, u32[]{:S(2)}, u32[]{:S(2)}) collective-permute-start(f32[2,2,128,128]{3,2,1,0:T(8,128)S(1)} %get-tuple-element.443), channel_id=1, source_target_pairs={{0,1},{1,2},{2,3},{3,4},{4,5},{5,6},{6,7},{8,9},{9,10},{10,11},{11... | collective-permute-start | bytes 786440 | tf_op jit(solution)/shard_map/while/body/eval_jaxpr/ppermute | solution.py:24
  329.0 2.9 fusion.198
  336.3 14.5 %collective-permute-done = f32[2,4,128,128]{3,2,1,0:T(8,128)S(1)} collective-permute-done((f32[2,4,128,128]{3,2,1,0:T(8,128)}, f32[2,4,128,128]{3,2,1,0:T(8,128)S(1)}, u32[]{:S(2)}, u32[]{:S(2)}) %collective-permute-start) | collective-permute-done | bytes 524320 | tf_op jit(solution)/shard_map/while/body/eval_jaxpr/ppermute | solution.py:36
  353.7 9.0 %collective-permute-start.2 = (f32[2,2,128,128]{3,2,1,0:T(8,128)S(1)}, f32[2,2,128,128]{3,2,1,0:T(8,128)}, u32[]{:S(2)}, u32[]{:S(2)}) collective-permute-start(f32[2,2,128,128]{3,2,1,0:T(8,128)S(1)} %get-tuple-element.443), channel_id=1, source_target_pairs={{0,1},{1,2},{2,3},{3,4},{4,5},{5,6},{6,7},{8,9},{9,10},{10,11},{11... | collective-permute-start | bytes 786440 | tf_op jit(solution)/shard_map/while/body/eval_jaxpr/ppermute | solution.py:24
  369.0 2.9 fusion.198
  376.3 14.5 %collective-permute-done = f32[2,4,128,128]{3,2,1,0:T(8,128)S(1)} collective-permute-done((f32[2,4,128,128]{3,2,1,0:T(8,128)}, f32[2,4,128,128]{3,2,1,0:T(8,128)S(1)}, u32[]{:S(2)}, u32[]{:S(2)}) %collective-permute-start) | collective-permute-done | bytes 524320 | tf_op jit(solution)/shard_map/while/body/eval_jaxpr/ppermute | solution.py:36
  393.7 9.0 %collective-permute-start.2 = (f32[2,2,128,128]{3,2,1,0:T(8,128)S(1)}, f32[2,2,128,128]{3,2,1,0:T(8,128)}, u32[]{:S(2)}, u32[]{:S(2)}) collective-permute-start(f32[2,2,128,128]{3,2,1,0:T(8,128)S(1)} %get-tuple-element.443), channel_id=1, source_target_pairs={{0,1},{1,2},{2,3},{3,4},{4,5},{5,6},{6,7},{8,9},{9,10},{10,11},{11... | collective-permute-start | bytes 786440 | tf_op jit(solution)/shard_map/while/body/eval_jaxpr/ppermute | solution.py:24
  409.0 2.9 fusion.198
  416.2 14.5 %collective-permute-done = f32[2,4,128,128]{3,2,1,0:T(8,128)S(1)} collective-permute-done((f32[2,4,128,128]{3,2,1,0:T(8,128)}, f32[2,4,128,128]{3,2,1,0:T(8,128)S(1)}, u32[]{:S(2)}, u32[]{:S(2)}) %collective-permute-start) | collective-permute-done | bytes 524320 | tf_op jit(solution)/shard_map/while/body/eval_jaxpr/ppermute | solution.py:36
  433.7 9.0 %collective-permute-start.2 = (f32[2,2,128,128]{3,2,1,0:T(8,128)S(1)}, f32[2,2,128,128]{3,2,1,0:T(8,128)}, u32[]{:S(2)}, u32[]{:S(2)}) collective-permute-start(f32[2,2,128,128]{3,2,1,0:T(8,128)S(1)} %get-tuple-element.443), channel_id=1, source_target_pairs={{0,1},{1,2},{2,3},{3,4},{4,5},{5,6},{6,7},{8,9},{9,10},{10,11},{11... | collective-permute-start | bytes 786440 | tf_op jit(solution)/shard_map/while/body/eval_jaxpr/ppermute | solution.py:24
  449.0 2.9 fusion.198
  456.2 14.5 %collective-permute-done = f32[2,4,128,128]{3,2,1,0:T(8,128)S(1)} collective-permute-done((f32[2,4,128,128]{3,2,1,0:T(8,128)}, f32[2,4,128,128]{3,2,1,0:T(8,128)S(1)}, u32[]{:S(2)}, u32[]{:S(2)}) %collective-permute-start) | collective-permute-done | bytes 524320 | tf_op jit(solution)/shard_map/while/body/eval_jaxpr/ppermute | solution.py:36
  473.7 9.0 %collective-permute-start.2 = (f32[2,2,128,128]{3,2,1,0:T(8,128)S(1)}, f32[2,2,128,128]{3,2,1,0:T(8,128)}, u32[]{:S(2)}, u32[]{:S(2)}) collective-permute-start(f32[2,2,128,128]{3,2,1,0:T(8,128)S(1)} %get-tuple-element.443), channel_id=1, source_target_pairs={{0,1},{1,2},{2,3},{3,4},{4,5},{5,6},{6,7},{8,9},{9,10},{10,11},{11... | collective-permute-start | bytes 786440 | tf_op jit(solution)/shard_map/while/body/eval_jaxpr/ppermute | solution.py:24
  488.9 2.9 fusion.198
  496.2 14.5 %collective-permute-done = f32[2,4,128,128]{3,2,1,0:T(8,128)S(1)} collective-permute-done((f32[2,4,128,128]{3,2,1,0:T(8,128)}, f32[2,4,128,128]{3,2,1,0:T(8,128)S(1)}, u32[]{:S(2)}, u32[]{:S(2)}) %collective-permute-start) | collective-permute-done | bytes 524320 | tf_op jit(solution)/shard_map/while/body/eval_jaxpr/ppermute | solution.py:36
  513.6 9.0 %collective-permute-start.2 = (f32[2,2,128,128]{3,2,1,0:T(8,128)S(1)}, f32[2,2,128,128]{3,2,1,0:T(8,128)}, u32[]{:S(2)}, u32[]{:S(2)}) collective-permute-start(f32[2,2,128,128]{3,2,1,0:T(8,128)S(1)} %get-tuple-element.443), channel_id=1, source_target_pairs={{0,1},{1,2},{2,3},{3,4},{4,5},{5,6},{6,7},{8,9},{9,10},{10,11},{11... | collective-permute-start | bytes 786440 | tf_op jit(solution)/shard_map/while/body/eval_jaxpr/ppermute | solution.py:24
  528.9 2.9 fusion.198
  536.2 14.5 %collective-permute-done = f32[2,4,128,128]{3,2,1,0:T(8,128)S(1)} collective-permute-done((f32[2,4,128,128]{3,2,1,0:T(8,128)}, f32[2,4,128,128]{3,2,1,0:T(8,128)S(1)}, u32[]{:S(2)}, u32[]{:S(2)}) %collective-permute-start) | collective-permute-done | bytes 524320 | tf_op jit(solution)/shard_map/while/body/eval_jaxpr/ppermute | solution.py:36
  553.6 9.0 %collective-permute-start.2 = (f32[2,2,128,128]{3,2,1,0:T(8,128)S(1)}, f32[2,2,128,128]{3,2,1,0:T(8,128)}, u32[]{:S(2)}, u32[]{:S(2)}) collective-permute-start(f32[2,2,128,128]{3,2,1,0:T(8,128)S(1)} %get-tuple-element.443), channel_id=1, source_target_pairs={{0,1},{1,2},{2,3},{3,4},{4,5},{5,6},{6,7},{8,9},{9,10},{10,11},{11... | collective-permute-start | bytes 786440 | tf_op jit(solution)/shard_map/while/body/eval_jaxpr/ppermute | solution.py:24
  568.9 2.9 fusion.198
  576.1 14.5 %collective-permute-done = f32[2,4,128,128]{3,2,1,0:T(8,128)S(1)} collective-permute-done((f32[2,4,128,128]{3,2,1,0:T(8,128)}, f32[2,4,128,128]{3,2,1,0:T(8,128)S(1)}, u32[]{:S(2)}, u32[]{:S(2)}) %collective-permute-start) | collective-permute-done | bytes 524320 | tf_op jit(solution)/shard_map/while/body/eval_jaxpr/ppermute | solution.py:36
  593.6 9.0 %collective-permute-start.2 = (f32[2,2,128,128]{3,2,1,0:T(8,128)S(1)}, f32[2,2,128,128]{3,2,1,0:T(8,128)}, u32[]{:S(2)}, u32[]{:S(2)}) collective-permute-start(f32[2,2,128,128]{3,2,1,0:T(8,128)S(1)} %get-tuple-element.443), channel_id=1, source_target_pairs={{0,1},{1,2},{2,3},{3,4},{4,5},{5,6},{6,7},{8,9},{9,10},{10,11},{11... | collective-permute-start | bytes 786440 | tf_op jit(solution)/shard_map/while/body/eval_jaxpr/ppermute | solution.py:24
  608.9 2.9 fusion.198
  616.1 14.5 %collective-permute-done = f32[2,4,128,128]{3,2,1,0:T(8,128)S(1)} collective-permute-done((f32[2,4,128,128]{3,2,1,0:T(8,128)}, f32[2,4,128,128]{3,2,1,0:T(8,128)S(1)}, u32[]{:S(2)}, u32[]{:S(2)}) %collective-permute-start) | collective-permute-done | bytes 524320 | tf_op jit(solution)/shard_map/while/body/eval_jaxpr/ppermute | solution.py:36
  633.6 9.0 %collective-permute-start.2 = (f32[2,2,128,128]{3,2,1,0:T(8,128)S(1)}, f32[2,2,128,128]{3,2,1,0:T(8,128)}, u32[]{:S(2)}, u32[]{:S(2)}) collective-permute-start(f32[2,2,128,128]{3,2,1,0:T(8,128)S(1)} %get-tuple-element.443), channel_id=1, source_target_pairs={{0,1},{1,2},{2,3},{3,4},{4,5},{5,6},{6,7},{8,9},{9,10},{10,11},{11... | collective-permute-start | bytes 786440 | tf_op jit(solution)/shard_map/while/body/eval_jaxpr/ppermute | solution.py:24
  648.8 2.9 fusion.198
  656.1 14.5 %collective-permute-done = f32[2,4,128,128]{3,2,1,0:T(8,128)S(1)} collective-permute-done((f32[2,4,128,128]{3,2,1,0:T(8,128)}, f32[2,4,128,128]{3,2,1,0:T(8,128)S(1)}, u32[]{:S(2)}, u32[]{:S(2)}) %collective-permute-start) | collective-permute-done | bytes 524320 | tf_op jit(solution)/shard_map/while/body/eval_jaxpr/ppermute | solution.py:36
  673.5 9.0 %collective-permute-start.2 = (f32[2,2,128,128]{3,2,1,0:T(8,128)S(1)}, f32[2,2,128,128]{3,2,1,0:T(8,128)}, u32[]{:S(2)}, u32[]{:S(2)}) collective-permute-start(f32[2,2,128,128]{3,2,1,0:T(8,128)S(1)} %get-tuple-element.443), channel_id=1, source_target_pairs={{0,1},{1,2},{2,3},{3,4},{4,5},{5,6},{6,7},{8,9},{9,10},{10,11},{11... | collective-permute-start | bytes 786440 | tf_op jit(solution)/shard_map/while/body/eval_jaxpr/ppermute | solution.py:24
  688.8 2.9 fusion.198
  696.1 14.5 %collective-permute-done = f32[2,4,128,128]{3,2,1,0:T(8,128)S(1)} collective-permute-done((f32[2,4,128,128]{3,2,1,0:T(8,128)}, f32[2,4,128,128]{3,2,1,0:T(8,128)S(1)}, u32[]{:S(2)}, u32[]{:S(2)}) %collective-permute-start) | collective-permute-done | bytes 524320 | tf_op jit(solution)/shard_map/while/body/eval_jaxpr/ppermute | solution.py:36
  713.5 9.0 %collective-permute-start.2 = (f32[2,2,128,128]{3,2,1,0:T(8,128)S(1)}, f32[2,2,128,128]{3,2,1,0:T(8,128)}, u32[]{:S(2)}, u32[]{:S(2)}) collective-permute-start(f32[2,2,128,128]{3,2,1,0:T(8,128)S(1)} %get-tuple-element.443), channel_id=1, source_target_pairs={{0,1},{1,2},{2,3},{3,4},{4,5},{5,6},{6,7},{8,9},{9,10},{10,11},{11... | collective-permute-start | bytes 786440 | tf_op jit(solution)/shard_map/while/body/eval_jaxpr/ppermute | solution.py:24
  728.8 2.9 fusion.198
  (490 shorter events, 241.8 us)
Async XLA Ops:
  1.3 13.9 %collective-permute-start.7 = (f32[3,2,128,128]{3,2,1,0:T(8,128)S(1)}, f32[3,2,128,128]{3,2,1,0:T(8,128)S(1)}, u32[]{:S(2)}, u32[]{:S(2)}) collective-permute-start(f32[3,2,128,128]{3,2,1,0:T(8,128)S(1)} %get-tuple-element.339), channel_id=1, source_target_pairs={{1,0},{2,1},{3,2},{4,3},{5,4},{6,5},{7,6},{9,8},{10,9},{11,10},{12... | collective-permute-start | bytes 1179656 | tf_op jit(solution)/shard_map/ppermute | solution.py:26
  2.6 12.6 %collective-permute-start.6 = (f32[3,2,128,128]{3,2,1,0:T(8,128)S(1)}, f32[3,2,128,128]{3,2,1,0:T(8,128)S(1)}, u32[]{:S(2)}, u32[]{:S(2)}) collective-permute-start(f32[3,2,128,128]{3,2,1,0:T(8,128)S(1)} %get-tuple-element.338), channel_id=1, source_target_pairs={{0,1},{1,2},{2,3},{3,4},{4,5},{5,6},{6,7},{8,9},{9,10},{10,11},{11... | collective-permute-start | bytes 1179656 | tf_op jit(solution)/shard_map/ppermute | solution.py:24
  7.1 18.1 %collective-permute-start.3 = (f32[2,4,128,128]{3,2,1,0:T(8,128)}, f32[2,4,128,128]{3,2,1,0:T(8,128)S(1)}, u32[]{:S(2)}, u32[]{:S(2)}) collective-permute-start(f32[2,4,128,128]{3,2,1,0:T(8,128)} %bitcast.1), channel_id=1, source_target_pairs={{0,8},{8,16},{16,24},{24,32},{32,40},{40,48},{48,56},{56,64},{64,7... | collective-permute-start | bytes 1572872 | tf_op jit(solution)/shard_map/ppermute | solution.py:36
  16.5 80.1 %copy-start.6 = (f32[1,8,128,128]{3,2,1,0:T(8,128)}, f32[1,8,128,128]{3,2,1,0:T(8,128)S(1)}, u32[]{:S(2)}) copy-start(f32[1,8,128,128]{3,2,1,0:T(8,128)S(1)} %pad_maximum_fusion.1) | copy-start | bytes 1572868
  25.4 13.8 %collective-permute-start.5 = (f32[2,2,128,128]{3,2,1,0:T(8,128)S(1)}, f32[2,2,128,128]{3,2,1,0:T(8,128)S(1)}, u32[]{:S(2)}, u32[]{:S(2)}) collective-permute-start(f32[2,2,128,128]{3,2,1,0:T(8,128)S(1)} %get-tuple-element.341), channel_id=1, source_target_pairs={{1,0},{2,1},{3,2},{4,3},{5,4},{6,5},{7,6},{9,8},{10,9},{11,10},{12... | collective-permute-start | bytes 786440 | tf_op jit(solution)/shard_map/ppermute | solution.py:26
  26.8 13.8 %collective-permute-start.4 = (f32[2,2,128,128]{3,2,1,0:T(8,128)S(1)}, f32[2,2,128,128]{3,2,1,0:T(8,128)S(1)}, u32[]{:S(2)}, u32[]{:S(2)}) collective-permute-start(f32[2,2,128,128]{3,2,1,0:T(8,128)S(1)} %get-tuple-element.340), channel_id=1, source_target_pairs={{0,1},{1,2},{2,3},{3,4},{4,5},{5,6},{6,7},{8,9},{9,10},{10,11},{11... | collective-permute-start | bytes 786440 | tf_op jit(solution)/shard_map/ppermute | solution.py:24
  37.7 55.9 %copy-start.8 = (f32[2,8,128,128]{3,2,1,0:T(8,128)}, f32[2,8,128,128]{3,2,1,0:T(8,128)S(1)}, u32[]{:S(2)}) copy-start(f32[2,8,128,128]{3,2,1,0:T(8,128)S(1)} %get-tuple-element.461) | copy-start | bytes 3145732
  37.7 59.0 %copy-start = (f32[2,8,128,128]{3,2,1,0:T(8,128)}, f32[2,8,128,128]{3,2,1,0:T(8,128)S(1)}, u32[]{:S(2)}) copy-start(f32[2,8,128,128]{3,2,1,0:T(8,128)S(1)} %get-tuple-element.458) | copy-start | bytes 3145732
  37.7 59.0 %copy-start.2 = (f32[2,8,128,128]{3,2,1,0:T(8,128)}, f32[2,8,128,128]{3,2,1,0:T(8,128)S(1)}, u32[]{:S(2)}) copy-start(f32[2,8,128,128]{3,2,1,0:T(8,128)S(1)} %get-tuple-element.457) | copy-start | bytes 3145732
  37.7 59.0 %copy-start.4 = (f32[2,8,128,128]{3,2,1,0:T(8,128)}, f32[2,8,128,128]{3,2,1,0:T(8,128)S(1)}, u32[]{:S(2)}) copy-start(f32[2,8,128,128]{3,2,1,0:T(8,128)S(1)} %get-tuple-element.456) | copy-start | bytes 3145732
  44.8 13.6 %collective-permute-start.9 = (f32[2,2,128,128]{3,2,1,0:T(8,128)S(1)}, f32[2,2,128,128]{3,2,1,0:T(8,128)S(1)}, u32[]{:S(2)}, u32[]{:S(2)}) collective-permute-start(f32[2,2,128,128]{3,2,1,0:T(8,128)S(1)} %get-tuple-element.337), channel_id=1, source_target_pairs={{1,0},{2,1},{3,2},{4,3},{5,4},{6,5},{7,6},{9,8},{10,9},{11,10},{12... | collective-permute-start | bytes 786440 | tf_op jit(solution)/shard_map/ppermute | solution.py:26
  46.1 14.1 %collective-permute-start.8 = (f32[2,2,128,128]{3,2,1,0:T(8,128)S(1)}, f32[2,2,128,128]{3,2,1,0:T(8,128)S(1)}, u32[]{:S(2)}, u32[]{:S(2)}) collective-permute-start(f32[2,2,128,128]{3,2,1,0:T(8,128)S(1)} %get-tuple-element.336), channel_id=1, source_target_pairs={{0,1},{1,2},{2,3},{3,4},{4,5},{5,6},{6,7},{8,9},{9,10},{10,11},{11... | collective-permute-start | bytes 786440 | tf_op jit(solution)/shard_map/ppermute | solution.py:24
  64.0 13.0 %collective-permute-start.11 = (f32[2,2,128,128]{3,2,1,0:T(8,128)S(1)}, f32[2,2,128,128]{3,2,1,0:T(8,128)S(1)}, u32[]{:S(2)}, u32[]{:S(2)}) collective-permute-start(f32[2,2,128,128]{3,2,1,0:T(8,128)S(1)} %get-tuple-element.335), channel_id=1, source_target_pairs={{1,0},{2,1},{3,2},{4,3},{5,4},{6,5},{7,6},{9,8},{10,9},{11,10},{12... | collective-permute-start | bytes 786440 | tf_op jit(solution)/shard_map/ppermute | solution.py:26
  65.3 12.6 %collective-permute-start.10 = (f32[2,2,128,128]{3,2,1,0:T(8,128)S(1)}, f32[2,2,128,128]{3,2,1,0:T(8,128)S(1)}, u32[]{:S(2)}, u32[]{:S(2)}) collective-permute-start(f32[2,2,128,128]{3,2,1,0:T(8,128)S(1)} %get-tuple-element.334), channel_id=1, source_target_pairs={{0,1},{1,2},{2,3},{3,4},{4,5},{5,6},{6,7},{8,9},{9,10},{10,11},{11... | collective-permute-start | bytes 786440 | tf_op jit(solution)/shard_map/ppermute | solution.py:24
  81.6 10.2 %collective-permute-start.13 = (f32[2,2,128,128]{3,2,1,0:T(8,128)S(1)}, f32[2,2,128,128]{3,2,1,0:T(8,128)S(1)}, u32[]{:S(2)}, u32[]{:S(2)}) collective-permute-start(f32[2,2,128,128]{3,2,1,0:T(8,128)S(1)} %get-tuple-element.333), channel_id=1, source_target_pairs={{1,0},{2,1},{3,2},{4,3},{5,4},{6,5},{7,6},{9,8},{10,9},{11,10},{12... | collective-permute-start | bytes 786440 | tf_op jit(solution)/shard_map/ppermute | solution.py:26
  82.9 10.4 %collective-permute-start.12 = (f32[2,2,128,128]{3,2,1,0:T(8,128)S(1)}, f32[2,2,128,128]{3,2,1,0:T(8,128)S(1)}, u32[]{:S(2)}, u32[]{:S(2)}) collective-permute-start(f32[2,2,128,128]{3,2,1,0:T(8,128)S(1)} %get-tuple-element.332), channel_id=1, source_target_pairs={{0,1},{1,2},{2,3},{3,4},{4,5},{5,6},{6,7},{8,9},{9,10},{10,11},{11... | collective-permute-start | bytes 786440 | tf_op jit(solution)/shard_map/ppermute | solution.py:24
  100.7 14.3 %collective-permute-start = (f32[2,4,128,128]{3,2,1,0:T(8,128)}, f32[2,4,128,128]{3,2,1,0:T(8,128)S(1)}, u32[]{:S(2)}, u32[]{:S(2)}) collective-permute-start(f32[2,4,128,128]{3,2,1,0:T(8,128)} %get-tuple-element.467), channel_id=1, source_target_pairs={{0,8},{8,16},{16,24},{24,32},{32,40},{40,48},{48,56},{56,64},{64,7... | collective-permute-start | bytes 1572872 | tf_op jit(solution)/shard_map/while/body/eval_jaxpr/ppermute | solution.py:36
  116.6 9.9 %collective-permute-start.1 = (f32[2,2,128,128]{3,2,1,0:T(8,128)}, f32[2,2,128,128]{3,2,1,0:T(8,128)}, u32[]{:S(2)}, u32[]{:S(2)}) collective-permute-start(f32[2,2,128,128]{3,2,1,0:T(8,128)} %get-tuple-element.442), channel_id=1, source_target_pairs={{1,0},{2,1},{3,2},{4,3},{5,4},{6,5},{7,6},{9,8},{10,9},{11,10},{12... | collective-permute-start | bytes 786440 | tf_op jit(solution)/shard_map/while/body/eval_jaxpr/ppermute | solution.py:26
  117.9 9.8 %collective-permute-start.2 = (f32[2,2,128,128]{3,2,1,0:T(8,128)S(1)}, f32[2,2,128,128]{3,2,1,0:T(8,128)}, u32[]{:S(2)}, u32[]{:S(2)}) collective-permute-start(f32[2,2,128,128]{3,2,1,0:T(8,128)S(1)} %get-tuple-element.443), channel_id=1, source_target_pairs={{0,1},{1,2},{2,3},{3,4},{4,5},{5,6},{6,7},{8,9},{9,10},{10,11},{11... | collective-permute-start | bytes 786440 | tf_op jit(solution)/shard_map/while/body/eval_jaxpr/ppermute | solution.py:24
  136.1 14.3 %collective-permute-start = (f32[2,4,128,128]{3,2,1,0:T(8,128)}, f32[2,4,128,128]{3,2,1,0:T(8,128)S(1)}, u32[]{:S(2)}, u32[]{:S(2)}) collective-permute-start(f32[2,4,128,128]{3,2,1,0:T(8,128)} %get-tuple-element.467), channel_id=1, source_target_pairs={{0,8},{8,16},{16,24},{24,32},{32,40},{40,48},{48,56},{56,64},{64,7... | collective-permute-start | bytes 1572872 | tf_op jit(solution)/shard_map/while/body/eval_jaxpr/ppermute | solution.py:36
  152.1 11.3 %collective-permute-start.1 = (f32[2,2,128,128]{3,2,1,0:T(8,128)}, f32[2,2,128,128]{3,2,1,0:T(8,128)}, u32[]{:S(2)}, u32[]{:S(2)}) collective-permute-start(f32[2,2,128,128]{3,2,1,0:T(8,128)} %get-tuple-element.442), channel_id=1, source_target_pairs={{1,0},{2,1},{3,2},{4,3},{5,4},{6,5},{7,6},{9,8},{10,9},{11,10},{12... | collective-permute-start | bytes 786440 | tf_op jit(solution)/shard_map/while/body/eval_jaxpr/ppermute | solution.py:26
  153.4 11.1 %collective-permute-start.2 = (f32[2,2,128,128]{3,2,1,0:T(8,128)S(1)}, f32[2,2,128,128]{3,2,1,0:T(8,128)}, u32[]{:S(2)}, u32[]{:S(2)}) collective-permute-start(f32[2,2,128,128]{3,2,1,0:T(8,128)S(1)} %get-tuple-element.443), channel_id=1, source_target_pairs={{0,1},{1,2},{2,3},{3,4},{4,5},{5,6},{6,7},{8,9},{9,10},{10,11},{11... | collective-permute-start | bytes 786440 | tf_op jit(solution)/shard_map/while/body/eval_jaxpr/ppermute | solution.py:24
  172.9 14.9 %collective-permute-start = (f32[2,4,128,128]{3,2,1,0:T(8,128)}, f32[2,4,128,128]{3,2,1,0:T(8,128)S(1)}, u32[]{:S(2)}, u32[]{:S(2)}) collective-permute-start(f32[2,4,128,128]{3,2,1,0:T(8,128)} %get-tuple-element.467), channel_id=1, source_target_pairs={{0,8},{8,16},{16,24},{24,32},{32,40},{40,48},{48,56},{56,64},{64,7... | collective-permute-start | bytes 1572872 | tf_op jit(solution)/shard_map/while/body/eval_jaxpr/ppermute | solution.py:36
  189.5 15.3 %collective-permute-start.1 = (f32[2,2,128,128]{3,2,1,0:T(8,128)}, f32[2,2,128,128]{3,2,1,0:T(8,128)}, u32[]{:S(2)}, u32[]{:S(2)}) collective-permute-start(f32[2,2,128,128]{3,2,1,0:T(8,128)} %get-tuple-element.442), channel_id=1, source_target_pairs={{1,0},{2,1},{3,2},{4,3},{5,4},{6,5},{7,6},{9,8},{10,9},{11,10},{12... | collective-permute-start | bytes 786440 | tf_op jit(solution)/shard_map/while/body/eval_jaxpr/ppermute | solution.py:26
  190.8 15.2 %collective-permute-start.2 = (f32[2,2,128,128]{3,2,1,0:T(8,128)S(1)}, f32[2,2,128,128]{3,2,1,0:T(8,128)}, u32[]{:S(2)}, u32[]{:S(2)}) collective-permute-start(f32[2,2,128,128]{3,2,1,0:T(8,128)S(1)} %get-tuple-element.443), channel_id=1, source_target_pairs={{0,1},{1,2},{2,3},{3,4},{4,5},{5,6},{6,7},{8,9},{9,10},{10,11},{11... | collective-permute-start | bytes 786440 | tf_op jit(solution)/shard_map/while/body/eval_jaxpr/ppermute | solution.py:24
  214.4 16.4 %collective-permute-start = (f32[2,4,128,128]{3,2,1,0:T(8,128)}, f32[2,4,128,128]{3,2,1,0:T(8,128)S(1)}, u32[]{:S(2)}, u32[]{:S(2)}) collective-permute-start(f32[2,4,128,128]{3,2,1,0:T(8,128)} %get-tuple-element.467), channel_id=1, source_target_pairs={{0,8},{8,16},{16,24},{24,32},{32,40},{40,48},{48,56},{56,64},{64,7... | collective-permute-start | bytes 1572872 | tf_op jit(solution)/shard_map/while/body/eval_jaxpr/ppermute | solution.py:36
  232.4 12.5 %collective-permute-start.1 = (f32[2,2,128,128]{3,2,1,0:T(8,128)}, f32[2,2,128,128]{3,2,1,0:T(8,128)}, u32[]{:S(2)}, u32[]{:S(2)}) collective-permute-start(f32[2,2,128,128]{3,2,1,0:T(8,128)} %get-tuple-element.442), channel_id=1, source_target_pairs={{1,0},{2,1},{3,2},{4,3},{5,4},{6,5},{7,6},{9,8},{10,9},{11,10},{12... | collective-permute-start | bytes 786440 | tf_op jit(solution)/shard_map/while/body/eval_jaxpr/ppermute | solution.py:26
  233.7 12.3 %collective-permute-start.2 = (f32[2,2,128,128]{3,2,1,0:T(8,128)S(1)}, f32[2,2,128,128]{3,2,1,0:T(8,128)}, u32[]{:S(2)}, u32[]{:S(2)}) collective-permute-start(f32[2,2,128,128]{3,2,1,0:T(8,128)S(1)} %get-tuple-element.443), channel_id=1, source_target_pairs={{0,1},{1,2},{2,3},{3,4},{4,5},{5,6},{6,7},{8,9},{9,10},{10,11},{11... | collective-permute-start | bytes 786440 | tf_op jit(solution)/shard_map/while/body/eval_jaxpr/ppermute | solution.py:24
  254.4 16.5 %collective-permute-start = (f32[2,4,128,128]{3,2,1,0:T(8,128)}, f32[2,4,128,128]{3,2,1,0:T(8,128)S(1)}, u32[]{:S(2)}, u32[]{:S(2)}) collective-permute-start(f32[2,4,128,128]{3,2,1,0:T(8,128)} %get-tuple-element.467), channel_id=1, source_target_pairs={{0,8},{8,16},{16,24},{24,32},{32,40},{40,48},{48,56},{56,64},{64,7... | collective-permute-start | bytes 1572872 | tf_op jit(solution)/shard_map/while/body/eval_jaxpr/ppermute | solution.py:36
  272.5 12.3 %collective-permute-start.1 = (f32[2,2,128,128]{3,2,1,0:T(8,128)}, f32[2,2,128,128]{3,2,1,0:T(8,128)}, u32[]{:S(2)}, u32[]{:S(2)}) collective-permute-start(f32[2,2,128,128]{3,2,1,0:T(8,128)} %get-tuple-element.442), channel_id=1, source_target_pairs={{1,0},{2,1},{3,2},{4,3},{5,4},{6,5},{7,6},{9,8},{10,9},{11,10},{12... | collective-permute-start | bytes 786440 | tf_op jit(solution)/shard_map/while/body/eval_jaxpr/ppermute | solution.py:26
  273.8 12.2 %collective-permute-start.2 = (f32[2,2,128,128]{3,2,1,0:T(8,128)S(1)}, f32[2,2,128,128]{3,2,1,0:T(8,128)}, u32[]{:S(2)}, u32[]{:S(2)}) collective-permute-start(f32[2,2,128,128]{3,2,1,0:T(8,128)S(1)} %get-tuple-element.443), channel_id=1, source_target_pairs={{0,1},{1,2},{2,3},{3,4},{4,5},{5,6},{6,7},{8,9},{9,10},{10,11},{11... | collective-permute-start | bytes 786440 | tf_op jit(solution)/shard_map/while/body/eval_jaxpr/ppermute | solution.py:24
  294.4 16.5 %collective-permute-start = (f32[2,4,128,128]{3,2,1,0:T(8,128)}, f32[2,4,128,128]{3,2,1,0:T(8,128)S(1)}, u32[]{:S(2)}, u32[]{:S(2)}) collective-permute-start(f32[2,4,128,128]{3,2,1,0:T(8,128)} %get-tuple-element.467), channel_id=1, source_target_pairs={{0,8},{8,16},{16,24},{24,32},{32,40},{40,48},{48,56},{56,64},{64,7... | collective-permute-start | bytes 1572872 | tf_op jit(solution)/shard_map/while/body/eval_jaxpr/ppermute | solution.py:36
  312.5 12.3 %collective-permute-start.1 = (f32[2,2,128,128]{3,2,1,0:T(8,128)}, f32[2,2,128,128]{3,2,1,0:T(8,128)}, u32[]{:S(2)}, u32[]{:S(2)}) collective-permute-start(f32[2,2,128,128]{3,2,1,0:T(8,128)} %get-tuple-element.442), channel_id=1, source_target_pairs={{1,0},{2,1},{3,2},{4,3},{5,4},{6,5},{7,6},{9,8},{10,9},{11,10},{12... | collective-permute-start | bytes 786440 | tf_op jit(solution)/shard_map/while/body/eval_jaxpr/ppermute | solution.py:26
  313.8 12.2 %collective-permute-start.2 = (f32[2,2,128,128]{3,2,1,0:T(8,128)S(1)}, f32[2,2,128,128]{3,2,1,0:T(8,128)}, u32[]{:S(2)}, u32[]{:S(2)}) collective-permute-start(f32[2,2,128,128]{3,2,1,0:T(8,128)S(1)} %get-tuple-element.443), channel_id=1, source_target_pairs={{0,1},{1,2},{2,3},{3,4},{4,5},{5,6},{6,7},{8,9},{9,10},{10,11},{11... | collective-permute-start | bytes 786440 | tf_op jit(solution)/shard_map/while/body/eval_jaxpr/ppermute | solution.py:24
  334.4 16.5 %collective-permute-start = (f32[2,4,128,128]{3,2,1,0:T(8,128)}, f32[2,4,128,128]{3,2,1,0:T(8,128)S(1)}, u32[]{:S(2)}, u32[]{:S(2)}) collective-permute-start(f32[2,4,128,128]{3,2,1,0:T(8,128)} %get-tuple-element.467), channel_id=1, source_target_pairs={{0,8},{8,16},{16,24},{24,32},{32,40},{40,48},{48,56},{56,64},{64,7... | collective-permute-start | bytes 1572872 | tf_op jit(solution)/shard_map/while/body/eval_jaxpr/ppermute | solution.py:36
  352.4 12.3 %collective-permute-start.1 = (f32[2,2,128,128]{3,2,1,0:T(8,128)}, f32[2,2,128,128]{3,2,1,0:T(8,128)}, u32[]{:S(2)}, u32[]{:S(2)}) collective-permute-start(f32[2,2,128,128]{3,2,1,0:T(8,128)} %get-tuple-element.442), channel_id=1, source_target_pairs={{1,0},{2,1},{3,2},{4,3},{5,4},{6,5},{7,6},{9,8},{10,9},{11,10},{12... | collective-permute-start | bytes 786440 | tf_op jit(solution)/shard_map/while/body/eval_jaxpr/ppermute | solution.py:26
  353.7 12.2 %collective-permute-start.2 = (f32[2,2,128,128]{3,2,1,0:T(8,128)S(1)}, f32[2,2,128,128]{3,2,1,0:T(8,128)}, u32[]{:S(2)}, u32[]{:S(2)}) collective-permute-start(f32[2,2,128,128]{3,2,1,0:T(8,128)S(1)} %get-tuple-element.443), channel_id=1, source_target_pairs={{0,1},{1,2},{2,3},{3,4},{4,5},{5,6},{6,7},{8,9},{9,10},{10,11},{11... | collective-permute-start | bytes 786440 | tf_op jit(solution)/shard_map/while/body/eval_jaxpr/ppermute | solution.py:24
  374.3 16.5 %collective-permute-start = (f32[2,4,128,128]{3,2,1,0:T(8,128)}, f32[2,4,128,128]{3,2,1,0:T(8,128)S(1)}, u32[]{:S(2)}, u32[]{:S(2)}) collective-permute-start(f32[2,4,128,128]{3,2,1,0:T(8,128)} %get-tuple-element.467), channel_id=1, source_target_pairs={{0,8},{8,16},{16,24},{24,32},{32,40},{40,48},{48,56},{56,64},{64,7... | collective-permute-start | bytes 1572872 | tf_op jit(solution)/shard_map/while/body/eval_jaxpr/ppermute | solution.py:36
  392.4 12.3 %collective-permute-start.1 = (f32[2,2,128,128]{3,2,1,0:T(8,128)}, f32[2,2,128,128]{3,2,1,0:T(8,128)}, u32[]{:S(2)}, u32[]{:S(2)}) collective-permute-start(f32[2,2,128,128]{3,2,1,0:T(8,128)} %get-tuple-element.442), channel_id=1, source_target_pairs={{1,0},{2,1},{3,2},{4,3},{5,4},{6,5},{7,6},{9,8},{10,9},{11,10},{12... | collective-permute-start | bytes 786440 | tf_op jit(solution)/shard_map/while/body/eval_jaxpr/ppermute | solution.py:26
  393.7 12.2 %collective-permute-start.2 = (f32[2,2,128,128]{3,2,1,0:T(8,128)S(1)}, f32[2,2,128,128]{3,2,1,0:T(8,128)}, u32[]{:S(2)}, u32[]{:S(2)}) collective-permute-start(f32[2,2,128,128]{3,2,1,0:T(8,128)S(1)} %get-tuple-element.443), channel_id=1, source_target_pairs={{0,1},{1,2},{2,3},{3,4},{4,5},{5,6},{6,7},{8,9},{9,10},{10,11},{11... | collective-permute-start | bytes 786440 | tf_op jit(solution)/shard_map/while/body/eval_jaxpr/ppermute | solution.py:24
  414.3 16.5 %collective-permute-start = (f32[2,4,128,128]{3,2,1,0:T(8,128)}, f32[2,4,128,128]{3,2,1,0:T(8,128)S(1)}, u32[]{:S(2)}, u32[]{:S(2)}) collective-permute-start(f32[2,4,128,128]{3,2,1,0:T(8,128)} %get-tuple-element.467), channel_id=1, source_target_pairs={{0,8},{8,16},{16,24},{24,32},{32,40},{40,48},{48,56},{56,64},{64,7... | collective-permute-start | bytes 1572872 | tf_op jit(solution)/shard_map/while/body/eval_jaxpr/ppermute | solution.py:36
  432.4 12.3 %collective-permute-start.1 = (f32[2,2,128,128]{3,2,1,0:T(8,128)}, f32[2,2,128,128]{3,2,1,0:T(8,128)}, u32[]{:S(2)}, u32[]{:S(2)}) collective-permute-start(f32[2,2,128,128]{3,2,1,0:T(8,128)} %get-tuple-element.442), channel_id=1, source_target_pairs={{1,0},{2,1},{3,2},{4,3},{5,4},{6,5},{7,6},{9,8},{10,9},{11,10},{12... | collective-permute-start | bytes 786440 | tf_op jit(solution)/shard_map/while/body/eval_jaxpr/ppermute | solution.py:26
  433.7 12.2 %collective-permute-start.2 = (f32[2,2,128,128]{3,2,1,0:T(8,128)S(1)}, f32[2,2,128,128]{3,2,1,0:T(8,128)}, u32[]{:S(2)}, u32[]{:S(2)}) collective-permute-start(f32[2,2,128,128]{3,2,1,0:T(8,128)S(1)} %get-tuple-element.443), channel_id=1, source_target_pairs={{0,1},{1,2},{2,3},{3,4},{4,5},{5,6},{6,7},{8,9},{9,10},{10,11},{11... | collective-permute-start | bytes 786440 | tf_op jit(solution)/shard_map/while/body/eval_jaxpr/ppermute | solution.py:24
  454.3 16.5 %collective-permute-start = (f32[2,4,128,128]{3,2,1,0:T(8,128)}, f32[2,4,128,128]{3,2,1,0:T(8,128)S(1)}, u32[]{:S(2)}, u32[]{:S(2)}) collective-permute-start(f32[2,4,128,128]{3,2,1,0:T(8,128)} %get-tuple-element.467), channel_id=1, source_target_pairs={{0,8},{8,16},{16,24},{24,32},{32,40},{40,48},{48,56},{56,64},{64,7... | collective-permute-start | bytes 1572872 | tf_op jit(solution)/shard_map/while/body/eval_jaxpr/ppermute | solution.py:36
  472.4 12.3 %collective-permute-start.1 = (f32[2,2,128,128]{3,2,1,0:T(8,128)}, f32[2,2,128,128]{3,2,1,0:T(8,128)}, u32[]{:S(2)}, u32[]{:S(2)}) collective-permute-start(f32[2,2,128,128]{3,2,1,0:T(8,128)} %get-tuple-element.442), channel_id=1, source_target_pairs={{1,0},{2,1},{3,2},{4,3},{5,4},{6,5},{7,6},{9,8},{10,9},{11,10},{12... | collective-permute-start | bytes 786440 | tf_op jit(solution)/shard_map/while/body/eval_jaxpr/ppermute | solution.py:26
  473.7 12.2 %collective-permute-start.2 = (f32[2,2,128,128]{3,2,1,0:T(8,128)S(1)}, f32[2,2,128,128]{3,2,1,0:T(8,128)}, u32[]{:S(2)}, u32[]{:S(2)}) collective-permute-start(f32[2,2,128,128]{3,2,1,0:T(8,128)S(1)} %get-tuple-element.443), channel_id=1, source_target_pairs={{0,1},{1,2},{2,3},{3,4},{4,5},{5,6},{6,7},{8,9},{9,10},{10,11},{11... | collective-permute-start | bytes 786440 | tf_op jit(solution)/shard_map/while/body/eval_jaxpr/ppermute | solution.py:24
  494.3 16.5 %collective-permute-start = (f32[2,4,128,128]{3,2,1,0:T(8,128)}, f32[2,4,128,128]{3,2,1,0:T(8,128)S(1)}, u32[]{:S(2)}, u32[]{:S(2)}) collective-permute-start(f32[2,4,128,128]{3,2,1,0:T(8,128)} %get-tuple-element.467), channel_id=1, source_target_pairs={{0,8},{8,16},{16,24},{24,32},{32,40},{40,48},{48,56},{56,64},{64,7... | collective-permute-start | bytes 1572872 | tf_op jit(solution)/shard_map/while/body/eval_jaxpr/ppermute | solution.py:36
  512.4 12.3 %collective-permute-start.1 = (f32[2,2,128,128]{3,2,1,0:T(8,128)}, f32[2,2,128,128]{3,2,1,0:T(8,128)}, u32[]{:S(2)}, u32[]{:S(2)}) collective-permute-start(f32[2,2,128,128]{3,2,1,0:T(8,128)} %get-tuple-element.442), channel_id=1, source_target_pairs={{1,0},{2,1},{3,2},{4,3},{5,4},{6,5},{7,6},{9,8},{10,9},{11,10},{12... | collective-permute-start | bytes 786440 | tf_op jit(solution)/shard_map/while/body/eval_jaxpr/ppermute | solution.py:26
  513.6 12.2 %collective-permute-start.2 = (f32[2,2,128,128]{3,2,1,0:T(8,128)S(1)}, f32[2,2,128,128]{3,2,1,0:T(8,128)}, u32[]{:S(2)}, u32[]{:S(2)}) collective-permute-start(f32[2,2,128,128]{3,2,1,0:T(8,128)S(1)} %get-tuple-element.443), channel_id=1, source_target_pairs={{0,1},{1,2},{2,3},{3,4},{4,5},{5,6},{6,7},{8,9},{9,10},{10,11},{11... | collective-permute-start | bytes 786440 | tf_op jit(solution)/shard_map/while/body/eval_jaxpr/ppermute | solution.py:24
  534.2 16.5 %collective-permute-start = (f32[2,4,128,128]{3,2,1,0:T(8,128)}, f32[2,4,128,128]{3,2,1,0:T(8,128)S(1)}, u32[]{:S(2)}, u32[]{:S(2)}) collective-permute-start(f32[2,4,128,128]{3,2,1,0:T(8,128)} %get-tuple-element.467), channel_id=1, source_target_pairs={{0,8},{8,16},{16,24},{24,32},{32,40},{40,48},{48,56},{56,64},{64,7... | collective-permute-start | bytes 1572872 | tf_op jit(solution)/shard_map/while/body/eval_jaxpr/ppermute | solution.py:36
  552.3 12.3 %collective-permute-start.1 = (f32[2,2,128,128]{3,2,1,0:T(8,128)}, f32[2,2,128,128]{3,2,1,0:T(8,128)}, u32[]{:S(2)}, u32[]{:S(2)}) collective-permute-start(f32[2,2,128,128]{3,2,1,0:T(8,128)} %get-tuple-element.442), channel_id=1, source_target_pairs={{1,0},{2,1},{3,2},{4,3},{5,4},{6,5},{7,6},{9,8},{10,9},{11,10},{12... | collective-permute-start | bytes 786440 | tf_op jit(solution)/shard_map/while/body/eval_jaxpr/ppermute | solution.py:26
  553.6 12.2 %collective-permute-start.2 = (f32[2,2,128,128]{3,2,1,0:T(8,128)S(1)}, f32[2,2,128,128]{3,2,1,0:T(8,128)}, u32[]{:S(2)}, u32[]{:S(2)}) collective-permute-start(f32[2,2,128,128]{3,2,1,0:T(8,128)S(1)} %get-tuple-element.443), channel_id=1, source_target_pairs={{0,1},{1,2},{2,3},{3,4},{4,5},{5,6},{6,7},{8,9},{9,10},{10,11},{11... | collective-permute-start | bytes 786440 | tf_op jit(solution)/shard_map/while/body/eval_jaxpr/ppermute | solution.py:24
  574.2 16.5 %collective-permute-start = (f32[2,4,128,128]{3,2,1,0:T(8,128)}, f32[2,4,128,128]{3,2,1,0:T(8,128)S(1)}, u32[]{:S(2)}, u32[]{:S(2)}) collective-permute-start(f32[2,4,128,128]{3,2,1,0:T(8,128)} %get-tuple-element.467), channel_id=1, source_target_pairs={{0,8},{8,16},{16,24},{24,32},{32,40},{40,48},{48,56},{56,64},{64,7... | collective-permute-start | bytes 1572872 | tf_op jit(solution)/shard_map/while/body/eval_jaxpr/ppermute | solution.py:36
  592.3 12.3 %collective-permute-start.1 = (f32[2,2,128,128]{3,2,1,0:T(8,128)}, f32[2,2,128,128]{3,2,1,0:T(8,128)}, u32[]{:S(2)}, u32[]{:S(2)}) collective-permute-start(f32[2,2,128,128]{3,2,1,0:T(8,128)} %get-tuple-element.442), channel_id=1, source_target_pairs={{1,0},{2,1},{3,2},{4,3},{5,4},{6,5},{7,6},{9,8},{10,9},{11,10},{12... | collective-permute-start | bytes 786440 | tf_op jit(solution)/shard_map/while/body/eval_jaxpr/ppermute | solution.py:26
  593.6 12.2 %collective-permute-start.2 = (f32[2,2,128,128]{3,2,1,0:T(8,128)S(1)}, f32[2,2,128,128]{3,2,1,0:T(8,128)}, u32[]{:S(2)}, u32[]{:S(2)}) collective-permute-start(f32[2,2,128,128]{3,2,1,0:T(8,128)S(1)} %get-tuple-element.443), channel_id=1, source_target_pairs={{0,1},{1,2},{2,3},{3,4},{4,5},{5,6},{6,7},{8,9},{9,10},{10,11},{11... | collective-permute-start | bytes 786440 | tf_op jit(solution)/shard_map/while/body/eval_jaxpr/ppermute | solution.py:24
  614.2 16.5 %collective-permute-start = (f32[2,4,128,128]{3,2,1,0:T(8,128)}, f32[2,4,128,128]{3,2,1,0:T(8,128)S(1)}, u32[]{:S(2)}, u32[]{:S(2)}) collective-permute-start(f32[2,4,128,128]{3,2,1,0:T(8,128)} %get-tuple-element.467), channel_id=1, source_target_pairs={{0,8},{8,16},{16,24},{24,32},{32,40},{40,48},{48,56},{56,64},{64,7... | collective-permute-start | bytes 1572872 | tf_op jit(solution)/shard_map/while/body/eval_jaxpr/ppermute | solution.py:36
  632.3 12.3 %collective-permute-start.1 = (f32[2,2,128,128]{3,2,1,0:T(8,128)}, f32[2,2,128,128]{3,2,1,0:T(8,128)}, u32[]{:S(2)}, u32[]{:S(2)}) collective-permute-start(f32[2,2,128,128]{3,2,1,0:T(8,128)} %get-tuple-element.442), channel_id=1, source_target_pairs={{1,0},{2,1},{3,2},{4,3},{5,4},{6,5},{7,6},{9,8},{10,9},{11,10},{12... | collective-permute-start | bytes 786440 | tf_op jit(solution)/shard_map/while/body/eval_jaxpr/ppermute | solution.py:26
  633.6 12.2 %collective-permute-start.2 = (f32[2,2,128,128]{3,2,1,0:T(8,128)S(1)}, f32[2,2,128,128]{3,2,1,0:T(8,128)}, u32[]{:S(2)}, u32[]{:S(2)}) collective-permute-start(f32[2,2,128,128]{3,2,1,0:T(8,128)S(1)} %get-tuple-element.443), channel_id=1, source_target_pairs={{0,1},{1,2},{2,3},{3,4},{4,5},{5,6},{6,7},{8,9},{9,10},{10,11},{11... | collective-permute-start | bytes 786440 | tf_op jit(solution)/shard_map/while/body/eval_jaxpr/ppermute | solution.py:24
  654.2 16.5 %collective-permute-start = (f32[2,4,128,128]{3,2,1,0:T(8,128)}, f32[2,4,128,128]{3,2,1,0:T(8,128)S(1)}, u32[]{:S(2)}, u32[]{:S(2)}) collective-permute-start(f32[2,4,128,128]{3,2,1,0:T(8,128)} %get-tuple-element.467), channel_id=1, source_target_pairs={{0,8},{8,16},{16,24},{24,32},{32,40},{40,48},{48,56},{56,64},{64,7... | collective-permute-start | bytes 1572872 | tf_op jit(solution)/shard_map/while/body/eval_jaxpr/ppermute | solution.py:36
  672.3 12.3 %collective-permute-start.1 = (f32[2,2,128,128]{3,2,1,0:T(8,128)}, f32[2,2,128,128]{3,2,1,0:T(8,128)}, u32[]{:S(2)}, u32[]{:S(2)}) collective-permute-start(f32[2,2,128,128]{3,2,1,0:T(8,128)} %get-tuple-element.442), channel_id=1, source_target_pairs={{1,0},{2,1},{3,2},{4,3},{5,4},{6,5},{7,6},{9,8},{10,9},{11,10},{12... | collective-permute-start | bytes 786440 | tf_op jit(solution)/shard_map/while/body/eval_jaxpr/ppermute | solution.py:26
  673.5 12.2 %collective-permute-start.2 = (f32[2,2,128,128]{3,2,1,0:T(8,128)S(1)}, f32[2,2,128,128]{3,2,1,0:T(8,128)}, u32[]{:S(2)}, u32[]{:S(2)}) collective-permute-start(f32[2,2,128,128]{3,2,1,0:T(8,128)S(1)} %get-tuple-element.443), channel_id=1, source_target_pairs={{0,1},{1,2},{2,3},{3,4},{4,5},{5,6},{6,7},{8,9},{9,10},{10,11},{11... | collective-permute-start | bytes 786440 | tf_op jit(solution)/shard_map/while/body/eval_jaxpr/ppermute | solution.py:24
  694.2 16.5 %collective-permute-start = (f32[2,4,128,128]{3,2,1,0:T(8,128)}, f32[2,4,128,128]{3,2,1,0:T(8,128)S(1)}, u32[]{:S(2)}, u32[]{:S(2)}) collective-permute-start(f32[2,4,128,128]{3,2,1,0:T(8,128)} %get-tuple-element.467), channel_id=1, source_target_pairs={{0,8},{8,16},{16,24},{24,32},{32,40},{40,48},{48,56},{56,64},{64,7... | collective-permute-start | bytes 1572872 | tf_op jit(solution)/shard_map/while/body/eval_jaxpr/ppermute | solution.py:36
  712.2 12.3 %collective-permute-start.1 = (f32[2,2,128,128]{3,2,1,0:T(8,128)}, f32[2,2,128,128]{3,2,1,0:T(8,128)}, u32[]{:S(2)}, u32[]{:S(2)}) collective-permute-start(f32[2,2,128,128]{3,2,1,0:T(8,128)} %get-tuple-element.442), channel_id=1, source_target_pairs={{1,0},{2,1},{3,2},{4,3},{5,4},{6,5},{7,6},{9,8},{10,9},{11,10},{12... | collective-permute-start | bytes 786440 | tf_op jit(solution)/shard_map/while/body/eval_jaxpr/ppermute | solution.py:26
  713.5 12.2 %collective-permute-start.2 = (f32[2,2,128,128]{3,2,1,0:T(8,128)S(1)}, f32[2,2,128,128]{3,2,1,0:T(8,128)}, u32[]{:S(2)}, u32[]{:S(2)}) collective-permute-start(f32[2,2,128,128]{3,2,1,0:T(8,128)S(1)} %get-tuple-element.443), channel_id=1, source_target_pairs={{0,1},{1,2},{2,3},{3,4},{4,5},{5,6},{6,7},{8,9},{9,10},{10,11},{11... | collective-permute-start | bytes 786440 | tf_op jit(solution)/shard_map/while/body/eval_jaxpr/ppermute | solution.py:24
  (105 other events, 200.8 us)
where the time goes:
time: 746 us; the launch traced here: 734 us
  waiting for transfers between devices  308 us (41%)
  starting transfers between devices  240 us (32%)
  other arithmetic  127 us (17%)
  local copies, waits for them, and re-layouts  57.7 us (8%)
    ppermute x17, waiting for transfers between devices, passed_along(): lax.ppermute(value, axis, [(source, source + steps) for source in range(f...  235 us
    ppermute x21, starting transfers between devices, extended(): lax.ppermute(tail, axis, [(i, (i + 1) % count) for i in range(ends)])  180 us
    mul x18, other arithmetic, jacobi_sweep(): defect = earlier + factor * inflow - pivot_value * current  50.8 us
    ppermute x21, waiting for transfers between devices, extended(): lax.ppermute(head, axis, [((i + 1) % count, i) for i in range(ends)])  48.3 us
    while x192, local copies, waits for them, and re-layouts  35.8 us
    ppermute x17, starting transfers between devices, passed_along(): lax.ppermute(value, axis, [(source, source + steps) for source in range(f...  32.4 us
    select_n x25, other arithmetic, impose(): return jnp.where(outside_right, 0.0, field)  32.2 us
    ppermute x21, starting transfers between devices, extended(): lax.ppermute(head, axis, [((i + 1) % count, i) for i in range(ends)])  27.1 us
  transfers between devices with their start and end apart: 59, of which 58 were waited for; matrix products, arithmetic and copies ran while one was open for 1% of the time, Pallas kernels for 0%

commit v1 on v0

v1 whole, which is shorter than its diff:
```python
import jax
import jax.numpy as jnp
from jax import lax
from jax.experimental import pallas as pl
from jax.experimental.pallas import tpu as pltpu
from jax.sharding import Mesh, PartitionSpec as P

SLABS = 16
BRICKS = 8
PLANES = 4
NX = 32
MIDDLE = 128
LAST = 128
STRIP = 16
HALF = 8
REACH = 10
EDGE = 16
ROWS = STRIP + 2 * EDGE
FRAME = HALF + 2 * EDGE
PART = ROWS // 2

RATE_ALONG = 4.0
RATE_ACROSS = 0.5
ADVECTION = 1.0
DAMPING = 0.8
COARSE = 4.0

ORDER = [0, 2, 4, 6, 7, 5, 3, 1]
AXES = ("chip", "core", "space")
MIB = 1 << 20

VMEM = pl.BlockSpec(memory_space=pltpu.VMEM)
SMEM = pl.BlockSpec(memory_space=pltpu.SMEM)
ANY = pl.BlockSpec(memory_space=pl.ANY)
F32 = jnp.float32


def shape(*dims):
    return jax.ShapeDtypeStruct(dims, F32)


def call(body, outs, in_specs, out_specs, scratch, limit, flops=1 << 20):
    return pl.pallas_call(
        body,
        out_shape=outs,
        in_specs=in_specs,
        out_specs=out_specs,
        scratch_shapes=scratch,
        compiler_params=pltpu.CompilerParams(vmem_limit_bytes=limit * MIB),
    )


def pack_kernel(where, guess, startup, conduct, couple, out, padded):
    core, slab = where[0], where[2]
    last = slab == SLABS - 1
    zero = jnp.zeros((EDGE * PLANES, LAST), F32)
    end = (EDGE + MIDDLE) * PLANES
    for i in range(5):
        padded[i, 0 : EDGE * PLANES] = zero
        padded[i, end : end + EDGE * PLANES] = zero
        for plane in range(PLANES):
            for first in range(0, MIDDLE, 8):
                rows = pl.ds(first, 8)
                if i < 2:
                    value = jnp.where(last, startup[i, plane, rows], guess[i, plane, rows])
                elif i < 4:
                    value = conduct[i - 2, plane, rows]
                else:
                    value = couple[plane, rows]
                padded[i, pl.ds((EDGE + first) * PLANES + plane, 8, stride=PLANES), :] = value
    tall, part = (STRIP + 2 * REACH) * PLANES, PART * PLANES
    for b in range(BRICKS):
        s = ORDER[b]
        start = (EDGE + STRIP * b - REACH) * PLANES
        for i in range(2):
            out[s, i * tall : (i + 1) * tall] = padded[i, start : start + tall]
        start = pl.multiple_of(STRIP * b * PLANES + part * core, 32)
        for i in range(3):
            at = 2 * tall + i * part
            out[s, at : at + part] = padded[2 + i, pl.ds(start, part)]


def unpack_kernel(got, state, coefficients):
    low = lax.broadcasted_iota(jnp.int32, (8, LAST), 0) < PLANES

    def widen(out, i, at, rows):
        for y in range(0, rows, 2):
            for t in range(NX // 8):
                a = got[2 * t, at + PLANES * y : at + PLANES * y + 8]
                b = got[2 * t + 1, at + PLANES * y : at + PLANES * y + 8]
                out[i, y, 8 * t : 8 * t + 8] = jnp.where(low, a, pltpu.roll(b, 4, 0))
                out[i, y + 1, 8 * t : 8 * t + 8] = jnp.where(low, pltpu.roll(a, 4, 0), b)

    tall, part = (STRIP + 2 * REACH) * PLANES, PART * PLANES
    for i in range(2):
        widen(state, i, i * tall, STRIP + 2 * REACH)
    for i in range(3):
        widen(coefficients, i, 2 * tall + i * part, PART)


def restore_kernel(got, out):
    for core in range(2):
        for b in range(BRICKS):
            source = core * BRICKS + ORDER[b]
            first = STRIP * b + HALF * core
            for i in range(2):
                for plane in range(PLANES):
                    out[0, i, plane, first : first + HALF] = got[
                        source, pl.ds(i * HALF * PLANES + plane, HALF, stride=PLANES), :
                    ]


def row_sweep(y, state, weights, earlier, opening, source):
    centre = (state[0, y], state[1, y])
    out = []
    for i in range(2):
        v = centre[i]
        w = lambda k: weights[y, 8 * i + k]
        along = w(0) * pltpu.roll(v, 1, 0) + w(1) * pltpu.roll(v, NX - 1, 0)
        middle = w(2) * state[i, y - 1] + w(3) * state[i, y + 1]
        across = w(4) * pltpu.roll(v, 1, 1) + w(5) * pltpu.roll(v, LAST - 1, 1)
        rest = w(6) * centre[1 - i]
        if opening:
            rest = rest + (0.2 + w(7)) * v
        else:
            rest = rest + 0.2 * v + w(7) * earlier[i, y]
        new = (along + middle) + (across + rest)
        if i == 1 and source is not None:
            new = jnp.concatenate([new[:8] + source[y], new[8:]], axis=0)
        out.append(new)
    return out


def sweep(state, weights, earlier, into, low, high, opening, source=None, unroll=4):
    def step(k, carry):
        for u in range(unroll):
            y = low + unroll * k + u
            new = row_sweep(y, state, weights, earlier, opening, source)
            into[0, y] = new[0]
            into[1, y] = new[1]
        return carry

    lax.fori_loop(0, (high - low + unroll - 1) // unroll, step, 0)


def advances(count, e, v, weights, low, high, source=None):
    def step(m, carry):
        sweep(e, weights, None, v, low + 2 * m + 1, high - 2 * m - 1, True, source)
        sweep(v, weights, e, e, low + 2 * m + 2, high - 2 * m - 2, False, source)
        return carry

    lax.fori_loop(0, count, step, 0)


def relax_kernel(where, begin, mine, other, inlet, w_out, base, give, own, c, w1, w4, feed, e, v, e0, sem):
    core, strip, slab = where[0], where[1], where[2]
    c[:, pl.ds(PART * core, PART)] = mine[...]
    c[:, pl.ds(PART - PART * core, PART)] = other[...]
    first = EDGE - REACH
    e[:, first : first + STRIP + 2 * REACH] = begin[...]
    e0[:, first : first + STRIP + 2 * REACH] = begin[...]

    plane = lax.broadcasted_iota(jnp.int32, (NX, LAST), 0)
    column = lax.broadcasted_iota(jnp.int32, (NX, LAST), 1)
    top = lax.broadcasted_iota(jnp.int32, (8, LAST), 0) == 0

    def weigh(r, carry):
        y = strip * STRIP - EDGE + r
        lower = jnp.where(y == 0, 0.0, 1.0).astype(F32)
        upper = jnp.where(y == MIDDLE - 1, 0.0, 1.0).astype(F32)
        exchange = c[2, r]
        warmth = inlet[pl.ds(jnp.clip(y, 0, MIDDLE - 1), 1), :]
        for i in range(2):
            here = c[i, r]
            xm = jnp.where(plane == 0, 0.0, pltpu.roll(here, 1, 0))
            xp = jnp.where(plane == NX - 1, 0.0, pltpu.roll(here, NX - 1, 0))
            zm = jnp.where(column == 0, 0.0, pltpu.roll(here, 1, 1))
            zp = jnp.where(column == LAST - 1, 0.0, pltpu.roll(here, LAST - 1, 1))
            half_along, half_across = 0.5 * RATE_ALONG, 0.5 * RATE_ACROSS
            wxm = half_along * (here + xm)
            if i == 1:
                wxm = wxm + ADVECTION
            wxp = half_along * (here + xp)
            wym = half_across * (here + c[i, r - 1])
            wyp = half_across * (here + c[i, r + 1])
            wzm = half_across * (here + zm)
            wzp = half_across * (here + zp)
            outflow = wxm + wxp + wym + wyp + wzm + wzp + exchange
            inner = (
                jnp.where(plane == 0, 0.0, wxm),
                jnp.where(plane == NX - 1, 0.0, wxp),
                wym * lower,
                wyp * upper,
                jnp.where(column == 0, 0.0, wzm),
                jnp.where(column == LAST - 1, 0.0, wzp),
                exchange,
            )
            for factor, w in ((1.0, w1), (COARSE, w4)):
                q = DAMPING / (1.0 + factor * outflow)
                fq = factor * q if factor != 1.0 else q
                for k in range(7):
                    w[r, 8 * i + k] = fq * inner[k]
                w[r, 8 * i + 7] = q
                if i == 1 and factor == 1.0:
                    feed[r] = jnp.where(top, (fq * wxm)[:8] * warmth, 0.0)
        return carry

    lax.fori_loop(1, ROWS - 1, weigh, 0)
    spill = pltpu.make_async_copy(w4.at[pl.ds(HALF * core, FRAME)], w_out, sem)
    spill.start()

    sweep(e0, w4, None, v, EDGE - 3, EDGE + STRIP + 3, True)
    sweep(v, w4, e0, e0, EDGE - 2, EDGE + STRIP + 2, False)
    advances(4, e, v, w1, first, first + STRIP + 2 * REACH, feed)
    keep = jnp.where(slab == SLABS - 1, 0.0, 1.0).astype(F32)
    rows = pl.ds(EDGE - 2, STRIP + 4)
    e[:, rows] = e[:, rows] - keep * e0[:, rows]
    sweep(e, w4, None, v, EDGE - 1, EDGE + STRIP + 1, True)
    sweep(v, w4, e, e0, EDGE, EDGE + STRIP, False)
    joined = jnp.where(slab == SLABS - 2, 0.0, 1.0).astype(F32)
    near, far = pl.ds(EDGE, HALF), pl.ds(EDGE + HALF, HALF)
    base[...] = jnp.where(core == 0, joined * e0[:, near], e[:, far])
    give[...] = jnp.where(core == 0, joined * e0[:, far], e[:, near])
    own[:, :HALF] = e[:, near]
    own[:, HALF:] = e[:, far]
    spill.wait()


def load_weights(w_hbm, w, low, high, sem):
    copy = pltpu.make_async_copy(w_hbm.at[pl.ds(low, high - low)], w.at[pl.ds(low, high - low)], sem)
    copy.start()
    return copy


def place(core, e, inward, outward, distance):
    e[:, pl.ds(EDGE + distance - 2 * distance * core, HALF)] = inward[...]
    e[:, pl.ds(EDGE - distance + 2 * distance * core, HALF)] = outward[...]


def far_kernel(where, own, near, far, swapped, swapped_near, local, w_hbm, out, w, e, v, sem):
    core = where[0]
    copy = load_weights(w_hbm, w, 0, FRAME, sem)
    e[:, EDGE : EDGE + HALF] = own[...]
    place(core, e, swapped, near, HALF)
    place(core, e, swapped_near, far, 2 * HALF)
    copy.wait()
    advances(8, e, v, w, 0, FRAME)
    out[...] = local[...] + e[:, EDGE : EDGE + HALF]


def mid_kernel(where, own, near, swapped, local, w_hbm, out, inner, outer, w, e, v, sem):
    core = where[0]
    copy = load_weights(w_hbm, w, HALF, FRAME - HALF, sem)
    e[:, EDGE : EDGE + HALF] = own[...]
    place(core, e, swapped, near, HALF)
    copy.wait()
    advances(4, e, v, w, EDGE - 8, EDGE + HALF + 8)
    out[...] = local[...] + e[:, EDGE : EDGE + HALF]
    inner[...] = out[:, pl.ds(6 - 6 * core, 2)]
    outer[...] = out[:, pl.ds(6 * core, 2)]


def last_kernel(where, own, near, swapped, c_own, c_near, c_swapped, g, w_hbm, out, w, e, v, r, sem):
    core = where[0]
    copy = load_weights(w_hbm, w, HALF, FRAME - HALF, sem)
    e[:, EDGE : EDGE + HALF] = own[...]
    place(core, e, swapped, near, HALF)
    r[:, EDGE : EDGE + HALF] = c_own[...]
    r[:, pl.ds(EDGE + HALF - 10 * core, 2)] = c_swapped[...]
    r[:, pl.ds(EDGE - 2 + 10 * core, 2)] = c_near[...]
    copy.wait()
    advances(2, e, v, w, EDGE - 6, EDGE + HALF + 6)
    rows = pl.ds(EDGE - 2, HALF + 4)
    r[:, rows] = r[:, rows] + e[:, rows]
    sweep(r, w, None, v, EDGE - 1, EDGE + HALF + 1, True)
    sweep(v, w, r, e, EDGE, EDGE + HALF, False)
    rows = pl.ds(EDGE, HALF)
    e[:, rows] = e[:, rows] + g[...]
    low = lax.broadcasted_iota(jnp.int32, (8, LAST), 0) < PLANES
    for label, source in ((0, r), (1, e)):
        for i in range(2):
            for y in range(0, HALF, 2):
                at = (i * HALF + y) * PLANES
                for t in range(NX // 8):
                    a = source[i, EDGE + y, 8 * t : 8 * t + 8]
                    b = source[i, EDGE + y + 1, 8 * t : 8 * t + 8]
                    out[label * BRICKS + 2 * t, at : at + 8] = jnp.where(low, a, pltpu.roll(b, 4, 0))
                    out[label * BRICKS + 2 * t + 1, at : at + 8] = jnp.where(low, pltpu.roll(a, 4, 0), b)


def index(chip, core, strip):
    return (chip * 2 + core) * BRICKS + ORDER[strip]


def sent(value, chips, flip, shift):
    pairs = []
    for source, target in chips:
        for core in range(2):
            for strip in range(BRICKS):
                beside = strip + shift * (1 if core == 0 else -1)
                if 0 <= beside < BRICKS:
                    pairs.append((index(source, core ^ flip, strip), index(target, core, beside)))
    return lax.ppermute(value, AXES, pairs)


SAME = [(c, c) for c in range(8)]
LEAP_FOUR = [((c - 4) % 8, c) for c in range(3, 7)]
LEAP_TWO = [((c - 2) % 8, c) for c in range(1, 7)]
HOME = [((c - 1) % 8, c) for c in range(8)]
HOME_ONE = [((c - 2) % 8, c) for c in range(1, 8)]


def swap(value):
    return sent(value, SAME, 1, 0)


def shards(startup, guess, conduct, couple, inlet):
    chip, core, space = (lax.axis_index(a) for a in AXES)
    slab = chip * 2 + core
    strip = jnp.take(jnp.array([ORDER.index(s) for s in range(BRICKS)], jnp.int32), space)
    where = jnp.stack([core, strip, slab]).astype(jnp.int32)

    tall = STRIP + 2 * REACH
    chunk = (2 * tall + 3 * PART) * PLANES
    half = shape(2, HALF, NX, LAST)
    packed = call(
        pack_kernel,
        shape(BRICKS, chunk, LAST),
        [SMEM] + [VMEM] * 4,
        VMEM,
        [pltpu.VMEM((5, (MIDDLE + 2 * EDGE) * PLANES, LAST), F32)],
        16,
    )(where, guess[0], startup, conduct, couple)
    got = lax.all_to_all(packed, "space", 0, 0, tiled=True)
    begin, mine = call(
        unpack_kernel, (shape(2, tall, NX, LAST), shape(3, PART, NX, LAST)), [VMEM], (VMEM, VMEM), [], 16
    )(got)
    other = swap(mine)

    field = pltpu.VMEM((2, ROWS + 4, NX, LAST), F32)
    w_all = pltpu.VMEM((ROWS, 16, NX, LAST), F32)
    weights, base, give, g = call(
        relax_kernel,
        (shape(FRAME, 16, NX, LAST), half, half, shape(2, STRIP, NX, LAST)),
        [SMEM] + [VMEM] * 4,
        (ANY, VMEM, VMEM, VMEM),
        [
            pltpu.VMEM((3, ROWS, NX, LAST), F32),
            w_all,
            w_all,
            pltpu.VMEM((ROWS, 8, LAST), F32),
            field,
            field,
            field,
            pltpu.SemaphoreType.DMA,
        ],
        48,
    )(where, begin, mine, other, inlet)
    u = base + swap(give)
    g_far = sent(g[:, HALF:], SAME, 1, 0)
    g_half = jnp.where(core == 0, g[:, :HALF], g_far)

    frame = pltpu.VMEM((2, FRAME + 4, NX, LAST), F32)
    w_frame = pltpu.VMEM((FRAME + 4, 16, NX, LAST), F32)
    own = sent(u, LEAP_FOUR, 0, 0)
    near = sent(u, LEAP_FOUR, 1, 1)
    far = sent(u, LEAP_FOUR, 0, 1)
    x = call(
        far_kernel,
        half,
        [SMEM] + [VMEM] * 6 + [ANY],
        VMEM,
        [w_frame, frame, frame, pltpu.SemaphoreType.DMA],
        32,
    )(where, own, near, far, swap(own), swap(near), u, weights)

    own = sent(x, LEAP_TWO, 0, 0)
    near = sent(x, LEAP_TWO, 1, 1)
    rim = shape(2, 2, NX, LAST)
    y, inner, outer = call(
        mid_kernel,
        (half, rim, rim),
        [SMEM] + [VMEM] * 4 + [ANY],
        (VMEM,) * 3,
        [w_frame, frame, frame, pltpu.SemaphoreType.DMA],
        32,
    )(where, own, near, swap(own), x, weights)

    own = sent(y, HOME_ONE, 0, 0)
    near = sent(y, HOME_ONE, 1, 1)
    c_own = sent(y, HOME, 0, 0)
    c_near = sent(outer, HOME, 1, 1)
    c_swapped = sent(inner, HOME, 1, 0)
    done = call(
        last_kernel,
        shape(2 * BRICKS, 2 * HALF * PLANES, LAST),
        [SMEM] + [VMEM] * 7 + [ANY],
        VMEM,
        [w_frame, frame, frame, frame, pltpu.SemaphoreType.DMA],
        32,
    )(where, own, near, swap(own), c_own, c_near, c_swapped, g_half, weights)
    back = lax.all_to_all(done, ("core", "space"), 0, 0, tiled=True)
    return call(restore_kernel, shape(1, 2, PLANES, MIDDLE, LAST), [VMEM], VMEM, [], 16)(back)


def solution(mesh):
    fine = Mesh(mesh.devices.reshape(SLABS // 2, 2, BRICKS), AXES)
    slabs = ("chip", "core")
    return jax.shard_map(
        shards,
        mesh=fine,
        in_specs=(
            P(None, "space", None, None),
            P(slabs, None, "space", None, None),
            P(None, "space", None, None),
            P("space", None, None),
            P(),
        ),
        out_specs=P(slabs, None, "space", None, None),
        check_vma=False,
    )
```

time: 746 us -> 188 us (0.25); the launches traced: 734 us -> 187 us
  waiting for transfers between devices: 308 us -> 22.2 us
  starting transfers between devices: 240 us -> 47.1 us
  other arithmetic: 127 us -> 0.16 us
  blocking collectives: 0 us -> 58.8 us
  Pallas kernels: 0 us -> 44.9 us
  local copies, waits for them, and re-layouts: 57.7 us -> 13.4 us
    ppermute x59 -> x17, waiting for transfers between devices: 308 us -> 22.2 us  [sent(): return lax.ppermute(value, AXES, pairs)]
    ppermute x59 -> x17, starting transfers between devices: 240 us -> 47.1 us  [sent(): return lax.ppermute(value, AXES, pairs)]
    all_to_all x0 -> x2, blocking collectives: none -> 58.8 us  [the longest x1 35 us: shards(): got = lax.all_to_all(packed, 'space', 0, 0, tiled=True)]
    mul x18 -> x0, other arithmetic: 50.8 us -> none  [jacobi_sweep(): defect = earlier + factor * inflow - pivot_value * current]
    pallas_call x0 -> x7, Pallas kernels: none -> 44.9 us  [the longest x1 17.7 us: shards(): call(relax_kernel, (shape(FRAME, 16, NX, LAST), half, half, shape(2, STRI...]
    add x34 -> x1, other arithmetic: 40.7 us -> 0.04 us  [shards(): u = base + swap(give)]
    while x192 -> x0, local copies, waits for them, and re-layouts: 35.8 us -> none
    select_n x42 -> x1, other arithmetic: 33.4 us -> 0.04 us  [shards(): g_half = jnp.where(core == 0, g[:, :HALF], g_far)]
  transfers between devices with their start and end apart: 59 -> 17, of which waited for: 58 -> 8; matrix products, arithmetic and copies ran while one was open for 1% -> 0% of each run, Pallas kernels for 0% -> 0%
where the time goes in v1:
time: 188 us; the launch traced here: 187 us
  blocking collectives  58.8 us (31%)
  starting transfers between devices  47.1 us (25%)
  Pallas kernels  44.9 us (24%)
  waiting for transfers between devices  22.2 us (12%)
  local copies, waits for them, and re-layouts  13.4 us (7%)
    ppermute x17, starting transfers between devices, sent(): return lax.ppermute(value, AXES, pairs)  47.1 us
    all_to_all x1, blocking collectives, shards(): got = lax.all_to_all(packed, 'space', 0, 0, tiled=True)  35 us
    all_to_all x1, blocking collectives, shards(): back = lax.all_to_all(done, ('core', 'space'), 0, 0, tiled=True)  23.8 us
    ppermute x17, waiting for transfers between devices, sent(): return lax.ppermute(value, AXES, pairs)  22.2 us
    pallas_call x1, Pallas kernels, shards(): call(relax_kernel, (shape(FRAME, 16, NX, LAST), half, half, shape(2, STRI...  17.7 us
    pallas_call x1, Pallas kernels, shards(): call(far_kernel, half, [SMEM] + [VMEM] * 6 + [ANY], VMEM, [w_frame, frame...  15.4 us
    unnamed x14, local copies, waits for them, and re-layouts  12 us
    pallas_call x1, Pallas kernels, shards(): call(mid_kernel, (half, rim, rim), [SMEM] + [VMEM] * 4 + [ANY], (VMEM,) *...  5.76 us
  transfers between devices with their start and end apart: 17, of which 8 were waited for; matrix products, arithmetic and copies ran while one was open for 0% of the time, Pallas kernels for 0%

profile of v1, /device:TPU:4, one launch (start us, length us, event | category | flops | bytes accessed | tf_op | source)
XLA Modules:
  0.0 187.5 jit_solution(483912140831094596)
XLA Ops:
  0.0 1.3 dynamic-slice.4
  2.0 0.1 pad_add_fusion.where
  2.1 0.0 copy-start.2
  2.1 1.0 copy-done.2
  3.1 0.0 copy-start.3
  3.1 1.0 copy-done.3
  4.2 0.0 copy-start.4
  4.2 1.0 copy-done.4
  5.2 0.0 copy-start.5
  5.2 0.9 copy-done.5
  6.2 0.9 shard_map.64
  7.0 35.0 %all_to_all.10.got = f32[8,576,128]{2,1,0:T(8,128)S(1)} all-to-all(f32[8,576,128]{2,1,0:T(8,128)S(1)} %shard_map.64), channel_id=1, replica_groups=mesh['chip'=8,'core'=2,'space'=8] {'space'}, dimensions={0} | all-to-all | bytes 4718592 | tf_op jit(solution)/shard_map/all_to_all | solution.py:334
  42.0 0.0 copy-start.6
  42.0 0.2 shard_map.65
  42.2 0.1 collective-permute-start
  42.3 2.8 %collective-permute-done.other = f32[3,24,32,128]{3,2,1,0:T(8,128)S(1)} collective-permute-done((f32[3,24,32,128]{3,2,1,0:T(8,128)S(1)}, f32[3,24,32,128]{3,2,1,0:T(8,128)S(1)}, u32[]{:S(2)}, u32[]{:S(2)}) %collective-permute-start) | collective-permute-done | bytes 1179680 | tf_op jit(solution)/shard_map/ppermute | solution.py:303
  45.1 0.0 copy-done.6
  45.1 17.7 %shard_map.66 = (f32[40,16,32,128]{3,2,1,0:T(8,128)}, f32[2,8,32,128]{3,2,1,0:T(8,128)S(1)}, f32[2,8,32,128]{3,2,1,0:T(8,128)S(1)}, f32[2,16,32,128]{3,2,1,0:T(8,128)S(1)}) custom-call(s32[3]{0:T(128)S(1)} %pad_add_fusion.where, f32[2,36,32,128]{3,2,1,0:T(8,128)S(1)} %get-tuple-element.14.begin, f32[3,24,32,128]{3,2,1,0:T(8,128)S(1)} %get-tuple-element.15.mine, ...), custom_call_target="tpu_custom_call" | custom-call | tf_op jit(solution)/shard_map/pallas_call | solution.py:342
  62.9 0.2 collective-permute-start.1
  63.1 1.4 collective-permute-done.1
  64.5 0.7 collective-permute-start.3
  65.2 1.3 collective-permute-start.2
  66.5 0.7 collective-permute-start.4
  67.2 0.0 collective-permute-done.3.near
  67.2 10.4 %collective-permute-start.6 = (f32[2,8,32,128]{3,2,1,0:T(8,128)S(1)}, f32[2,8,32,128]{3,2,1,0:T(8,128)S(1)}, u32[]{:S(2)}, u32[]{:S(2)}) collective-permute-start(f32[2,8,32,128]{3,2,1,0:T(8,128)S(1)} %collective-permute-done.3.near), channel_id=1, source_target_pairs={{8,0},{10,2},{12,4},{14,6},{15,7},{13,5},{11,3},{9,1},{0,8},{2,10}... | collective-permute-start | bytes 786440 | tf_op jit(solution)/shard_map/ppermute | solution.py:303
  77.6 0.3 collective-permute-done.2.own
  77.9 2.0 %collective-permute-start.5 = (f32[2,8,32,128]{3,2,1,0:T(8,128)S(1)}, f32[2,8,32,128]{3,2,1,0:T(8,128)S(1)}, u32[]{:S(2)}, u32[]{:S(2)}) collective-permute-start(f32[2,8,32,128]{3,2,1,0:T(8,128)S(1)} %collective-permute-done.2.own), channel_id=1, source_target_pairs={{8,0},{10,2},{12,4},{14,6},{15,7},{13,5},{11,3},{9,1},{0,8},{2,10}... | collective-permute-start | bytes 786440 | tf_op jit(solution)/shard_map/ppermute | solution.py:303
  79.8 0.0 collective-permute-done.4.far
  79.8 0.0 collective-permute-done.6.swapped_near
  79.8 1.2 collective-permute-done.5.swapped
  81.0 0.0 copy-start
  81.0 4.0 %copy-done = f32[40,16,32,128]{3,2,1,0:T(8,128)S(1)} copy-done((f32[40,16,32,128]{3,2,1,0:T(8,128)S(1)}, f32[40,16,32,128]{3,2,1,0:T(8,128)}, u32[]{:S(2)}) %copy-start) | copy-done | bytes 10485784
  85.0 15.4 %shard_map.67.local = f32[2,8,32,128]{3,2,1,0:T(8,128)S(1)} custom-call(s32[3]{0:T(128)S(1)} %pad_add_fusion.where, f32[2,8,32,128]{3,2,1,0:T(8,128)S(1)} %collective-permute-done.2.own, f32[2,8,32,128]{3,2,1,0:T(8,128)S(1)} %collective-permute-done.3.near, f32[2,8,32,128]{3,2,1,0:T(8,128)S(1)} %collective-permute-done.4.far, ...), custom_call_target="tpu_custom_call" | custom-call | tf_op jit(solution)/shard_map/pallas_call | solution.py:368
  100.3 5.8 %collective-permute-start.7 = (f32[2,8,32,128]{3,2,1,0:T(8,128)S(1)}, f32[2,8,32,128]{3,2,1,0:T(8,128)S(1)}, u32[]{:S(2)}, u32[]{:S(2)}) collective-permute-start(f32[2,8,32,128]{3,2,1,0:T(8,128)S(1)} %shard_map.67.local), channel_id=1, source_target_pairs={{112,16},{114,18},{116,20},{118,22},{119,23},{117,21},{115,19},{11... | collective-permute-start | bytes 786440 | tf_op jit(solution)/shard_map/ppermute | solution.py:303
  106.1 0.7 collective-permute-start.8
  106.8 5.7 %collective-permute-done.7.own = f32[2,8,32,128]{3,2,1,0:T(8,128)S(1)} collective-permute-done((f32[2,8,32,128]{3,2,1,0:T(8,128)S(1)}, f32[2,8,32,128]{3,2,1,0:T(8,128)S(1)}, u32[]{:S(2)}, u32[]{:S(2)}) %collective-permute-start.7) | collective-permute-done | bytes 262176 | tf_op jit(solution)/shard_map/ppermute | solution.py:303
  112.5 4.1 %collective-permute-start.9 = (f32[2,8,32,128]{3,2,1,0:T(8,128)S(1)}, f32[2,8,32,128]{3,2,1,0:T(8,128)S(1)}, u32[]{:S(2)}, u32[]{:S(2)}) collective-permute-start(f32[2,8,32,128]{3,2,1,0:T(8,128)S(1)} %collective-permute-done.7.own), channel_id=1, source_target_pairs={{8,0},{10,2},{12,4},{14,6},{15,7},{13,5},{11,3},{9,1},{0,8},{2,10}... | collective-permute-start | bytes 786440 | tf_op jit(solution)/shard_map/ppermute | solution.py:303
  116.6 0.0 collective-permute-done.8.near
  116.6 1.2 collective-permute-done.9.swapped
  117.8 5.8 %shard_map.68 = (f32[2,8,32,128]{3,2,1,0:T(8,128)S(1)}, f32[2,2,32,128]{3,2,1,0:T(8,128)S(1)}, f32[2,2,32,128]{3,2,1,0:T(8,128)S(1)}) custom-call(s32[3]{0:T(128)S(1)} %pad_add_fusion.where, f32[2,8,32,128]{3,2,1,0:T(8,128)S(1)} %collective-permute-done.7.own, f32[2,8,32,128]{3,2,1,0:T(8,128)S(1)} %collective-permute-done.8.near, ...), custom_call_target="tpu_custom_call" | custom-call | tf_op jit(solution)/shard_map/pallas_call | solution.py:380
  123.5 3.4 %collective-permute-start.10 = (f32[2,8,32,128]{3,2,1,0:T(8,128)S(1)}, f32[2,8,32,128]{3,2,1,0:T(8,128)S(1)}, u32[]{:S(2)}, u32[]{:S(2)}) collective-permute-start(f32[2,8,32,128]{3,2,1,0:T(8,128)S(1)} %get-tuple-element.19), channel_id=1, source_target_pairs={{112,16},{114,18},{116,20},{118,22},{119,23},{117,21},{115,19},{11... | collective-permute-start | bytes 786440 | tf_op jit(solution)/shard_map/ppermute | solution.py:303
  127.0 5.6 %collective-permute-start.16 = (f32[2,8,32,128]{3,2,1,0:T(8,128)S(1)}, f32[2,8,32,128]{3,2,1,0:T(8,128)S(1)}, u32[]{:S(2)}, u32[]{:S(2)}) collective-permute-start(f32[2,8,32,128]{3,2,1,0:T(8,128)S(1)} %slice.7), channel_id=1, source_target_pairs={{8,0},{10,2},{12,4},{14,6},{15,7},{13,5},{11,3},{9,1},{0,8},{2,10}... | collective-permute-start | bytes 786440 | tf_op jit(solution)/shard_map/ppermute | solution.py:303
  132.6 0.0 collective-permute-start.13
  132.6 0.7 collective-permute-start.11
  133.2 2.5 %collective-permute-done.10.own = f32[2,8,32,128]{3,2,1,0:T(8,128)S(1)} collective-permute-done((f32[2,8,32,128]{3,2,1,0:T(8,128)S(1)}, f32[2,8,32,128]{3,2,1,0:T(8,128)S(1)}, u32[]{:S(2)}, u32[]{:S(2)}) %collective-permute-start.10) | collective-permute-done | bytes 262176 | tf_op jit(solution)/shard_map/ppermute | solution.py:303
  135.7 7.1 %collective-permute-start.12 = (f32[2,8,32,128]{3,2,1,0:T(8,128)S(1)}, f32[2,8,32,128]{3,2,1,0:T(8,128)S(1)}, u32[]{:S(2)}, u32[]{:S(2)}) collective-permute-start(f32[2,8,32,128]{3,2,1,0:T(8,128)S(1)} %collective-permute-done.10.own), channel_id=1, source_target_pairs={{8,0},{10,2},{12,4},{14,6},{15,7},{13,5},{11,3},{9,1},{0,8},{2,10}... | collective-permute-start | bytes 786440 | tf_op jit(solution)/shard_map/ppermute | solution.py:303
  142.8 0.7 collective-permute-start.14
  143.5 0.0 collective-permute-done.16
  143.5 3.9 %collective-permute-start.15 = (f32[2,2,32,128]{3,2,1,0:T(8,128)S(1)}, f32[2,2,32,128]{3,2,1,0:T(8,128)S(1)}, u32[]{:S(2)}, u32[]{:S(2)}) collective-permute-start(f32[2,2,32,128]{3,2,1,0:T(8,128)S(1)} %get-tuple-element.21), channel_id=1, source_target_pairs={{120,0},{122,2},{124,4},{126,6},{127,7},{125,5},{123,3},{121,1},{1... | collective-permute-start | bytes 196616 | tf_op jit(solution)/shard_map/ppermute | solution.py:303
  147.4 0.0 collective-permute-done.14.c_near
  147.4 7.2 %collective-permute-done.15.c_swapped = f32[2,2,32,128]{3,2,1,0:T(8,128)S(1)} collective-permute-done((f32[2,2,32,128]{3,2,1,0:T(8,128)S(1)}, f32[2,2,32,128]{3,2,1,0:T(8,128)S(1)}, u32[]{:S(2)}, u32[]{:S(2)}) %collective-permute-start.15) | collective-permute-done | bytes 65568 | tf_op jit(solution)/shard_map/ppermute | solution.py:303
  154.6 0.0 collective-permute-done.13.c_own
  154.6 0.0 collective-permute-done.11.near
  154.7 0.0 collective-permute-done.12.swapped
  154.7 0.0 copy-start.1
  154.7 4.0 %copy-done.1 = f32[40,16,32,128]{3,2,1,0:T(8,128)S(1)} copy-done((f32[40,16,32,128]{3,2,1,0:T(8,128)S(1)}, f32[40,16,32,128]{3,2,1,0:T(8,128)}, u32[]{:S(2)}) %copy-start.1) | copy-done | bytes 10485784
  158.6 4.2 %shard_map.69 = f32[16,64,128]{2,1,0:T(8,128)S(1)} custom-call(s32[3]{0:T(128)S(1)} %pad_add_fusion.where, f32[2,8,32,128]{3,2,1,0:T(8,128)S(1)} %collective-permute-done.10.own, f32[2,8,32,128]{3,2,1,0:T(8,128)S(1)} %collective-permute-done.11.near, f32[2,8,32,128]{3,2,1,0:T(8,128)S(1)} %collective-permute-done.12.swapped, ...), custom_call_target="tpu_custom_call" | custom-call | tf_op jit(solution)/shard_map/pallas_call | solution.py:394
  162.9 23.8 %all_to_all.11.got = f32[16,64,128]{2,1,0:T(8,128)S(1)} all-to-all(f32[16,64,128]{2,1,0:T(8,128)S(1)} %shard_map.69), channel_id=1, replica_groups=mesh['chip'=8,'core'=2,'space'=8] {'core','space'}, dimensions={0} | all-to-all | bytes 1048576 | tf_op jit(solution)/shard_map/all_to_all | solution.py:402
  186.6 0.8 shard_map.70
  (3 shorter events, 0.1 us)
Async XLA Ops:
  2.1 1.0 copy-start.2
  3.1 1.0 copy-start.3
  4.2 1.0 copy-start.4
  5.2 0.9 copy-start.5
  42.0 3.1 %copy-start.6 = (f32[128,128]{1,0:T(8,128)S(1)}, f32[128,128]{1,0:T(8,128)}, u32[]{:S(2)}) copy-start(f32[128,128]{1,0:T(8,128)} %inlet.1) | copy-start | bytes 196612
  42.2 2.9 %collective-permute-start = (f32[3,24,32,128]{3,2,1,0:T(8,128)S(1)}, f32[3,24,32,128]{3,2,1,0:T(8,128)S(1)}, u32[]{:S(2)}, u32[]{:S(2)}) collective-permute-start(f32[3,24,32,128]{3,2,1,0:T(8,128)S(1)} %get-tuple-element.15.mine), channel_id=1, source_target_pairs={{8,0},{10,2},{12,4},{14,6},{15,7},{13,5},{11,3},{9,1},{0,8},{2,10}... | collective-permute-start | bytes 3538952 | tf_op jit(solution)/shard_map/ppermute | solution.py:303
  62.9 1.6 collective-permute-start.1
  64.5 2.7 %collective-permute-start.3 = (f32[2,8,32,128]{3,2,1,0:T(8,128)S(1)}, f32[2,8,32,128]{3,2,1,0:T(8,128)S(1)}, u32[]{:S(2)}, u32[]{:S(2)}) collective-permute-start(f32[2,8,32,128]{3,2,1,0:T(8,128)S(1)} %add.12.local), channel_id=1, source_target_pairs={{120,50},{122,52},{124,54},{126,55},{127,53},{125,51},{123,49},{11... | collective-permute-start | bytes 786440 | tf_op jit(solution)/shard_map/ppermute | solution.py:303
  65.2 12.6 %collective-permute-start.2 = (f32[2,8,32,128]{3,2,1,0:T(8,128)S(1)}, f32[2,8,32,128]{3,2,1,0:T(8,128)S(1)}, u32[]{:S(2)}, u32[]{:S(2)}) collective-permute-start(f32[2,8,32,128]{3,2,1,0:T(8,128)S(1)} %add.12.local), channel_id=1, source_target_pairs={{112,48},{114,50},{116,52},{118,54},{119,55},{117,53},{115,51},{11... | collective-permute-start | bytes 786440 | tf_op jit(solution)/shard_map/ppermute | solution.py:303
  66.5 13.3 %collective-permute-start.4 = (f32[2,8,32,128]{3,2,1,0:T(8,128)S(1)}, f32[2,8,32,128]{3,2,1,0:T(8,128)S(1)}, u32[]{:S(2)}, u32[]{:S(2)}) collective-permute-start(f32[2,8,32,128]{3,2,1,0:T(8,128)S(1)} %add.12.local), channel_id=1, source_target_pairs={{112,50},{114,52},{116,54},{118,55},{119,53},{117,51},{115,49},{12... | collective-permute-start | bytes 786440 | tf_op jit(solution)/shard_map/ppermute | solution.py:303
  67.2 12.6 %collective-permute-start.6 = (f32[2,8,32,128]{3,2,1,0:T(8,128)S(1)}, f32[2,8,32,128]{3,2,1,0:T(8,128)S(1)}, u32[]{:S(2)}, u32[]{:S(2)}) collective-permute-start(f32[2,8,32,128]{3,2,1,0:T(8,128)S(1)} %collective-permute-done.3.near), channel_id=1, source_target_pairs={{8,0},{10,2},{12,4},{14,6},{15,7},{13,5},{11,3},{9,1},{0,8},{2,10}... | collective-permute-start | bytes 786440 | tf_op jit(solution)/shard_map/ppermute | solution.py:303
  77.9 3.1 %collective-permute-start.5 = (f32[2,8,32,128]{3,2,1,0:T(8,128)S(1)}, f32[2,8,32,128]{3,2,1,0:T(8,128)S(1)}, u32[]{:S(2)}, u32[]{:S(2)}) collective-permute-start(f32[2,8,32,128]{3,2,1,0:T(8,128)S(1)} %collective-permute-done.2.own), channel_id=1, source_target_pairs={{8,0},{10,2},{12,4},{14,6},{15,7},{13,5},{11,3},{9,1},{0,8},{2,10}... | collective-permute-start | bytes 786440 | tf_op jit(solution)/shard_map/ppermute | solution.py:303
  81.0 4.0 %copy-start = (f32[40,16,32,128]{3,2,1,0:T(8,128)S(1)}, f32[40,16,32,128]{3,2,1,0:T(8,128)}, u32[]{:S(2)}) copy-start(f32[40,16,32,128]{3,2,1,0:T(8,128)} %get-tuple-element.18.w_hbm) | copy-start | bytes 31457284
  100.3 12.2 %collective-permute-start.7 = (f32[2,8,32,128]{3,2,1,0:T(8,128)S(1)}, f32[2,8,32,128]{3,2,1,0:T(8,128)S(1)}, u32[]{:S(2)}, u32[]{:S(2)}) collective-permute-start(f32[2,8,32,128]{3,2,1,0:T(8,128)S(1)} %shard_map.67.local), channel_id=1, source_target_pairs={{112,16},{114,18},{116,20},{118,22},{119,23},{117,21},{115,19},{11... | collective-permute-start | bytes 786440 | tf_op jit(solution)/shard_map/ppermute | solution.py:303
  106.1 10.5 %collective-permute-start.8 = (f32[2,8,32,128]{3,2,1,0:T(8,128)S(1)}, f32[2,8,32,128]{3,2,1,0:T(8,128)S(1)}, u32[]{:S(2)}, u32[]{:S(2)}) collective-permute-start(f32[2,8,32,128]{3,2,1,0:T(8,128)S(1)} %shard_map.67.local), channel_id=1, source_target_pairs={{120,18},{122,20},{124,22},{126,23},{127,21},{125,19},{123,17},{11... | collective-permute-start | bytes 786440 | tf_op jit(solution)/shard_map/ppermute | solution.py:303
  112.5 5.3 %collective-permute-start.9 = (f32[2,8,32,128]{3,2,1,0:T(8,128)S(1)}, f32[2,8,32,128]{3,2,1,0:T(8,128)S(1)}, u32[]{:S(2)}, u32[]{:S(2)}) collective-permute-start(f32[2,8,32,128]{3,2,1,0:T(8,128)S(1)} %collective-permute-done.7.own), channel_id=1, source_target_pairs={{8,0},{10,2},{12,4},{14,6},{15,7},{13,5},{11,3},{9,1},{0,8},{2,10}... | collective-permute-start | bytes 786440 | tf_op jit(solution)/shard_map/ppermute | solution.py:303
  123.5 12.2 %collective-permute-start.10 = (f32[2,8,32,128]{3,2,1,0:T(8,128)S(1)}, f32[2,8,32,128]{3,2,1,0:T(8,128)S(1)}, u32[]{:S(2)}, u32[]{:S(2)}) collective-permute-start(f32[2,8,32,128]{3,2,1,0:T(8,128)S(1)} %get-tuple-element.19), channel_id=1, source_target_pairs={{112,16},{114,18},{116,20},{118,22},{119,23},{117,21},{115,19},{11... | collective-permute-start | bytes 786440 | tf_op jit(solution)/shard_map/ppermute | solution.py:303
  127.0 16.5 %collective-permute-start.16 = (f32[2,8,32,128]{3,2,1,0:T(8,128)S(1)}, f32[2,8,32,128]{3,2,1,0:T(8,128)S(1)}, u32[]{:S(2)}, u32[]{:S(2)}) collective-permute-start(f32[2,8,32,128]{3,2,1,0:T(8,128)S(1)} %slice.7), channel_id=1, source_target_pairs={{8,0},{10,2},{12,4},{14,6},{15,7},{13,5},{11,3},{9,1},{0,8},{2,10}... | collective-permute-start | bytes 786440 | tf_op jit(solution)/shard_map/ppermute | solution.py:303
  132.6 22.1 %collective-permute-start.13 = (f32[2,8,32,128]{3,2,1,0:T(8,128)S(1)}, f32[2,8,32,128]{3,2,1,0:T(8,128)S(1)}, u32[]{:S(2)}, u32[]{:S(2)}) collective-permute-start(f32[2,8,32,128]{3,2,1,0:T(8,128)S(1)} %get-tuple-element.19), channel_id=1, source_target_pairs={{112,0},{114,2},{116,4},{118,6},{119,7},{117,5},{115,3},{113,1},{1... | collective-permute-start | bytes 786440 | tf_op jit(solution)/shard_map/ppermute | solution.py:303
  132.6 22.1 %collective-permute-start.11 = (f32[2,8,32,128]{3,2,1,0:T(8,128)S(1)}, f32[2,8,32,128]{3,2,1,0:T(8,128)S(1)}, u32[]{:S(2)}, u32[]{:S(2)}) collective-permute-start(f32[2,8,32,128]{3,2,1,0:T(8,128)S(1)} %get-tuple-element.19), channel_id=1, source_target_pairs={{120,18},{122,20},{124,22},{126,23},{127,21},{125,19},{123,17},{11... | collective-permute-start | bytes 786440 | tf_op jit(solution)/shard_map/ppermute | solution.py:303
  135.7 18.9 %collective-permute-start.12 = (f32[2,8,32,128]{3,2,1,0:T(8,128)S(1)}, f32[2,8,32,128]{3,2,1,0:T(8,128)S(1)}, u32[]{:S(2)}, u32[]{:S(2)}) collective-permute-start(f32[2,8,32,128]{3,2,1,0:T(8,128)S(1)} %collective-permute-done.10.own), channel_id=1, source_target_pairs={{8,0},{10,2},{12,4},{14,6},{15,7},{13,5},{11,3},{9,1},{0,8},{2,10}... | collective-permute-start | bytes 786440 | tf_op jit(solution)/shard_map/ppermute | solution.py:303
  142.8 4.6 %collective-permute-start.14 = (f32[2,2,32,128]{3,2,1,0:T(8,128)S(1)}, f32[2,2,32,128]{3,2,1,0:T(8,128)S(1)}, u32[]{:S(2)}, u32[]{:S(2)}) collective-permute-start(f32[2,2,32,128]{3,2,1,0:T(8,128)S(1)} %get-tuple-element.20), channel_id=1, source_target_pairs={{120,2},{122,4},{124,6},{126,7},{127,5},{125,3},{123,1},{114,8},{1... | collective-permute-start | bytes 196616 | tf_op jit(solution)/shard_map/ppermute | solution.py:303
  143.5 11.1 %collective-permute-start.15 = (f32[2,2,32,128]{3,2,1,0:T(8,128)S(1)}, f32[2,2,32,128]{3,2,1,0:T(8,128)S(1)}, u32[]{:S(2)}, u32[]{:S(2)}) collective-permute-start(f32[2,2,32,128]{3,2,1,0:T(8,128)S(1)} %get-tuple-element.21), channel_id=1, source_target_pairs={{120,0},{122,2},{124,4},{126,6},{127,7},{125,5},{123,3},{121,1},{1... | collective-permute-start | bytes 196616 | tf_op jit(solution)/shard_map/ppermute | solution.py:303
  154.7 4.0 %copy-start.1 = (f32[40,16,32,128]{3,2,1,0:T(8,128)S(1)}, f32[40,16,32,128]{3,2,1,0:T(8,128)}, u32[]{:S(2)}) copy-start(f32[40,16,32,128]{3,2,1,0:T(8,128)} %get-tuple-element.18.w_hbm) | copy-start | bytes 31457284

commit v2 on v1

--- a/solution.py
+++ b/solution.py
@@ -16,7 +16,7 @@
 REACH = 10
 EDGE = 16
 ROWS = STRIP + 2 * EDGE
-FRAME = HALF + 2 * EDGE
+HELD = ROWS + 4
 PART = ROWS // 2
 
 RATE_ALONG = 4.0
@@ -30,8 +30,7 @@
 MIB = 1 << 20
 
 VMEM = pl.BlockSpec(memory_space=pltpu.VMEM)
-SMEM = pl.BlockSpec(memory_space=pltpu.SMEM)
-ANY = pl.BlockSpec(memory_space=pl.ANY)
+HBM = pl.BlockSpec(memory_space=pltpu.HBM)
 F32 = jnp.float32
 
 
@@ -39,9 +38,10 @@
     return jax.ShapeDtypeStruct(dims, F32)
 
 
-def call(body, outs, in_specs, out_specs, scratch, limit, flops=1 << 20):
+def call(body, outs, in_specs, out_specs, scratch, limit, flops=0):
     return pl.pallas_call(
         body,
+        cost_estimate=pl.CostEstimate(flops=flops, bytes_accessed=1 << 20, transcendentals=0) if flops else None,
         out_shape=outs,
         in_specs=in_specs,
         out_specs=out_specs,
@@ -50,23 +50,41 @@
     )
 
 
-def pack_kernel(where, guess, startup, conduct, couple, out, padded):
-    core, slab = where[0], where[2]
+def position():
+    chip, core, space = (lax.axis_index(a) for a in AXES)
+    y, odd = space // 2, space % 2
+    return core, jnp.where(odd == 0, y, BRICKS - 1 - y), chip * 2 + core
+
+
+def pack_kernel(startup, guess, conduct, couple, out, padded, state, others, sems):
+    core, _, slab = position()
     last = slab == SLABS - 1
+    from_startup = [pltpu.make_async_copy(startup.at[i], state.at[i], sems.at[i]) for i in range(2)]
+    from_guess = [pltpu.make_async_copy(guess.at[0, i], state.at[i], sems.at[i]) for i in range(2)]
+    copies = [pltpu.make_async_copy(conduct.at[i], others.at[i], sems.at[2 + i]) for i in range(2)]
+    copies.append(pltpu.make_async_copy(couple, others.at[2], sems.at[4]))
+
+    @pl.when(last)
+    def _():
+        for copy in from_startup:
+            copy.start()
+
+    @pl.when(jnp.logical_not(last))
+    def _():
+        for copy in from_guess:
+            copy.start()
+
+    for copy in copies:
+        copy.start()
     zero = jnp.zeros((EDGE * PLANES, LAST), F32)
     end = (EDGE + MIDDLE) * PLANES
     for i in range(5):
         padded[i, 0 : EDGE * PLANES] = zero
         padded[i, end : end + EDGE * PLANES] = zero
+        (from_guess + copies)[i].wait()
         for plane in range(PLANES):
             for first in range(0, MIDDLE, 8):
-                rows = pl.ds(first, 8)
-                if i < 2:
-                    value = jnp.where(last, startup[i, plane, rows], guess[i, plane, rows])
-                elif i < 4:
-                    value = conduct[i - 2, plane, rows]
-                else:
-                    value = couple[plane, rows]
+                value = state[i, plane, first : first + 8] if i < 2 else others[i - 2, plane, first : first + 8]
                 padded[i, pl.ds((EDGE + first) * PLANES + plane, 8, stride=PLANES), :] = value
     tall, part = (STRIP + 2 * REACH) * PLANES, PART * PLANES
     for b in range(BRICKS):
@@ -99,15 +117,15 @@
 
 
 def restore_kernel(got, out):
-    for core in range(2):
+    core, _, _ = position()
+    for part in range(2):
+        half = core if part == 0 else 1 - core
         for b in range(BRICKS):
-            source = core * BRICKS + ORDER[b]
-            first = STRIP * b + HALF * core
+            first = pl.multiple_of(STRIP * b + HALF * half, HALF)
             for i in range(2):
                 for plane in range(PLANES):
-                    out[0, i, plane, first : first + HALF] = got[
-                        source, pl.ds(i * HALF * PLANES + plane, HALF, stride=PLANES), :
-                    ]
+                    at = (part * 2 + i) * HALF * PLANES + plane
+                    out[0, i, plane, pl.ds(first, HALF), :] = got[ORDER[b], pl.ds(at, HALF, stride=PLANES), :]
 
 
 def row_sweep(y, state, weights, earlier, opening, source):
@@ -152,8 +170,8 @@
     lax.fori_loop(0, count, step, 0)
 
 
-def relax_kernel(where, begin, mine, other, inlet, w_out, base, give, own, c, w1, w4, feed, e, v, e0, sem):
-    core, strip, slab = where[0], where[1], where[2]
+def relax_kernel(begin, mine, other, inlet, w4, base, give, own, c, w1, feed, e, v, e0):
+    core, strip, slab = position()
     c[:, pl.ds(PART * core, PART)] = mine[...]
     c[:, pl.ds(PART - PART * core, PART)] = other[...]
     first = EDGE - REACH
@@ -206,9 +224,6 @@
         return carry
 
     lax.fori_loop(1, ROWS - 1, weigh, 0)
-    spill = pltpu.make_async_copy(w4.at[pl.ds(HALF * core, FRAME)], w_out, sem)
-    spill.start()
-
     sweep(e0, w4, None, v, EDGE - 3, EDGE + STRIP + 3, True)
     sweep(v, w4, e0, e0, EDGE - 2, EDGE + STRIP + 2, False)
     advances(4, e, v, w1, first, first + STRIP + 2 * REACH, feed)
@@ -220,72 +235,66 @@
     joined = jnp.where(slab == SLABS - 2, 0.0, 1.0).astype(F32)
     near, far = pl.ds(EDGE, HALF), pl.ds(EDGE + HALF, HALF)
     base[...] = jnp.where(core == 0, joined * e0[:, near], e[:, far])
-    give[...] = jnp.where(core == 0, joined * e0[:, far], e[:, near])
-    own[:, :HALF] = e[:, near]
-    own[:, HALF:] = e[:, far]
-    spill.wait()
-
-
-def load_weights(w_hbm, w, low, high, sem):
-    copy = pltpu.make_async_copy(w_hbm.at[pl.ds(low, high - low)], w.at[pl.ds(low, high - low)], sem)
-    copy.start()
-    return copy
-
-
-def place(core, e, inward, outward, distance):
-    e[:, pl.ds(EDGE + distance - 2 * distance * core, HALF)] = inward[...]
-    e[:, pl.ds(EDGE - distance + 2 * distance * core, HALF)] = outward[...]
-
-
-def far_kernel(where, own, near, far, swapped, swapped_near, local, w_hbm, out, w, e, v, sem):
-    core = where[0]
-    copy = load_weights(w_hbm, w, 0, FRAME, sem)
-    e[:, EDGE : EDGE + HALF] = own[...]
-    place(core, e, swapped, near, HALF)
-    place(core, e, swapped_near, far, 2 * HALF)
-    copy.wait()
-    advances(8, e, v, w, 0, FRAME)
-    out[...] = local[...] + e[:, EDGE : EDGE + HALF]
-
-
-def mid_kernel(where, own, near, swapped, local, w_hbm, out, inner, outer, w, e, v, sem):
-    core = where[0]
-    copy = load_weights(w_hbm, w, HALF, FRAME - HALF, sem)
-    e[:, EDGE : EDGE + HALF] = own[...]
-    place(core, e, swapped, near, HALF)
-    copy.wait()
-    advances(4, e, v, w, EDGE - 8, EDGE + HALF + 8)
-    out[...] = local[...] + e[:, EDGE : EDGE + HALF]
+    give[0:2] = jnp.where(core == 0, joined * e0[:, far], e[:, near])
+    give[2:4] = e[:, far]
+    own[...] = e[:, near]
+
+
+def place(core, e, middle, inward, outward, distance):
+    step = distance * (1 - 2 * core)
+    e[:, pl.ds(middle + step, inward.shape[1])] = inward[...]
+    e[:, pl.ds(middle - step, outward.shape[1])] = outward[...]
+
+
+def far_kernel(own, near, far, swapped, swapped_near, w, out, e, v):
+    core, _, _ = position()
+    middle = EDGE + HALF * core
+    rows = pl.ds(middle, HALF)
+    e[:, rows] = own[...]
+    place(core, e, middle, swapped, near, HALF)
+    place(core, e, middle, swapped_near, far, 2 * HALF)
+    advances(8, e, v, w, middle - 16, middle + HALF + 16)
+    out[...] = e[:, rows]
+
+
+def mid_kernel(own, near, swapped, local, w, out, inner, outer, e, v):
+    core, _, _ = position()
+    middle = EDGE + HALF * core
+    rows = pl.ds(middle, HALF)
+    e[:, rows] = own[...]
+    place(core, e, middle, swapped, near, HALF)
+    advances(4, e, v, w, middle - 8, middle + HALF + 8)
+    out[...] = local[...] + e[:, rows]
     inner[...] = out[:, pl.ds(6 - 6 * core, 2)]
     outer[...] = out[:, pl.ds(6 * core, 2)]
 
 
-def last_kernel(where, own, near, swapped, c_own, c_near, c_swapped, g, w_hbm, out, w, e, v, r, sem):
-    core = where[0]
-    copy = load_weights(w_hbm, w, HALF, FRAME - HALF, sem)
-    e[:, EDGE : EDGE + HALF] = own[...]
-    place(core, e, swapped, near, HALF)
-    r[:, EDGE : EDGE + HALF] = c_own[...]
-    r[:, pl.ds(EDGE + HALF - 10 * core, 2)] = c_swapped[...]
-    r[:, pl.ds(EDGE - 2 + 10 * core, 2)] = c_near[...]
-    copy.wait()
-    advances(2, e, v, w, EDGE - 6, EDGE + HALF + 6)
-    rows = pl.ds(EDGE - 2, HALF + 4)
-    r[:, rows] = r[:, rows] + e[:, rows]
-    sweep(r, w, None, v, EDGE - 1, EDGE + HALF + 1, True)
-    sweep(v, w, r, e, EDGE, EDGE + HALF, False)
-    rows = pl.ds(EDGE, HALF)
-    e[:, rows] = e[:, rows] + g[...]
+def last_kernel(own, near, swapped, c_own, c_near, c_swapped, g, taken, w, keep, send, e, v, r):
+    core, _, _ = position()
+    middle = EDGE + HALF * core
+    rows = pl.ds(middle, HALF)
+    e[:, rows] = own[...]
+    place(core, e, middle, swapped, near, HALF)
+    r[:, rows] = c_own[...]
+    r[:, pl.ds(middle + HALF - 10 * core, 2)] = c_swapped[...]
+    r[:, pl.ds(middle - 2 + 10 * core, 2)] = c_near[...]
+    advances(2, e, v, w, middle - 6, middle + HALF + 6)
+    wide = pl.ds(middle - 2, HALF + 4)
+    r[:, wide] = r[:, wide] + e[:, wide]
+    sweep(r, w, None, v, middle - 1, middle + HALF + 1, True)
+    sweep(v, w, r, e, middle, middle + HALF, False)
+    e[:, rows] = e[:, rows] + jnp.where(core == 0, g[...], taken[2:4])
     low = lax.broadcasted_iota(jnp.int32, (8, LAST), 0) < PLANES
-    for label, source in ((0, r), (1, e)):
+    for out, other in ((keep, 0), (send, 1)):
+        pick = lambda *at: jnp.where(core == other, r[at], e[at])
         for i in range(2):
             for y in range(0, HALF, 2):
                 at = (i * HALF + y) * PLANES
                 for t in range(NX // 8):
-                    a = source[i, EDGE + y, 8 * t : 8 * t + 8]
-                    b = source[i, EDGE + y + 1, 8 * t : 8 * t + 8]
-                    out[label * BRICKS + 2 * t, at : at + 8] = jnp.where(low, a, pltpu.roll(b, 4, 0))
-                    out[label * BRICKS + 2 * t + 1, at : at + 8] = jnp.where(low, pltpu.roll(a, 4, 0), b)
+                    a = pick(i, middle + y, slice(8 * t, 8 * t + 8))
+                    b = pick(i, middle + y + 1, slice(8 * t, 8 * t + 8))
+                    out[2 * t, at : at + 8] = jnp.where(low, a, pltpu.roll(b, 4, 0))
+                    out[2 * t + 1, at : at + 8] = jnp.where(low, pltpu.roll(a, 4, 0), b)
 
 
 def index(chip, core, strip):
@@ -304,10 +313,10 @@
 
 
 SAME = [(c, c) for c in range(8)]
-LEAP_FOUR = [((c - 4) % 8, c) for c in range(3, 7)]
-LEAP_TWO = [((c - 2) % 8, c) for c in range(1, 7)]
 HOME = [((c - 1) % 8, c) for c in range(8)]
-HOME_ONE = [((c - 2) % 8, c) for c in range(1, 8)]
+LEAP_FOUR = [((c - 5) % 8, c) for c in range(4, 8)]
+LEAP_TWO = [(c - 2, c) for c in range(2, 8)]
+LEAP_ONE = [(c - 1, c) for c in range(1, 8)]
 
 
 def swap(value):
@@ -315,91 +324,71 @@
 
 
 def shards(startup, guess, conduct, couple, inlet):
-    chip, core, space = (lax.axis_index(a) for a in AXES)
-    slab = chip * 2 + core
-    strip = jnp.take(jnp.array([ORDER.index(s) for s in range(BRICKS)], jnp.int32), space)
-    where = jnp.stack([core, strip, slab]).astype(jnp.int32)
-
     tall = STRIP + 2 * REACH
     chunk = (2 * tall + 3 * PART) * PLANES
     half = shape(2, HALF, NX, LAST)
     packed = call(
         pack_kernel,
         shape(BRICKS, chunk, LAST),
-        [SMEM] + [VMEM] * 4,
+        [HBM] * 4,
         VMEM,
-        [pltpu.VMEM((5, (MIDDLE + 2 * EDGE) * PLANES, LAST), F32)],
+        [
+            pltpu.VMEM((5, (MIDDLE + 2 * EDGE) * PLANES, LAST), F32),
+            pltpu.VMEM((2, PLANES, MIDDLE, LAST), F32),
+            pltpu.VMEM((3, PLANES, MIDDLE, LAST), F32),
+            pltpu.SemaphoreType.DMA((5,)),
+        ],
         16,
-    )(where, guess[0], startup, conduct, couple)
+    )(startup, guess, conduct, couple)
     got = lax.all_to_all(packed, "space", 0, 0, tiled=True)
     begin, mine = call(
         unpack_kernel, (shape(2, tall, NX, LAST), shape(3, PART, NX, LAST)), [VMEM], (VMEM, VMEM), [], 16
     )(got)
     other = swap(mine)
 
-    field = pltpu.VMEM((2, ROWS + 4, NX, LAST), F32)
-    w_all = pltpu.VMEM((ROWS, 16, NX, LAST), F32)
+    field = pltpu.VMEM((2, HELD, NX, LAST), F32)
     weights, base, give, g = call(
         relax_kernel,
-        (shape(FRAME, 16, NX, LAST), half, half, shape(2, STRIP, NX, LAST)),
-        [SMEM] + [VMEM] * 4,
-        (ANY, VMEM, VMEM, VMEM),
+        (shape(HELD, 16, NX, LAST), half, shape(4, HALF, NX, LAST), half),
+        [VMEM] * 4,
+        (VMEM,) * 4,
         [
             pltpu.VMEM((3, ROWS, NX, LAST), F32),
-            w_all,
-            w_all,
-            pltpu.VMEM((ROWS, 8, LAST), F32),
+            pltpu.VMEM((HELD, 16, NX, LAST), F32),
+            pltpu.VMEM((HELD, 8, LAST), F32),
             field,
             field,
             field,
-            pltpu.SemaphoreType.DMA,
         ],
-        48,
-    )(where, begin, mine, other, inlet)
-    u = base + swap(give)
-    g_far = sent(g[:, HALF:], SAME, 1, 0)
-    g_half = jnp.where(core == 0, g[:, :HALF], g_far)
-
-    frame = pltpu.VMEM((2, FRAME + 4, NX, LAST), F32)
-    w_frame = pltpu.VMEM((FRAME + 4, 16, NX, LAST), F32)
+        42,
+    )(begin, mine, other, inlet)
+    taken = swap(give)
+    u = base + taken[:2]
+
     own = sent(u, LEAP_FOUR, 0, 0)
     near = sent(u, LEAP_FOUR, 1, 1)
     far = sent(u, LEAP_FOUR, 0, 1)
-    x = call(
-        far_kernel,
-        half,
-        [SMEM] + [VMEM] * 6 + [ANY],
-        VMEM,
-        [w_frame, frame, frame, pltpu.SemaphoreType.DMA],
-        32,
-    )(where, own, near, far, swap(own), swap(near), u, weights)
+    local = sent(u, HOME, 0, 0)
+    x = call(far_kernel, half, [VMEM] * 6, VMEM, [field, field], 26, 1 << 27)(
+        own, near, far, swap(own), swap(near), weights
+    )
+    x = x + local
 
     own = sent(x, LEAP_TWO, 0, 0)
     near = sent(x, LEAP_TWO, 1, 1)
     rim = shape(2, 2, NX, LAST)
-    y, inner, outer = call(
-        mid_kernel,
-        (half, rim, rim),
-        [SMEM] + [VMEM] * 4 + [ANY],
-        (VMEM,) * 3,
-        [w_frame, frame, frame, pltpu.SemaphoreType.DMA],
-        32,
-    )(where, own, near, swap(own), x, weights)
-
-    own = sent(y, HOME_ONE, 0, 0)
-    near = sent(y, HOME_ONE, 1, 1)
-    c_own = sent(y, HOME, 0, 0)
-    c_near = sent(outer, HOME, 1, 1)
-    c_swapped = sent(inner, HOME, 1, 0)
-    done = call(
-        last_kernel,
-        shape(2 * BRICKS, 2 * HALF * PLANES, LAST),
-        [SMEM] + [VMEM] * 7 + [ANY],
-        VMEM,
-        [w_frame, frame, frame, frame, pltpu.SemaphoreType.DMA],
-        32,
-    )(where, own, near, swap(own), c_own, c_near, c_swapped, g_half, weights)
-    back = lax.all_to_all(done, ("core", "space"), 0, 0, tiled=True)
+    y, inner, outer = call(mid_kernel, (half, rim, rim), [VMEM] * 5, (VMEM,) * 3, [field, field], 26)(
+        own, near, swap(own), x, weights
+    )
+
+    own = sent(y, LEAP_ONE, 0, 0)
+    near = sent(y, LEAP_ONE, 1, 1)
+    c_near = sent(outer, SAME, 1, 1)
+    parcel = shape(BRICKS, 2 * HALF * PLANES, LAST)
+    keep, send = call(last_kernel, (parcel, parcel), [VMEM] * 9, (VMEM,) * 2, [field, field, field], 26)(
+        own, near, swap(own), y, c_near, swap(inner), g, taken, weights
+    )
+    back = lax.all_to_all(jnp.concatenate([keep, swap(send)], axis=1), "space", 0, 0, tiled=True)
     return call(restore_kernel, shape(1, 2, PLANES, MIDDLE, LAST), [VMEM], VMEM, [], 16)(back)
 
 

time: 188 us -> 181 us (0.963)
  waiting for transfers between devices: 22.2 us -> 33 us
  starting transfers between devices: 47.1 us -> 37.2 us
  local copies, waits for them, and re-layouts: 13.4 us -> 8.95 us
  blocking collectives: 58.8 us -> 55.3 us
    ppermute x17, waiting for transfers between devices: 22.2 us -> 33 us  [sent(): return lax.ppermute(value, AXES, pairs)]
    ppermute x17, starting transfers between devices: 47.1 us -> 37.2 us  [sent(): return lax.ppermute(value, AXES, pairs)]
    all_to_all x1, blocking collectives: 23.8 us -> 20.3 us  [shards(): lax.all_to_all(jnp.concatenate([keep, swap(send)], axis=1), 'space', 0, 0...]
    unnamed x14 -> x12, local copies, waits for them, and re-layouts: 12 us -> 8.95 us
  transfers between devices with their start and end apart: 17 -> 17, of which waited for: 8 -> 9; matrix products, arithmetic and copies ran while one was open for 0% -> 0% of each run, Pallas kernels for 0% -> 8%
where the time goes in v2:
time: 181 us; the launch traced here: 180 us
  blocking collectives  55.3 us (31%)
  Pallas kernels  45.6 us (25%)
  starting transfers between devices  37.2 us (21%)
  waiting for transfers between devices  33 us (18%)
  local copies, waits for them, and re-layouts  8.95 us (5%)
    ppermute x17, starting transfers between devices, sent(): return lax.ppermute(value, AXES, pairs)  37.2 us
    all_to_all x1, blocking collectives, shards(): got = lax.all_to_all(packed, 'space', 0, 0, tiled=True)  35 us
    ppermute x17, waiting for transfers between devices, sent(): return lax.ppermute(value, AXES, pairs)  33 us
    pallas_call x1, Pallas kernels, shards(): call(relax_kernel, (shape(HELD, 16, NX, LAST), half, shape(4, HALF, NX, L...  21.9 us
    all_to_all x1, blocking collectives, shards(): lax.all_to_all(jnp.concatenate([keep, swap(send)], axis=1), 'space', 0, 0...  20.3 us
    pallas_call x1, Pallas kernels, shards(): call(far_kernel, half, [VMEM] * 6, VMEM, [field, field], 26, 1 << 27)  14.1 us
    unnamed x12, local copies, waits for them, and re-layouts  8.95 us
    pallas_call x1, Pallas kernels, shards(): call(mid_kernel, (half, rim, rim), [VMEM] * 5, (VMEM,) * 3, [field, field...  4.79 us
  transfers between devices with their start and end apart: 17, of which 9 were waited for; matrix products, arithmetic and copies ran while one was open for 0% of the time, Pallas kernels for 8%

profile of v2, /device:TPU:4, one launch (start us, length us, event | category | flops | bytes accessed | tf_op | source)
XLA Modules:
  0.0 180.4 jit_solution(8901026311755818989)
XLA Ops:
  0.0 0.0 copy-start.1
  0.0 1.0 copy-done.1
  1.0 0.0 copy-start.2
  1.0 1.0 copy-done.2
  2.1 0.0 copy-start.3
  2.1 1.0 copy-done.3
  3.1 0.0 copy-start.4
  3.1 0.9 copy-done.4
  4.1 0.5 shard_map.55
  4.5 35.0 %all_to_all.10.got = f32[8,576,128]{2,1,0:T(8,128)S(1)} all-to-all(f32[8,576,128]{2,1,0:T(8,128)S(1)} %shard_map.55), channel_id=1, replica_groups=mesh['chip'=8,'core'=2,'space'=8] {'space'}, dimensions={0} | all-to-all | bytes 4718592 | tf_op jit(solution)/shard_map/all_to_all | solution.py:343
  39.5 0.0 copy-start.5
  39.5 0.2 shard_map.56
  39.7 0.1 collective-permute-start
  39.8 2.8 %collective-permute-done.other = f32[3,24,32,128]{3,2,1,0:T(8,128)S(1)} collective-permute-done((f32[3,24,32,128]{3,2,1,0:T(8,128)S(1)}, f32[3,24,32,128]{3,2,1,0:T(8,128)S(1)}, u32[]{:S(2)}, u32[]{:S(2)}) %collective-permute-start) | collective-permute-done | bytes 1179680 | tf_op jit(solution)/shard_map/ppermute | solution.py:312
  42.6 0.0 copy-done.5
  42.6 21.9 %shard_map.57 = (f32[52,16,32,128]{3,2,1,0:T(8,128)}, f32[2,8,32,128]{3,2,1,0:T(8,128)S(1)}, f32[4,8,32,128]{3,2,1,0:T(8,128)S(1)}, f32[2,8,32,128]{3,2,1,0:T(8,128)S(1)}) custom-call(f32[2,36,32,128]{3,2,1,0:T(8,128)S(1)} %get-tuple-element.16.begin, f32[3,24,32,128]{3,2,1,0:T(8,128)S(1)} %get-tuple-element.17.mine, ...), custom_call_target="tpu_custom_call" | custom-call | tf_op jit(solution)/shard_map/pallas_call | solution.py:350
  64.6 0.1 collective-permute-start.1
  64.7 1.8 collective-permute-done.1.taken
  66.5 0.7 collective-permute-start.3
  67.2 1.3 collective-permute-start.2
  68.5 0.7 collective-permute-start.4
  69.2 0.0 collective-permute-done.3.near
  69.2 7.4 %collective-permute-start.6 = (f32[2,8,32,128]{3,2,1,0:T(8,128)S(1)}, f32[2,8,32,128]{3,2,1,0:T(8,128)S(1)}, u32[]{:S(2)}, u32[]{:S(2)}) collective-permute-start(f32[2,8,32,128]{3,2,1,0:T(8,128)S(1)} %collective-permute-done.3.near), channel_id=1, source_target_pairs={{8,0},{10,2},{12,4},{14,6},{15,7},{13,5},{11,3},{9,1},{0,8},{2,10}... | collective-permute-start | bytes 786440 | tf_op jit(solution)/shard_map/ppermute | solution.py:312
  76.6 8.4 %collective-permute-done.2.own = f32[2,8,32,128]{3,2,1,0:T(8,128)S(1)} collective-permute-done((f32[2,8,32,128]{3,2,1,0:T(8,128)S(1)}, f32[2,8,32,128]{3,2,1,0:T(8,128)S(1)}, u32[]{:S(2)}, u32[]{:S(2)}) %collective-permute-start.2) | collective-permute-done | bytes 262176 | tf_op jit(solution)/shard_map/ppermute | solution.py:312
  85.0 0.1 collective-permute-start.5
  85.1 1.0 collective-permute-start.7
  86.1 0.0 collective-permute-done.4.far
  86.1 0.0 collective-permute-done.6.swapped_near
  86.1 0.4 collective-permute-done.5.swapped
  86.5 0.0 copy-start
  86.5 4.9 %copy-done = f32[52,16,32,128]{3,2,1,0:T(8,128)S(1)} copy-done((f32[52,16,32,128]{3,2,1,0:T(8,128)S(1)}, f32[52,16,32,128]{3,2,1,0:T(8,128)}, u32[]{:S(2)}) %copy-start) | copy-done | bytes 13631512
  91.4 14.1 %shard_map.58 = f32[2,8,32,128]{3,2,1,0:T(8,128)S(1)} custom-call(f32[2,8,32,128]{3,2,1,0:T(8,128)S(1)} %collective-permute-done.2.own, f32[2,8,32,128]{3,2,1,0:T(8,128)S(1)} %collective-permute-done.3.near, f32[2,8,32,128]{3,2,1,0:T(8,128)S(1)} %collective-permute-done.4.far, f32[2,8,32,128]{3,2,1,0:T(8,128)S(1)} %collective-permute-done.5.swapped, ...), custom_call_target="tpu_custom_call" | custom-call | flops 134217728 | bytes 1048576 | tf_op jit(solution)/shard_map/pallas_call | solution.py:372
  105.5 0.0 collective-permute-done.7
  105.6 5.1 %collective-permute-start.8 = (f32[2,8,32,128]{3,2,1,0:T(8,128)S(1)}, f32[2,8,32,128]{3,2,1,0:T(8,128)S(1)}, u32[]{:S(2)}, u32[]{:S(2)}) collective-permute-start(f32[2,8,32,128]{3,2,1,0:T(8,128)S(1)} %add.7.local), channel_id=1, source_target_pairs={{0,32},{2,34},{4,36},{6,38},{7,39},{5,37},{3,35},{1,33},{8,40},{10... | collective-permute-start | bytes 786440 | tf_op jit(solution)/shard_map/ppermute | solution.py:312
  110.7 0.7 collective-permute-start.9
  111.4 8.4 %collective-permute-done.8.own = f32[2,8,32,128]{3,2,1,0:T(8,128)S(1)} collective-permute-done((f32[2,8,32,128]{3,2,1,0:T(8,128)S(1)}, f32[2,8,32,128]{3,2,1,0:T(8,128)S(1)}, u32[]{:S(2)}, u32[]{:S(2)}) %collective-permute-start.8) | collective-permute-done | bytes 262176 | tf_op jit(solution)/shard_map/ppermute | solution.py:312
  119.8 0.0 collective-permute-start.10
  119.8 0.0 collective-permute-done.9.near
  119.8 1.5 collective-permute-done.10.swapped
  121.3 4.8 %shard_map.59 = (f32[2,8,32,128]{3,2,1,0:T(8,128)S(1)}, f32[2,2,32,128]{3,2,1,0:T(8,128)S(1)}, f32[2,2,32,128]{3,2,1,0:T(8,128)S(1)}) custom-call(f32[2,8,32,128]{3,2,1,0:T(8,128)S(1)} %collective-permute-done.8.own, f32[2,8,32,128]{3,2,1,0:T(8,128)S(1)} %collective-permute-done.9.near, f32[2,8,32,128]{3,2,1,0:T(8,128)S(1)} %collective-permute-done.10.swapped, ...), custom_call_target="tpu_custom_call" | custom-call | tf_op jit(solution)/shard_map/pallas_call | solution.py:380
  126.1 3.7 %collective-permute-start.11 = (f32[2,8,32,128]{3,2,1,0:T(8,128)S(1)}, f32[2,8,32,128]{3,2,1,0:T(8,128)S(1)}, u32[]{:S(2)}, u32[]{:S(2)}) collective-permute-start(f32[2,8,32,128]{3,2,1,0:T(8,128)S(1)} %get-tuple-element.21.c_own), channel_id=1, source_target_pairs={{0,16},{2,18},{4,20},{6,22},{7,23},{5,21},{3,19},{1,17},{8,24},{10... | collective-permute-start | bytes 786440 | tf_op jit(solution)/shard_map/ppermute | solution.py:312
  129.8 0.7 collective-permute-start.12
  130.5 7.5 %collective-permute-done.11.own = f32[2,8,32,128]{3,2,1,0:T(8,128)S(1)} collective-permute-done((f32[2,8,32,128]{3,2,1,0:T(8,128)S(1)}, f32[2,8,32,128]{3,2,1,0:T(8,128)S(1)}, u32[]{:S(2)}, u32[]{:S(2)}) %collective-permute-start.11) | collective-permute-done | bytes 262176 | tf_op jit(solution)/shard_map/ppermute | solution.py:312
  138.0 8.5 %collective-permute-start.13 = (f32[2,8,32,128]{3,2,1,0:T(8,128)S(1)}, f32[2,8,32,128]{3,2,1,0:T(8,128)S(1)}, u32[]{:S(2)}, u32[]{:S(2)}) collective-permute-start(f32[2,8,32,128]{3,2,1,0:T(8,128)S(1)} %collective-permute-done.11.own), channel_id=1, source_target_pairs={{8,0},{10,2},{12,4},{14,6},{15,7},{13,5},{11,3},{9,1},{0,8},{2,10}... | collective-permute-start | bytes 786440 | tf_op jit(solution)/shard_map/ppermute | solution.py:312
  146.5 0.7 collective-permute-start.14
  147.2 5.6 %collective-permute-start.15 = (f32[2,2,32,128]{3,2,1,0:T(8,128)S(1)}, f32[2,2,32,128]{3,2,1,0:T(8,128)S(1)}, u32[]{:S(2)}, u32[]{:S(2)}) collective-permute-start(f32[2,2,32,128]{3,2,1,0:T(8,128)S(1)} %get-tuple-element.23), channel_id=1, source_target_pairs={{8,0},{10,2},{12,4},{14,6},{15,7},{13,5},{11,3},{9,1},{0,8},{2,10}... | collective-permute-start | bytes 196616 | tf_op jit(solution)/shard_map/ppermute | solution.py:312
  152.8 0.0 collective-permute-done.14.c_near
  152.8 0.9 collective-permute-done.15.c_swapped
  153.7 0.0 collective-permute-done.12.near
  153.7 0.0 collective-permute-done.13.swapped
  153.7 3.3 %shard_map.60 = (f32[8,64,128]{2,1,0:T(8,128)S(1)}, f32[8,64,128]{2,1,0:T(8,128)S(1)}) custom-call(f32[2,8,32,128]{3,2,1,0:T(8,128)S(1)} %collective-permute-done.11.own, f32[2,8,32,128]{3,2,1,0:T(8,128)S(1)} %collective-permute-done.12.near, f32[2,8,32,128]{3,2,1,0:T(8,128)S(1)} %collective-permute-done.13.swapped, ...), custom_call_target="tpu_custom_call" | custom-call | tf_op jit(solution)/shard_map/pallas_call | solution.py:388
  157.0 1.0 collective-permute-start.16
  158.0 1.2 collective-permute-done.16
  159.2 20.3 %all_to_all.11.got = f32[8,128,128]{2,1,0:T(8,128)S(1)} all-to-all(f32[8,128,128]{2,1,0:T(8,128)S(1)} %pad_maximum_fusion), channel_id=1, replica_groups=mesh['chip'=8,'core'=2,'space'=8] {'space'}, dimensions={0} | all-to-all | bytes 1048576 | tf_op jit(solution)/shard_map/all_to_all | solution.py:391
  179.6 0.8 shard_map.61
  (3 shorter events, 0.1 us)
Async XLA Ops:
  0.0 1.0 copy-start.1
  1.0 1.0 copy-start.2
  2.1 1.0 copy-start.3
  3.1 0.9 copy-start.4
  39.5 3.1 %copy-start.5 = (f32[128,128]{1,0:T(8,128)S(1)}, f32[128,128]{1,0:T(8,128)}, u32[]{:S(2)}) copy-start(f32[128,128]{1,0:T(8,128)} %inlet.1) | copy-start | bytes 196612
  39.7 2.9 %collective-permute-start = (f32[3,24,32,128]{3,2,1,0:T(8,128)S(1)}, f32[3,24,32,128]{3,2,1,0:T(8,128)S(1)}, u32[]{:S(2)}, u32[]{:S(2)}) collective-permute-start(f32[3,24,32,128]{3,2,1,0:T(8,128)S(1)} %get-tuple-element.17.mine), channel_id=1, source_target_pairs={{8,0},{10,2},{12,4},{14,6},{15,7},{13,5},{11,3},{9,1},{0,8},{2,10}... | collective-permute-start | bytes 3538952 | tf_op jit(solution)/shard_map/ppermute | solution.py:312
  64.6 1.9 %collective-permute-start.1 = (f32[4,8,32,128]{3,2,1,0:T(8,128)S(1)}, f32[4,8,32,128]{3,2,1,0:T(8,128)S(1)}, u32[]{:S(2)}, u32[]{:S(2)}) collective-permute-start(f32[4,8,32,128]{3,2,1,0:T(8,128)S(1)} %get-tuple-element.19), channel_id=1, source_target_pairs={{8,0},{10,2},{12,4},{14,6},{15,7},{13,5},{11,3},{9,1},{0,8},{2,10}... | collective-permute-start | bytes 1572872 | tf_op jit(solution)/shard_map/ppermute | solution.py:312
  66.5 2.7 %collective-permute-start.3 = (f32[2,8,32,128]{3,2,1,0:T(8,128)S(1)}, f32[2,8,32,128]{3,2,1,0:T(8,128)S(1)}, u32[]{:S(2)}, u32[]{:S(2)}) collective-permute-start(f32[2,8,32,128]{3,2,1,0:T(8,128)S(1)} %slice_add_fusion), channel_id=1, source_target_pairs={{120,66},{122,68},{124,70},{126,71},{127,69},{125,67},{123,65},{11... | collective-permute-start | bytes 786440 | tf_op jit(solution)/shard_map/ppermute | solution.py:312
  67.2 17.8 %collective-permute-start.2 = (f32[2,8,32,128]{3,2,1,0:T(8,128)S(1)}, f32[2,8,32,128]{3,2,1,0:T(8,128)S(1)}, u32[]{:S(2)}, u32[]{:S(2)}) collective-permute-start(f32[2,8,32,128]{3,2,1,0:T(8,128)S(1)} %slice_add_fusion), channel_id=1, source_target_pairs={{112,64},{114,66},{116,68},{118,70},{119,71},{117,69},{115,67},{11... | collective-permute-start | bytes 786440 | tf_op jit(solution)/shard_map/ppermute | solution.py:312
  68.5 17.6 %collective-permute-start.4 = (f32[2,8,32,128]{3,2,1,0:T(8,128)S(1)}, f32[2,8,32,128]{3,2,1,0:T(8,128)S(1)}, u32[]{:S(2)}, u32[]{:S(2)}) collective-permute-start(f32[2,8,32,128]{3,2,1,0:T(8,128)S(1)} %slice_add_fusion), channel_id=1, source_target_pairs={{112,66},{114,68},{116,70},{118,71},{119,69},{117,67},{115,65},{12... | collective-permute-start | bytes 786440 | tf_op jit(solution)/shard_map/ppermute | solution.py:312
  69.2 16.9 %collective-permute-start.6 = (f32[2,8,32,128]{3,2,1,0:T(8,128)S(1)}, f32[2,8,32,128]{3,2,1,0:T(8,128)S(1)}, u32[]{:S(2)}, u32[]{:S(2)}) collective-permute-start(f32[2,8,32,128]{3,2,1,0:T(8,128)S(1)} %collective-permute-done.3.near), channel_id=1, source_target_pairs={{8,0},{10,2},{12,4},{14,6},{15,7},{13,5},{11,3},{9,1},{0,8},{2,10}... | collective-permute-start | bytes 786440 | tf_op jit(solution)/shard_map/ppermute | solution.py:312
  85.0 1.5 collective-permute-start.5
  85.1 20.4 %collective-permute-start.7 = (f32[2,8,32,128]{3,2,1,0:T(8,128)S(1)}, f32[2,8,32,128]{3,2,1,0:T(8,128)S(1)}, u32[]{:S(2)}, u32[]{:S(2)}) collective-permute-start(f32[2,8,32,128]{3,2,1,0:T(8,128)S(1)} %slice_add_fusion), channel_id=1, source_target_pairs={{112,0},{114,2},{116,4},{118,6},{119,7},{117,5},{115,3},{113,1},{1... | collective-permute-start | bytes 786440 | tf_op jit(solution)/shard_map/ppermute | solution.py:312
  86.5 4.9 %copy-start = (f32[52,16,32,128]{3,2,1,0:T(8,128)S(1)}, f32[52,16,32,128]{3,2,1,0:T(8,128)}, u32[]{:S(2)}) copy-start(f32[52,16,32,128]{3,2,1,0:T(8,128)} %get-tuple-element.20.w) | copy-start | bytes 40894468
  105.6 14.1 %collective-permute-start.8 = (f32[2,8,32,128]{3,2,1,0:T(8,128)S(1)}, f32[2,8,32,128]{3,2,1,0:T(8,128)S(1)}, u32[]{:S(2)}, u32[]{:S(2)}) collective-permute-start(f32[2,8,32,128]{3,2,1,0:T(8,128)S(1)} %add.7.local), channel_id=1, source_target_pairs={{0,32},{2,34},{4,36},{6,38},{7,39},{5,37},{3,35},{1,33},{8,40},{10... | collective-permute-start | bytes 786440 | tf_op jit(solution)/shard_map/ppermute | solution.py:312
  110.7 9.1 %collective-permute-start.9 = (f32[2,8,32,128]{3,2,1,0:T(8,128)S(1)}, f32[2,8,32,128]{3,2,1,0:T(8,128)S(1)}, u32[]{:S(2)}, u32[]{:S(2)}) collective-permute-start(f32[2,8,32,128]{3,2,1,0:T(8,128)S(1)} %add.7.local), channel_id=1, source_target_pairs={{8,34},{10,36},{12,38},{14,39},{15,37},{13,35},{11,33},{2,40},{4,4... | collective-permute-start | bytes 786440 | tf_op jit(solution)/shard_map/ppermute | solution.py:312
  119.8 1.5 collective-permute-start.10
  126.1 11.9 %collective-permute-start.11 = (f32[2,8,32,128]{3,2,1,0:T(8,128)S(1)}, f32[2,8,32,128]{3,2,1,0:T(8,128)S(1)}, u32[]{:S(2)}, u32[]{:S(2)}) collective-permute-start(f32[2,8,32,128]{3,2,1,0:T(8,128)S(1)} %get-tuple-element.21.c_own), channel_id=1, source_target_pairs={{0,16},{2,18},{4,20},{6,22},{7,23},{5,21},{3,19},{1,17},{8,24},{10... | collective-permute-start | bytes 786440 | tf_op jit(solution)/shard_map/ppermute | solution.py:312
  129.8 23.9 %collective-permute-start.12 = (f32[2,8,32,128]{3,2,1,0:T(8,128)S(1)}, f32[2,8,32,128]{3,2,1,0:T(8,128)S(1)}, u32[]{:S(2)}, u32[]{:S(2)}) collective-permute-start(f32[2,8,32,128]{3,2,1,0:T(8,128)S(1)} %get-tuple-element.21.c_own), channel_id=1, source_target_pairs={{8,18},{10,20},{12,22},{14,23},{15,21},{13,19},{11,17},{2,24},{4,2... | collective-permute-start | bytes 786440 | tf_op jit(solution)/shard_map/ppermute | solution.py:312
  138.0 15.7 %collective-permute-start.13 = (f32[2,8,32,128]{3,2,1,0:T(8,128)S(1)}, f32[2,8,32,128]{3,2,1,0:T(8,128)S(1)}, u32[]{:S(2)}, u32[]{:S(2)}) collective-permute-start(f32[2,8,32,128]{3,2,1,0:T(8,128)S(1)} %collective-permute-done.11.own), channel_id=1, source_target_pairs={{8,0},{10,2},{12,4},{14,6},{15,7},{13,5},{11,3},{9,1},{0,8},{2,10}... | collective-permute-start | bytes 786440 | tf_op jit(solution)/shard_map/ppermute | solution.py:312
  146.5 6.3 %collective-permute-start.14 = (f32[2,2,32,128]{3,2,1,0:T(8,128)S(1)}, f32[2,2,32,128]{3,2,1,0:T(8,128)S(1)}, u32[]{:S(2)}, u32[]{:S(2)}) collective-permute-start(f32[2,2,32,128]{3,2,1,0:T(8,128)S(1)} %get-tuple-element.22), channel_id=1, source_target_pairs={{8,2},{10,4},{12,6},{14,7},{15,5},{13,3},{11,1},{2,8},{4,10},{6,12... | collective-permute-start | bytes 196616 | tf_op jit(solution)/shard_map/ppermute | solution.py:312
  147.2 6.5 %collective-permute-start.15 = (f32[2,2,32,128]{3,2,1,0:T(8,128)S(1)}, f32[2,2,32,128]{3,2,1,0:T(8,128)S(1)}, u32[]{:S(2)}, u32[]{:S(2)}) collective-permute-start(f32[2,2,32,128]{3,2,1,0:T(8,128)S(1)} %get-tuple-element.23), channel_id=1, source_target_pairs={{8,0},{10,2},{12,4},{14,6},{15,7},{13,5},{11,3},{9,1},{0,8},{2,10}... | collective-permute-start | bytes 196616 | tf_op jit(solution)/shard_map/ppermute | solution.py:312
  157.0 2.2 %collective-permute-start.16 = (f32[8,64,128]{2,1,0:T(8,128)S(1)}, f32[8,64,128]{2,1,0:T(8,128)S(1)}, u32[]{:S(2)}, u32[]{:S(2)}) collective-permute-start(f32[8,64,128]{2,1,0:T(8,128)S(1)} %get-tuple-element.26), channel_id=1, source_target_pairs={{8,0},{10,2},{12,4},{14,6},{15,7},{13,5},{11,3},{9,1},{0,8},{2,10}... | collective-permute-start | bytes 786440 | tf_op jit(solution)/shard_map/ppermute | solution.py:312

commit v3 on v2

--- a/solution.py
+++ b/solution.py
@@ -1,3 +1,5 @@
+import functools
+
 import jax
 import jax.numpy as jnp
 from jax import lax
@@ -13,8 +15,7 @@
 LAST = 128
 STRIP = 16
 HALF = 8
-REACH = 10
-EDGE = 16
+EDGE = 10
 ROWS = STRIP + 2 * EDGE
 HELD = ROWS + 4
 PART = ROWS // 2
@@ -23,7 +24,7 @@
 RATE_ACROSS = 0.5
 ADVECTION = 1.0
 DAMPING = 0.8
-COARSE = 4.0
+COARSE_FACTOR = 4.0
 
 ORDER = [0, 2, 4, 6, 7, 5, 3, 1]
 AXES = ("chip", "core", "space")
@@ -31,6 +32,8 @@
 
 VMEM = pl.BlockSpec(memory_space=pltpu.VMEM)
 HBM = pl.BlockSpec(memory_space=pltpu.HBM)
+PAIR = 9
+FINE, COARSE = 7, 8
 F32 = jnp.float32
 
 
@@ -86,10 +89,10 @@
             for first in range(0, MIDDLE, 8):
                 value = state[i, plane, first : first + 8] if i < 2 else others[i - 2, plane, first : first + 8]
                 padded[i, pl.ds((EDGE + first) * PLANES + plane, 8, stride=PLANES), :] = value
-    tall, part = (STRIP + 2 * REACH) * PLANES, PART * PLANES
+    tall, part = (STRIP + 2 * EDGE) * PLANES, PART * PLANES
     for b in range(BRICKS):
         s = ORDER[b]
-        start = (EDGE + STRIP * b - REACH) * PLANES
+        start = (STRIP * b) * PLANES
         for i in range(2):
             out[s, i * tall : (i + 1) * tall] = padded[i, start : start + tall]
         start = pl.multiple_of(STRIP * b * PLANES + part * core, 32)
@@ -109,9 +112,9 @@
                 out[i, y, 8 * t : 8 * t + 8] = jnp.where(low, a, pltpu.roll(b, 4, 0))
                 out[i, y + 1, 8 * t : 8 * t + 8] = jnp.where(low, pltpu.roll(a, 4, 0), b)
 
-    tall, part = (STRIP + 2 * REACH) * PLANES, PART * PLANES
+    tall, part = (STRIP + 2 * EDGE) * PLANES, PART * PLANES
     for i in range(2):
-        widen(state, i, i * tall, STRIP + 2 * REACH)
+        widen(state, i, i * tall, STRIP + 2 * EDGE)
     for i in range(3):
         widen(coefficients, i, 2 * tall + i * part, PART)
 
@@ -128,55 +131,52 @@
                     out[0, i, plane, pl.ds(first, HALF), :] = got[ORDER[b], pl.ds(at, HALF, stride=PLANES), :]
 
 
-def row_sweep(y, state, weights, earlier, opening, source):
+def row_sweep(y, state, weights, earlier, step, source):
     centre = (state[0, y], state[1, y])
     out = []
     for i in range(2):
         v = centre[i]
-        w = lambda k: weights[y, 8 * i + k]
+        w = lambda k: weights[y, PAIR * i + k]
         along = w(0) * pltpu.roll(v, 1, 0) + w(1) * pltpu.roll(v, NX - 1, 0)
         middle = w(2) * state[i, y - 1] + w(3) * state[i, y + 1]
         across = w(4) * pltpu.roll(v, 1, 1) + w(5) * pltpu.roll(v, LAST - 1, 1)
-        rest = w(6) * centre[1 - i]
-        if opening:
-            rest = rest + (0.2 + w(7)) * v
-        else:
-            rest = rest + 0.2 * v + w(7) * earlier[i, y]
-        new = (along + middle) + (across + rest)
+        begin = v if earlier is None else earlier[i, y]
+        if step == COARSE:
+            begin = (1.0 / COARSE_FACTOR) * begin
+        gain = (along + middle) + (across + (w(6) * centre[1 - i] + begin))
         if i == 1 and source is not None:
-            new = jnp.concatenate([new[:8] + source[y], new[8:]], axis=0)
-        out.append(new)
+            gain = jnp.concatenate([gain[:8] + source[y], gain[8:]], axis=0)
+        out.append((1.0 - DAMPING) * v + w(step) * gain)
     return out
 
 
-def sweep(state, weights, earlier, into, low, high, opening, source=None, unroll=4):
-    def step(k, carry):
+def sweep(state, weights, earlier, into, low, high, step, source=None, unroll=4):
+    def rows(k, carry):
         for u in range(unroll):
             y = low + unroll * k + u
-            new = row_sweep(y, state, weights, earlier, opening, source)
+            new = row_sweep(y, state, weights, earlier, step, source)
             into[0, y] = new[0]
             into[1, y] = new[1]
         return carry
 
-    lax.fori_loop(0, (high - low + unroll - 1) // unroll, step, 0)
-
-
-def advances(count, e, v, weights, low, high, source=None):
-    def step(m, carry):
-        sweep(e, weights, None, v, low + 2 * m + 1, high - 2 * m - 1, True, source)
-        sweep(v, weights, e, e, low + 2 * m + 2, high - 2 * m - 2, False, source)
+    lax.fori_loop(0, (high - low + unroll - 1) // unroll, rows, 0)
+
+
+def advances(count, e, v, weights, low, high, step, source=None):
+    def one(m, carry):
+        sweep(e, weights, None, v, low + 2 * m + 1, high - 2 * m - 1, step, source)
+        sweep(v, weights, e, e, low + 2 * m + 2, high - 2 * m - 2, step, source)
         return carry
 
-    lax.fori_loop(0, count, step, 0)
-
-
-def relax_kernel(begin, mine, other, inlet, w4, base, give, own, c, w1, feed, e, v, e0):
+    lax.fori_loop(0, count, one, 0)
+
+
+def relax_kernel(begin, mine, other, inlet, w, base, give, own, c, feed, e, v, e0):
     core, strip, slab = position()
     c[:, pl.ds(PART * core, PART)] = mine[...]
     c[:, pl.ds(PART - PART * core, PART)] = other[...]
-    first = EDGE - REACH
-    e[:, first : first + STRIP + 2 * REACH] = begin[...]
-    e0[:, first : first + STRIP + 2 * REACH] = begin[...]
+    e[:, :ROWS] = begin[...]
+    e0[:, :ROWS] = begin[...]
 
     plane = lax.broadcasted_iota(jnp.int32, (NX, LAST), 0)
     column = lax.broadcasted_iota(jnp.int32, (NX, LAST), 1)
@@ -213,25 +213,23 @@
                 jnp.where(column == LAST - 1, 0.0, wzp),
                 exchange,
             )
-            for factor, w in ((1.0, w1), (COARSE, w4)):
-                q = DAMPING / (1.0 + factor * outflow)
-                fq = factor * q if factor != 1.0 else q
-                for k in range(7):
-                    w[r, 8 * i + k] = fq * inner[k]
-                w[r, 8 * i + 7] = q
-                if i == 1 and factor == 1.0:
-                    feed[r] = jnp.where(top, (fq * wxm)[:8] * warmth, 0.0)
+            for k in range(7):
+                w[r, PAIR * i + k] = inner[k]
+            w[r, PAIR * i + FINE] = DAMPING / (1.0 + outflow)
+            w[r, PAIR * i + COARSE] = (DAMPING * COARSE_FACTOR) / (1.0 + COARSE_FACTOR * outflow)
+            if i == 1:
+                feed[r] = jnp.where(top, wxm[:8] * warmth, 0.0)
         return carry
 
     lax.fori_loop(1, ROWS - 1, weigh, 0)
-    sweep(e0, w4, None, v, EDGE - 3, EDGE + STRIP + 3, True)
-    sweep(v, w4, e0, e0, EDGE - 2, EDGE + STRIP + 2, False)
-    advances(4, e, v, w1, first, first + STRIP + 2 * REACH, feed)
+    sweep(e0, w, None, v, EDGE - 3, EDGE + STRIP + 3, COARSE)
+    sweep(v, w, e0, e0, EDGE - 2, EDGE + STRIP + 2, COARSE)
+    advances(4, e, v, w, 0, ROWS, FINE, feed)
     keep = jnp.where(slab == SLABS - 1, 0.0, 1.0).astype(F32)
     rows = pl.ds(EDGE - 2, STRIP + 4)
     e[:, rows] = e[:, rows] - keep * e0[:, rows]
-    sweep(e, w4, None, v, EDGE - 1, EDGE + STRIP + 1, True)
-    sweep(v, w4, e, e0, EDGE, EDGE + STRIP, False)
+    sweep(e, w, None, v, EDGE - 1, EDGE + STRIP + 1, COARSE)
+    sweep(v, w, e, e0, EDGE, EDGE + STRIP, COARSE)
     joined = jnp.where(slab == SLABS - 2, 0.0, 1.0).astype(F32)
     near, far = pl.ds(EDGE, HALF), pl.ds(EDGE + HALF, HALF)
     base[...] = jnp.where(core == 0, joined * e0[:, near], e[:, far])
@@ -240,33 +238,27 @@
     own[...] = e[:, near]
 
 
-def place(core, e, middle, inward, outward, distance):
-    step = distance * (1 - 2 * core)
-    e[:, pl.ds(middle + step, inward.shape[1])] = inward[...]
-    e[:, pl.ds(middle - step, outward.shape[1])] = outward[...]
-
-
-def far_kernel(own, near, far, swapped, swapped_near, w, out, e, v):
+def place(core, state, middle, inward, outward):
+    many, rim = inward.shape[1], outward.shape[1]
+    state[:, pl.ds(middle + HALF - (HALF + many) * core, many)] = inward[...]
+    state[:, pl.ds(middle - rim + (HALF + rim) * core, rim)] = outward[...]
+
+
+def leap_kernel(summed, *refs):
     core, _, _ = position()
     middle = EDGE + HALF * core
     rows = pl.ds(middle, HALF)
+    own, near, swapped, w = refs[:4]
+    local, (out, *rims, e, v) = (refs[4], refs[5:]) if summed else (None, refs[4:])
     e[:, rows] = own[...]
-    place(core, e, middle, swapped, near, HALF)
-    place(core, e, middle, swapped_near, far, 2 * HALF)
-    advances(8, e, v, w, middle - 16, middle + HALF + 16)
-    out[...] = e[:, rows]
-
-
-def mid_kernel(own, near, swapped, local, w, out, inner, outer, e, v):
-    core, _, _ = position()
-    middle = EDGE + HALF * core
-    rows = pl.ds(middle, HALF)
-    e[:, rows] = own[...]
-    place(core, e, middle, swapped, near, HALF)
-    advances(4, e, v, w, middle - 8, middle + HALF + 8)
-    out[...] = local[...] + e[:, rows]
-    inner[...] = out[:, pl.ds(6 - 6 * core, 2)]
-    outer[...] = out[:, pl.ds(6 * core, 2)]
+    place(core, e, middle, swapped, near)
+    advances(4, e, v, w, middle - HALF, middle + 2 * HALF, COARSE)
+    out[...] = local[...] + e[:, rows] if summed else e[:, rows]
+    if rims:
+        inner, outer, outer_wide = rims
+        inner[...] = out[:, pl.ds(6 - 6 * core, 2)]
+        outer[...] = out[:, pl.ds(6 * core, 2)]
+        outer_wide[...] = out[:, pl.ds(2 * core, 6)]
 
 
 def last_kernel(own, near, swapped, c_own, c_near, c_swapped, g, taken, w, keep, send, e, v, r):
@@ -274,15 +266,14 @@
     middle = EDGE + HALF * core
     rows = pl.ds(middle, HALF)
     e[:, rows] = own[...]
-    place(core, e, middle, swapped, near, HALF)
+    place(core, e, middle, swapped, near)
     r[:, rows] = c_own[...]
-    r[:, pl.ds(middle + HALF - 10 * core, 2)] = c_swapped[...]
-    r[:, pl.ds(middle - 2 + 10 * core, 2)] = c_near[...]
-    advances(2, e, v, w, middle - 6, middle + HALF + 6)
+    place(core, r, middle, c_swapped, c_near)
+    advances(2, e, v, w, middle - 6, middle + HALF + 6, COARSE)
     wide = pl.ds(middle - 2, HALF + 4)
     r[:, wide] = r[:, wide] + e[:, wide]
-    sweep(r, w, None, v, middle - 1, middle + HALF + 1, True)
-    sweep(v, w, r, e, middle, middle + HALF, False)
+    sweep(r, w, None, v, middle - 1, middle + HALF + 1, COARSE)
+    sweep(v, w, r, e, middle, middle + HALF, COARSE)
     e[:, rows] = e[:, rows] + jnp.where(core == 0, g[...], taken[2:4])
     low = lax.broadcasted_iota(jnp.int32, (8, LAST), 0) < PLANES
     for out, other in ((keep, 0), (send, 1)):
@@ -314,6 +305,7 @@
 
 SAME = [(c, c) for c in range(8)]
 HOME = [((c - 1) % 8, c) for c in range(8)]
+UPPER = [(c, c) for c in range(4, 8)]
 LEAP_FOUR = [((c - 5) % 8, c) for c in range(4, 8)]
 LEAP_TWO = [(c - 2, c) for c in range(2, 8)]
 LEAP_ONE = [(c - 1, c) for c in range(1, 8)]
@@ -324,9 +316,9 @@
 
 
 def shards(startup, guess, conduct, couple, inlet):
-    tall = STRIP + 2 * REACH
-    chunk = (2 * tall + 3 * PART) * PLANES
+    chunk = (2 * ROWS + 3 * PART) * PLANES
     half = shape(2, HALF, NX, LAST)
+    arrays = [pltpu.with_memory_space_constraint(a, pltpu.HBM) for a in (startup, guess, conduct, couple)]
     packed = call(
         pack_kernel,
         shape(BRICKS, chunk, LAST),
@@ -339,54 +331,50 @@
             pltpu.SemaphoreType.DMA((5,)),
         ],
         16,
-    )(startup, guess, conduct, couple)
+    )(*arrays)
     got = lax.all_to_all(packed, "space", 0, 0, tiled=True)
     begin, mine = call(
-        unpack_kernel, (shape(2, tall, NX, LAST), shape(3, PART, NX, LAST)), [VMEM], (VMEM, VMEM), [], 16
+        unpack_kernel, (shape(2, ROWS, NX, LAST), shape(3, PART, NX, LAST)), [VMEM], (VMEM, VMEM), [], 16
     )(got)
     other = swap(mine)
 
     field = pltpu.VMEM((2, HELD, NX, LAST), F32)
     weights, base, give, g = call(
         relax_kernel,
-        (shape(HELD, 16, NX, LAST), half, shape(4, HALF, NX, LAST), half),
+        (pltpu.VMEM((HELD, 2 * PAIR, NX, LAST), F32), half, shape(4, HALF, NX, LAST), half),
         [VMEM] * 4,
         (VMEM,) * 4,
-        [
-            pltpu.VMEM((3, ROWS, NX, LAST), F32),
-            pltpu.VMEM((HELD, 16, NX, LAST), F32),
-            pltpu.VMEM((HELD, 8, LAST), F32),
-            field,
-            field,
-            field,
-        ],
-        42,
+        [pltpu.VMEM((3, ROWS, NX, LAST), F32), pltpu.VMEM((HELD, 8, LAST), F32), field, field, field],
+        24,
     )(begin, mine, other, inlet)
     taken = swap(give)
     u = base + taken[:2]
 
-    own = sent(u, LEAP_FOUR, 0, 0)
-    near = sent(u, LEAP_FOUR, 1, 1)
-    far = sent(u, LEAP_FOUR, 0, 1)
-    local = sent(u, HOME, 0, 0)
-    x = call(far_kernel, half, [VMEM] * 6, VMEM, [field, field], 26, 1 << 27)(
-        own, near, far, swap(own), swap(near), weights
+    def leap(own, near, local=None, rims=()):
+        operands = [own, near, swap(own), weights] + ([] if local is None else [local])
+        return call(
+            functools.partial(leap_kernel, local is not None),
+            (half,) + rims,
+            [VMEM] * len(operands),
+            (VMEM,) * (1 + len(rims)),
+            [field, field],
+            20,
+            1 << 26,
+        )(*operands)
+
+    (z,) = leap(sent(u, LEAP_FOUR, 0, 0), sent(u, LEAP_FOUR, 1, 1))
+    (x,) = leap(z, sent(z, UPPER, 1, 1), sent(u, HOME, 0, 0))
+    rim = shape(2, 2, NX, LAST)
+    y, inner, outer, outer_wide = leap(
+        sent(x, LEAP_TWO, 0, 0), sent(x, LEAP_TWO, 1, 1), x, (rim, rim, shape(2, 6, NX, LAST))
     )
-    x = x + local
-
-    own = sent(x, LEAP_TWO, 0, 0)
-    near = sent(x, LEAP_TWO, 1, 1)
-    rim = shape(2, 2, NX, LAST)
-    y, inner, outer = call(mid_kernel, (half, rim, rim), [VMEM] * 5, (VMEM,) * 3, [field, field], 26)(
-        own, near, swap(own), x, weights
-    )
-
-    own = sent(y, LEAP_ONE, 0, 0)
-    near = sent(y, LEAP_ONE, 1, 1)
-    c_near = sent(outer, SAME, 1, 1)
+
+    c_near, c_swapped = sent(outer, SAME, 1, 1), swap(inner)
+    near, own = sent(outer_wide, LEAP_ONE, 1, 1), sent(y, LEAP_ONE, 0, 0)
+    own, near, c_near, c_swapped = lax.optimization_barrier((own, near, c_near, c_swapped))
     parcel = shape(BRICKS, 2 * HALF * PLANES, LAST)
-    keep, send = call(last_kernel, (parcel, parcel), [VMEM] * 9, (VMEM,) * 2, [field, field, field], 26)(
-        own, near, swap(own), y, c_near, swap(inner), g, taken, weights
+    keep, send = call(last_kernel, (parcel, parcel), [VMEM] * 9, (VMEM,) * 2, [field, field, field], 22)(
+        own, near, swap(own), y, c_near, c_swapped, g, taken, weights
     )
     back = lax.all_to_all(jnp.concatenate([keep, swap(send)], axis=1), "space", 0, 0, tiled=True)
     return call(restore_kernel, shape(1, 2, PLANES, MIDDLE, LAST), [VMEM], VMEM, [], 16)(back)

time: 181 us -> 155 us (0.86)
  Pallas kernels: 45.6 us -> 34.7 us
  blocking collectives: 55.3 us -> 46.1 us
  local copies, waits for them, and re-layouts: 8.95 us -> 0.01 us
  waiting for transfers between devices: 33 us -> 38.5 us
  starting transfers between devices: 37.2 us -> 35.2 us
    pallas_call x4 -> x5, Pallas kernels: 41 us -> 29.1 us  [the longest x1 14.6 us: shards(): call(relax_kernel, (pltpu.VMEM((HELD, 2 * PAIR, NX, LAST), F32), half, sh...]
    unnamed x12 -> x2, local copies, waits for them, and re-layouts: 8.95 us -> 0.01 us
    all_to_all x1, blocking collectives: 20.3 us -> 14.4 us  [shards(): lax.all_to_all(jnp.concatenate([keep, swap(send)], axis=1), 'space', 0, 0...]
    ppermute x17, waiting for transfers between devices: 33 us -> 38.5 us  [sent(): return lax.ppermute(value, AXES, pairs)]
    all_to_all x1, blocking collectives: 35 us -> 31.8 us  [shards(): got = lax.all_to_all(packed, 'space', 0, 0, tiled=True)]
    ppermute x17, starting transfers between devices: 37.2 us -> 35.2 us  [sent(): return lax.ppermute(value, AXES, pairs)]
  transfers between devices with their start and end apart: 17 -> 17, of which waited for: 9 -> 10; matrix products, arithmetic and copies ran while one was open for 0% -> 0% of each run, Pallas kernels for 8% -> 3%
where the time goes in v3:
time: 155 us
  blocking collectives  46.1 us (30%)
  waiting for transfers between devices  38.5 us (25%)
  starting transfers between devices  35.2 us (23%)
  Pallas kernels  34.7 us (22%)
    ppermute x17, waiting for transfers between devices, sent(): return lax.ppermute(value, AXES, pairs)  38.5 us
    ppermute x17, starting transfers between devices, sent(): return lax.ppermute(value, AXES, pairs)  35.2 us
    all_to_all x1, blocking collectives, shards(): got = lax.all_to_all(packed, 'space', 0, 0, tiled=True)  31.8 us
    pallas_call x1, Pallas kernels, shards(): call(relax_kernel, (pltpu.VMEM((HELD, 2 * PAIR, NX, LAST), F32), half, sh...  14.6 us
    pallas_call x3, Pallas kernels, leap(): call(functools.partial(leap_kernel, local is not None), (half,) + rims, [...  14.4 us
    all_to_all x1, blocking collectives, shards(): lax.all_to_all(jnp.concatenate([keep, swap(send)], axis=1), 'space', 0, 0...  14.4 us
    pallas_call x1, Pallas kernels, shards(): call(last_kernel, (parcel, parcel), [VMEM] * 9, (VMEM,) * 2, [field, fiel...  3.31 us
  transfers between devices with their start and end apart: 17, of which 10 were waited for; matrix products, arithmetic and copies ran while one was open for 0% of the time, Pallas kernels for 3%

profile of v3, /device:TPU:4, one launch (start us, length us, event | category | flops | bytes accessed | tf_op | source)
XLA Modules:
  0.0 154.7 jit_solution(1157314428274464582)
XLA Ops:
  0.0 1.5 shard_map.55
  1.5 31.8 %all_to_all.10.got = f32[8,504,128]{2,1,0:T(8,128)S(1)} all-to-all(f32[8,504,128]{2,1,0:T(8,128)S(1)} %shard_map.55), channel_id=1, replica_groups=mesh['chip'=8,'core'=2,'space'=8] {'space'}, dimensions={0} | all-to-all | bytes 4128768 | tf_op jit(solution)/shard_map/all_to_all | solution.py:335
  33.3 0.0 copy-start
  33.3 0.1 shard_map.56
  33.4 0.1 collective-permute-start
  33.5 2.4 %collective-permute-done.other = f32[3,18,32,128]{3,2,1,0:T(8,128)S(1)} collective-permute-done((f32[3,18,32,128]{3,2,1,0:T(8,128)S(1)}, f32[3,18,32,128]{3,2,1,0:T(8,128)S(1)}, u32[]{:S(2)}, u32[]{:S(2)}) %collective-permute-start) | collective-permute-done | bytes 884768 | tf_op jit(solution)/shard_map/ppermute | solution.py:303
  35.9 0.0 copy-done
  35.9 14.6 %shard_map.57 = (f32[40,18,32,128]{3,2,1,0:T(8,128)S(1)}, f32[2,8,32,128]{3,2,1,0:T(8,128)S(1)}, f32[4,8,32,128]{3,2,1,0:T(8,128)S(1)}, f32[2,8,32,128]{3,2,1,0:T(8,128)S(1)}) custom-call(f32[2,36,32,128]{3,2,1,0:T(8,128)S(1)} %get-tuple-element.21.begin, f32[3,18,32,128]{3,2,1,0:T(8,128)S(1)} %get-tuple-element.22.mine, ...), custom_call_target="tpu_custom_call" | custom-call | tf_op jit(solution)/shard_map/pallas_call | solution.py:342
  50.5 0.2 collective-permute-start.1
  50.7 1.8 %collective-permute-done.1.taken = f32[4,8,32,128]{3,2,1,0:T(8,128)S(1)} collective-permute-done((f32[4,8,32,128]{3,2,1,0:T(8,128)S(1)}, f32[4,8,32,128]{3,2,1,0:T(8,128)S(1)}, u32[]{:S(2)}, u32[]{:S(2)}) %collective-permute-start.1) | collective-permute-done | bytes 524320 | tf_op jit(solution)/shard_map/ppermute | solution.py:303
  52.5 1.3 collective-permute-start.2
  53.8 0.7 collective-permute-start.3
  54.5 13.4 %collective-permute-done.2.refs_0_ = f32[2,8,32,128]{3,2,1,0:T(8,128)S(1)} collective-permute-done((f32[2,8,32,128]{3,2,1,0:T(8,128)S(1)}, f32[2,8,32,128]{3,2,1,0:T(8,128)S(1)}, u32[]{:S(2)}, u32[]{:S(2)}) %collective-permute-start.2) | collective-permute-done | bytes 262176 | tf_op jit(solution)/shard_map/ppermute | solution.py:303
  67.9 0.0 collective-permute-start.4
  67.9 0.0 collective-permute-start.7
  67.9 0.0 collective-permute-done.3.refs_1_
  67.9 1.5 collective-permute-done.4.refs_2_
  69.4 4.8 %shard_map.58.refs_0_ = f32[2,8,32,128]{3,2,1,0:T(8,128)S(1)} custom-call(f32[2,8,32,128]{3,2,1,0:T(8,128)S(1)} %collective-permute-done.2.refs_0_, f32[2,8,32,128]{3,2,1,0:T(8,128)S(1)} %collective-permute-done.3.refs_1_, f32[2,8,32,128]{3,2,1,0:T(8,128)S(1)} %collective-permute-done.4.refs_2_, f32[40,18,32,128]{3,2,1,0:T(8,128)S(1)} %get-tuple-element.25.refs_3_.w), custom_call_target="tpu_custom_call" | custom-call | flops 67108864 | bytes 1048576 | tf_op jit(solution)/shard_map/pallas_call | solution.py:355
  74.2 0.2 collective-permute-start.6
  74.4 0.7 collective-permute-start.5
  75.1 5.1 %collective-permute-done.7.refs_4_ = f32[2,8,32,128]{3,2,1,0:T(8,128)S(1)} collective-permute-done((f32[2,8,32,128]{3,2,1,0:T(8,128)S(1)}, f32[2,8,32,128]{3,2,1,0:T(8,128)S(1)}, u32[]{:S(2)}, u32[]{:S(2)}) %collective-permute-start.7) | collective-permute-done | bytes 262176 | tf_op jit(solution)/shard_map/ppermute | solution.py:303
  80.2 0.0 collective-permute-done.6.refs_2_
  80.2 0.0 collective-permute-done.5.refs_1_
  80.2 4.8 %shard_map.59.refs_4_ = f32[2,8,32,128]{3,2,1,0:T(8,128)S(1)} custom-call(f32[2,8,32,128]{3,2,1,0:T(8,128)S(1)} %shard_map.58.refs_0_, f32[2,8,32,128]{3,2,1,0:T(8,128)S(1)} %collective-permute-done.5.refs_1_, f32[2,8,32,128]{3,2,1,0:T(8,128)S(1)} %collective-permute-done.6.refs_2_, f32[40,18,32,128]{3,2,1,0:T(8,128)S(1)} %get-tuple-element.25.refs_3_.w, ...), custom_call_target="tpu_custom_call" | custom-call | flops 67108864 | bytes 1048576 | tf_op jit(solution)/shard_map/pallas_call | solution.py:355
  85.0 2.0 %collective-permute-start.8 = (f32[2,8,32,128]{3,2,1,0:T(8,128)S(1)}, f32[2,8,32,128]{3,2,1,0:T(8,128)S(1)}, u32[]{:S(2)}, u32[]{:S(2)}) collective-permute-start(f32[2,8,32,128]{3,2,1,0:T(8,128)S(1)} %shard_map.59.refs_4_), channel_id=1, source_target_pairs={{0,32},{2,34},{4,36},{6,38},{7,39},{5,37},{3,35},{1,33},{8,40},{10... | collective-permute-start | bytes 786440 | tf_op jit(solution)/shard_map/ppermute | solution.py:303
  87.0 0.7 collective-permute-start.9
  87.7 9.9 %collective-permute-done.8.refs_0_ = f32[2,8,32,128]{3,2,1,0:T(8,128)S(1)} collective-permute-done((f32[2,8,32,128]{3,2,1,0:T(8,128)S(1)}, f32[2,8,32,128]{3,2,1,0:T(8,128)S(1)}, u32[]{:S(2)}, u32[]{:S(2)}) %collective-permute-start.8) | collective-permute-done | bytes 262176 | tf_op jit(solution)/shard_map/ppermute | solution.py:303
  97.6 2.2 %collective-permute-start.10 = (f32[2,8,32,128]{3,2,1,0:T(8,128)S(1)}, f32[2,8,32,128]{3,2,1,0:T(8,128)S(1)}, u32[]{:S(2)}, u32[]{:S(2)}) collective-permute-start(f32[2,8,32,128]{3,2,1,0:T(8,128)S(1)} %collective-permute-done.8.refs_0_), channel_id=1, source_target_pairs={{8,0},{10,2},{12,4},{14,6},{15,7},{13,5},{11,3},{9,1},{0,8},{2,10}... | collective-permute-start | bytes 786440 | tf_op jit(solution)/shard_map/ppermute | solution.py:303
  99.8 0.0 collective-permute-done.9.refs_1_
  99.8 1.2 collective-permute-done.10.refs_2_
  101.0 4.8 %shard_map.60 = (f32[2,8,32,128]{3,2,1,0:T(8,128)S(1)}, f32[2,2,32,128]{3,2,1,0:T(8,128)S(1)}, f32[2,2,32,128]{3,2,1,0:T(8,128)S(1)}, f32[2,6,32,128]{3,2,1,0:T(8,128)S(1)}) custom-call(f32[2,8,32,128]{3,2,1,0:T(8,128)S(1)} %collective-permute-done.8.refs_0_, f32[2,8,32,128]{3,2,1,0:T(8,128)S(1)} %collective-permute-done.9.refs_1_, ...), custom_call_target="tpu_custom_call" | custom-call | flops 67108864 | bytes 1048576 | tf_op jit(solution)/shard_map/pallas_call | solution.py:355
  105.8 2.8 %collective-permute-start.11 = (f32[2,8,32,128]{3,2,1,0:T(8,128)S(1)}, f32[2,8,32,128]{3,2,1,0:T(8,128)S(1)}, u32[]{:S(2)}, u32[]{:S(2)}) collective-permute-start(f32[2,8,32,128]{3,2,1,0:T(8,128)S(1)} %get-tuple-element.26.c_own), channel_id=1, source_target_pairs={{0,16},{2,18},{4,20},{6,22},{7,23},{5,21},{3,19},{1,17},{8,24},{10... | collective-permute-start | bytes 786440 | tf_op jit(solution)/shard_map/ppermute | solution.py:303
  108.6 0.7 collective-permute-start.12
  109.3 0.7 collective-permute-start.13
  110.0 12.0 %collective-permute-start.14 = (f32[2,2,32,128]{3,2,1,0:T(8,128)S(1)}, f32[2,2,32,128]{3,2,1,0:T(8,128)S(1)}, u32[]{:S(2)}, u32[]{:S(2)}) collective-permute-start(f32[2,2,32,128]{3,2,1,0:T(8,128)S(1)} %get-tuple-element.29), channel_id=1, source_target_pairs={{8,0},{10,2},{12,4},{14,6},{15,7},{13,5},{11,3},{9,1},{0,8},{2,10}... | collective-permute-start | bytes 196616 | tf_op jit(solution)/shard_map/ppermute | solution.py:303
  122.0 0.0 collective-permute-done.13.c_near
  122.0 0.9 collective-permute-done.14.c_swapped
  122.9 0.0 collective-permute-done.12.near
  122.9 0.0 collective-permute-done.11.own
  122.9 10.5 %collective-permute-start.15 = (f32[2,8,32,128]{3,2,1,0:T(8,128)S(1)}, f32[2,8,32,128]{3,2,1,0:T(8,128)S(1)}, u32[]{:S(2)}, u32[]{:S(2)}) collective-permute-start(f32[2,8,32,128]{3,2,1,0:T(8,128)S(1)} %collective-permute-done.11.own), channel_id=1, source_target_pairs={{8,0},{10,2},{12,4},{14,6},{15,7},{13,5},{11,3},{9,1},{0,8},{2,10}... | collective-permute-start | bytes 786440 | tf_op jit(solution)/shard_map/ppermute | solution.py:303
  133.4 1.2 collective-permute-done.15.swapped
  134.6 3.3 %shard_map.61 = (f32[8,64,128]{2,1,0:T(8,128)S(1)}, f32[8,64,128]{2,1,0:T(8,128)S(1)}) custom-call(f32[2,8,32,128]{3,2,1,0:T(8,128)S(1)} %collective-permute-done.11.own, f32[2,6,32,128]{3,2,1,0:T(8,128)S(1)} %collective-permute-done.12.near, f32[2,8,32,128]{3,2,1,0:T(8,128)S(1)} %collective-permute-done.15.swapped, ...), custom_call_target="tpu_custom_call" | custom-call | tf_op jit(solution)/shard_map/pallas_call | solution.py:376
  137.9 0.5 collective-permute-start.16
  138.3 1.2 collective-permute-done.16
  139.5 14.4 %all_to_all.11.got = f32[8,128,128]{2,1,0:T(8,128)S(1)} all-to-all(f32[8,128,128]{2,1,0:T(8,128)S(1)} %pad_maximum_fusion), channel_id=1, replica_groups=mesh['chip'=8,'core'=2,'space'=8] {'space'}, dimensions={0} | all-to-all | bytes 1048576 | tf_op jit(solution)/shard_map/all_to_all | solution.py:379
  153.9 0.8 shard_map.62
  (2 shorter events, 0.1 us)
Async XLA Ops:
  33.3 2.7 %copy-start = (f32[128,128]{1,0:T(8,128)S(1)}, f32[128,128]{1,0:T(8,128)}, u32[]{:S(2)}) copy-start(f32[128,128]{1,0:T(8,128)} %inlet.1) | copy-start | bytes 196612
  33.4 2.5 %collective-permute-start = (f32[3,18,32,128]{3,2,1,0:T(8,128)S(1)}, f32[3,18,32,128]{3,2,1,0:T(8,128)S(1)}, u32[]{:S(2)}, u32[]{:S(2)}) collective-permute-start(f32[3,18,32,128]{3,2,1,0:T(8,128)S(1)} %get-tuple-element.22.mine), channel_id=1, source_target_pairs={{8,0},{10,2},{12,4},{14,6},{15,7},{13,5},{11,3},{9,1},{0,8},{2,10}... | collective-permute-start | bytes 2654216 | tf_op jit(solution)/shard_map/ppermute | solution.py:303
  50.5 2.0 %collective-permute-start.1 = (f32[4,8,32,128]{3,2,1,0:T(8,128)S(1)}, f32[4,8,32,128]{3,2,1,0:T(8,128)S(1)}, u32[]{:S(2)}, u32[]{:S(2)}) collective-permute-start(f32[4,8,32,128]{3,2,1,0:T(8,128)S(1)} %get-tuple-element.24), channel_id=1, source_target_pairs={{8,0},{10,2},{12,4},{14,6},{15,7},{13,5},{11,3},{9,1},{0,8},{2,10}... | collective-permute-start | bytes 1572872 | tf_op jit(solution)/shard_map/ppermute | solution.py:303
  52.5 15.4 %collective-permute-start.2 = (f32[2,8,32,128]{3,2,1,0:T(8,128)S(1)}, f32[2,8,32,128]{3,2,1,0:T(8,128)S(1)}, u32[]{:S(2)}, u32[]{:S(2)}) collective-permute-start(f32[2,8,32,128]{3,2,1,0:T(8,128)S(1)} %slice_add_fusion), channel_id=1, source_target_pairs={{112,64},{114,66},{116,68},{118,70},{119,71},{117,69},{115,67},{11... | collective-permute-start | bytes 786440 | tf_op jit(solution)/shard_map/ppermute | solution.py:303
  53.8 14.1 %collective-permute-start.3 = (f32[2,8,32,128]{3,2,1,0:T(8,128)S(1)}, f32[2,8,32,128]{3,2,1,0:T(8,128)S(1)}, u32[]{:S(2)}, u32[]{:S(2)}) collective-permute-start(f32[2,8,32,128]{3,2,1,0:T(8,128)S(1)} %slice_add_fusion), channel_id=1, source_target_pairs={{120,66},{122,68},{124,70},{126,71},{127,69},{125,67},{123,65},{11... | collective-permute-start | bytes 786440 | tf_op jit(solution)/shard_map/ppermute | solution.py:303
  67.9 1.5 collective-permute-start.4
  67.9 12.3 %collective-permute-start.7 = (f32[2,8,32,128]{3,2,1,0:T(8,128)S(1)}, f32[2,8,32,128]{3,2,1,0:T(8,128)S(1)}, u32[]{:S(2)}, u32[]{:S(2)}) collective-permute-start(f32[2,8,32,128]{3,2,1,0:T(8,128)S(1)} %slice_add_fusion), channel_id=1, source_target_pairs={{112,0},{114,2},{116,4},{118,6},{119,7},{117,5},{115,3},{113,1},{1... | collective-permute-start | bytes 786440 | tf_op jit(solution)/shard_map/ppermute | solution.py:303
  74.2 6.0 %collective-permute-start.6 = (f32[2,8,32,128]{3,2,1,0:T(8,128)S(1)}, f32[2,8,32,128]{3,2,1,0:T(8,128)S(1)}, u32[]{:S(2)}, u32[]{:S(2)}) collective-permute-start(f32[2,8,32,128]{3,2,1,0:T(8,128)S(1)} %shard_map.58.refs_0_), channel_id=1, source_target_pairs={{8,0},{10,2},{12,4},{14,6},{15,7},{13,5},{11,3},{9,1},{0,8},{2,10}... | collective-permute-start | bytes 786440 | tf_op jit(solution)/shard_map/ppermute | solution.py:303
  74.4 5.8 %collective-permute-start.5 = (f32[2,8,32,128]{3,2,1,0:T(8,128)S(1)}, f32[2,8,32,128]{3,2,1,0:T(8,128)S(1)}, u32[]{:S(2)}, u32[]{:S(2)}) collective-permute-start(f32[2,8,32,128]{3,2,1,0:T(8,128)S(1)} %shard_map.58.refs_0_), channel_id=1, source_target_pairs={{72,66},{74,68},{76,70},{78,71},{79,69},{77,67},{75,65},{66,72},{6... | collective-permute-start | bytes 786440 | tf_op jit(solution)/shard_map/ppermute | solution.py:303
  85.0 12.6 %collective-permute-start.8 = (f32[2,8,32,128]{3,2,1,0:T(8,128)S(1)}, f32[2,8,32,128]{3,2,1,0:T(8,128)S(1)}, u32[]{:S(2)}, u32[]{:S(2)}) collective-permute-start(f32[2,8,32,128]{3,2,1,0:T(8,128)S(1)} %shard_map.59.refs_4_), channel_id=1, source_target_pairs={{0,32},{2,34},{4,36},{6,38},{7,39},{5,37},{3,35},{1,33},{8,40},{10... | collective-permute-start | bytes 786440 | tf_op jit(solution)/shard_map/ppermute | solution.py:303
  87.0 12.8 %collective-permute-start.9 = (f32[2,8,32,128]{3,2,1,0:T(8,128)S(1)}, f32[2,8,32,128]{3,2,1,0:T(8,128)S(1)}, u32[]{:S(2)}, u32[]{:S(2)}) collective-permute-start(f32[2,8,32,128]{3,2,1,0:T(8,128)S(1)} %shard_map.59.refs_4_), channel_id=1, source_target_pairs={{8,34},{10,36},{12,38},{14,39},{15,37},{13,35},{11,33},{2,40},{4,4... | collective-permute-start | bytes 786440 | tf_op jit(solution)/shard_map/ppermute | solution.py:303
  97.6 3.4 %collective-permute-start.10 = (f32[2,8,32,128]{3,2,1,0:T(8,128)S(1)}, f32[2,8,32,128]{3,2,1,0:T(8,128)S(1)}, u32[]{:S(2)}, u32[]{:S(2)}) collective-permute-start(f32[2,8,32,128]{3,2,1,0:T(8,128)S(1)} %collective-permute-done.8.refs_0_), channel_id=1, source_target_pairs={{8,0},{10,2},{12,4},{14,6},{15,7},{13,5},{11,3},{9,1},{0,8},{2,10}... | collective-permute-start | bytes 786440 | tf_op jit(solution)/shard_map/ppermute | solution.py:303
  105.8 17.1 %collective-permute-start.11 = (f32[2,8,32,128]{3,2,1,0:T(8,128)S(1)}, f32[2,8,32,128]{3,2,1,0:T(8,128)S(1)}, u32[]{:S(2)}, u32[]{:S(2)}) collective-permute-start(f32[2,8,32,128]{3,2,1,0:T(8,128)S(1)} %get-tuple-element.26.c_own), channel_id=1, source_target_pairs={{0,16},{2,18},{4,20},{6,22},{7,23},{5,21},{3,19},{1,17},{8,24},{10... | collective-permute-start | bytes 786440 | tf_op jit(solution)/shard_map/ppermute | solution.py:303
  108.6 14.3 %collective-permute-start.12 = (f32[2,6,32,128]{3,2,1,0:T(8,128)S(1)}, f32[2,6,32,128]{3,2,1,0:T(8,128)S(1)}, u32[]{:S(2)}, u32[]{:S(2)}) collective-permute-start(f32[2,6,32,128]{3,2,1,0:T(8,128)S(1)} %get-tuple-element.27), channel_id=1, source_target_pairs={{8,18},{10,20},{12,22},{14,23},{15,21},{13,19},{11,17},{2,24},{4,2... | collective-permute-start | bytes 589832 | tf_op jit(solution)/shard_map/ppermute | solution.py:303
  109.3 12.7 %collective-permute-start.13 = (f32[2,2,32,128]{3,2,1,0:T(8,128)S(1)}, f32[2,2,32,128]{3,2,1,0:T(8,128)S(1)}, u32[]{:S(2)}, u32[]{:S(2)}) collective-permute-start(f32[2,2,32,128]{3,2,1,0:T(8,128)S(1)} %get-tuple-element.28), channel_id=1, source_target_pairs={{8,2},{10,4},{12,6},{14,7},{15,5},{13,3},{11,1},{2,8},{4,10},{6,12... | collective-permute-start | bytes 196616 | tf_op jit(solution)/shard_map/ppermute | solution.py:303
  110.0 12.9 %collective-permute-start.14 = (f32[2,2,32,128]{3,2,1,0:T(8,128)S(1)}, f32[2,2,32,128]{3,2,1,0:T(8,128)S(1)}, u32[]{:S(2)}, u32[]{:S(2)}) collective-permute-start(f32[2,2,32,128]{3,2,1,0:T(8,128)S(1)} %get-tuple-element.29), channel_id=1, source_target_pairs={{8,0},{10,2},{12,4},{14,6},{15,7},{13,5},{11,3},{9,1},{0,8},{2,10}... | collective-permute-start | bytes 196616 | tf_op jit(solution)/shard_map/ppermute | solution.py:303
  122.9 11.7 %collective-permute-start.15 = (f32[2,8,32,128]{3,2,1,0:T(8,128)S(1)}, f32[2,8,32,128]{3,2,1,0:T(8,128)S(1)}, u32[]{:S(2)}, u32[]{:S(2)}) collective-permute-start(f32[2,8,32,128]{3,2,1,0:T(8,128)S(1)} %collective-permute-done.11.own), channel_id=1, source_target_pairs={{8,0},{10,2},{12,4},{14,6},{15,7},{13,5},{11,3},{9,1},{0,8},{2,10}... | collective-permute-start | bytes 786440 | tf_op jit(solution)/shard_map/ppermute | solution.py:303
  137.9 1.6 %collective-permute-start.16 = (f32[8,64,128]{2,1,0:T(8,128)S(1)}, f32[8,64,128]{2,1,0:T(8,128)S(1)}, u32[]{:S(2)}, u32[]{:S(2)}) collective-permute-start(f32[8,64,128]{2,1,0:T(8,128)S(1)} %get-tuple-element.36), channel_id=1, source_target_pairs={{8,0},{10,2},{12,4},{14,6},{15,7},{13,5},{11,3},{9,1},{0,8},{2,10}... | collective-permute-start | bytes 786440 | tf_op jit(solution)/shard_map/ppermute | solution.py:303

commit v4 on v3

--- a/solution.py
+++ b/solution.py
@@ -244,34 +244,43 @@
     state[:, pl.ds(middle - rim + (HALF + rim) * core, rim)] = outward[...]
 
 
-def leap_kernel(summed, *refs):
+def leap_kernel(own, near, swapped, w, odd, *refs):
     core, _, _ = position()
     middle = EDGE + HALF * core
     rows = pl.ds(middle, HALF)
-    own, near, swapped, w = refs[:4]
-    local, (out, *rims, e, v) = (refs[4], refs[5:]) if summed else (None, refs[4:])
+    *more, e, v = refs
+    reach = HALF if more else HALF // 2
     e[:, rows] = own[...]
     place(core, e, middle, swapped, near)
-    advances(4, e, v, w, middle - HALF, middle + 2 * HALF, COARSE)
-    out[...] = local[...] + e[:, rows] if summed else e[:, rows]
-    if rims:
-        inner, outer, outer_wide = rims
-        inner[...] = out[:, pl.ds(6 - 6 * core, 2)]
-        outer[...] = out[:, pl.ds(6 * core, 2)]
-        outer_wide[...] = out[:, pl.ds(2 * core, 6)]
-
-
-def last_kernel(own, near, swapped, c_own, c_near, c_swapped, g, taken, w, keep, send, e, v, r):
+    advances(2, e, v, w, middle - reach, middle + HALF + reach, COARSE)
+    odd[...] = e[:, rows]
+    if more:
+        even, *rims = more
+        advances(2, e, v, w, middle - 4, middle + HALF + 4, COARSE)
+        even[...] = e[:, rows]
+        if rims:
+            inner, outer = rims
+            inner[...] = even[:, pl.ds(4 - 4 * core, 4)]
+            outer[...] = even[:, pl.ds(4 * core, 4)]
+
+
+def sum_kernel(local, *refs):
+    core, _, slab = position()
+    *arrived, out, inner, outer = refs
+    total = arrived[0][...]
+    for ref in arrived[1:]:
+        total = total + ref[...]
+    out[...] = total + jnp.where(slab // 2 == SLABS // 2 - 1, local[...], 0.0)
+    inner[...] = out[:, pl.ds(6 - 6 * core, 2)]
+    outer[...] = out[:, pl.ds(6 * core, 2)]
+
+
+def last_kernel(own, near, swapped, g, taken, w, keep, send, r, v, e):
     core, _, _ = position()
     middle = EDGE + HALF * core
     rows = pl.ds(middle, HALF)
-    e[:, rows] = own[...]
-    place(core, e, middle, swapped, near)
-    r[:, rows] = c_own[...]
-    place(core, r, middle, c_swapped, c_near)
-    advances(2, e, v, w, middle - 6, middle + HALF + 6, COARSE)
-    wide = pl.ds(middle - 2, HALF + 4)
-    r[:, wide] = r[:, wide] + e[:, wide]
+    r[:, rows] = own[...]
+    place(core, r, middle, swapped, near)
     sweep(r, w, None, v, middle - 1, middle + HALF + 1, COARSE)
     sweep(v, w, r, e, middle, middle + HALF, COARSE)
     e[:, rows] = e[:, rows] + jnp.where(core == 0, g[...], taken[2:4])
@@ -303,12 +312,12 @@
     return lax.ppermute(value, AXES, pairs)
 
 
-SAME = [(c, c) for c in range(8)]
-HOME = [((c - 1) % 8, c) for c in range(8)]
-UPPER = [(c, c) for c in range(4, 8)]
-LEAP_FOUR = [((c - 5) % 8, c) for c in range(4, 8)]
-LEAP_TWO = [(c - 2, c) for c in range(2, 8)]
-LEAP_ONE = [(c - 1, c) for c in range(1, 8)]
+CHIPS = SLABS // 2
+SAME = [(c, c) for c in range(CHIPS)]
+
+
+def onward(power):
+    return [((j - 1) % CHIPS, j + power) for j in range(CHIPS - power)]
 
 
 def swap(value):
@@ -350,31 +359,25 @@
     taken = swap(give)
     u = base + taken[:2]
 
-    def leap(own, near, local=None, rims=()):
-        operands = [own, near, swap(own), weights] + ([] if local is None else [local])
-        return call(
-            functools.partial(leap_kernel, local is not None),
-            (half,) + rims,
-            [VMEM] * len(operands),
-            (VMEM,) * (1 + len(rims)),
-            [field, field],
-            20,
-            1 << 26,
-        )(*operands)
-
-    (z,) = leap(sent(u, LEAP_FOUR, 0, 0), sent(u, LEAP_FOUR, 1, 1))
-    (x,) = leap(z, sent(z, UPPER, 1, 1), sent(u, HOME, 0, 0))
-    rim = shape(2, 2, NX, LAST)
-    y, inner, outer, outer_wide = leap(
-        sent(x, LEAP_TWO, 0, 0), sent(x, LEAP_TWO, 1, 1), x, (rim, rim, shape(2, 6, NX, LAST))
-    )
-
-    c_near, c_swapped = sent(outer, SAME, 1, 1), swap(inner)
-    near, own = sent(outer_wide, LEAP_ONE, 1, 1), sent(y, LEAP_ONE, 0, 0)
-    own, near, c_near, c_swapped = lax.optimization_barrier((own, near, c_near, c_swapped))
+    def leap(own, near, swapped, *rims, second=True):
+        outs = (half,) * (1 + second) + rims
+        return call(leap_kernel, outs, [VMEM] * 4, (VMEM,) * len(outs), [field, field], 20, 1 << 26)(
+            own, near, swapped, weights
+        )
+
+    def beside(value):
+        return sent(value, SAME, 1, 1)
+
+    rim4, rim2 = shape(2, 4, NX, LAST), shape(2, 2, NX, LAST)
+    u1, u2 = leap(u, beside(u), swap(u))
+    u3, u4 = leap(u2, beside(u2), swap(u2))
+    u5, u6, inner, outer = leap(u4, beside(u4), swap(u4), rim4, rim4)
+    (u7,) = leap(u6, beside(outer), swap(inner), second=False)
+    arrived = [sent(power, onward(k), 0, 0) for k, power in enumerate((u, u1, u2, u3, u4, u5, u6))]
+    c, inner, outer = call(sum_kernel, (half, rim2, rim2), [VMEM] * 8, (VMEM,) * 3, [], 16)(u7, *arrived)
     parcel = shape(BRICKS, 2 * HALF * PLANES, LAST)
-    keep, send = call(last_kernel, (parcel, parcel), [VMEM] * 9, (VMEM,) * 2, [field, field, field], 22)(
-        own, near, swap(own), y, c_near, c_swapped, g, taken, weights
+    keep, send = call(last_kernel, (parcel, parcel), [VMEM] * 6, (VMEM,) * 2, [field, field, field], 22)(
+        c, beside(outer), swap(inner), g, taken, weights
     )
     back = lax.all_to_all(jnp.concatenate([keep, swap(send)], axis=1), "space", 0, 0, tiled=True)
     return call(restore_kernel, shape(1, 2, PLANES, MIDDLE, LAST), [VMEM], VMEM, [], 16)(back)

time: 155 us -> 153 us (0.987)
  the two profiles are of different devices: /device:TPU:4 before, /device:TPU:100 now
where the time goes in v4:
time: 153 us; the launch traced here: 152 us
  blocking collectives  46.8 us (31%)
  starting transfers between devices  42.2 us (28%)
  Pallas kernels  34.3 us (22%)
  waiting for transfers between devices  28.7 us (19%)
    ppermute x20, starting transfers between devices, sent(): return lax.ppermute(value, AXES, pairs)  42.2 us
    all_to_all x1, blocking collectives, shards(): got = lax.all_to_all(packed, 'space', 0, 0, tiled=True)  31.8 us
    ppermute x20, waiting for transfers between devices, sent(): return lax.ppermute(value, AXES, pairs)  28.7 us
    pallas_call x4, Pallas kernels, leap(): call(leap_kernel, outs, [VMEM] * 4, (VMEM,) * len(outs), [field, field],...  16.2 us
    all_to_all x1, blocking collectives, shards(): lax.all_to_all(jnp.concatenate([keep, swap(send)], axis=1), 'space', 0, 0...  15 us
    pallas_call x1, Pallas kernels, shards(): call(relax_kernel, (pltpu.VMEM((HELD, 2 * PAIR, NX, LAST), F32), half, sh...  14.6 us
  transfers between devices with their start and end apart: 20, of which 9 were waited for; matrix products, arithmetic and copies ran while one was open for 0% of the time, Pallas kernels for 4%

profile of v4, /device:TPU:100, one launch (start us, length us, event | category | flops | bytes accessed | tf_op | source)
XLA Modules:
  0.0 152.2 jit_solution(7170863697778173137)
XLA Ops:
  0.0 1.5 shard_map.55
  1.5 31.8 %all_to_all.10.got = f32[8,504,128]{2,1,0:T(8,128)S(1)} all-to-all(f32[8,504,128]{2,1,0:T(8,128)S(1)} %shard_map.55), channel_id=1, replica_groups=mesh['chip'=8,'core'=2,'space'=8] {'space'}, dimensions={0} | all-to-all | bytes 4128768 | tf_op jit(solution)/shard_map/all_to_all | solution.py:344
  33.3 0.0 copy-start
  33.3 0.1 shard_map.56
  33.4 0.1 collective-permute-start
  33.5 2.4 %collective-permute-done.other = f32[3,18,32,128]{3,2,1,0:T(8,128)S(1)} collective-permute-done((f32[3,18,32,128]{3,2,1,0:T(8,128)S(1)}, f32[3,18,32,128]{3,2,1,0:T(8,128)S(1)}, u32[]{:S(2)}, u32[]{:S(2)}) %collective-permute-start) | collective-permute-done | bytes 884768 | tf_op jit(solution)/shard_map/ppermute | solution.py:312
  35.9 0.0 copy-done
  35.9 14.6 %shard_map.57 = (f32[40,18,32,128]{3,2,1,0:T(8,128)S(1)}, f32[2,8,32,128]{3,2,1,0:T(8,128)S(1)}, f32[4,8,32,128]{3,2,1,0:T(8,128)S(1)}, f32[2,8,32,128]{3,2,1,0:T(8,128)S(1)}) custom-call(f32[2,36,32,128]{3,2,1,0:T(8,128)S(1)} %get-tuple-element.24.begin, f32[3,18,32,128]{3,2,1,0:T(8,128)S(1)} %get-tuple-element.25.mine, ...), custom_call_target="tpu_custom_call" | custom-call | tf_op jit(solution)/shard_map/pallas_call | solution.py:351
  50.5 0.2 collective-permute-start.1
  50.7 1.8 %collective-permute-done.1.taken = f32[4,8,32,128]{3,2,1,0:T(8,128)S(1)} collective-permute-done((f32[4,8,32,128]{3,2,1,0:T(8,128)S(1)}, f32[4,8,32,128]{3,2,1,0:T(8,128)S(1)}, u32[]{:S(2)}, u32[]{:S(2)}) %collective-permute-start.1) | collective-permute-done | bytes 524320 | tf_op jit(solution)/shard_map/ppermute | solution.py:312
  52.5 0.2 collective-permute-start.3
  52.8 0.7 collective-permute-start.2
  53.4 0.7 collective-permute-done.3.swapped
  54.2 0.0 collective-permute-done.2.near
  54.2 4.8 %shard_map.58 = (f32[2,8,32,128]{3,2,1,0:T(8,128)S(1)}, f32[2,8,32,128]{3,2,1,0:T(8,128)S(1)}) custom-call(f32[2,8,32,128]{3,2,1,0:T(8,128)S(1)} %slice_add_fusion.own, f32[2,8,32,128]{3,2,1,0:T(8,128)S(1)} %collective-permute-done.2.near, f32[2,8,32,128]{3,2,1,0:T(8,128)S(1)} %collective-permute-done.3.swapped, f32[40,18,32,128]{3,2,1,0:T(8,128)S(1)} %get-tuple-element.28.w), custom_call_target="tpu_custom_call" | custom-call | flops 67108864 | bytes 1048576 | tf_op jit(solution)/shard_map/pallas_call | solution.py:364
  59.0 6.7 %collective-permute-start.5 = (f32[2,8,32,128]{3,2,1,0:T(8,128)S(1)}, f32[2,8,32,128]{3,2,1,0:T(8,128)S(1)}, u32[]{:S(2)}, u32[]{:S(2)}) collective-permute-start(f32[2,8,32,128]{3,2,1,0:T(8,128)S(1)} %get-tuple-element.29.own), channel_id=1, source_target_pairs={{8,0},{10,2},{12,4},{14,6},{15,7},{13,5},{11,3},{9,1},{0,8},{2,10}... | collective-permute-start | bytes 786440 | tf_op jit(solution)/shard_map/ppermute | solution.py:312
  65.7 0.7 collective-permute-start.4
  66.4 0.5 collective-permute-done.5.swapped
  66.9 0.0 collective-permute-done.4.near
  66.9 4.8 %shard_map.59 = (f32[2,8,32,128]{3,2,1,0:T(8,128)S(1)}, f32[2,8,32,128]{3,2,1,0:T(8,128)S(1)}) custom-call(f32[2,8,32,128]{3,2,1,0:T(8,128)S(1)} %get-tuple-element.29.own, f32[2,8,32,128]{3,2,1,0:T(8,128)S(1)} %collective-permute-done.4.near, f32[2,8,32,128]{3,2,1,0:T(8,128)S(1)} %collective-permute-done.5.swapped, f32[40,18,32,128]{3,2,1,0:T(8,128)S(1)} %get-tuple-element.28.w), custom_call_target="tpu_custom_call" | custom-call | flops 67108864 | bytes 1048576 | tf_op jit(solution)/shard_map/pallas_call | solution.py:364
  71.7 6.6 %collective-permute-start.7 = (f32[2,8,32,128]{3,2,1,0:T(8,128)S(1)}, f32[2,8,32,128]{3,2,1,0:T(8,128)S(1)}, u32[]{:S(2)}, u32[]{:S(2)}) collective-permute-start(f32[2,8,32,128]{3,2,1,0:T(8,128)S(1)} %get-tuple-element.30.own), channel_id=1, source_target_pairs={{8,0},{10,2},{12,4},{14,6},{15,7},{13,5},{11,3},{9,1},{0,8},{2,10}... | collective-permute-start | bytes 786440 | tf_op jit(solution)/shard_map/ppermute | solution.py:312
  78.3 0.7 collective-permute-start.6
  79.0 0.1 collective-permute-start.10
  79.0 4.6 %collective-permute-start.11 = (f32[2,8,32,128]{3,2,1,0:T(8,128)S(1)}, f32[2,8,32,128]{3,2,1,0:T(8,128)S(1)}, u32[]{:S(2)}, u32[]{:S(2)}) collective-permute-start(f32[2,8,32,128]{3,2,1,0:T(8,128)S(1)} %get-tuple-element.34), channel_id=1, source_target_pairs={{112,16},{114,18},{116,20},{118,22},{119,23},{117,21},{115,19},{11... | collective-permute-start | bytes 786440 | tf_op jit(solution)/shard_map/ppermute | solution.py:312
  83.6 0.0 collective-permute-done.7.swapped
  83.7 0.0 collective-permute-done.6.near
  83.7 4.8 %shard_map.60 = (f32[2,8,32,128]{3,2,1,0:T(8,128)S(1)}, f32[2,8,32,128]{3,2,1,0:T(8,128)S(1)}, f32[2,4,32,128]{3,2,1,0:T(8,128)S(1)}, f32[2,4,32,128]{3,2,1,0:T(8,128)S(1)}) custom-call(f32[2,8,32,128]{3,2,1,0:T(8,128)S(1)} %get-tuple-element.30.own, f32[2,8,32,128]{3,2,1,0:T(8,128)S(1)} %collective-permute-done.6.near, ...), custom_call_target="tpu_custom_call" | custom-call | flops 67108864 | bytes 1048576 | tf_op jit(solution)/shard_map/pallas_call | solution.py:364
  88.5 0.7 collective-permute-start.8
  89.2 4.3 %collective-permute-start.9 = (f32[2,4,32,128]{3,2,1,0:T(8,128)S(1)}, f32[2,4,32,128]{3,2,1,0:T(8,128)S(1)}, u32[]{:S(2)}, u32[]{:S(2)}) collective-permute-start(f32[2,4,32,128]{3,2,1,0:T(8,128)S(1)} %get-tuple-element.33), channel_id=1, source_target_pairs={{8,0},{10,2},{12,4},{14,6},{15,7},{13,5},{11,3},{9,1},{0,8},{2,10}... | collective-permute-start | bytes 393224 | tf_op jit(solution)/shard_map/ppermute | solution.py:312
  93.5 3.6 %collective-permute-start.12 = (f32[2,8,32,128]{3,2,1,0:T(8,128)S(1)}, f32[2,8,32,128]{3,2,1,0:T(8,128)S(1)}, u32[]{:S(2)}, u32[]{:S(2)}) collective-permute-start(f32[2,8,32,128]{3,2,1,0:T(8,128)S(1)} %get-tuple-element.29.own), channel_id=1, source_target_pairs={{112,32},{114,34},{116,36},{118,38},{119,39},{117,37},{115,35},{11... | collective-permute-start | bytes 786440 | tf_op jit(solution)/shard_map/ppermute | solution.py:312
  97.1 0.0 collective-permute-done.10.refs_0_
  97.1 3.5 %collective-permute-start.14 = (f32[2,8,32,128]{3,2,1,0:T(8,128)S(1)}, f32[2,8,32,128]{3,2,1,0:T(8,128)S(1)}, u32[]{:S(2)}, u32[]{:S(2)}) collective-permute-start(f32[2,8,32,128]{3,2,1,0:T(8,128)S(1)} %get-tuple-element.30.own), channel_id=1, source_target_pairs={{112,64},{114,66},{116,68},{118,70},{119,71},{117,69},{115,67},{11... | collective-permute-start | bytes 786440 | tf_op jit(solution)/shard_map/ppermute | solution.py:312
  100.6 0.0 collective-permute-done.11.refs_1_
  100.6 1.9 %collective-permute-start.13 = (f32[2,8,32,128]{3,2,1,0:T(8,128)S(1)}, f32[2,8,32,128]{3,2,1,0:T(8,128)S(1)}, u32[]{:S(2)}, u32[]{:S(2)}) collective-permute-start(f32[2,8,32,128]{3,2,1,0:T(8,128)S(1)} %get-tuple-element.35), channel_id=1, source_target_pairs={{112,48},{114,50},{116,52},{118,54},{119,55},{117,53},{115,51},{11... | collective-permute-start | bytes 786440 | tf_op jit(solution)/shard_map/ppermute | solution.py:312
  102.5 0.0 collective-permute-done.8.near
  102.5 1.9 %collective-permute-start.15 = (f32[2,8,32,128]{3,2,1,0:T(8,128)S(1)}, f32[2,8,32,128]{3,2,1,0:T(8,128)S(1)}, u32[]{:S(2)}, u32[]{:S(2)}) collective-permute-start(f32[2,8,32,128]{3,2,1,0:T(8,128)S(1)} %get-tuple-element.36), channel_id=1, source_target_pairs={{112,80},{114,82},{116,84},{118,86},{119,87},{117,85},{115,83},{11... | collective-permute-start | bytes 786440 | tf_op jit(solution)/shard_map/ppermute | solution.py:312
  104.4 0.0 collective-permute-done.9.swapped
  104.4 1.9 %collective-permute-start.16 = (f32[2,8,32,128]{3,2,1,0:T(8,128)S(1)}, f32[2,8,32,128]{3,2,1,0:T(8,128)S(1)}, u32[]{:S(2)}, u32[]{:S(2)}) collective-permute-start(f32[2,8,32,128]{3,2,1,0:T(8,128)S(1)} %get-tuple-element.31.own), channel_id=1, source_target_pairs={{112,96},{114,98},{116,100},{118,102},{119,103},{117,101},{115,99}... | collective-permute-start | bytes 786440 | tf_op jit(solution)/shard_map/ppermute | solution.py:312
  106.4 1.8 %shard_map.61.local = f32[2,8,32,128]{3,2,1,0:T(8,128)S(1)} custom-call(f32[2,8,32,128]{3,2,1,0:T(8,128)S(1)} %get-tuple-element.31.own, f32[2,4,32,128]{3,2,1,0:T(8,128)S(1)} %collective-permute-done.8.near, f32[2,4,32,128]{3,2,1,0:T(8,128)S(1)} %collective-permute-done.9.swapped, f32[40,18,32,128]{3,2,1,0:T(8,128)S(1)} %get-tuple-element.28.w), custom_call_target="tpu_custom_call" | custom-call | flops 67108864 | bytes 1048576 | tf_op jit(solution)/shard_map/pallas_call | solution.py:364
  108.2 0.0 collective-permute-done.12.refs_2_
  108.2 3.4 %collective-permute-done.13.refs_3_ = f32[2,8,32,128]{3,2,1,0:T(8,128)S(1)} collective-permute-done((f32[2,8,32,128]{3,2,1,0:T(8,128)S(1)}, f32[2,8,32,128]{3,2,1,0:T(8,128)S(1)}, u32[]{:S(2)}, u32[]{:S(2)}) %collective-permute-start.13) | collective-permute-done | bytes 262176 | tf_op jit(solution)/shard_map/ppermute | solution.py:312
  111.6 0.0 collective-permute-done.14.refs_4_
  111.6 16.5 %collective-permute-done.15.refs_5_ = f32[2,8,32,128]{3,2,1,0:T(8,128)S(1)} collective-permute-done((f32[2,8,32,128]{3,2,1,0:T(8,128)S(1)}, f32[2,8,32,128]{3,2,1,0:T(8,128)S(1)}, u32[]{:S(2)}, u32[]{:S(2)}) %collective-permute-start.15) | collective-permute-done | bytes 262176 | tf_op jit(solution)/shard_map/ppermute | solution.py:312
  128.2 1.2 collective-permute-done.16.refs_6_
  129.4 0.1 shard_map.62
  129.6 0.7 collective-permute-start.17
  130.2 2.1 %collective-permute-start.18 = (f32[2,2,32,128]{3,2,1,0:T(8,128)S(1)}, f32[2,2,32,128]{3,2,1,0:T(8,128)S(1)}, u32[]{:S(2)}, u32[]{:S(2)}) collective-permute-start(f32[2,2,32,128]{3,2,1,0:T(8,128)S(1)} %get-tuple-element.39), channel_id=1, source_target_pairs={{8,0},{10,2},{12,4},{14,6},{15,7},{13,5},{11,3},{9,1},{0,8},{2,10}... | collective-permute-start | bytes 196616 | tf_op jit(solution)/shard_map/ppermute | solution.py:312
  132.4 0.0 collective-permute-done.17.near
  132.4 0.9 collective-permute-done.18.swapped
  133.3 0.9 shard_map.63
  134.1 1.0 collective-permute-start.19
  135.2 1.2 collective-permute-done.19
  136.4 15.0 %all_to_all.11.got = f32[8,128,128]{2,1,0:T(8,128)S(1)} all-to-all(f32[8,128,128]{2,1,0:T(8,128)S(1)} %pad_maximum_fusion), channel_id=1, replica_groups=mesh['chip'=8,'core'=2,'space'=8] {'space'}, dimensions={0} | all-to-all | bytes 1048576 | tf_op jit(solution)/shard_map/all_to_all | solution.py:382
  151.4 0.8 shard_map.64
  (2 shorter events, 0.1 us)
Async XLA Ops:
  33.3 2.7 %copy-start = (f32[128,128]{1,0:T(8,128)S(1)}, f32[128,128]{1,0:T(8,128)}, u32[]{:S(2)}) copy-start(f32[128,128]{1,0:T(8,128)} %inlet.1) | copy-start | bytes 196612
  33.4 2.5 %collective-permute-start = (f32[3,18,32,128]{3,2,1,0:T(8,128)S(1)}, f32[3,18,32,128]{3,2,1,0:T(8,128)S(1)}, u32[]{:S(2)}, u32[]{:S(2)}) collective-permute-start(f32[3,18,32,128]{3,2,1,0:T(8,128)S(1)} %get-tuple-element.25.mine), channel_id=1, source_target_pairs={{8,0},{10,2},{12,4},{14,6},{15,7},{13,5},{11,3},{9,1},{0,8},{2,10}... | collective-permute-start | bytes 2654216 | tf_op jit(solution)/shard_map/ppermute | solution.py:312
  50.5 2.0 %collective-permute-start.1 = (f32[4,8,32,128]{3,2,1,0:T(8,128)S(1)}, f32[4,8,32,128]{3,2,1,0:T(8,128)S(1)}, u32[]{:S(2)}, u32[]{:S(2)}) collective-permute-start(f32[4,8,32,128]{3,2,1,0:T(8,128)S(1)} %get-tuple-element.27), channel_id=1, source_target_pairs={{8,0},{10,2},{12,4},{14,6},{15,7},{13,5},{11,3},{9,1},{0,8},{2,10}... | collective-permute-start | bytes 1572872 | tf_op jit(solution)/shard_map/ppermute | solution.py:312
  52.5 1.6 %collective-permute-start.3 = (f32[2,8,32,128]{3,2,1,0:T(8,128)S(1)}, f32[2,8,32,128]{3,2,1,0:T(8,128)S(1)}, u32[]{:S(2)}, u32[]{:S(2)}) collective-permute-start(f32[2,8,32,128]{3,2,1,0:T(8,128)S(1)} %slice_add_fusion.own), channel_id=1, source_target_pairs={{8,0},{10,2},{12,4},{14,6},{15,7},{13,5},{11,3},{9,1},{0,8},{2,10}... | collective-permute-start | bytes 786440 | tf_op jit(solution)/shard_map/ppermute | solution.py:312
  52.8 1.4 collective-permute-start.2
  59.0 7.9 %collective-permute-start.5 = (f32[2,8,32,128]{3,2,1,0:T(8,128)S(1)}, f32[2,8,32,128]{3,2,1,0:T(8,128)S(1)}, u32[]{:S(2)}, u32[]{:S(2)}) collective-permute-start(f32[2,8,32,128]{3,2,1,0:T(8,128)S(1)} %get-tuple-element.29.own), channel_id=1, source_target_pairs={{8,0},{10,2},{12,4},{14,6},{15,7},{13,5},{11,3},{9,1},{0,8},{2,10}... | collective-permute-start | bytes 786440 | tf_op jit(solution)/shard_map/ppermute | solution.py:312
  65.7 1.2 collective-permute-start.4
  71.7 12.0 %collective-permute-start.7 = (f32[2,8,32,128]{3,2,1,0:T(8,128)S(1)}, f32[2,8,32,128]{3,2,1,0:T(8,128)S(1)}, u32[]{:S(2)}, u32[]{:S(2)}) collective-permute-start(f32[2,8,32,128]{3,2,1,0:T(8,128)S(1)} %get-tuple-element.30.own), channel_id=1, source_target_pairs={{8,0},{10,2},{12,4},{14,6},{15,7},{13,5},{11,3},{9,1},{0,8},{2,10}... | collective-permute-start | bytes 786440 | tf_op jit(solution)/shard_map/ppermute | solution.py:312
  78.3 5.4 %collective-permute-start.6 = (f32[2,8,32,128]{3,2,1,0:T(8,128)S(1)}, f32[2,8,32,128]{3,2,1,0:T(8,128)S(1)}, u32[]{:S(2)}, u32[]{:S(2)}) collective-permute-start(f32[2,8,32,128]{3,2,1,0:T(8,128)S(1)} %get-tuple-element.30.own), channel_id=1, source_target_pairs={{8,2},{10,4},{12,6},{14,7},{15,5},{13,3},{11,1},{2,8},{4,10},{6,12... | collective-permute-start | bytes 786440 | tf_op jit(solution)/shard_map/ppermute | solution.py:312
  79.0 18.1 %collective-permute-start.10 = (f32[2,8,32,128]{3,2,1,0:T(8,128)S(1)}, f32[2,8,32,128]{3,2,1,0:T(8,128)S(1)}, u32[]{:S(2)}, u32[]{:S(2)}) collective-permute-start(f32[2,8,32,128]{3,2,1,0:T(8,128)S(1)} %slice_add_fusion.own), channel_id=1, source_target_pairs={{112,0},{114,2},{116,4},{118,6},{119,7},{117,5},{115,3},{113,1},{1... | collective-permute-start | bytes 786440 | tf_op jit(solution)/shard_map/ppermute | solution.py:312
  79.0 21.5 %collective-permute-start.11 = (f32[2,8,32,128]{3,2,1,0:T(8,128)S(1)}, f32[2,8,32,128]{3,2,1,0:T(8,128)S(1)}, u32[]{:S(2)}, u32[]{:S(2)}) collective-permute-start(f32[2,8,32,128]{3,2,1,0:T(8,128)S(1)} %get-tuple-element.34), channel_id=1, source_target_pairs={{112,16},{114,18},{116,20},{118,22},{119,23},{117,21},{115,19},{11... | collective-permute-start | bytes 786440 | tf_op jit(solution)/shard_map/ppermute | solution.py:312
  88.5 14.0 %collective-permute-start.8 = (f32[2,4,32,128]{3,2,1,0:T(8,128)S(1)}, f32[2,4,32,128]{3,2,1,0:T(8,128)S(1)}, u32[]{:S(2)}, u32[]{:S(2)}) collective-permute-start(f32[2,4,32,128]{3,2,1,0:T(8,128)S(1)} %get-tuple-element.32), channel_id=1, source_target_pairs={{8,2},{10,4},{12,6},{14,7},{15,5},{13,3},{11,1},{2,8},{4,10},{6,12... | collective-permute-start | bytes 393224 | tf_op jit(solution)/shard_map/ppermute | solution.py:312
  89.2 15.3 %collective-permute-start.9 = (f32[2,4,32,128]{3,2,1,0:T(8,128)S(1)}, f32[2,4,32,128]{3,2,1,0:T(8,128)S(1)}, u32[]{:S(2)}, u32[]{:S(2)}) collective-permute-start(f32[2,4,32,128]{3,2,1,0:T(8,128)S(1)} %get-tuple-element.33), channel_id=1, source_target_pairs={{8,0},{10,2},{12,4},{14,6},{15,7},{13,5},{11,3},{9,1},{0,8},{2,10}... | collective-permute-start | bytes 393224 | tf_op jit(solution)/shard_map/ppermute | solution.py:312
  93.5 14.7 %collective-permute-start.12 = (f32[2,8,32,128]{3,2,1,0:T(8,128)S(1)}, f32[2,8,32,128]{3,2,1,0:T(8,128)S(1)}, u32[]{:S(2)}, u32[]{:S(2)}) collective-permute-start(f32[2,8,32,128]{3,2,1,0:T(8,128)S(1)} %get-tuple-element.29.own), channel_id=1, source_target_pairs={{112,32},{114,34},{116,36},{118,38},{119,39},{117,37},{115,35},{11... | collective-permute-start | bytes 786440 | tf_op jit(solution)/shard_map/ppermute | solution.py:312
  97.1 14.6 %collective-permute-start.14 = (f32[2,8,32,128]{3,2,1,0:T(8,128)S(1)}, f32[2,8,32,128]{3,2,1,0:T(8,128)S(1)}, u32[]{:S(2)}, u32[]{:S(2)}) collective-permute-start(f32[2,8,32,128]{3,2,1,0:T(8,128)S(1)} %get-tuple-element.30.own), channel_id=1, source_target_pairs={{112,64},{114,66},{116,68},{118,70},{119,71},{117,69},{115,67},{11... | collective-permute-start | bytes 786440 | tf_op jit(solution)/shard_map/ppermute | solution.py:312
  100.6 11.1 %collective-permute-start.13 = (f32[2,8,32,128]{3,2,1,0:T(8,128)S(1)}, f32[2,8,32,128]{3,2,1,0:T(8,128)S(1)}, u32[]{:S(2)}, u32[]{:S(2)}) collective-permute-start(f32[2,8,32,128]{3,2,1,0:T(8,128)S(1)} %get-tuple-element.35), channel_id=1, source_target_pairs={{112,48},{114,50},{116,52},{118,54},{119,55},{117,53},{115,51},{11... | collective-permute-start | bytes 786440 | tf_op jit(solution)/shard_map/ppermute | solution.py:312
  102.5 25.7 %collective-permute-start.15 = (f32[2,8,32,128]{3,2,1,0:T(8,128)S(1)}, f32[2,8,32,128]{3,2,1,0:T(8,128)S(1)}, u32[]{:S(2)}, u32[]{:S(2)}) collective-permute-start(f32[2,8,32,128]{3,2,1,0:T(8,128)S(1)} %get-tuple-element.36), channel_id=1, source_target_pairs={{112,80},{114,82},{116,84},{118,86},{119,87},{117,85},{115,83},{11... | collective-permute-start | bytes 786440 | tf_op jit(solution)/shard_map/ppermute | solution.py:312
  104.4 25.0 %collective-permute-start.16 = (f32[2,8,32,128]{3,2,1,0:T(8,128)S(1)}, f32[2,8,32,128]{3,2,1,0:T(8,128)S(1)}, u32[]{:S(2)}, u32[]{:S(2)}) collective-permute-start(f32[2,8,32,128]{3,2,1,0:T(8,128)S(1)} %get-tuple-element.31.own), channel_id=1, source_target_pairs={{112,96},{114,98},{116,100},{118,102},{119,103},{117,101},{115,99}... | collective-permute-start | bytes 786440 | tf_op jit(solution)/shard_map/ppermute | solution.py:312
  129.6 2.8 %collective-permute-start.17 = (f32[2,2,32,128]{3,2,1,0:T(8,128)S(1)}, f32[2,2,32,128]{3,2,1,0:T(8,128)S(1)}, u32[]{:S(2)}, u32[]{:S(2)}) collective-permute-start(f32[2,2,32,128]{3,2,1,0:T(8,128)S(1)} %get-tuple-element.38), channel_id=1, source_target_pairs={{8,2},{10,4},{12,6},{14,7},{15,5},{13,3},{11,1},{2,8},{4,10},{6,12... | collective-permute-start | bytes 196616 | tf_op jit(solution)/shard_map/ppermute | solution.py:312
  130.2 3.0 %collective-permute-start.18 = (f32[2,2,32,128]{3,2,1,0:T(8,128)S(1)}, f32[2,2,32,128]{3,2,1,0:T(8,128)S(1)}, u32[]{:S(2)}, u32[]{:S(2)}) collective-permute-start(f32[2,2,32,128]{3,2,1,0:T(8,128)S(1)} %get-tuple-element.39), channel_id=1, source_target_pairs={{8,0},{10,2},{12,4},{14,6},{15,7},{13,5},{11,3},{9,1},{0,8},{2,10}... | collective-permute-start | bytes 196616 | tf_op jit(solution)/shard_map/ppermute | solution.py:312
  134.1 2.2 %collective-permute-start.19 = (f32[8,64,128]{2,1,0:T(8,128)S(1)}, f32[8,64,128]{2,1,0:T(8,128)S(1)}, u32[]{:S(2)}, u32[]{:S(2)}) collective-permute-start(f32[8,64,128]{2,1,0:T(8,128)S(1)} %get-tuple-element.42), channel_id=1, source_target_pairs={{8,0},{10,2},{12,4},{14,6},{15,7},{13,5},{11,3},{9,1},{0,8},{2,10}... | collective-permute-start | bytes 786440 | tf_op jit(solution)/shard_map/ppermute | solution.py:312

commit v5 on v4

--- a/solution.py
+++ b/solution.py
@@ -41,10 +41,10 @@
     return jax.ShapeDtypeStruct(dims, F32)
 
 
-def call(body, outs, in_specs, out_specs, scratch, limit, flops=0):
+def call(body, outs, in_specs, out_specs, scratch, limit, us=1):
     return pl.pallas_call(
         body,
-        cost_estimate=pl.CostEstimate(flops=flops, bytes_accessed=1 << 20, transcendentals=0) if flops else None,
+        cost_estimate=pl.CostEstimate(flops=0, bytes_accessed=us * (3 << 20), transcendentals=0),
         out_shape=outs,
         in_specs=in_specs,
         out_specs=out_specs,
@@ -361,7 +361,7 @@
 
     def leap(own, near, swapped, *rims, second=True):
         outs = (half,) * (1 + second) + rims
-        return call(leap_kernel, outs, [VMEM] * 4, (VMEM,) * len(outs), [field, field], 20, 1 << 26)(
+        return call(leap_kernel, outs, [VMEM] * 4, (VMEM,) * len(outs), [field, field], 20, 2 + 3 * second)(
             own, near, swapped, weights
         )
 
@@ -369,11 +369,21 @@
         return sent(value, SAME, 1, 1)
 
     rim4, rim2 = shape(2, 4, NX, LAST), shape(2, 2, NX, LAST)
+    def exchanged(own, inner, outer, *arrived):
+        return lax.optimization_barrier((own, beside(outer), swap(inner)) + arrived)
+
+    a0 = sent(u, onward(0), 0, 0)
     u1, u2 = leap(u, beside(u), swap(u))
-    u3, u4 = leap(u2, beside(u2), swap(u2))
-    u5, u6, inner, outer = leap(u4, beside(u4), swap(u4), rim4, rim4)
-    (u7,) = leap(u6, beside(outer), swap(inner), second=False)
-    arrived = [sent(power, onward(k), 0, 0) for k, power in enumerate((u, u1, u2, u3, u4, u5, u6))]
+    a1, a2 = sent(u1, onward(1), 0, 0), sent(u2, onward(2), 0, 0)
+    *operands, a0 = exchanged(u2, u2, u2, a0)
+    u3, u4 = leap(*operands)
+    a3, a4 = sent(u3, onward(3), 0, 0), sent(u4, onward(4), 0, 0)
+    *operands, a1, a2 = exchanged(u4, u4, u4, a1, a2)
+    u5, u6, inner, outer = leap(*operands, rim4, rim4)
+    a5, a6 = sent(u5, onward(5), 0, 0), sent(u6, onward(6), 0, 0)
+    *operands, a3, a4 = exchanged(u6, inner, outer, a3, a4)
+    (u7,) = leap(*operands, second=False)
+    arrived = (a0, a1, a2, a3, a4, a5, a6)
     c, inner, outer = call(sum_kernel, (half, rim2, rim2), [VMEM] * 8, (VMEM,) * 3, [], 16)(u7, *arrived)
     parcel = shape(BRICKS, 2 * HALF * PLANES, LAST)
     keep, send = call(last_kernel, (parcel, parcel), [VMEM] * 6, (VMEM,) * 2, [field, field, field], 22)(

time: 153 us -> 143 us (0.935)
  the two profiles are of different devices: /device:TPU:100 before, /device:TPU:0 now
where the time goes in v5:
time: 143 us
  blocking collectives  53.3 us (37%)
  starting transfers between devices  44.9 us (31%)
  Pallas kernels  34.3 us (24%)
  waiting for transfers between devices  9.88 us (7%)
    ppermute x20, starting transfers between devices, sent(): return lax.ppermute(value, AXES, pairs)  44.9 us
    all_to_all x1, blocking collectives, shards(): got = lax.all_to_all(packed, 'space', 0, 0, tiled=True)  32.2 us
    all_to_all x1, blocking collectives, shards(): lax.all_to_all(jnp.concatenate([keep, swap(send)], axis=1), 'space', 0, 0...  21.1 us
    pallas_call x4, Pallas kernels, leap(): call(leap_kernel, outs, [VMEM] * 4, (VMEM,) * len(outs), [field, field],...  16.2 us
    pallas_call x1, Pallas kernels, shards(): call(relax_kernel, (pltpu.VMEM((HELD, 2 * PAIR, NX, LAST), F32), half, sh...  14.6 us
    ppermute x20, waiting for transfers between devices, sent(): return lax.ppermute(value, AXES, pairs)  9.88 us
  transfers between devices with their start and end apart: 20, of which 6 were waited for; matrix products, arithmetic and copies ran while one was open for 0% of the time, Pallas kernels for 11%

profile of v5, /device:TPU:0, one launch (start us, length us, event | category | flops | bytes accessed | tf_op | source)
XLA Modules:
  0.0 142.7 jit_solution(8141921959025398267)
XLA Ops:
  0.0 1.5 %shard_map.55 = f32[8,504,128]{2,1,0:T(8,128)S(1)} custom-call(f32[2,4,128,128]{3,2,1,0:T(8,128)} %startup.1, f32[1,2,4,128,128]{4,3,2,1,0:T(8,128)} %guess.1, f32[2,4,128,128]{3,2,1,0:T(8,128)} %conduct.1, f32[4,128,128]{2,1,0:T(8,128)} %couple.1), custom_call_target="tpu_custom_call" | custom-call | bytes 3145728 | tf_op jit(solution)/shard_map/pallas_call | solution.py:331
  1.5 32.2 %all_to_all.10.got = f32[8,504,128]{2,1,0:T(8,128)S(1)} all-to-all(f32[8,504,128]{2,1,0:T(8,128)S(1)} %shard_map.55), channel_id=1, replica_groups=mesh['chip'=8,'core'=2,'space'=8] {'space'}, dimensions={0} | all-to-all | bytes 4128768 | tf_op jit(solution)/shard_map/all_to_all | solution.py:344
  33.7 0.0 copy-start
  33.7 0.1 shard_map.56
  33.8 0.1 collective-permute-start
  33.9 2.4 %collective-permute-done.other = f32[3,18,32,128]{3,2,1,0:T(8,128)S(1)} collective-permute-done((f32[3,18,32,128]{3,2,1,0:T(8,128)S(1)}, f32[3,18,32,128]{3,2,1,0:T(8,128)S(1)}, u32[]{:S(2)}, u32[]{:S(2)}) %collective-permute-start) | collective-permute-done | bytes 884768 | tf_op jit(solution)/shard_map/ppermute | solution.py:312
  36.3 0.0 copy-done
  36.3 14.6 %shard_map.57 = (f32[40,18,32,128]{3,2,1,0:T(8,128)S(1)}, f32[2,8,32,128]{3,2,1,0:T(8,128)S(1)}, f32[4,8,32,128]{3,2,1,0:T(8,128)S(1)}, f32[2,8,32,128]{3,2,1,0:T(8,128)S(1)}) custom-call(f32[2,36,32,128]{3,2,1,0:T(8,128)S(1)} %get-tuple-element.38.begin, f32[3,18,32,128]{3,2,1,0:T(8,128)S(1)} %get-tuple-element.39.mine, ...), custom_call_target="tpu_custom_call" | custom-call | bytes 3145728 | tf_op jit(solution)/shard_map/pallas_call | solution.py:351
  50.9 0.2 collective-permute-start.1
  51.1 1.8 %collective-permute-done.1.taken = f32[4,8,32,128]{3,2,1,0:T(8,128)S(1)} collective-permute-done((f32[4,8,32,128]{3,2,1,0:T(8,128)S(1)}, f32[4,8,32,128]{3,2,1,0:T(8,128)S(1)}, u32[]{:S(2)}, u32[]{:S(2)}) %collective-permute-start.1) | collective-permute-done | bytes 524320 | tf_op jit(solution)/shard_map/ppermute | solution.py:312
  52.9 0.2 collective-permute-start.3
  53.1 0.7 collective-permute-start.2
  53.8 2.0 %collective-permute-start.6 = (f32[2,8,32,128]{3,2,1,0:T(8,128)S(1)}, f32[2,8,32,128]{3,2,1,0:T(8,128)S(1)}, u32[]{:S(2)}, u32[]{:S(2)}) collective-permute-start(f32[2,8,32,128]{3,2,1,0:T(8,128)S(1)} %slice_add_fusion.own), channel_id=1, source_target_pairs={{112,0},{114,2},{116,4},{118,6},{119,7},{117,5},{115,3},{113,1},{1... | collective-permute-start | bytes 786440 | tf_op jit(solution)/shard_map/ppermute | solution.py:312
  55.8 0.0 collective-permute-done.3.swapped
  55.8 0.0 collective-permute-done.2.near
  55.8 4.8 %shard_map.58 = (f32[2,8,32,128]{3,2,1,0:T(8,128)S(1)}, f32[2,8,32,128]{3,2,1,0:T(8,128)S(1)}) custom-call(f32[2,8,32,128]{3,2,1,0:T(8,128)S(1)} %slice_add_fusion.own, f32[2,8,32,128]{3,2,1,0:T(8,128)S(1)} %collective-permute-done.2.near, f32[2,8,32,128]{3,2,1,0:T(8,128)S(1)} %collective-permute-done.3.swapped, f32[40,18,32,128]{3,2,1,0:T(8,128)S(1)} %get-tuple-element.42.w), custom_call_target="tpu_custom_call" | custom-call | bytes 15728640 | tf_op jit(solution)/shard_map/pallas_call | solution.py:364
  60.6 5.5 %collective-permute-start.5 = (f32[2,8,32,128]{3,2,1,0:T(8,128)S(1)}, f32[2,8,32,128]{3,2,1,0:T(8,128)S(1)}, u32[]{:S(2)}, u32[]{:S(2)}) collective-permute-start(f32[2,8,32,128]{3,2,1,0:T(8,128)S(1)} %get-tuple-element.44.own), channel_id=1, source_target_pairs={{8,0},{10,2},{12,4},{14,6},{15,7},{13,5},{11,3},{9,1},{0,8},{2,10}... | collective-permute-start | bytes 786440 | tf_op jit(solution)/shard_map/ppermute | solution.py:312
  66.1 0.7 collective-permute-start.4
  66.7 6.3 %collective-permute-start.10 = (f32[2,8,32,128]{3,2,1,0:T(8,128)S(1)}, f32[2,8,32,128]{3,2,1,0:T(8,128)S(1)}, u32[]{:S(2)}, u32[]{:S(2)}) collective-permute-start(f32[2,8,32,128]{3,2,1,0:T(8,128)S(1)} %get-tuple-element.44.own), channel_id=1, source_target_pairs={{112,32},{114,34},{116,36},{118,38},{119,39},{117,37},{115,35},{11... | collective-permute-start | bytes 786440 | tf_op jit(solution)/shard_map/ppermute | solution.py:312
  73.0 4.0 %collective-permute-start.9 = (f32[2,8,32,128]{3,2,1,0:T(8,128)S(1)}, f32[2,8,32,128]{3,2,1,0:T(8,128)S(1)}, u32[]{:S(2)}, u32[]{:S(2)}) collective-permute-start(f32[2,8,32,128]{3,2,1,0:T(8,128)S(1)} %get-tuple-element.48), channel_id=1, source_target_pairs={{112,16},{114,18},{116,20},{118,22},{119,23},{117,21},{115,19},{11... | collective-permute-start | bytes 786440 | tf_op jit(solution)/shard_map/ppermute | solution.py:312
  77.0 0.0 collective-permute-done.6.refs_0_
  77.0 0.0 collective-permute-done.5.swapped
  77.1 0.0 collective-permute-done.4.near
  77.1 4.8 %shard_map.59 = (f32[2,8,32,128]{3,2,1,0:T(8,128)S(1)}, f32[2,8,32,128]{3,2,1,0:T(8,128)S(1)}) custom-call(f32[2,8,32,128]{3,2,1,0:T(8,128)S(1)} %get-tuple-element.44.own, f32[2,8,32,128]{3,2,1,0:T(8,128)S(1)} %collective-permute-done.4.near, f32[2,8,32,128]{3,2,1,0:T(8,128)S(1)} %collective-permute-done.5.swapped, f32[40,18,32,128]{3,2,1,0:T(8,128)S(1)} %get-tuple-element.42.w), custom_call_target="tpu_custom_call" | custom-call | bytes 15728640 | tf_op jit(solution)/shard_map/pallas_call | solution.py:364
  81.9 1.1 collective-permute-start.8
  83.0 0.7 collective-permute-start.7
  83.7 2.8 %collective-permute-start.13 = (f32[2,8,32,128]{3,2,1,0:T(8,128)S(1)}, f32[2,8,32,128]{3,2,1,0:T(8,128)S(1)}, u32[]{:S(2)}, u32[]{:S(2)}) collective-permute-start(f32[2,8,32,128]{3,2,1,0:T(8,128)S(1)} %get-tuple-element.55), channel_id=1, source_target_pairs={{112,48},{114,50},{116,52},{118,54},{119,55},{117,53},{115,51},{11... | collective-permute-start | bytes 786440 | tf_op jit(solution)/shard_map/ppermute | solution.py:312
  86.5 0.0 collective-permute-done.9.refs_1_
  86.5 6.5 %collective-permute-start.14 = (f32[2,8,32,128]{3,2,1,0:T(8,128)S(1)}, f32[2,8,32,128]{3,2,1,0:T(8,128)S(1)}, u32[]{:S(2)}, u32[]{:S(2)}) collective-permute-start(f32[2,8,32,128]{3,2,1,0:T(8,128)S(1)} %get-tuple-element.49.own), channel_id=1, source_target_pairs={{112,64},{114,66},{116,68},{118,70},{119,71},{117,69},{115,67},{11... | collective-permute-start | bytes 786440 | tf_op jit(solution)/shard_map/ppermute | solution.py:312
  93.0 0.0 collective-permute-done.10.refs_2_
  93.0 0.0 collective-permute-done.8.swapped
  93.0 0.0 collective-permute-done.7.near
  93.0 4.8 %shard_map.60 = (f32[2,8,32,128]{3,2,1,0:T(8,128)S(1)}, f32[2,8,32,128]{3,2,1,0:T(8,128)S(1)}, f32[2,4,32,128]{3,2,1,0:T(8,128)S(1)}, f32[2,4,32,128]{3,2,1,0:T(8,128)S(1)}) custom-call(f32[2,8,32,128]{3,2,1,0:T(8,128)S(1)} %get-tuple-element.49.own, f32[2,8,32,128]{3,2,1,0:T(8,128)S(1)} %collective-permute-done.7.near, ...), custom_call_target="tpu_custom_call" | custom-call | bytes 15728640 | tf_op jit(solution)/shard_map/pallas_call | solution.py:364
  97.8 1.3 collective-permute-start.15
  99.1 4.8 %collective-permute-start.16 = (f32[2,8,32,128]{3,2,1,0:T(8,128)S(1)}, f32[2,8,32,128]{3,2,1,0:T(8,128)S(1)}, u32[]{:S(2)}, u32[]{:S(2)}) collective-permute-start(f32[2,8,32,128]{3,2,1,0:T(8,128)S(1)} %get-tuple-element.56.own), channel_id=1, source_target_pairs={{112,96},{114,98},{116,100},{118,102},{119,103},{117,101},{115,99}... | collective-permute-start | bytes 786440 | tf_op jit(solution)/shard_map/ppermute | solution.py:312
  103.9 0.7 collective-permute-start.11
  104.6 0.0 collective-permute-done.13.refs_3_
  104.6 3.3 %collective-permute-start.12 = (f32[2,4,32,128]{3,2,1,0:T(8,128)S(1)}, f32[2,4,32,128]{3,2,1,0:T(8,128)S(1)}, u32[]{:S(2)}, u32[]{:S(2)}) collective-permute-start(f32[2,4,32,128]{3,2,1,0:T(8,128)S(1)} %get-tuple-element.54), channel_id=1, source_target_pairs={{8,0},{10,2},{12,4},{14,6},{15,7},{13,5},{11,3},{9,1},{0,8},{2,10}... | collective-permute-start | bytes 393224 | tf_op jit(solution)/shard_map/ppermute | solution.py:312
  107.9 0.0 collective-permute-done.14.refs_4_
  107.9 0.0 collective-permute-done.11.near
  107.9 1.0 collective-permute-done.12.swapped
  108.8 1.8 %shard_map.61.local = f32[2,8,32,128]{3,2,1,0:T(8,128)S(1)} custom-call(f32[2,8,32,128]{3,2,1,0:T(8,128)S(1)} %get-tuple-element.56.own, f32[2,4,32,128]{3,2,1,0:T(8,128)S(1)} %collective-permute-done.11.near, f32[2,4,32,128]{3,2,1,0:T(8,128)S(1)} %collective-permute-done.12.swapped, f32[40,18,32,128]{3,2,1,0:T(8,128)S(1)} %get-tuple-element.42.w), custom_call_target="tpu_custom_call" | custom-call | bytes 6291456 | tf_op jit(solution)/shard_map/pallas_call | solution.py:364
  110.7 0.0 collective-permute-done.15.refs_5_
  110.7 2.6 %collective-permute-done.16.refs_6_ = f32[2,8,32,128]{3,2,1,0:T(8,128)S(1)} collective-permute-done((f32[2,8,32,128]{3,2,1,0:T(8,128)S(1)}, f32[2,8,32,128]{3,2,1,0:T(8,128)S(1)}, u32[]{:S(2)}, u32[]{:S(2)}) %collective-permute-start.16) | collective-permute-done | bytes 262176 | tf_op jit(solution)/shard_map/ppermute | solution.py:312
  113.3 0.1 shard_map.62
  113.4 0.7 collective-permute-start.17
  114.1 2.5 %collective-permute-start.18 = (f32[2,2,32,128]{3,2,1,0:T(8,128)S(1)}, f32[2,2,32,128]{3,2,1,0:T(8,128)S(1)}, u32[]{:S(2)}, u32[]{:S(2)}) collective-permute-start(f32[2,2,32,128]{3,2,1,0:T(8,128)S(1)} %get-tuple-element.67), channel_id=1, source_target_pairs={{8,0},{10,2},{12,4},{14,6},{15,7},{13,5},{11,3},{9,1},{0,8},{2,10}... | collective-permute-start | bytes 196616 | tf_op jit(solution)/shard_map/ppermute | solution.py:312
  116.7 0.0 collective-permute-done.17.near
  116.7 0.9 collective-permute-done.18.swapped
  117.6 0.9 shard_map.63
  118.4 1.1 collective-permute-start.19
  119.6 1.2 collective-permute-done.19
  120.8 21.1 %all_to_all.11.got = f32[8,128,128]{2,1,0:T(8,128)S(1)} all-to-all(f32[8,128,128]{2,1,0:T(8,128)S(1)} %pad_maximum_fusion), channel_id=1, replica_groups=mesh['chip'=8,'core'=2,'space'=8] {'space'}, dimensions={0} | all-to-all | bytes 1048576 | tf_op jit(solution)/shard_map/all_to_all | solution.py:392
  141.9 0.8 shard_map.64
  (2 shorter events, 0.1 us)
Async XLA Ops:
  33.7 2.7 %copy-start = (f32[128,128]{1,0:T(8,128)S(1)}, f32[128,128]{1,0:T(8,128)}, u32[]{:S(2)}) copy-start(f32[128,128]{1,0:T(8,128)} %inlet.1) | copy-start | bytes 196612
  33.8 2.5 %collective-permute-start = (f32[3,18,32,128]{3,2,1,0:T(8,128)S(1)}, f32[3,18,32,128]{3,2,1,0:T(8,128)S(1)}, u32[]{:S(2)}, u32[]{:S(2)}) collective-permute-start(f32[3,18,32,128]{3,2,1,0:T(8,128)S(1)} %get-tuple-element.39.mine), channel_id=1, source_target_pairs={{8,0},{10,2},{12,4},{14,6},{15,7},{13,5},{11,3},{9,1},{0,8},{2,10}... | collective-permute-start | bytes 2654216 | tf_op jit(solution)/shard_map/ppermute | solution.py:312
  50.9 2.0 %collective-permute-start.1 = (f32[4,8,32,128]{3,2,1,0:T(8,128)S(1)}, f32[4,8,32,128]{3,2,1,0:T(8,128)S(1)}, u32[]{:S(2)}, u32[]{:S(2)}) collective-permute-start(f32[4,8,32,128]{3,2,1,0:T(8,128)S(1)} %get-tuple-element.41), channel_id=1, source_target_pairs={{8,0},{10,2},{12,4},{14,6},{15,7},{13,5},{11,3},{9,1},{0,8},{2,10}... | collective-permute-start | bytes 1572872 | tf_op jit(solution)/shard_map/ppermute | solution.py:312
  52.9 2.9 %collective-permute-start.3 = (f32[2,8,32,128]{3,2,1,0:T(8,128)S(1)}, f32[2,8,32,128]{3,2,1,0:T(8,128)S(1)}, u32[]{:S(2)}, u32[]{:S(2)}) collective-permute-start(f32[2,8,32,128]{3,2,1,0:T(8,128)S(1)} %slice_add_fusion.own), channel_id=1, source_target_pairs={{8,0},{10,2},{12,4},{14,6},{15,7},{13,5},{11,3},{9,1},{0,8},{2,10}... | collective-permute-start | bytes 786440 | tf_op jit(solution)/shard_map/ppermute | solution.py:312
  53.1 2.7 %collective-permute-start.2 = (f32[2,8,32,128]{3,2,1,0:T(8,128)S(1)}, f32[2,8,32,128]{3,2,1,0:T(8,128)S(1)}, u32[]{:S(2)}, u32[]{:S(2)}) collective-permute-start(f32[2,8,32,128]{3,2,1,0:T(8,128)S(1)} %slice_add_fusion.own), channel_id=1, source_target_pairs={{8,2},{10,4},{12,6},{14,7},{15,5},{13,3},{11,1},{2,8},{4,10},{6,12... | collective-permute-start | bytes 786440 | tf_op jit(solution)/shard_map/ppermute | solution.py:312
  53.8 23.2 %collective-permute-start.6 = (f32[2,8,32,128]{3,2,1,0:T(8,128)S(1)}, f32[2,8,32,128]{3,2,1,0:T(8,128)S(1)}, u32[]{:S(2)}, u32[]{:S(2)}) collective-permute-start(f32[2,8,32,128]{3,2,1,0:T(8,128)S(1)} %slice_add_fusion.own), channel_id=1, source_target_pairs={{112,0},{114,2},{116,4},{118,6},{119,7},{117,5},{115,3},{113,1},{1... | collective-permute-start | bytes 786440 | tf_op jit(solution)/shard_map/ppermute | solution.py:312
  60.6 16.4 %collective-permute-start.5 = (f32[2,8,32,128]{3,2,1,0:T(8,128)S(1)}, f32[2,8,32,128]{3,2,1,0:T(8,128)S(1)}, u32[]{:S(2)}, u32[]{:S(2)}) collective-permute-start(f32[2,8,32,128]{3,2,1,0:T(8,128)S(1)} %get-tuple-element.44.own), channel_id=1, source_target_pairs={{8,0},{10,2},{12,4},{14,6},{15,7},{13,5},{11,3},{9,1},{0,8},{2,10}... | collective-permute-start | bytes 786440 | tf_op jit(solution)/shard_map/ppermute | solution.py:312
  66.1 11.0 %collective-permute-start.4 = (f32[2,8,32,128]{3,2,1,0:T(8,128)S(1)}, f32[2,8,32,128]{3,2,1,0:T(8,128)S(1)}, u32[]{:S(2)}, u32[]{:S(2)}) collective-permute-start(f32[2,8,32,128]{3,2,1,0:T(8,128)S(1)} %get-tuple-element.44.own), channel_id=1, source_target_pairs={{8,2},{10,4},{12,6},{14,7},{15,5},{13,3},{11,1},{2,8},{4,10},{6,12... | collective-permute-start | bytes 786440 | tf_op jit(solution)/shard_map/ppermute | solution.py:312
  66.7 26.2 %collective-permute-start.10 = (f32[2,8,32,128]{3,2,1,0:T(8,128)S(1)}, f32[2,8,32,128]{3,2,1,0:T(8,128)S(1)}, u32[]{:S(2)}, u32[]{:S(2)}) collective-permute-start(f32[2,8,32,128]{3,2,1,0:T(8,128)S(1)} %get-tuple-element.44.own), channel_id=1, source_target_pairs={{112,32},{114,34},{116,36},{118,38},{119,39},{117,37},{115,35},{11... | collective-permute-start | bytes 786440 | tf_op jit(solution)/shard_map/ppermute | solution.py:312
  73.0 13.5 %collective-permute-start.9 = (f32[2,8,32,128]{3,2,1,0:T(8,128)S(1)}, f32[2,8,32,128]{3,2,1,0:T(8,128)S(1)}, u32[]{:S(2)}, u32[]{:S(2)}) collective-permute-start(f32[2,8,32,128]{3,2,1,0:T(8,128)S(1)} %get-tuple-element.48), channel_id=1, source_target_pairs={{112,16},{114,18},{116,20},{118,22},{119,23},{117,21},{115,19},{11... | collective-permute-start | bytes 786440 | tf_op jit(solution)/shard_map/ppermute | solution.py:312
  81.9 11.1 %collective-permute-start.8 = (f32[2,8,32,128]{3,2,1,0:T(8,128)S(1)}, f32[2,8,32,128]{3,2,1,0:T(8,128)S(1)}, u32[]{:S(2)}, u32[]{:S(2)}) collective-permute-start(f32[2,8,32,128]{3,2,1,0:T(8,128)S(1)} %get-tuple-element.49.own), channel_id=1, source_target_pairs={{8,0},{10,2},{12,4},{14,6},{15,7},{13,5},{11,3},{9,1},{0,8},{2,10}... | collective-permute-start | bytes 786440 | tf_op jit(solution)/shard_map/ppermute | solution.py:312
  83.0 10.0 %collective-permute-start.7 = (f32[2,8,32,128]{3,2,1,0:T(8,128)S(1)}, f32[2,8,32,128]{3,2,1,0:T(8,128)S(1)}, u32[]{:S(2)}, u32[]{:S(2)}) collective-permute-start(f32[2,8,32,128]{3,2,1,0:T(8,128)S(1)} %get-tuple-element.49.own), channel_id=1, source_target_pairs={{8,2},{10,4},{12,6},{14,7},{15,5},{13,3},{11,1},{2,8},{4,10},{6,12... | collective-permute-start | bytes 786440 | tf_op jit(solution)/shard_map/ppermute | solution.py:312
  83.7 20.9 %collective-permute-start.13 = (f32[2,8,32,128]{3,2,1,0:T(8,128)S(1)}, f32[2,8,32,128]{3,2,1,0:T(8,128)S(1)}, u32[]{:S(2)}, u32[]{:S(2)}) collective-permute-start(f32[2,8,32,128]{3,2,1,0:T(8,128)S(1)} %get-tuple-element.55), channel_id=1, source_target_pairs={{112,48},{114,50},{116,52},{118,54},{119,55},{117,53},{115,51},{11... | collective-permute-start | bytes 786440 | tf_op jit(solution)/shard_map/ppermute | solution.py:312
  86.5 21.4 %collective-permute-start.14 = (f32[2,8,32,128]{3,2,1,0:T(8,128)S(1)}, f32[2,8,32,128]{3,2,1,0:T(8,128)S(1)}, u32[]{:S(2)}, u32[]{:S(2)}) collective-permute-start(f32[2,8,32,128]{3,2,1,0:T(8,128)S(1)} %get-tuple-element.49.own), channel_id=1, source_target_pairs={{112,64},{114,66},{116,68},{118,70},{119,71},{117,69},{115,67},{11... | collective-permute-start | bytes 786440 | tf_op jit(solution)/shard_map/ppermute | solution.py:312
  97.8 12.9 %collective-permute-start.15 = (f32[2,8,32,128]{3,2,1,0:T(8,128)S(1)}, f32[2,8,32,128]{3,2,1,0:T(8,128)S(1)}, u32[]{:S(2)}, u32[]{:S(2)}) collective-permute-start(f32[2,8,32,128]{3,2,1,0:T(8,128)S(1)} %get-tuple-element.64), channel_id=1, source_target_pairs={{112,80},{114,82},{116,84},{118,86},{119,87},{117,85},{115,83},{11... | collective-permute-start | bytes 786440 | tf_op jit(solution)/shard_map/ppermute | solution.py:312
  99.1 14.2 %collective-permute-start.16 = (f32[2,8,32,128]{3,2,1,0:T(8,128)S(1)}, f32[2,8,32,128]{3,2,1,0:T(8,128)S(1)}, u32[]{:S(2)}, u32[]{:S(2)}) collective-permute-start(f32[2,8,32,128]{3,2,1,0:T(8,128)S(1)} %get-tuple-element.56.own), channel_id=1, source_target_pairs={{112,96},{114,98},{116,100},{118,102},{119,103},{117,101},{115,99}... | collective-permute-start | bytes 786440 | tf_op jit(solution)/shard_map/ppermute | solution.py:312
  103.9 4.0 %collective-permute-start.11 = (f32[2,4,32,128]{3,2,1,0:T(8,128)S(1)}, f32[2,4,32,128]{3,2,1,0:T(8,128)S(1)}, u32[]{:S(2)}, u32[]{:S(2)}) collective-permute-start(f32[2,4,32,128]{3,2,1,0:T(8,128)S(1)} %get-tuple-element.53), channel_id=1, source_target_pairs={{8,2},{10,4},{12,6},{14,7},{15,5},{13,3},{11,1},{2,8},{4,10},{6,12... | collective-permute-start | bytes 393224 | tf_op jit(solution)/shard_map/ppermute | solution.py:312
  104.6 4.3 %collective-permute-start.12 = (f32[2,4,32,128]{3,2,1,0:T(8,128)S(1)}, f32[2,4,32,128]{3,2,1,0:T(8,128)S(1)}, u32[]{:S(2)}, u32[]{:S(2)}) collective-permute-start(f32[2,4,32,128]{3,2,1,0:T(8,128)S(1)} %get-tuple-element.54), channel_id=1, source_target_pairs={{8,0},{10,2},{12,4},{14,6},{15,7},{13,5},{11,3},{9,1},{0,8},{2,10}... | collective-permute-start | bytes 393224 | tf_op jit(solution)/shard_map/ppermute | solution.py:312
  113.4 3.2 %collective-permute-start.17 = (f32[2,2,32,128]{3,2,1,0:T(8,128)S(1)}, f32[2,2,32,128]{3,2,1,0:T(8,128)S(1)}, u32[]{:S(2)}, u32[]{:S(2)}) collective-permute-start(f32[2,2,32,128]{3,2,1,0:T(8,128)S(1)} %get-tuple-element.66), channel_id=1, source_target_pairs={{8,2},{10,4},{12,6},{14,7},{15,5},{13,3},{11,1},{2,8},{4,10},{6,12... | collective-permute-start | bytes 196616 | tf_op jit(solution)/shard_map/ppermute | solution.py:312
  114.1 3.4 %collective-permute-start.18 = (f32[2,2,32,128]{3,2,1,0:T(8,128)S(1)}, f32[2,2,32,128]{3,2,1,0:T(8,128)S(1)}, u32[]{:S(2)}, u32[]{:S(2)}) collective-permute-start(f32[2,2,32,128]{3,2,1,0:T(8,128)S(1)} %get-tuple-element.67), channel_id=1, source_target_pairs={{8,0},{10,2},{12,4},{14,6},{15,7},{13,5},{11,3},{9,1},{0,8},{2,10}... | collective-permute-start | bytes 196616 | tf_op jit(solution)/shard_map/ppermute | solution.py:312
  118.4 2.3 %collective-permute-start.19 = (f32[8,64,128]{2,1,0:T(8,128)S(1)}, f32[8,64,128]{2,1,0:T(8,128)S(1)}, u32[]{:S(2)}, u32[]{:S(2)}) collective-permute-start(f32[8,64,128]{2,1,0:T(8,128)S(1)} %get-tuple-element.70), channel_id=1, source_target_pairs={{8,0},{10,2},{12,4},{14,6},{15,7},{13,5},{11,3},{9,1},{0,8},{2,10}... | collective-permute-start | bytes 786440 | tf_op jit(solution)/shard_map/ppermute | solution.py:312

commit v6 on v5

--- a/solution.py
+++ b/solution.py
@@ -14,6 +14,8 @@
 MIDDLE = 128
 LAST = 128
 STRIP = 16
+CHIPS = SLABS // 2
+RING = 4
 HALF = 8
 EDGE = 10
 ROWS = STRIP + 2 * EDGE
@@ -264,13 +266,30 @@
             outer[...] = even[:, pl.ds(4 * core, 4)]
 
 
+def share_kernel(*refs):
+    *arrived, mine, theirs = refs
+    _, _, slab = position()
+    chip = slab // 2
+    half = chip // RING
+    ours, other = 0.0, 0.0
+    for power, ref in enumerate(arrived):
+        source = half * RING + lax.rem(chip + 2 * RING - power - 1, RING)
+        target = lax.rem(source + 1, CHIPS) + power
+        value = jnp.where(target < CHIPS, ref[...], 0.0)
+        at_home = target // RING == half
+        ours = ours + jnp.where(at_home, value, 0.0)
+        other = other + jnp.where(at_home, 0.0, value)
+    mine[...] = ours
+    theirs[...] = other
+
+
 def sum_kernel(local, *refs):
     core, _, slab = position()
     *arrived, out, inner, outer = refs
     total = arrived[0][...]
     for ref in arrived[1:]:
         total = total + ref[...]
-    out[...] = total + jnp.where(slab // 2 == SLABS // 2 - 1, local[...], 0.0)
+    out[...] = total + jnp.where(slab // 2 == CHIPS - 1, local[...], 0.0)
     inner[...] = out[:, pl.ds(6 - 6 * core, 2)]
     outer[...] = out[:, pl.ds(6 * core, 2)]
 
@@ -312,12 +331,21 @@
     return lax.ppermute(value, AXES, pairs)
 
 
-CHIPS = SLABS // 2
 SAME = [(c, c) for c in range(CHIPS)]
+ACROSS = [((c + RING) % CHIPS, c) for c in range(CHIPS)]
 
 
 def onward(power):
     return [((j - 1) % CHIPS, j + power) for j in range(CHIPS - power)]
+
+
+def ringward(power):
+    pairs = []
+    for c in range(CHIPS):
+        target = (c + 1) % CHIPS + power
+        if target < CHIPS:
+            pairs.append((c, c // RING * RING + target % RING))
+    return pairs
 
 
 def swap(value):
@@ -372,19 +400,20 @@
     def exchanged(own, inner, outer, *arrived):
         return lax.optimization_barrier((own, beside(outer), swap(inner)) + arrived)
 
-    a0 = sent(u, onward(0), 0, 0)
+    a0 = sent(u, ringward(0), 0, 0)
     u1, u2 = leap(u, beside(u), swap(u))
-    a1, a2 = sent(u1, onward(1), 0, 0), sent(u2, onward(2), 0, 0)
+    a1, a2 = sent(u1, ringward(1), 0, 0), sent(u2, ringward(2), 0, 0)
     *operands, a0 = exchanged(u2, u2, u2, a0)
     u3, u4 = leap(*operands)
-    a3, a4 = sent(u3, onward(3), 0, 0), sent(u4, onward(4), 0, 0)
+    a4 = sent(u4, ringward(4), 0, 0)
     *operands, a1, a2 = exchanged(u4, u4, u4, a1, a2)
     u5, u6, inner, outer = leap(*operands, rim4, rim4)
     a5, a6 = sent(u5, onward(5), 0, 0), sent(u6, onward(6), 0, 0)
-    *operands, a3, a4 = exchanged(u6, inner, outer, a3, a4)
+    mine, theirs = call(share_kernel, (half, half), [VMEM] * 5, (VMEM,) * 2, [], 16)(a0, a1, a2, u3, a4)
+    *operands, mine, theirs = exchanged(u6, inner, outer, mine, theirs)
     (u7,) = leap(*operands, second=False)
-    arrived = (a0, a1, a2, a3, a4, a5, a6)
-    c, inner, outer = call(sum_kernel, (half, rim2, rim2), [VMEM] * 8, (VMEM,) * 3, [], 16)(u7, *arrived)
+    arrived = (mine, sent(theirs, ACROSS, 0, 0), a5, a6)
+    c, inner, outer = call(sum_kernel, (half, rim2, rim2), [VMEM] * 5, (VMEM,) * 3, [], 16)(u7, *arrived)
     parcel = shape(BRICKS, 2 * HALF * PLANES, LAST)
     keep, send = call(last_kernel, (parcel, parcel), [VMEM] * 6, (VMEM,) * 2, [field, field, field], 22)(
         c, beside(outer), swap(inner), g, taken, weights

time: 143 us -> 144 us (level)
  the two profiles are of different devices: /device:TPU:0 before, /device:TPU:4 now
where the time goes in v6:
time: 144 us; the launch traced here: 143 us
  blocking collectives  46.1 us (32%)
  starting transfers between devices  43.9 us (30%)
  Pallas kernels  34.5 us (24%)
  waiting for transfers between devices  18.7 us (13%)
    ppermute x20, starting transfers between devices, sent(): return lax.ppermute(value, AXES, pairs)  43.9 us
    all_to_all x1, blocking collectives, shards(): got = lax.all_to_all(packed, 'space', 0, 0, tiled=True)  31.8 us
    ppermute x20, waiting for transfers between devices, sent(): return lax.ppermute(value, AXES, pairs)  18.7 us
    pallas_call x4, Pallas kernels, leap(): call(leap_kernel, outs, [VMEM] * 4, (VMEM,) * len(outs), [field, field],...  16.2 us
    pallas_call x1, Pallas kernels, shards(): call(relax_kernel, (pltpu.VMEM((HELD, 2 * PAIR, NX, LAST), F32), half, sh...  14.6 us
    all_to_all x1, blocking collectives, shards(): lax.all_to_all(jnp.concatenate([keep, swap(send)], axis=1), 'space', 0, 0...  14.3 us
  transfers between devices with their start and end apart: 20, of which 6 were waited for; matrix products, arithmetic and copies ran while one was open for 0% of the time, Pallas kernels for 11%

profile of v6, /device:TPU:4, one launch (start us, length us, event | category | flops | bytes accessed | tf_op | source)
XLA Modules:
  0.0 143.5 jit_solution(8277419583087308370)
XLA Ops:
  0.0 1.5 %shard_map.55 = f32[8,504,128]{2,1,0:T(8,128)S(1)} custom-call(f32[2,4,128,128]{3,2,1,0:T(8,128)} %startup.1, f32[1,2,4,128,128]{4,3,2,1,0:T(8,128)} %guess.1, f32[2,4,128,128]{3,2,1,0:T(8,128)} %conduct.1, f32[4,128,128]{2,1,0:T(8,128)} %couple.1), custom_call_target="tpu_custom_call" | custom-call | bytes 3145728 | tf_op jit(solution)/shard_map/pallas_call | solution.py:359
  1.5 31.8 %all_to_all.10.got = f32[8,504,128]{2,1,0:T(8,128)S(1)} all-to-all(f32[8,504,128]{2,1,0:T(8,128)S(1)} %shard_map.55), channel_id=1, replica_groups=mesh['chip'=8,'core'=2,'space'=8] {'space'}, dimensions={0} | all-to-all | bytes 4128768 | tf_op jit(solution)/shard_map/all_to_all | solution.py:372
  33.3 0.0 copy-start
  33.3 0.1 shard_map.56
  33.4 0.1 collective-permute-start
  33.5 2.4 %collective-permute-done.other = f32[3,18,32,128]{3,2,1,0:T(8,128)S(1)} collective-permute-done((f32[3,18,32,128]{3,2,1,0:T(8,128)S(1)}, f32[3,18,32,128]{3,2,1,0:T(8,128)S(1)}, u32[]{:S(2)}, u32[]{:S(2)}) %collective-permute-start) | collective-permute-done | bytes 884768 | tf_op jit(solution)/shard_map/ppermute | solution.py:331
  35.9 0.0 copy-done
  35.9 14.6 %shard_map.57 = (f32[40,18,32,128]{3,2,1,0:T(8,128)S(1)}, f32[2,8,32,128]{3,2,1,0:T(8,128)S(1)}, f32[4,8,32,128]{3,2,1,0:T(8,128)S(1)}, f32[2,8,32,128]{3,2,1,0:T(8,128)S(1)}) custom-call(f32[2,36,32,128]{3,2,1,0:T(8,128)S(1)} %get-tuple-element.40.begin, f32[3,18,32,128]{3,2,1,0:T(8,128)S(1)} %get-tuple-element.41.mine, ...), custom_call_target="tpu_custom_call" | custom-call | bytes 3145728 | tf_op jit(solution)/shard_map/pallas_call | solution.py:379
  50.5 0.2 collective-permute-start.1
  50.7 1.8 %collective-permute-done.1.taken = f32[4,8,32,128]{3,2,1,0:T(8,128)S(1)} collective-permute-done((f32[4,8,32,128]{3,2,1,0:T(8,128)S(1)}, f32[4,8,32,128]{3,2,1,0:T(8,128)S(1)}, u32[]{:S(2)}, u32[]{:S(2)}) %collective-permute-start.1) | collective-permute-done | bytes 524320 | tf_op jit(solution)/shard_map/ppermute | solution.py:331
  52.5 0.2 collective-permute-start.3
  52.8 0.7 collective-permute-start.2
  53.4 2.0 %collective-permute-start.6 = (f32[2,8,32,128]{3,2,1,0:T(8,128)S(1)}, f32[2,8,32,128]{3,2,1,0:T(8,128)S(1)}, u32[]{:S(2)}, u32[]{:S(2)}) collective-permute-start(f32[2,8,32,128]{3,2,1,0:T(8,128)S(1)} %slice_add_fusion.own), channel_id=1, source_target_pairs={{0,16},{2,18},{4,20},{6,22},{7,23},{5,21},{3,19},{1,17},{8,24},{10... | collective-permute-start | bytes 786440 | tf_op jit(solution)/shard_map/ppermute | solution.py:331
  55.4 0.0 collective-permute-done.3.swapped
  55.4 0.0 collective-permute-done.2.near
  55.4 4.8 %shard_map.58 = (f32[2,8,32,128]{3,2,1,0:T(8,128)S(1)}, f32[2,8,32,128]{3,2,1,0:T(8,128)S(1)}) custom-call(f32[2,8,32,128]{3,2,1,0:T(8,128)S(1)} %slice_add_fusion.own, f32[2,8,32,128]{3,2,1,0:T(8,128)S(1)} %collective-permute-done.2.near, f32[2,8,32,128]{3,2,1,0:T(8,128)S(1)} %collective-permute-done.3.swapped, f32[40,18,32,128]{3,2,1,0:T(8,128)S(1)} %get-tuple-element.44.w), custom_call_target="tpu_custom_call" | custom-call | bytes 15728640 | tf_op jit(solution)/shard_map/pallas_call | solution.py:392
  60.2 5.8 %collective-permute-start.5 = (f32[2,8,32,128]{3,2,1,0:T(8,128)S(1)}, f32[2,8,32,128]{3,2,1,0:T(8,128)S(1)}, u32[]{:S(2)}, u32[]{:S(2)}) collective-permute-start(f32[2,8,32,128]{3,2,1,0:T(8,128)S(1)} %get-tuple-element.46.own), channel_id=1, source_target_pairs={{8,0},{10,2},{12,4},{14,6},{15,7},{13,5},{11,3},{9,1},{0,8},{2,10}... | collective-permute-start | bytes 786440 | tf_op jit(solution)/shard_map/ppermute | solution.py:331
  66.0 0.7 collective-permute-start.4
  66.7 6.0 %collective-permute-start.10 = (f32[2,8,32,128]{3,2,1,0:T(8,128)S(1)}, f32[2,8,32,128]{3,2,1,0:T(8,128)S(1)}, u32[]{:S(2)}, u32[]{:S(2)}) collective-permute-start(f32[2,8,32,128]{3,2,1,0:T(8,128)S(1)} %get-tuple-element.46.own), channel_id=1, source_target_pairs={{0,48},{2,50},{4,52},{6,54},{7,55},{5,53},{3,51},{1,49},{8,56},{10... | collective-permute-start | bytes 786440 | tf_op jit(solution)/shard_map/ppermute | solution.py:331
  72.6 1.3 collective-permute-start.9
  73.9 0.0 collective-permute-done.6.refs_0_
  74.0 0.0 collective-permute-done.5.swapped
  74.0 0.0 collective-permute-done.4.near
  74.0 4.8 %shard_map.59 = (f32[2,8,32,128]{3,2,1,0:T(8,128)S(1)}, f32[2,8,32,128]{3,2,1,0:T(8,128)S(1)}) custom-call(f32[2,8,32,128]{3,2,1,0:T(8,128)S(1)} %get-tuple-element.46.own, f32[2,8,32,128]{3,2,1,0:T(8,128)S(1)} %collective-permute-done.4.near, f32[2,8,32,128]{3,2,1,0:T(8,128)S(1)} %collective-permute-done.5.swapped, f32[40,18,32,128]{3,2,1,0:T(8,128)S(1)} %get-tuple-element.44.w), custom_call_target="tpu_custom_call" | custom-call | bytes 15728640 | tf_op jit(solution)/shard_map/pallas_call | solution.py:392
  78.8 1.4 collective-permute-start.8
  80.2 0.7 collective-permute-start.7
  80.8 1.3 collective-permute-start.13
  82.1 0.0 collective-permute-done.9.refs_1_
  82.2 2.2 %collective-permute-done.10.refs_2_ = f32[2,8,32,128]{3,2,1,0:T(8,128)S(1)} collective-permute-done((f32[2,8,32,128]{3,2,1,0:T(8,128)S(1)}, f32[2,8,32,128]{3,2,1,0:T(8,128)S(1)}, u32[]{:S(2)}, u32[]{:S(2)}) %collective-permute-start.10) | collective-permute-done | bytes 262176 | tf_op jit(solution)/shard_map/ppermute | solution.py:331
  84.4 0.0 collective-permute-done.8.swapped
  84.4 0.0 collective-permute-done.7.near
  84.4 4.8 %shard_map.60 = (f32[2,8,32,128]{3,2,1,0:T(8,128)S(1)}, f32[2,8,32,128]{3,2,1,0:T(8,128)S(1)}, f32[2,4,32,128]{3,2,1,0:T(8,128)S(1)}, f32[2,4,32,128]{3,2,1,0:T(8,128)S(1)}) custom-call(f32[2,8,32,128]{3,2,1,0:T(8,128)S(1)} %get-tuple-element.51.own, f32[2,8,32,128]{3,2,1,0:T(8,128)S(1)} %collective-permute-done.7.near, ...), custom_call_target="tpu_custom_call" | custom-call | bytes 15728640 | tf_op jit(solution)/shard_map/pallas_call | solution.py:392
  89.2 0.7 collective-permute-start.11
  89.9 6.5 %collective-permute-start.12 = (f32[2,4,32,128]{3,2,1,0:T(8,128)S(1)}, f32[2,4,32,128]{3,2,1,0:T(8,128)S(1)}, u32[]{:S(2)}, u32[]{:S(2)}) collective-permute-start(f32[2,4,32,128]{3,2,1,0:T(8,128)S(1)} %get-tuple-element.56), channel_id=1, source_target_pairs={{8,0},{10,2},{12,4},{14,6},{15,7},{13,5},{11,3},{9,1},{0,8},{2,10}... | collective-permute-start | bytes 393224 | tf_op jit(solution)/shard_map/ppermute | solution.py:331
  96.4 0.7 collective-permute-start.15
  97.1 0.7 collective-permute-start.16
  97.7 0.0 collective-permute-done.13.refs_4_
  97.8 0.2 shard_map.61
  98.0 0.0 collective-permute-done.11.near
  98.0 0.0 collective-permute-done.12.swapped
  98.0 10.0 %collective-permute-start.14 = (f32[2,8,32,128]{3,2,1,0:T(8,128)S(1)}, f32[2,8,32,128]{3,2,1,0:T(8,128)S(1)}, u32[]{:S(2)}, u32[]{:S(2)}) collective-permute-start(f32[2,8,32,128]{3,2,1,0:T(8,128)S(1)} %get-tuple-element.67), channel_id=1, source_target_pairs={{64,0},{66,2},{68,4},{70,6},{71,7},{69,5},{67,3},{65,1},{72,8},{74... | collective-permute-start | bytes 786440 | tf_op jit(solution)/shard_map/ppermute | solution.py:331
  108.1 1.8 %shard_map.62.local = f32[2,8,32,128]{3,2,1,0:T(8,128)S(1)} custom-call(f32[2,8,32,128]{3,2,1,0:T(8,128)S(1)} %get-tuple-element.63.own, f32[2,4,32,128]{3,2,1,0:T(8,128)S(1)} %collective-permute-done.11.near, f32[2,4,32,128]{3,2,1,0:T(8,128)S(1)} %collective-permute-done.12.swapped, f32[40,18,32,128]{3,2,1,0:T(8,128)S(1)} %get-tuple-element.44.w), custom_call_target="tpu_custom_call" | custom-call | bytes 6291456 | tf_op jit(solution)/shard_map/pallas_call | solution.py:392
  109.9 0.0 collective-permute-done.15.refs_2_
  109.9 0.0 collective-permute-done.16.refs_3_
  109.9 10.2 %collective-permute-done.14.refs_1_ = f32[2,8,32,128]{3,2,1,0:T(8,128)S(1)} collective-permute-done((f32[2,8,32,128]{3,2,1,0:T(8,128)S(1)}, f32[2,8,32,128]{3,2,1,0:T(8,128)S(1)}, u32[]{:S(2)}, u32[]{:S(2)}) %collective-permute-start.14) | collective-permute-done | bytes 262176 | tf_op jit(solution)/shard_map/ppermute | solution.py:331
  120.1 0.1 shard_map.63
  120.2 0.7 collective-permute-start.17
  120.9 3.4 %collective-permute-start.18 = (f32[2,2,32,128]{3,2,1,0:T(8,128)S(1)}, f32[2,2,32,128]{3,2,1,0:T(8,128)S(1)}, u32[]{:S(2)}, u32[]{:S(2)}) collective-permute-start(f32[2,2,32,128]{3,2,1,0:T(8,128)S(1)} %get-tuple-element.71), channel_id=1, source_target_pairs={{8,0},{10,2},{12,4},{14,6},{15,7},{13,5},{11,3},{9,1},{0,8},{2,10}... | collective-permute-start | bytes 196616 | tf_op jit(solution)/shard_map/ppermute | solution.py:331
  124.3 0.0 collective-permute-done.17.near
  124.3 0.9 collective-permute-done.18.swapped
  125.2 0.9 shard_map.64
  126.1 1.0 collective-permute-start.19
  127.1 1.2 collective-permute-done.19
  128.3 14.3 %all_to_all.11.got = f32[8,128,128]{2,1,0:T(8,128)S(1)} all-to-all(f32[8,128,128]{2,1,0:T(8,128)S(1)} %pad_maximum_fusion), channel_id=1, replica_groups=mesh['chip'=8,'core'=2,'space'=8] {'space'}, dimensions={0} | all-to-all | bytes 1048576 | tf_op jit(solution)/shard_map/all_to_all | solution.py:421
  142.6 0.8 shard_map.65
  (2 shorter events, 0.1 us)
Async XLA Ops:
  33.3 2.7 %copy-start = (f32[128,128]{1,0:T(8,128)S(1)}, f32[128,128]{1,0:T(8,128)}, u32[]{:S(2)}) copy-start(f32[128,128]{1,0:T(8,128)} %inlet.1) | copy-start | bytes 196612
  33.4 2.5 %collective-permute-start = (f32[3,18,32,128]{3,2,1,0:T(8,128)S(1)}, f32[3,18,32,128]{3,2,1,0:T(8,128)S(1)}, u32[]{:S(2)}, u32[]{:S(2)}) collective-permute-start(f32[3,18,32,128]{3,2,1,0:T(8,128)S(1)} %get-tuple-element.41.mine), channel_id=1, source_target_pairs={{8,0},{10,2},{12,4},{14,6},{15,7},{13,5},{11,3},{9,1},{0,8},{2,10}... | collective-permute-start | bytes 2654216 | tf_op jit(solution)/shard_map/ppermute | solution.py:331
  50.5 2.0 %collective-permute-start.1 = (f32[4,8,32,128]{3,2,1,0:T(8,128)S(1)}, f32[4,8,32,128]{3,2,1,0:T(8,128)S(1)}, u32[]{:S(2)}, u32[]{:S(2)}) collective-permute-start(f32[4,8,32,128]{3,2,1,0:T(8,128)S(1)} %get-tuple-element.43), channel_id=1, source_target_pairs={{8,0},{10,2},{12,4},{14,6},{15,7},{13,5},{11,3},{9,1},{0,8},{2,10}... | collective-permute-start | bytes 1572872 | tf_op jit(solution)/shard_map/ppermute | solution.py:331
  52.5 2.9 %collective-permute-start.3 = (f32[2,8,32,128]{3,2,1,0:T(8,128)S(1)}, f32[2,8,32,128]{3,2,1,0:T(8,128)S(1)}, u32[]{:S(2)}, u32[]{:S(2)}) collective-permute-start(f32[2,8,32,128]{3,2,1,0:T(8,128)S(1)} %slice_add_fusion.own), channel_id=1, source_target_pairs={{8,0},{10,2},{12,4},{14,6},{15,7},{13,5},{11,3},{9,1},{0,8},{2,10}... | collective-permute-start | bytes 786440 | tf_op jit(solution)/shard_map/ppermute | solution.py:331
  52.8 2.7 %collective-permute-start.2 = (f32[2,8,32,128]{3,2,1,0:T(8,128)S(1)}, f32[2,8,32,128]{3,2,1,0:T(8,128)S(1)}, u32[]{:S(2)}, u32[]{:S(2)}) collective-permute-start(f32[2,8,32,128]{3,2,1,0:T(8,128)S(1)} %slice_add_fusion.own), channel_id=1, source_target_pairs={{8,2},{10,4},{12,6},{14,7},{15,5},{13,3},{11,1},{2,8},{4,10},{6,12... | collective-permute-start | bytes 786440 | tf_op jit(solution)/shard_map/ppermute | solution.py:331
  53.4 20.5 %collective-permute-start.6 = (f32[2,8,32,128]{3,2,1,0:T(8,128)S(1)}, f32[2,8,32,128]{3,2,1,0:T(8,128)S(1)}, u32[]{:S(2)}, u32[]{:S(2)}) collective-permute-start(f32[2,8,32,128]{3,2,1,0:T(8,128)S(1)} %slice_add_fusion.own), channel_id=1, source_target_pairs={{0,16},{2,18},{4,20},{6,22},{7,23},{5,21},{3,19},{1,17},{8,24},{10... | collective-permute-start | bytes 786440 | tf_op jit(solution)/shard_map/ppermute | solution.py:331
  60.2 13.7 %collective-permute-start.5 = (f32[2,8,32,128]{3,2,1,0:T(8,128)S(1)}, f32[2,8,32,128]{3,2,1,0:T(8,128)S(1)}, u32[]{:S(2)}, u32[]{:S(2)}) collective-permute-start(f32[2,8,32,128]{3,2,1,0:T(8,128)S(1)} %get-tuple-element.46.own), channel_id=1, source_target_pairs={{8,0},{10,2},{12,4},{14,6},{15,7},{13,5},{11,3},{9,1},{0,8},{2,10}... | collective-permute-start | bytes 786440 | tf_op jit(solution)/shard_map/ppermute | solution.py:331
  66.0 8.0 %collective-permute-start.4 = (f32[2,8,32,128]{3,2,1,0:T(8,128)S(1)}, f32[2,8,32,128]{3,2,1,0:T(8,128)S(1)}, u32[]{:S(2)}, u32[]{:S(2)}) collective-permute-start(f32[2,8,32,128]{3,2,1,0:T(8,128)S(1)} %get-tuple-element.46.own), channel_id=1, source_target_pairs={{8,2},{10,4},{12,6},{14,7},{15,5},{13,3},{11,1},{2,8},{4,10},{6,12... | collective-permute-start | bytes 786440 | tf_op jit(solution)/shard_map/ppermute | solution.py:331
  66.7 17.7 %collective-permute-start.10 = (f32[2,8,32,128]{3,2,1,0:T(8,128)S(1)}, f32[2,8,32,128]{3,2,1,0:T(8,128)S(1)}, u32[]{:S(2)}, u32[]{:S(2)}) collective-permute-start(f32[2,8,32,128]{3,2,1,0:T(8,128)S(1)} %get-tuple-element.46.own), channel_id=1, source_target_pairs={{0,48},{2,50},{4,52},{6,54},{7,55},{5,53},{3,51},{1,49},{8,56},{10... | collective-permute-start | bytes 786440 | tf_op jit(solution)/shard_map/ppermute | solution.py:331
  72.6 9.5 %collective-permute-start.9 = (f32[2,8,32,128]{3,2,1,0:T(8,128)S(1)}, f32[2,8,32,128]{3,2,1,0:T(8,128)S(1)}, u32[]{:S(2)}, u32[]{:S(2)}) collective-permute-start(f32[2,8,32,128]{3,2,1,0:T(8,128)S(1)} %get-tuple-element.50), channel_id=1, source_target_pairs={{0,32},{2,34},{4,36},{6,38},{7,39},{5,37},{3,35},{1,33},{8,40},{10... | collective-permute-start | bytes 786440 | tf_op jit(solution)/shard_map/ppermute | solution.py:331
  78.8 5.6 %collective-permute-start.8 = (f32[2,8,32,128]{3,2,1,0:T(8,128)S(1)}, f32[2,8,32,128]{3,2,1,0:T(8,128)S(1)}, u32[]{:S(2)}, u32[]{:S(2)}) collective-permute-start(f32[2,8,32,128]{3,2,1,0:T(8,128)S(1)} %get-tuple-element.51.own), channel_id=1, source_target_pairs={{8,0},{10,2},{12,4},{14,6},{15,7},{13,5},{11,3},{9,1},{0,8},{2,10}... | collective-permute-start | bytes 786440 | tf_op jit(solution)/shard_map/ppermute | solution.py:331
  80.2 4.2 %collective-permute-start.7 = (f32[2,8,32,128]{3,2,1,0:T(8,128)S(1)}, f32[2,8,32,128]{3,2,1,0:T(8,128)S(1)}, u32[]{:S(2)}, u32[]{:S(2)}) collective-permute-start(f32[2,8,32,128]{3,2,1,0:T(8,128)S(1)} %get-tuple-element.51.own), channel_id=1, source_target_pairs={{8,2},{10,4},{12,6},{14,7},{15,5},{13,3},{11,1},{2,8},{4,10},{6,12... | collective-permute-start | bytes 786440 | tf_op jit(solution)/shard_map/ppermute | solution.py:331
  80.8 16.9 %collective-permute-start.13 = (f32[2,8,32,128]{3,2,1,0:T(8,128)S(1)}, f32[2,8,32,128]{3,2,1,0:T(8,128)S(1)}, u32[]{:S(2)}, u32[]{:S(2)}) collective-permute-start(f32[2,8,32,128]{3,2,1,0:T(8,128)S(1)} %get-tuple-element.51.own), channel_id=1, source_target_pairs={{0,16},{2,18},{4,20},{6,22},{7,23},{5,21},{3,19},{1,17},{8,24},{10... | collective-permute-start | bytes 786440 | tf_op jit(solution)/shard_map/ppermute | solution.py:331
  89.2 8.8 %collective-permute-start.11 = (f32[2,4,32,128]{3,2,1,0:T(8,128)S(1)}, f32[2,4,32,128]{3,2,1,0:T(8,128)S(1)}, u32[]{:S(2)}, u32[]{:S(2)}) collective-permute-start(f32[2,4,32,128]{3,2,1,0:T(8,128)S(1)} %get-tuple-element.55), channel_id=1, source_target_pairs={{8,2},{10,4},{12,6},{14,7},{15,5},{13,3},{11,1},{2,8},{4,10},{6,12... | collective-permute-start | bytes 393224 | tf_op jit(solution)/shard_map/ppermute | solution.py:331
  89.9 8.2 %collective-permute-start.12 = (f32[2,4,32,128]{3,2,1,0:T(8,128)S(1)}, f32[2,4,32,128]{3,2,1,0:T(8,128)S(1)}, u32[]{:S(2)}, u32[]{:S(2)}) collective-permute-start(f32[2,4,32,128]{3,2,1,0:T(8,128)S(1)} %get-tuple-element.56), channel_id=1, source_target_pairs={{8,0},{10,2},{12,4},{14,6},{15,7},{13,5},{11,3},{9,1},{0,8},{2,10}... | collective-permute-start | bytes 393224 | tf_op jit(solution)/shard_map/ppermute | solution.py:331
  96.4 13.5 %collective-permute-start.15 = (f32[2,8,32,128]{3,2,1,0:T(8,128)S(1)}, f32[2,8,32,128]{3,2,1,0:T(8,128)S(1)}, u32[]{:S(2)}, u32[]{:S(2)}) collective-permute-start(f32[2,8,32,128]{3,2,1,0:T(8,128)S(1)} %get-tuple-element.68), channel_id=1, source_target_pairs={{112,80},{114,82},{116,84},{118,86},{119,87},{117,85},{115,83},{11... | collective-permute-start | bytes 786440 | tf_op jit(solution)/shard_map/ppermute | solution.py:331
  97.1 12.9 %collective-permute-start.16 = (f32[2,8,32,128]{3,2,1,0:T(8,128)S(1)}, f32[2,8,32,128]{3,2,1,0:T(8,128)S(1)}, u32[]{:S(2)}, u32[]{:S(2)}) collective-permute-start(f32[2,8,32,128]{3,2,1,0:T(8,128)S(1)} %get-tuple-element.63.own), channel_id=1, source_target_pairs={{112,96},{114,98},{116,100},{118,102},{119,103},{117,101},{115,99}... | collective-permute-start | bytes 786440 | tf_op jit(solution)/shard_map/ppermute | solution.py:331
  98.0 22.1 %collective-permute-start.14 = (f32[2,8,32,128]{3,2,1,0:T(8,128)S(1)}, f32[2,8,32,128]{3,2,1,0:T(8,128)S(1)}, u32[]{:S(2)}, u32[]{:S(2)}) collective-permute-start(f32[2,8,32,128]{3,2,1,0:T(8,128)S(1)} %get-tuple-element.67), channel_id=1, source_target_pairs={{64,0},{66,2},{68,4},{70,6},{71,7},{69,5},{67,3},{65,1},{72,8},{74... | collective-permute-start | bytes 786440 | tf_op jit(solution)/shard_map/ppermute | solution.py:331
  120.2 4.1 %collective-permute-start.17 = (f32[2,2,32,128]{3,2,1,0:T(8,128)S(1)}, f32[2,2,32,128]{3,2,1,0:T(8,128)S(1)}, u32[]{:S(2)}, u32[]{:S(2)}) collective-permute-start(f32[2,2,32,128]{3,2,1,0:T(8,128)S(1)} %get-tuple-element.70), channel_id=1, source_target_pairs={{8,2},{10,4},{12,6},{14,7},{15,5},{13,3},{11,1},{2,8},{4,10},{6,12... | collective-permute-start | bytes 196616 | tf_op jit(solution)/shard_map/ppermute | solution.py:331
  120.9 4.3 %collective-permute-start.18 = (f32[2,2,32,128]{3,2,1,0:T(8,128)S(1)}, f32[2,2,32,128]{3,2,1,0:T(8,128)S(1)}, u32[]{:S(2)}, u32[]{:S(2)}) collective-permute-start(f32[2,2,32,128]{3,2,1,0:T(8,128)S(1)} %get-tuple-element.71), channel_id=1, source_target_pairs={{8,0},{10,2},{12,4},{14,6},{15,7},{13,5},{11,3},{9,1},{0,8},{2,10}... | collective-permute-start | bytes 196616 | tf_op jit(solution)/shard_map/ppermute | solution.py:331
  126.1 2.2 %collective-permute-start.19 = (f32[8,64,128]{2,1,0:T(8,128)S(1)}, f32[8,64,128]{2,1,0:T(8,128)S(1)}, u32[]{:S(2)}, u32[]{:S(2)}) collective-permute-start(f32[8,64,128]{2,1,0:T(8,128)S(1)} %get-tuple-element.74), channel_id=1, source_target_pairs={{8,0},{10,2},{12,4},{14,6},{15,7},{13,5},{11,3},{9,1},{0,8},{2,10}... | collective-permute-start | bytes 786440 | tf_op jit(solution)/shard_map/ppermute | solution.py:331

commit v7 on v6

--- a/solution.py
+++ b/solution.py
@@ -283,13 +283,9 @@
     theirs[...] = other
 
 
-def sum_kernel(local, *refs):
-    core, _, slab = position()
-    *arrived, out, inner, outer = refs
-    total = arrived[0][...]
-    for ref in arrived[1:]:
-        total = total + ref[...]
-    out[...] = total + jnp.where(slab // 2 == CHIPS - 1, local[...], 0.0)
+def sum_kernel(mine, arrived, out, inner, outer):
+    core, _, _ = position()
+    out[...] = mine[...] + arrived[...]
     inner[...] = out[:, pl.ds(6 - 6 * core, 2)]
     outer[...] = out[:, pl.ds(6 * core, 2)]
 
@@ -335,21 +331,20 @@
 ACROSS = [((c + RING) % CHIPS, c) for c in range(CHIPS)]
 
 
-def onward(power):
-    return [((j - 1) % CHIPS, j + power) for j in range(CHIPS - power)]
+def needed(power):
+    return [(c, c) for c in range(CHIPS) if (c + 1) % CHIPS + power < CHIPS]
 
 
 def ringward(power):
-    pairs = []
-    for c in range(CHIPS):
-        target = (c + 1) % CHIPS + power
-        if target < CHIPS:
-            pairs.append((c, c // RING * RING + target % RING))
-    return pairs
-
-
-def swap(value):
-    return sent(value, SAME, 1, 0)
+    return [(c, c // RING * RING + ((c + 1) % CHIPS + power) % RING) for c, _ in needed(power)]
+
+
+def swap(value, chips=SAME):
+    return sent(value, chips, 1, 0)
+
+
+def beside(value, chips=SAME):
+    return sent(value, chips, 1, 1)
 
 
 def shards(startup, guess, conduct, couple, inlet):
@@ -393,27 +388,29 @@
             own, near, swapped, weights
         )
 
-    def beside(value):
-        return sent(value, SAME, 1, 1)
-
     rim4, rim2 = shape(2, 4, NX, LAST), shape(2, 2, NX, LAST)
-    def exchanged(own, inner, outer, *arrived):
-        return lax.optimization_barrier((own, beside(outer), swap(inner)) + arrived)
-
-    a0 = sent(u, ringward(0), 0, 0)
-    u1, u2 = leap(u, beside(u), swap(u))
-    a1, a2 = sent(u1, ringward(1), 0, 0), sent(u2, ringward(2), 0, 0)
-    *operands, a0 = exchanged(u2, u2, u2, a0)
+    def exchanged(power, own, inner, outer, *arrived):
+        chips = needed(power)
+        return lax.optimization_barrier((own, beside(outer, chips), swap(inner, chips)) + arrived)
+
+    def along(value, power):
+        return sent(value, ringward(power), 0, 0)
+
+    a0 = along(u, 0)
+    u1, u2 = leap(*exchanged(1, u, u, u))
+    a1, a2 = along(u1, 1), along(u2, 2)
+    *operands, a0 = exchanged(3, u2, u2, u2, a0)
     u3, u4 = leap(*operands)
-    a4 = sent(u4, ringward(4), 0, 0)
-    *operands, a1, a2 = exchanged(u4, u4, u4, a1, a2)
+    a4 = along(u4, 4)
+    *operands, a1, a2 = exchanged(5, u4, u4, u4, a1, a2)
     u5, u6, inner, outer = leap(*operands, rim4, rim4)
-    a5, a6 = sent(u5, onward(5), 0, 0), sent(u6, onward(6), 0, 0)
-    mine, theirs = call(share_kernel, (half, half), [VMEM] * 5, (VMEM,) * 2, [], 16)(a0, a1, a2, u3, a4)
-    *operands, mine, theirs = exchanged(u6, inner, outer, mine, theirs)
+    a5, a6 = along(u5, 5), along(u6, 6)
+    *operands, a4 = exchanged(7, u6, inner, outer, a4)
     (u7,) = leap(*operands, second=False)
-    arrived = (mine, sent(theirs, ACROSS, 0, 0), a5, a6)
-    c, inner, outer = call(sum_kernel, (half, rim2, rim2), [VMEM] * 5, (VMEM,) * 3, [], 16)(u7, *arrived)
+    mine, theirs = call(share_kernel, (half, half), [VMEM] * 8, (VMEM,) * 2, [], 16)(a0, a1, a2, u3, a4, a5, a6, u7)
+    c, inner, outer = call(sum_kernel, (half, rim2, rim2), [VMEM] * 2, (VMEM,) * 3, [], 16)(
+        mine, sent(theirs, ACROSS, 0, 0)
+    )
     parcel = shape(BRICKS, 2 * HALF * PLANES, LAST)
     keep, send = call(last_kernel, (parcel, parcel), [VMEM] * 6, (VMEM,) * 2, [field, field, field], 22)(
         c, beside(outer), swap(inner), g, taken, weights

time: 144 us -> 147 us (1.021); the launches traced: 143 us -> 144 us
  starting transfers between devices: 43.9 us -> 45.6 us
  waiting for transfers between devices: 18.7 us -> 17.2 us
    ppermute x20, starting transfers between devices: 43.9 us -> 45.6 us  [sent(): return lax.ppermute(value, AXES, pairs)]
  transfers between devices with their start and end apart: 20 -> 20, of which waited for: 6 -> 7; matrix products, arithmetic and copies ran while one was open for 0% -> 0% of each run, Pallas kernels for 11% -> 11%
where the time goes in v7:
time: 147 us; the launch traced here: 144 us
  blocking collectives  46.4 us (32%)
  starting transfers between devices  45.6 us (31%)
  Pallas kernels  34.6 us (24%)
  waiting for transfers between devices  17.2 us (12%)
    ppermute x20, starting transfers between devices, sent(): return lax.ppermute(value, AXES, pairs)  45.6 us
    all_to_all x1, blocking collectives, shards(): got = lax.all_to_all(packed, 'space', 0, 0, tiled=True)  31.8 us
    ppermute x20, waiting for transfers between devices, sent(): return lax.ppermute(value, AXES, pairs)  17.2 us
    pallas_call x4, Pallas kernels, leap(): call(leap_kernel, outs, [VMEM] * 4, (VMEM,) * len(outs), [field, field],...  16.2 us
    pallas_call x1, Pallas kernels, shards(): call(relax_kernel, (pltpu.VMEM((HELD, 2 * PAIR, NX, LAST), F32), half, sh...  14.6 us
    all_to_all x1, blocking collectives, shards(): lax.all_to_all(jnp.concatenate([keep, swap(send)], axis=1), 'space', 0, 0...  14.6 us
  transfers between devices with their start and end apart: 20, of which 7 were waited for; matrix products, arithmetic and copies ran while one was open for 0% of the time, Pallas kernels for 11%

profile of v7, /device:TPU:4, one launch (start us, length us, event | category | flops | bytes accessed | tf_op | source)
XLA Modules:
  0.0 144.0 jit_solution(2167841570166679444)
XLA Ops:
  0.0 1.5 %shard_map.55 = f32[8,504,128]{2,1,0:T(8,128)S(1)} custom-call(f32[2,4,128,128]{3,2,1,0:T(8,128)} %startup.1, f32[1,2,4,128,128]{4,3,2,1,0:T(8,128)} %guess.1, f32[2,4,128,128]{3,2,1,0:T(8,128)} %conduct.1, f32[4,128,128]{2,1,0:T(8,128)} %couple.1), custom_call_target="tpu_custom_call" | custom-call | bytes 3145728 | tf_op jit(solution)/shard_map/pallas_call | solution.py:354
  1.5 31.8 %all_to_all.10.got = f32[8,504,128]{2,1,0:T(8,128)S(1)} all-to-all(f32[8,504,128]{2,1,0:T(8,128)S(1)} %shard_map.55), channel_id=1, replica_groups=mesh['chip'=8,'core'=2,'space'=8] {'space'}, dimensions={0} | all-to-all | bytes 4128768 | tf_op jit(solution)/shard_map/all_to_all | solution.py:367
  33.3 0.0 copy-start
  33.3 0.1 shard_map.56
  33.4 0.1 collective-permute-start
  33.5 2.4 %collective-permute-done.other = f32[3,18,32,128]{3,2,1,0:T(8,128)S(1)} collective-permute-done((f32[3,18,32,128]{3,2,1,0:T(8,128)S(1)}, f32[3,18,32,128]{3,2,1,0:T(8,128)S(1)}, u32[]{:S(2)}, u32[]{:S(2)}) %collective-permute-start) | collective-permute-done | bytes 884768 | tf_op jit(solution)/shard_map/ppermute | solution.py:327
  35.9 0.0 copy-done
  35.9 14.6 %shard_map.57 = (f32[40,18,32,128]{3,2,1,0:T(8,128)S(1)}, f32[2,8,32,128]{3,2,1,0:T(8,128)S(1)}, f32[4,8,32,128]{3,2,1,0:T(8,128)S(1)}, f32[2,8,32,128]{3,2,1,0:T(8,128)S(1)}) custom-call(f32[2,36,32,128]{3,2,1,0:T(8,128)S(1)} %get-tuple-element.42.begin, f32[3,18,32,128]{3,2,1,0:T(8,128)S(1)} %get-tuple-element.43.mine, ...), custom_call_target="tpu_custom_call" | custom-call | bytes 3145728 | tf_op jit(solution)/shard_map/pallas_call | solution.py:374
  50.5 0.2 collective-permute-start.1
  50.7 1.8 %collective-permute-done.1.taken = f32[4,8,32,128]{3,2,1,0:T(8,128)S(1)} collective-permute-done((f32[4,8,32,128]{3,2,1,0:T(8,128)S(1)}, f32[4,8,32,128]{3,2,1,0:T(8,128)S(1)}, u32[]{:S(2)}, u32[]{:S(2)}) %collective-permute-start.1) | collective-permute-done | bytes 524320 | tf_op jit(solution)/shard_map/ppermute | solution.py:327
  52.5 2.0 %collective-permute-start.3 = (f32[2,8,32,128]{3,2,1,0:T(8,128)S(1)}, f32[2,8,32,128]{3,2,1,0:T(8,128)S(1)}, u32[]{:S(2)}, u32[]{:S(2)}) collective-permute-start(f32[2,8,32,128]{3,2,1,0:T(8,128)S(1)} %slice_add_fusion.own), channel_id=1, source_target_pairs={{8,0},{10,2},{12,4},{14,6},{15,7},{13,5},{11,3},{9,1},{0,8},{2,10}... | collective-permute-start | bytes 786440 | tf_op jit(solution)/shard_map/ppermute | solution.py:327
  54.6 0.7 collective-permute-start.2
  55.3 2.0 %collective-permute-start.6 = (f32[2,8,32,128]{3,2,1,0:T(8,128)S(1)}, f32[2,8,32,128]{3,2,1,0:T(8,128)S(1)}, u32[]{:S(2)}, u32[]{:S(2)}) collective-permute-start(f32[2,8,32,128]{3,2,1,0:T(8,128)S(1)} %slice_add_fusion.own), channel_id=1, source_target_pairs={{0,16},{2,18},{4,20},{6,22},{7,23},{5,21},{3,19},{1,17},{8,24},{10... | collective-permute-start | bytes 786440 | tf_op jit(solution)/shard_map/ppermute | solution.py:327
  57.3 0.0 collective-permute-done.3.swapped
  57.3 0.0 collective-permute-done.2.near
  57.3 4.8 %shard_map.58 = (f32[2,8,32,128]{3,2,1,0:T(8,128)S(1)}, f32[2,8,32,128]{3,2,1,0:T(8,128)S(1)}) custom-call(f32[2,8,32,128]{3,2,1,0:T(8,128)S(1)} %slice_add_fusion.own, f32[2,8,32,128]{3,2,1,0:T(8,128)S(1)} %collective-permute-done.2.near, f32[2,8,32,128]{3,2,1,0:T(8,128)S(1)} %collective-permute-done.3.swapped, f32[40,18,32,128]{3,2,1,0:T(8,128)S(1)} %get-tuple-element.49.w), custom_call_target="tpu_custom_call" | custom-call | bytes 15728640 | tf_op jit(solution)/shard_map/pallas_call | solution.py:387
  62.1 0.7 collective-permute-start.5
  62.8 0.7 collective-permute-start.4
  63.5 12.9 %collective-permute-start.10 = (f32[2,8,32,128]{3,2,1,0:T(8,128)S(1)}, f32[2,8,32,128]{3,2,1,0:T(8,128)S(1)}, u32[]{:S(2)}, u32[]{:S(2)}) collective-permute-start(f32[2,8,32,128]{3,2,1,0:T(8,128)S(1)} %get-tuple-element.52.own), channel_id=1, source_target_pairs={{0,48},{2,50},{4,52},{6,54},{7,55},{5,53},{3,51},{1,49},{8,56},{10... | collective-permute-start | bytes 786440 | tf_op jit(solution)/shard_map/ppermute | solution.py:327
  76.3 1.3 collective-permute-start.9
  77.6 0.0 collective-permute-done.6.refs_0_
  77.7 0.0 collective-permute-done.5.swapped
  77.7 0.0 collective-permute-done.4.near
  77.7 4.8 %shard_map.59 = (f32[2,8,32,128]{3,2,1,0:T(8,128)S(1)}, f32[2,8,32,128]{3,2,1,0:T(8,128)S(1)}) custom-call(f32[2,8,32,128]{3,2,1,0:T(8,128)S(1)} %get-tuple-element.52.own, f32[2,8,32,128]{3,2,1,0:T(8,128)S(1)} %collective-permute-done.4.near, f32[2,8,32,128]{3,2,1,0:T(8,128)S(1)} %collective-permute-done.5.swapped, f32[40,18,32,128]{3,2,1,0:T(8,128)S(1)} %get-tuple-element.49.w), custom_call_target="tpu_custom_call" | custom-call | bytes 15728640 | tf_op jit(solution)/shard_map/pallas_call | solution.py:387
  82.5 0.7 collective-permute-start.8
  83.2 0.7 collective-permute-start.7
  83.9 1.3 collective-permute-start.13
  85.2 0.0 collective-permute-done.9.refs_1_
  85.2 2.9 %collective-permute-done.10.refs_2_ = f32[2,8,32,128]{3,2,1,0:T(8,128)S(1)} collective-permute-done((f32[2,8,32,128]{3,2,1,0:T(8,128)S(1)}, f32[2,8,32,128]{3,2,1,0:T(8,128)S(1)}, u32[]{:S(2)}, u32[]{:S(2)}) %collective-permute-start.10) | collective-permute-done | bytes 262176 | tf_op jit(solution)/shard_map/ppermute | solution.py:327
  88.0 0.0 collective-permute-done.8.swapped
  88.1 0.0 collective-permute-done.7.near
  88.1 4.8 %shard_map.60 = (f32[2,8,32,128]{3,2,1,0:T(8,128)S(1)}, f32[2,8,32,128]{3,2,1,0:T(8,128)S(1)}, f32[2,4,32,128]{3,2,1,0:T(8,128)S(1)}, f32[2,4,32,128]{3,2,1,0:T(8,128)S(1)}) custom-call(f32[2,8,32,128]{3,2,1,0:T(8,128)S(1)} %get-tuple-element.60.own, f32[2,8,32,128]{3,2,1,0:T(8,128)S(1)} %collective-permute-done.7.near, ...), custom_call_target="tpu_custom_call" | custom-call | bytes 15728640 | tf_op jit(solution)/shard_map/pallas_call | solution.py:387
  92.9 0.7 collective-permute-start.14
  93.6 0.7 collective-permute-start.15
  94.2 0.7 collective-permute-start.11
  94.9 0.7 collective-permute-start.12
  95.6 1.3 collective-permute-done.13.refs_4_
  96.9 0.0 collective-permute-done.11.near
  96.9 0.0 collective-permute-done.12.swapped
  96.9 1.8 %shard_map.61.refs_7_ = f32[2,8,32,128]{3,2,1,0:T(8,128)S(1)} custom-call(f32[2,8,32,128]{3,2,1,0:T(8,128)S(1)} %get-tuple-element.68.own, f32[2,4,32,128]{3,2,1,0:T(8,128)S(1)} %collective-permute-done.11.near, f32[2,4,32,128]{3,2,1,0:T(8,128)S(1)} %collective-permute-done.12.swapped, f32[40,18,32,128]{3,2,1,0:T(8,128)S(1)} %get-tuple-element.49.w), custom_call_target="tpu_custom_call" | custom-call | bytes 6291456 | tf_op jit(solution)/shard_map/pallas_call | solution.py:387
  98.7 0.0 collective-permute-done.14.refs_5_
  98.7 0.0 collective-permute-done.15.refs_6_
  98.7 0.4 shard_map.62
  99.1 13.1 %collective-permute-start.16 = (f32[2,8,32,128]{3,2,1,0:T(8,128)S(1)}, f32[2,8,32,128]{3,2,1,0:T(8,128)S(1)}, u32[]{:S(2)}, u32[]{:S(2)}) collective-permute-start(f32[2,8,32,128]{3,2,1,0:T(8,128)S(1)} %get-tuple-element.72), channel_id=1, source_target_pairs={{64,0},{66,2},{68,4},{70,6},{71,7},{69,5},{67,3},{65,1},{72,8},{74... | collective-permute-start | bytes 786440 | tf_op jit(solution)/shard_map/ppermute | solution.py:327
  112.2 6.8 %collective-permute-done.16.arrived = f32[2,8,32,128]{3,2,1,0:T(8,128)S(1)} collective-permute-done((f32[2,8,32,128]{3,2,1,0:T(8,128)S(1)}, f32[2,8,32,128]{3,2,1,0:T(8,128)S(1)}, u32[]{:S(2)}, u32[]{:S(2)}) %collective-permute-start.16) | collective-permute-done | bytes 262176 | tf_op jit(solution)/shard_map/ppermute | solution.py:327
  119.0 0.7 collective-permute-start.17
  119.7 4.9 %collective-permute-start.18 = (f32[2,2,32,128]{3,2,1,0:T(8,128)S(1)}, f32[2,2,32,128]{3,2,1,0:T(8,128)S(1)}, u32[]{:S(2)}, u32[]{:S(2)}) collective-permute-start(f32[2,2,32,128]{3,2,1,0:T(8,128)S(1)} %get-tuple-element.75), channel_id=1, source_target_pairs={{8,0},{10,2},{12,4},{14,6},{15,7},{13,5},{11,3},{9,1},{0,8},{2,10}... | collective-permute-start | bytes 196616 | tf_op jit(solution)/shard_map/ppermute | solution.py:327
  124.6 0.0 collective-permute-done.17.near
  124.6 0.9 collective-permute-done.18.swapped
  125.5 0.9 shard_map.64
  126.4 1.0 collective-permute-start.19
  127.4 1.2 collective-permute-done.19
  128.6 14.6 %all_to_all.11.got = f32[8,128,128]{2,1,0:T(8,128)S(1)} all-to-all(f32[8,128,128]{2,1,0:T(8,128)S(1)} %pad_maximum_fusion), channel_id=1, replica_groups=mesh['chip'=8,'core'=2,'space'=8] {'space'}, dimensions={0} | all-to-all | bytes 1048576 | tf_op jit(solution)/shard_map/all_to_all | solution.py:418
  143.2 0.8 shard_map.65
  (3 shorter events, 0.1 us)
Async XLA Ops:
  33.3 2.7 %copy-start = (f32[128,128]{1,0:T(8,128)S(1)}, f32[128,128]{1,0:T(8,128)}, u32[]{:S(2)}) copy-start(f32[128,128]{1,0:T(8,128)} %inlet.1) | copy-start | bytes 196612
  33.4 2.5 %collective-permute-start = (f32[3,18,32,128]{3,2,1,0:T(8,128)S(1)}, f32[3,18,32,128]{3,2,1,0:T(8,128)S(1)}, u32[]{:S(2)}, u32[]{:S(2)}) collective-permute-start(f32[3,18,32,128]{3,2,1,0:T(8,128)S(1)} %get-tuple-element.43.mine), channel_id=1, source_target_pairs={{8,0},{10,2},{12,4},{14,6},{15,7},{13,5},{11,3},{9,1},{0,8},{2,10}... | collective-permute-start | bytes 2654216 | tf_op jit(solution)/shard_map/ppermute | solution.py:327
  50.5 2.0 %collective-permute-start.1 = (f32[4,8,32,128]{3,2,1,0:T(8,128)S(1)}, f32[4,8,32,128]{3,2,1,0:T(8,128)S(1)}, u32[]{:S(2)}, u32[]{:S(2)}) collective-permute-start(f32[4,8,32,128]{3,2,1,0:T(8,128)S(1)} %get-tuple-element.45), channel_id=1, source_target_pairs={{8,0},{10,2},{12,4},{14,6},{15,7},{13,5},{11,3},{9,1},{0,8},{2,10}... | collective-permute-start | bytes 1572872 | tf_op jit(solution)/shard_map/ppermute | solution.py:327
  52.5 4.7 %collective-permute-start.3 = (f32[2,8,32,128]{3,2,1,0:T(8,128)S(1)}, f32[2,8,32,128]{3,2,1,0:T(8,128)S(1)}, u32[]{:S(2)}, u32[]{:S(2)}) collective-permute-start(f32[2,8,32,128]{3,2,1,0:T(8,128)S(1)} %slice_add_fusion.own), channel_id=1, source_target_pairs={{8,0},{10,2},{12,4},{14,6},{15,7},{13,5},{11,3},{9,1},{0,8},{2,10}... | collective-permute-start | bytes 786440 | tf_op jit(solution)/shard_map/ppermute | solution.py:327
  54.6 2.7 %collective-permute-start.2 = (f32[2,8,32,128]{3,2,1,0:T(8,128)S(1)}, f32[2,8,32,128]{3,2,1,0:T(8,128)S(1)}, u32[]{:S(2)}, u32[]{:S(2)}) collective-permute-start(f32[2,8,32,128]{3,2,1,0:T(8,128)S(1)} %slice_add_fusion.own), channel_id=1, source_target_pairs={{8,2},{10,4},{12,6},{14,7},{15,5},{13,3},{11,1},{2,8},{4,10},{6,12... | collective-permute-start | bytes 786440 | tf_op jit(solution)/shard_map/ppermute | solution.py:327
  55.3 22.4 %collective-permute-start.6 = (f32[2,8,32,128]{3,2,1,0:T(8,128)S(1)}, f32[2,8,32,128]{3,2,1,0:T(8,128)S(1)}, u32[]{:S(2)}, u32[]{:S(2)}) collective-permute-start(f32[2,8,32,128]{3,2,1,0:T(8,128)S(1)} %slice_add_fusion.own), channel_id=1, source_target_pairs={{0,16},{2,18},{4,20},{6,22},{7,23},{5,21},{3,19},{1,17},{8,24},{10... | collective-permute-start | bytes 786440 | tf_op jit(solution)/shard_map/ppermute | solution.py:327
  62.1 15.6 %collective-permute-start.5 = (f32[2,8,32,128]{3,2,1,0:T(8,128)S(1)}, f32[2,8,32,128]{3,2,1,0:T(8,128)S(1)}, u32[]{:S(2)}, u32[]{:S(2)}) collective-permute-start(f32[2,8,32,128]{3,2,1,0:T(8,128)S(1)} %get-tuple-element.52.own), channel_id=1, source_target_pairs={{8,0},{10,2},{12,4},{14,6},{15,7},{13,5},{11,3},{9,1},{0,8},{2,10}... | collective-permute-start | bytes 786440 | tf_op jit(solution)/shard_map/ppermute | solution.py:327
  62.8 14.9 %collective-permute-start.4 = (f32[2,8,32,128]{3,2,1,0:T(8,128)S(1)}, f32[2,8,32,128]{3,2,1,0:T(8,128)S(1)}, u32[]{:S(2)}, u32[]{:S(2)}) collective-permute-start(f32[2,8,32,128]{3,2,1,0:T(8,128)S(1)} %get-tuple-element.52.own), channel_id=1, source_target_pairs={{8,2},{10,4},{12,6},{14,7},{15,5},{13,3},{11,1},{2,8},{4,10},{6,12... | collective-permute-start | bytes 786440 | tf_op jit(solution)/shard_map/ppermute | solution.py:327
  63.5 24.6 %collective-permute-start.10 = (f32[2,8,32,128]{3,2,1,0:T(8,128)S(1)}, f32[2,8,32,128]{3,2,1,0:T(8,128)S(1)}, u32[]{:S(2)}, u32[]{:S(2)}) collective-permute-start(f32[2,8,32,128]{3,2,1,0:T(8,128)S(1)} %get-tuple-element.52.own), channel_id=1, source_target_pairs={{0,48},{2,50},{4,52},{6,54},{7,55},{5,53},{3,51},{1,49},{8,56},{10... | collective-permute-start | bytes 786440 | tf_op jit(solution)/shard_map/ppermute | solution.py:327
  76.3 8.8 %collective-permute-start.9 = (f32[2,8,32,128]{3,2,1,0:T(8,128)S(1)}, f32[2,8,32,128]{3,2,1,0:T(8,128)S(1)}, u32[]{:S(2)}, u32[]{:S(2)}) collective-permute-start(f32[2,8,32,128]{3,2,1,0:T(8,128)S(1)} %get-tuple-element.56), channel_id=1, source_target_pairs={{0,32},{2,34},{4,36},{6,38},{7,39},{5,37},{3,35},{1,33},{8,40},{10... | collective-permute-start | bytes 786440 | tf_op jit(solution)/shard_map/ppermute | solution.py:327
  82.5 5.6 %collective-permute-start.8 = (f32[2,8,32,128]{3,2,1,0:T(8,128)S(1)}, f32[2,8,32,128]{3,2,1,0:T(8,128)S(1)}, u32[]{:S(2)}, u32[]{:S(2)}) collective-permute-start(f32[2,8,32,128]{3,2,1,0:T(8,128)S(1)} %get-tuple-element.60.own), channel_id=1, source_target_pairs={{8,0},{10,2},{12,4},{14,6},{15,7},{13,5},{11,3},{9,1},{0,8},{2,10}... | collective-permute-start | bytes 786440 | tf_op jit(solution)/shard_map/ppermute | solution.py:327
  83.2 4.9 %collective-permute-start.7 = (f32[2,8,32,128]{3,2,1,0:T(8,128)S(1)}, f32[2,8,32,128]{3,2,1,0:T(8,128)S(1)}, u32[]{:S(2)}, u32[]{:S(2)}) collective-permute-start(f32[2,8,32,128]{3,2,1,0:T(8,128)S(1)} %get-tuple-element.60.own), channel_id=1, source_target_pairs={{8,2},{10,4},{12,6},{14,7},{15,5},{13,3},{11,1},{2,8},{4,10},{6,12... | collective-permute-start | bytes 786440 | tf_op jit(solution)/shard_map/ppermute | solution.py:327
  83.9 13.0 %collective-permute-start.13 = (f32[2,8,32,128]{3,2,1,0:T(8,128)S(1)}, f32[2,8,32,128]{3,2,1,0:T(8,128)S(1)}, u32[]{:S(2)}, u32[]{:S(2)}) collective-permute-start(f32[2,8,32,128]{3,2,1,0:T(8,128)S(1)} %get-tuple-element.60.own), channel_id=1, source_target_pairs={{0,16},{2,18},{4,20},{6,22},{7,23},{5,21},{3,19},{1,17},{8,24},{10... | collective-permute-start | bytes 786440 | tf_op jit(solution)/shard_map/ppermute | solution.py:327
  92.9 5.9 %collective-permute-start.14 = (f32[2,8,32,128]{3,2,1,0:T(8,128)S(1)}, f32[2,8,32,128]{3,2,1,0:T(8,128)S(1)}, u32[]{:S(2)}, u32[]{:S(2)}) collective-permute-start(f32[2,8,32,128]{3,2,1,0:T(8,128)S(1)} %get-tuple-element.67), channel_id=1, source_target_pairs={{0,32},{2,34},{4,36},{6,38},{7,39},{5,37},{3,35},{1,33},{8,40},{10... | collective-permute-start | bytes 786440 | tf_op jit(solution)/shard_map/ppermute | solution.py:327
  93.6 5.2 %collective-permute-start.15 = (f32[2,8,32,128]{3,2,1,0:T(8,128)S(1)}, f32[2,8,32,128]{3,2,1,0:T(8,128)S(1)}, u32[]{:S(2)}, u32[]{:S(2)}) collective-permute-start(f32[2,8,32,128]{3,2,1,0:T(8,128)S(1)} %get-tuple-element.68.own), channel_id=1, source_target_pairs={{0,48},{2,50},{4,52},{6,54},{7,55},{5,53},{3,51},{1,49},{8,56},{10... | collective-permute-start | bytes 786440 | tf_op jit(solution)/shard_map/ppermute | solution.py:327
  94.2 2.6 %collective-permute-start.11 = (f32[2,4,32,128]{3,2,1,0:T(8,128)S(1)}, f32[2,4,32,128]{3,2,1,0:T(8,128)S(1)}, u32[]{:S(2)}, u32[]{:S(2)}) collective-permute-start(f32[2,4,32,128]{3,2,1,0:T(8,128)S(1)} %get-tuple-element.64), channel_id=1, source_target_pairs={{120,114},{122,116},{124,118},{126,119},{127,117},{125,115},{123,1... | collective-permute-start | bytes 393224 | tf_op jit(solution)/shard_map/ppermute | solution.py:327
  94.9 2.0 %collective-permute-start.12 = (f32[2,4,32,128]{3,2,1,0:T(8,128)S(1)}, f32[2,4,32,128]{3,2,1,0:T(8,128)S(1)}, u32[]{:S(2)}, u32[]{:S(2)}) collective-permute-start(f32[2,4,32,128]{3,2,1,0:T(8,128)S(1)} %get-tuple-element.65), channel_id=1, source_target_pairs={{120,112},{122,114},{124,116},{126,118},{127,119},{125,117},{123,1... | collective-permute-start | bytes 393224 | tf_op jit(solution)/shard_map/ppermute | solution.py:327
  99.1 19.8 %collective-permute-start.16 = (f32[2,8,32,128]{3,2,1,0:T(8,128)S(1)}, f32[2,8,32,128]{3,2,1,0:T(8,128)S(1)}, u32[]{:S(2)}, u32[]{:S(2)}) collective-permute-start(f32[2,8,32,128]{3,2,1,0:T(8,128)S(1)} %get-tuple-element.72), channel_id=1, source_target_pairs={{64,0},{66,2},{68,4},{70,6},{71,7},{69,5},{67,3},{65,1},{72,8},{74... | collective-permute-start | bytes 786440 | tf_op jit(solution)/shard_map/ppermute | solution.py:327
  119.0 5.6 %collective-permute-start.17 = (f32[2,2,32,128]{3,2,1,0:T(8,128)S(1)}, f32[2,2,32,128]{3,2,1,0:T(8,128)S(1)}, u32[]{:S(2)}, u32[]{:S(2)}) collective-permute-start(f32[2,2,32,128]{3,2,1,0:T(8,128)S(1)} %get-tuple-element.74), channel_id=1, source_target_pairs={{8,2},{10,4},{12,6},{14,7},{15,5},{13,3},{11,1},{2,8},{4,10},{6,12... | collective-permute-start | bytes 196616 | tf_op jit(solution)/shard_map/ppermute | solution.py:327
  119.7 5.8 %collective-permute-start.18 = (f32[2,2,32,128]{3,2,1,0:T(8,128)S(1)}, f32[2,2,32,128]{3,2,1,0:T(8,128)S(1)}, u32[]{:S(2)}, u32[]{:S(2)}) collective-permute-start(f32[2,2,32,128]{3,2,1,0:T(8,128)S(1)} %get-tuple-element.75), channel_id=1, source_target_pairs={{8,0},{10,2},{12,4},{14,6},{15,7},{13,5},{11,3},{9,1},{0,8},{2,10}... | collective-permute-start | bytes 196616 | tf_op jit(solution)/shard_map/ppermute | solution.py:327
  126.4 2.2 %collective-permute-start.19 = (f32[8,64,128]{2,1,0:T(8,128)S(1)}, f32[8,64,128]{2,1,0:T(8,128)S(1)}, u32[]{:S(2)}, u32[]{:S(2)}) collective-permute-start(f32[8,64,128]{2,1,0:T(8,128)S(1)} %get-tuple-element.78), channel_id=1, source_target_pairs={{8,0},{10,2},{12,4},{14,6},{15,7},{13,5},{11,3},{9,1},{0,8},{2,10}... | collective-permute-start | bytes 786440 | tf_op jit(solution)/shard_map/ppermute | solution.py:327

commit v8 on v5

--- a/solution.py
+++ b/solution.py
@@ -14,6 +14,8 @@
 MIDDLE = 128
 LAST = 128
 STRIP = 16
+CHIPS = SLABS // 2
+RING = 4
 HALF = 8
 EDGE = 10
 ROWS = STRIP + 2 * EDGE
@@ -244,7 +246,8 @@
     state[:, pl.ds(middle - rim + (HALF + rim) * core, rim)] = outward[...]
 
 
-def leap_kernel(own, near, swapped, w, odd, *refs):
+def leap_kernel(joined, own, near, swapped, w, *refs):
+    high, (odd, *refs) = (refs[0], refs[1:]) if joined else (None, refs)
     core, _, _ = position()
     middle = EDGE + HALF * core
     rows = pl.ds(middle, HALF)
@@ -257,20 +260,23 @@
     if more:
         even, *rims = more
         advances(2, e, v, w, middle - 4, middle + HALF + 4, COARSE)
-        even[...] = e[:, rows]
+        even[...] = e[:, rows] + high[...] if joined else e[:, rows]
         if rims:
             inner, outer = rims
             inner[...] = even[:, pl.ds(4 - 4 * core, 4)]
             outer[...] = even[:, pl.ds(4 * core, 4)]
 
 
-def sum_kernel(local, *refs):
+def share_kernel(*refs):
+    *arrived, out, inner, outer = refs
     core, _, slab = position()
-    *arrived, out, inner, outer = refs
-    total = arrived[0][...]
-    for ref in arrived[1:]:
-        total = total + ref[...]
-    out[...] = total + jnp.where(slab // 2 == SLABS // 2 - 1, local[...], 0.0)
+    chip = slab // 2
+    late = chip // RING
+    total = 0.0
+    for power, ref in enumerate(arrived):
+        target = lax.rem(chip + 2 * RING - power, RING) + power
+        total = total + jnp.where((target // RING == late) & (target < 2 * RING), ref[...], 0.0)
+    out[...] = total
     inner[...] = out[:, pl.ds(6 - 6 * core, 2)]
     outer[...] = out[:, pl.ds(6 * core, 2)]
 
@@ -306,22 +312,30 @@
     for source, target in chips:
         for core in range(2):
             for strip in range(BRICKS):
-                beside = strip + shift * (1 if core == 0 else -1)
-                if 0 <= beside < BRICKS:
-                    pairs.append((index(source, core ^ flip, strip), index(target, core, beside)))
+                beside = (strip + shift * (1 if core == 0 else -1)) % BRICKS
+                pairs.append((index(source, core ^ flip, strip), index(target, core, beside)))
     return lax.ppermute(value, AXES, pairs)
 
 
-CHIPS = SLABS // 2
 SAME = [(c, c) for c in range(CHIPS)]
-
-
-def onward(power):
-    return [((j - 1) % CHIPS, j + power) for j in range(CHIPS - power)]
+ACROSS = [((c + RING) % CHIPS, c) for c in range(CHIPS)]
+
+
+def along(value, power):
+    pairs = [(c, c // RING * RING + (c + 1 + power) % RING) for c in range(CHIPS)]
+    return sent(value, pairs, 0, 0)
 
 
 def swap(value):
     return sent(value, SAME, 1, 0)
+
+
+def beside(value):
+    return sent(value, SAME, 1, 1)
+
+
+def exchanged(own, inner, outer, *arrived):
+    return lax.optimization_barrier((own, beside(outer), swap(inner)) + arrived)
 
 
 def shards(startup, guess, conduct, couple, inlet):
@@ -359,32 +373,32 @@
     taken = swap(give)
     u = base + taken[:2]
 
-    def leap(own, near, swapped, *rims, second=True):
+    def leap(own, near, swapped, *rims, second=True, high=None):
         outs = (half,) * (1 + second) + rims
-        return call(leap_kernel, outs, [VMEM] * 4, (VMEM,) * len(outs), [field, field], 20, 2 + 3 * second)(
-            own, near, swapped, weights
-        )
-
-    def beside(value):
-        return sent(value, SAME, 1, 1)
+        operands = [own, near, swapped, weights] + ([] if high is None else [high])
+        body = functools.partial(leap_kernel, high is not None)
+        return call(body, outs, [VMEM] * len(operands), (VMEM,) * len(outs), [field, field], 20, 2 + 3 * second)(*operands)
+
+    chip = lax.axis_index("chip")
+    across = sent(u, ACROSS, 0, 0)
+    stays = (chip < RING - 1) | (chip == CHIPS - 1)
+    low, high = jnp.where(stays, u, across), jnp.where(stays, across, u)
 
     rim4, rim2 = shape(2, 4, NX, LAST), shape(2, 2, NX, LAST)
-    def exchanged(own, inner, outer, *arrived):
-        return lax.optimization_barrier((own, beside(outer), swap(inner)) + arrived)
-
-    a0 = sent(u, onward(0), 0, 0)
-    u1, u2 = leap(u, beside(u), swap(u))
-    a1, a2 = sent(u1, onward(1), 0, 0), sent(u2, onward(2), 0, 0)
+    a0 = along(low, 0)
+    u1, u2 = leap(*exchanged(low, low, low))
+    a1, a2 = along(u1, 1), along(u2, 2)
     *operands, a0 = exchanged(u2, u2, u2, a0)
-    u3, u4 = leap(*operands)
-    a3, a4 = sent(u3, onward(3), 0, 0), sent(u4, onward(4), 0, 0)
+    u3, u4 = leap(*operands, high=high)
+    a4 = along(u4, 4)
     *operands, a1, a2 = exchanged(u4, u4, u4, a1, a2)
     u5, u6, inner, outer = leap(*operands, rim4, rim4)
-    a5, a6 = sent(u5, onward(5), 0, 0), sent(u6, onward(6), 0, 0)
-    *operands, a3, a4 = exchanged(u6, inner, outer, a3, a4)
+    a5, a6 = along(u5, 5), along(u6, 6)
+    *operands, a4 = exchanged(u6, inner, outer, a4)
     (u7,) = leap(*operands, second=False)
-    arrived = (a0, a1, a2, a3, a4, a5, a6)
-    c, inner, outer = call(sum_kernel, (half, rim2, rim2), [VMEM] * 8, (VMEM,) * 3, [], 16)(u7, *arrived)
+    c, inner, outer = call(share_kernel, (half, rim2, rim2), [VMEM] * 8, (VMEM,) * 3, [], 16)(
+        a0, a1, a2, u3, a4, a5, a6, u7
+    )
     parcel = shape(BRICKS, 2 * HALF * PLANES, LAST)
     keep, send = call(last_kernel, (parcel, parcel), [VMEM] * 6, (VMEM,) * 2, [field, field, field], 22)(
         c, beside(outer), swap(inner), g, taken, weights

time: 143 us -> 141 us (0.986)
  the two profiles are of different devices: /device:TPU:0 before, /device:TPU:4 now
where the time goes in v8:
time: 141 us
  blocking collectives  44.9 us (32%)
  waiting for transfers between devices  36.2 us (26%)
  Pallas kernels  34.3 us (24%)
  starting transfers between devices  16.3 us (12%)
  local copies, waits for them, and re-layouts  8.69 us (6%)
    ppermute x20, waiting for transfers between devices, sent(): return lax.ppermute(value, AXES, pairs)  36.2 us
    all_to_all x1, blocking collectives, shards(): got = lax.all_to_all(packed, 'space', 0, 0, tiled=True)  31.8 us
    ppermute x20, starting transfers between devices, sent(): return lax.ppermute(value, AXES, pairs)  16.3 us
    pallas_call x4, Pallas kernels, leap(): call(body, outs, [VMEM] * len(operands), (VMEM,) * len(outs), [field, fie...  16.2 us
    pallas_call x1, Pallas kernels, shards(): call(relax_kernel, (pltpu.VMEM((HELD, 2 * PAIR, NX, LAST), F32), half, sh...  14.6 us
    all_to_all x1, blocking collectives, shards(): lax.all_to_all(jnp.concatenate([keep, swap(send)], axis=1), 'space', 0, 0...  13.1 us
    unnamed x12, local copies, waits for them, and re-layouts  8.69 us
  transfers between devices with their start and end apart: 20, of which 12 were waited for; matrix products, arithmetic and copies ran while one was open for 0% of the time, Pallas kernels for 12%

profile of v8, /device:TPU:4, one launch (start us, length us, event | category | flops | bytes accessed | tf_op | source)
XLA Modules:
  0.0 140.7 jit_solution(5391526582929856776)
XLA Ops:
  0.0 1.5 %shard_map.55 = f32[8,504,128]{2,1,0:T(8,128)S(1)} custom-call(f32[2,4,128,128]{3,2,1,0:T(8,128)} %startup.1, f32[1,2,4,128,128]{4,3,2,1,0:T(8,128)} %guess.1, f32[2,4,128,128]{3,2,1,0:T(8,128)} %conduct.1, f32[4,128,128]{2,1,0:T(8,128)} %couple.1), custom_call_target="tpu_custom_call" | custom-call | bytes 3145728 | tf_op jit(solution)/shard_map/pallas_call | solution.py:345
  1.5 31.8 %all_to_all.10.got = f32[8,504,128]{2,1,0:T(8,128)S(1)} all-to-all(f32[8,504,128]{2,1,0:T(8,128)S(1)} %shard_map.55), channel_id=1, replica_groups=mesh['chip'=8,'core'=2,'space'=8] {'space'}, dimensions={0} | all-to-all | bytes 4128768 | tf_op jit(solution)/shard_map/all_to_all | solution.py:358
  33.3 0.0 copy-start.2
  33.3 0.1 shard_map.56
  33.4 0.1 collective-permute-start
  33.5 2.4 %collective-permute-done.other = f32[3,18,32,128]{3,2,1,0:T(8,128)S(1)} collective-permute-done((f32[3,18,32,128]{3,2,1,0:T(8,128)S(1)}, f32[3,18,32,128]{3,2,1,0:T(8,128)S(1)}, u32[]{:S(2)}, u32[]{:S(2)}) %collective-permute-start) | collective-permute-done | bytes 884768 | tf_op jit(solution)/shard_map/ppermute | solution.py:317
  35.9 0.0 copy-done.2
  35.9 14.6 %shard_map.57 = (f32[40,18,32,128]{3,2,1,0:T(8,128)S(1)}, f32[2,8,32,128]{3,2,1,0:T(8,128)S(1)}, f32[4,8,32,128]{3,2,1,0:T(8,128)S(1)}, f32[2,8,32,128]{3,2,1,0:T(8,128)S(1)}) custom-call(f32[2,36,32,128]{3,2,1,0:T(8,128)S(1)} %get-tuple-element.40.begin, f32[3,18,32,128]{3,2,1,0:T(8,128)S(1)} %get-tuple-element.41.mine, ...), custom_call_target="tpu_custom_call" | custom-call | bytes 3145728 | tf_op jit(solution)/shard_map/pallas_call | solution.py:365
  50.5 0.0 copy-start
  50.5 4.3 %copy-done = f32[40,18,32,128]{3,2,1,0:T(8,128)} copy-done((f32[40,18,32,128]{3,2,1,0:T(8,128)}, f32[40,18,32,128]{3,2,1,0:T(8,128)S(1)}, u32[]{:S(2)}) %copy-start) | copy-done | bytes 11796504
  54.9 0.1 collective-permute-start.1
  55.0 1.8 %collective-permute-done.1.taken = f32[4,8,32,128]{3,2,1,0:T(8,128)S(1)} collective-permute-done((f32[4,8,32,128]{3,2,1,0:T(8,128)S(1)}, f32[4,8,32,128]{3,2,1,0:T(8,128)S(1)}, u32[]{:S(2)}, u32[]{:S(2)}) %collective-permute-start.1) | collective-permute-done | bytes 524320 | tf_op jit(solution)/shard_map/ppermute | solution.py:317
  56.8 0.9 collective-permute-start.2
  57.7 9.1 %collective-permute-done.2 = f32[2,8,32,128]{3,2,1,0:T(8,128)S(1)} collective-permute-done((f32[2,8,32,128]{3,2,1,0:T(8,128)S(1)}, f32[2,8,32,128]{3,2,1,0:T(8,128)S(1)}, u32[]{:S(2)}, u32[]{:S(2)}) %collective-permute-start.2) | collective-permute-done | bytes 262176 | tf_op jit(solution)/shard_map/ppermute | solution.py:317
  66.8 0.1 collective-permute-start.3
  66.9 0.3 collective-permute-start.4
  67.2 1.9 %collective-permute-start.7 = (f32[2,8,32,128]{3,2,1,0:T(8,128)S(1)}, f32[2,8,32,128]{3,2,1,0:T(8,128)S(1)}, u32[]{:S(2)}, u32[]{:S(2)}) collective-permute-start(f32[2,8,32,128]{3,2,1,0:T(8,128)S(1)} %get-tuple-element.44.own), channel_id=1, source_target_pairs={{0,16},{2,18},{4,20},{6,22},{7,23},{5,21},{3,19},{1,17},{8,24},{10... | collective-permute-start | bytes 786440 | tf_op jit(solution)/shard_map/ppermute | solution.py:317
  69.1 3.5 %collective-permute-done.3.near = f32[2,8,32,128]{3,2,1,0:T(8,128)S(1)} collective-permute-done((f32[2,8,32,128]{3,2,1,0:T(8,128)S(1)}, f32[2,8,32,128]{3,2,1,0:T(8,128)S(1)}, u32[]{:S(2)}, u32[]{:S(2)}) %collective-permute-start.3) | collective-permute-done | bytes 262176 | tf_op jit(solution)/shard_map/ppermute | solution.py:317
  72.7 0.0 collective-permute-done.4.swapped
  72.7 0.0 copy-start.1
  72.7 4.4 %copy-done.1 = f32[40,18,32,128]{3,2,1,0:T(8,128)S(1)} copy-done((f32[40,18,32,128]{3,2,1,0:T(8,128)S(1)}, f32[40,18,32,128]{3,2,1,0:T(8,128)}, u32[]{:S(2)}) %copy-start.1) | copy-done | bytes 11796504
  77.0 4.8 %shard_map.58 = (f32[2,8,32,128]{3,2,1,0:T(8,128)S(1)}, f32[2,8,32,128]{3,2,1,0:T(8,128)S(1)}) custom-call(f32[2,8,32,128]{3,2,1,0:T(8,128)S(1)} %get-tuple-element.44.own, f32[2,8,32,128]{3,2,1,0:T(8,128)S(1)} %collective-permute-done.3.near, f32[2,8,32,128]{3,2,1,0:T(8,128)S(1)} %collective-permute-done.4.swapped, f32[40,18,32,128]{3,2,1,0:T(8,128)S(1)} %copy-done.1), custom_call_target="tpu_custom_call" | custom-call | bytes 15728640 | tf_op jit(solution)/shard_map/pallas_call | solution.py:380
  81.8 0.3 collective-permute-start.5
  82.2 0.1 collective-permute-start.6
  82.3 4.0 %collective-permute-start.11 = (f32[2,8,32,128]{3,2,1,0:T(8,128)S(1)}, f32[2,8,32,128]{3,2,1,0:T(8,128)S(1)}, u32[]{:S(2)}, u32[]{:S(2)}) collective-permute-start(f32[2,8,32,128]{3,2,1,0:T(8,128)S(1)} %get-tuple-element.50.own), channel_id=1, source_target_pairs={{0,48},{2,50},{4,52},{6,54},{7,55},{5,53},{3,51},{1,49},{8,56},{10... | collective-permute-start | bytes 786440 | tf_op jit(solution)/shard_map/ppermute | solution.py:317
  86.3 0.0 collective-permute-start.10
  86.3 0.0 collective-permute-done.7.refs_0_
  86.3 1.4 collective-permute-done.5.near
  87.7 0.0 collective-permute-done.6.swapped
  87.7 4.8 %shard_map.59 = (f32[2,8,32,128]{3,2,1,0:T(8,128)S(1)}, f32[2,8,32,128]{3,2,1,0:T(8,128)S(1)}) custom-call(f32[2,8,32,128]{3,2,1,0:T(8,128)S(1)} %get-tuple-element.50.own, f32[2,8,32,128]{3,2,1,0:T(8,128)S(1)} %collective-permute-done.5.near, f32[2,8,32,128]{3,2,1,0:T(8,128)S(1)} %collective-permute-done.6.swapped, f32[40,18,32,128]{3,2,1,0:T(8,128)S(1)} %copy-done.1, ...), custom_call_target="tpu_custom_call" | custom-call | bytes 15728640 | tf_op jit(solution)/shard_map/pallas_call | solution.py:380
  92.5 0.6 collective-permute-start.8
  93.2 0.0 collective-permute-start.9
  93.2 1.9 %collective-permute-start.14 = (f32[2,8,32,128]{3,2,1,0:T(8,128)S(1)}, f32[2,8,32,128]{3,2,1,0:T(8,128)S(1)}, u32[]{:S(2)}, u32[]{:S(2)}) collective-permute-start(f32[2,8,32,128]{3,2,1,0:T(8,128)S(1)} %get-tuple-element.58.own), channel_id=1, source_target_pairs={{0,16},{2,18},{4,20},{6,22},{7,23},{5,21},{3,19},{1,17},{8,24},{10... | collective-permute-start | bytes 786440 | tf_op jit(solution)/shard_map/ppermute | solution.py:317
  95.1 1.1 collective-permute-done.10.refs_1_
  96.2 1.9 %collective-permute-done.11.refs_2_ = f32[2,8,32,128]{3,2,1,0:T(8,128)S(1)} collective-permute-done((f32[2,8,32,128]{3,2,1,0:T(8,128)S(1)}, f32[2,8,32,128]{3,2,1,0:T(8,128)S(1)}, u32[]{:S(2)}, u32[]{:S(2)}) %collective-permute-start.11) | collective-permute-done | bytes 262176 | tf_op jit(solution)/shard_map/ppermute | solution.py:317
  98.1 0.3 collective-permute-done.8.near
  98.4 0.0 collective-permute-done.9.swapped
  98.4 0.0 slice-start
  98.4 0.0 slice-start.1
  98.4 4.8 %shard_map.60 = (f32[2,8,32,128]{3,2,1,0:T(8,128)S(1)}, f32[2,8,32,128]{3,2,1,0:T(8,128)S(1)}, f32[2,4,32,128]{3,2,1,0:T(8,128)S(1)}, f32[2,4,32,128]{3,2,1,0:T(8,128)S(1)}) custom-call(f32[2,8,32,128]{3,2,1,0:T(8,128)S(1)} %get-tuple-element.58.own, f32[2,8,32,128]{3,2,1,0:T(8,128)S(1)} %collective-permute-done.8.near, ...), custom_call_target="tpu_custom_call" | custom-call | bytes 15728640 | tf_op jit(solution)/shard_map/pallas_call | solution.py:380
  103.2 4.0 %collective-permute-start.15 = (f32[2,8,32,128]{3,2,1,0:T(8,128)S(1)}, f32[2,8,32,128]{3,2,1,0:T(8,128)S(1)}, u32[]{:S(2)}, u32[]{:S(2)}) collective-permute-start(f32[2,8,32,128]{3,2,1,0:T(8,128)S(1)} %get-tuple-element.65), channel_id=1, source_target_pairs={{0,32},{2,34},{4,36},{6,38},{7,39},{5,37},{3,35},{1,33},{8,40},{10... | collective-permute-start | bytes 786440 | tf_op jit(solution)/shard_map/ppermute | solution.py:317
  107.2 0.7 collective-permute-start.16
  107.9 0.3 collective-permute-start.12
  108.2 0.0 slice-start.2
  108.2 0.2 collective-permute-start.13
  108.5 0.0 collective-permute-done.14.refs_4_
  108.5 3.8 %collective-permute-done.12.near = f32[2,4,32,128]{3,2,1,0:T(8,128)S(1)} collective-permute-done((f32[2,4,32,128]{3,2,1,0:T(8,128)S(1)}, f32[2,4,32,128]{3,2,1,0:T(8,128)S(1)}, u32[]{:S(2)}, u32[]{:S(2)}) %collective-permute-start.12) | collective-permute-done | bytes 131104 | tf_op jit(solution)/shard_map/ppermute | solution.py:317
  112.3 0.0 collective-permute-done.13.swapped
  112.3 1.8 %shard_map.61.refs_7_ = f32[2,8,32,128]{3,2,1,0:T(8,128)S(1)} custom-call(f32[2,8,32,128]{3,2,1,0:T(8,128)S(1)} %get-tuple-element.66.own, f32[2,4,32,128]{3,2,1,0:T(8,128)S(1)} %collective-permute-done.12.near, f32[2,4,32,128]{3,2,1,0:T(8,128)S(1)} %collective-permute-done.13.swapped, f32[40,18,32,128]{3,2,1,0:T(8,128)S(1)} %copy-done.1), custom_call_target="tpu_custom_call" | custom-call | bytes 6291456 | tf_op jit(solution)/shard_map/pallas_call | solution.py:380
  114.1 0.0 collective-permute-done.15.refs_5_
  114.1 6.1 %collective-permute-done.16.refs_6_ = f32[2,8,32,128]{3,2,1,0:T(8,128)S(1)} collective-permute-done((f32[2,8,32,128]{3,2,1,0:T(8,128)S(1)}, f32[2,8,32,128]{3,2,1,0:T(8,128)S(1)}, u32[]{:S(2)}, u32[]{:S(2)}) %collective-permute-start.16) | collective-permute-done | bytes 262176 | tf_op jit(solution)/shard_map/ppermute | solution.py:317
  120.2 0.2 shard_map.62
  120.4 0.1 collective-permute-start.17
  120.5 0.3 collective-permute-start.18
  120.8 3.3 %collective-permute-done.17.near = f32[2,2,32,128]{3,2,1,0:T(8,128)S(1)} collective-permute-done((f32[2,2,32,128]{3,2,1,0:T(8,128)S(1)}, f32[2,2,32,128]{3,2,1,0:T(8,128)S(1)}, u32[]{:S(2)}, u32[]{:S(2)}) %collective-permute-start.17) | collective-permute-done | bytes 65568 | tf_op jit(solution)/shard_map/ppermute | solution.py:317
  124.2 0.0 collective-permute-done.18.swapped
  124.2 0.0 slice-done
  124.2 0.0 slice-done.1
  124.2 0.0 slice-done.2
  124.2 0.9 shard_map.63
  125.1 0.1 collective-permute-start.19
  125.2 1.5 %collective-permute-done.19 = f32[8,64,128]{2,1,0:T(8,128)S(1)} collective-permute-done((f32[8,64,128]{2,1,0:T(8,128)S(1)}, f32[8,64,128]{2,1,0:T(8,128)S(1)}, u32[]{:S(2)}, u32[]{:S(2)}) %collective-permute-start.19) | collective-permute-done | bytes 262176 | tf_op jit(solution)/shard_map/ppermute | solution.py:317
  126.7 13.1 %all_to_all.11.got = f32[8,128,128]{2,1,0:T(8,128)S(1)} all-to-all(f32[8,128,128]{2,1,0:T(8,128)S(1)} %pad_maximum_fusion), channel_id=1, replica_groups=mesh['chip'=8,'core'=2,'space'=8] {'space'}, dimensions={0} | all-to-all | bytes 1048576 | tf_op jit(solution)/shard_map/all_to_all | solution.py:406
  139.8 0.8 shard_map.64
  (4 shorter events, 0.1 us)
Async XLA Ops:
  33.3 2.7 %copy-start.2 = (f32[128,128]{1,0:T(8,128)S(1)}, f32[128,128]{1,0:T(8,128)}, u32[]{:S(2)}) copy-start(f32[128,128]{1,0:T(8,128)} %inlet.1) | copy-start | bytes 196612
  33.4 2.5 %collective-permute-start = (f32[3,18,32,128]{3,2,1,0:T(8,128)S(1)}, f32[3,18,32,128]{3,2,1,0:T(8,128)S(1)}, u32[]{:S(2)}, u32[]{:S(2)}) collective-permute-start(f32[3,18,32,128]{3,2,1,0:T(8,128)S(1)} %get-tuple-element.41.mine), channel_id=1, source_target_pairs={{8,0},{10,2},{12,4},{14,6},{15,7},{13,5},{11,3},{9,1},{0,8},{2,10}... | collective-permute-start | bytes 2654216 | tf_op jit(solution)/shard_map/ppermute | solution.py:317
  50.5 4.3 %copy-start = (f32[40,18,32,128]{3,2,1,0:T(8,128)}, f32[40,18,32,128]{3,2,1,0:T(8,128)S(1)}, u32[]{:S(2)}) copy-start(f32[40,18,32,128]{3,2,1,0:T(8,128)S(1)} %get-tuple-element.47.w) | copy-start | bytes 35389444
  54.9 1.9 %collective-permute-start.1 = (f32[4,8,32,128]{3,2,1,0:T(8,128)S(1)}, f32[4,8,32,128]{3,2,1,0:T(8,128)S(1)}, u32[]{:S(2)}, u32[]{:S(2)}) collective-permute-start(f32[4,8,32,128]{3,2,1,0:T(8,128)S(1)} %get-tuple-element.43), channel_id=1, source_target_pairs={{8,0},{10,2},{12,4},{14,6},{15,7},{13,5},{11,3},{9,1},{0,8},{2,10}... | collective-permute-start | bytes 1572872 | tf_op jit(solution)/shard_map/ppermute | solution.py:317
  56.8 9.9 %collective-permute-start.2 = (f32[2,8,32,128]{3,2,1,0:T(8,128)S(1)}, f32[2,8,32,128]{3,2,1,0:T(8,128)S(1)}, u32[]{:S(2)}, u32[]{:S(2)}) collective-permute-start(f32[2,8,32,128]{3,2,1,0:T(8,128)S(1)} %slice_add_fusion), channel_id=1, source_target_pairs={{64,0},{66,2},{68,4},{70,6},{71,7},{69,5},{67,3},{65,1},{72,8},{74... | collective-permute-start | bytes 786440 | tf_op jit(solution)/shard_map/ppermute | solution.py:317
  66.8 5.9 %collective-permute-start.3 = (f32[2,8,32,128]{3,2,1,0:T(8,128)S(1)}, f32[2,8,32,128]{3,2,1,0:T(8,128)S(1)}, u32[]{:S(2)}, u32[]{:S(2)}) collective-permute-start(f32[2,8,32,128]{3,2,1,0:T(8,128)S(1)} %get-tuple-element.44.own), channel_id=1, source_target_pairs={{8,2},{10,4},{12,6},{14,7},{15,5},{13,3},{11,1},{9,0},{0,9},{2,8},... | collective-permute-start | bytes 786440 | tf_op jit(solution)/shard_map/ppermute | solution.py:317
  66.9 5.8 %collective-permute-start.4 = (f32[2,8,32,128]{3,2,1,0:T(8,128)S(1)}, f32[2,8,32,128]{3,2,1,0:T(8,128)S(1)}, u32[]{:S(2)}, u32[]{:S(2)}) collective-permute-start(f32[2,8,32,128]{3,2,1,0:T(8,128)S(1)} %get-tuple-element.44.own), channel_id=1, source_target_pairs={{8,0},{10,2},{12,4},{14,6},{15,7},{13,5},{11,3},{9,1},{0,8},{2,10}... | collective-permute-start | bytes 786440 | tf_op jit(solution)/shard_map/ppermute | solution.py:317
  67.2 19.1 %collective-permute-start.7 = (f32[2,8,32,128]{3,2,1,0:T(8,128)S(1)}, f32[2,8,32,128]{3,2,1,0:T(8,128)S(1)}, u32[]{:S(2)}, u32[]{:S(2)}) collective-permute-start(f32[2,8,32,128]{3,2,1,0:T(8,128)S(1)} %get-tuple-element.44.own), channel_id=1, source_target_pairs={{0,16},{2,18},{4,20},{6,22},{7,23},{5,21},{3,19},{1,17},{8,24},{10... | collective-permute-start | bytes 786440 | tf_op jit(solution)/shard_map/ppermute | solution.py:317
  72.7 4.4 %copy-start.1 = (f32[40,18,32,128]{3,2,1,0:T(8,128)S(1)}, f32[40,18,32,128]{3,2,1,0:T(8,128)}, u32[]{:S(2)}) copy-start(f32[40,18,32,128]{3,2,1,0:T(8,128)} %copy-done) | copy-start | bytes 35389444
  81.8 5.9 %collective-permute-start.5 = (f32[2,8,32,128]{3,2,1,0:T(8,128)S(1)}, f32[2,8,32,128]{3,2,1,0:T(8,128)S(1)}, u32[]{:S(2)}, u32[]{:S(2)}) collective-permute-start(f32[2,8,32,128]{3,2,1,0:T(8,128)S(1)} %get-tuple-element.50.own), channel_id=1, source_target_pairs={{8,2},{10,4},{12,6},{14,7},{15,5},{13,3},{11,1},{9,0},{0,9},{2,8},... | collective-permute-start | bytes 786440 | tf_op jit(solution)/shard_map/ppermute | solution.py:317
  82.2 5.5 %collective-permute-start.6 = (f32[2,8,32,128]{3,2,1,0:T(8,128)S(1)}, f32[2,8,32,128]{3,2,1,0:T(8,128)S(1)}, u32[]{:S(2)}, u32[]{:S(2)}) collective-permute-start(f32[2,8,32,128]{3,2,1,0:T(8,128)S(1)} %get-tuple-element.50.own), channel_id=1, source_target_pairs={{8,0},{10,2},{12,4},{14,6},{15,7},{13,5},{11,3},{9,1},{0,8},{2,10}... | collective-permute-start | bytes 786440 | tf_op jit(solution)/shard_map/ppermute | solution.py:317
  82.3 15.8 %collective-permute-start.11 = (f32[2,8,32,128]{3,2,1,0:T(8,128)S(1)}, f32[2,8,32,128]{3,2,1,0:T(8,128)S(1)}, u32[]{:S(2)}, u32[]{:S(2)}) collective-permute-start(f32[2,8,32,128]{3,2,1,0:T(8,128)S(1)} %get-tuple-element.50.own), channel_id=1, source_target_pairs={{0,48},{2,50},{4,52},{6,54},{7,55},{5,53},{3,51},{1,49},{8,56},{10... | collective-permute-start | bytes 786440 | tf_op jit(solution)/shard_map/ppermute | solution.py:317
  86.3 9.9 %collective-permute-start.10 = (f32[2,8,32,128]{3,2,1,0:T(8,128)S(1)}, f32[2,8,32,128]{3,2,1,0:T(8,128)S(1)}, u32[]{:S(2)}, u32[]{:S(2)}) collective-permute-start(f32[2,8,32,128]{3,2,1,0:T(8,128)S(1)} %get-tuple-element.54), channel_id=1, source_target_pairs={{0,32},{2,34},{4,36},{6,38},{7,39},{5,37},{3,35},{1,33},{8,40},{10... | collective-permute-start | bytes 786440 | tf_op jit(solution)/shard_map/ppermute | solution.py:317
  92.5 5.9 %collective-permute-start.8 = (f32[2,8,32,128]{3,2,1,0:T(8,128)S(1)}, f32[2,8,32,128]{3,2,1,0:T(8,128)S(1)}, u32[]{:S(2)}, u32[]{:S(2)}) collective-permute-start(f32[2,8,32,128]{3,2,1,0:T(8,128)S(1)} %get-tuple-element.58.own), channel_id=1, source_target_pairs={{8,2},{10,4},{12,6},{14,7},{15,5},{13,3},{11,1},{9,0},{0,9},{2,8},... | collective-permute-start | bytes 786440 | tf_op jit(solution)/shard_map/ppermute | solution.py:317
  93.2 5.2 %collective-permute-start.9 = (f32[2,8,32,128]{3,2,1,0:T(8,128)S(1)}, f32[2,8,32,128]{3,2,1,0:T(8,128)S(1)}, u32[]{:S(2)}, u32[]{:S(2)}) collective-permute-start(f32[2,8,32,128]{3,2,1,0:T(8,128)S(1)} %get-tuple-element.58.own), channel_id=1, source_target_pairs={{8,0},{10,2},{12,4},{14,6},{15,7},{13,5},{11,3},{9,1},{0,8},{2,10}... | collective-permute-start | bytes 786440 | tf_op jit(solution)/shard_map/ppermute | solution.py:317
  93.2 15.3 %collective-permute-start.14 = (f32[2,8,32,128]{3,2,1,0:T(8,128)S(1)}, f32[2,8,32,128]{3,2,1,0:T(8,128)S(1)}, u32[]{:S(2)}, u32[]{:S(2)}) collective-permute-start(f32[2,8,32,128]{3,2,1,0:T(8,128)S(1)} %get-tuple-element.58.own), channel_id=1, source_target_pairs={{0,16},{2,18},{4,20},{6,22},{7,23},{5,21},{3,19},{1,17},{8,24},{10... | collective-permute-start | bytes 786440 | tf_op jit(solution)/shard_map/ppermute | solution.py:317
  98.4 25.8 %slice-start = ((s8[11796480]{0:T(1024)(128)(4,1)}), s8[4194304]{0:T(1024)(128)(4,1)S(1)}, s32[]{:S(2)}) async-start(s8[11796480]{0:T(1024)(128)(4,1)} %bitcast), calls=%async_computation.2 | async-start | bytes 8388608
  98.4 25.8 %slice-start.1 = ((s8[11796480]{0:T(1024)(128)(4,1)}), s8[4194304]{0:T(1024)(128)(4,1)S(1)}, s32[]{:S(2)}) async-start(s8[11796480]{0:T(1024)(128)(4,1)} %bitcast), calls=%async_computation.3 | async-start | bytes 8388608
  103.2 10.9 %collective-permute-start.15 = (f32[2,8,32,128]{3,2,1,0:T(8,128)S(1)}, f32[2,8,32,128]{3,2,1,0:T(8,128)S(1)}, u32[]{:S(2)}, u32[]{:S(2)}) collective-permute-start(f32[2,8,32,128]{3,2,1,0:T(8,128)S(1)} %get-tuple-element.65), channel_id=1, source_target_pairs={{0,32},{2,34},{4,36},{6,38},{7,39},{5,37},{3,35},{1,33},{8,40},{10... | collective-permute-start | bytes 786440 | tf_op jit(solution)/shard_map/ppermute | solution.py:317
  107.2 13.1 %collective-permute-start.16 = (f32[2,8,32,128]{3,2,1,0:T(8,128)S(1)}, f32[2,8,32,128]{3,2,1,0:T(8,128)S(1)}, u32[]{:S(2)}, u32[]{:S(2)}) collective-permute-start(f32[2,8,32,128]{3,2,1,0:T(8,128)S(1)} %get-tuple-element.66.own), channel_id=1, source_target_pairs={{0,48},{2,50},{4,52},{6,54},{7,55},{5,53},{3,51},{1,49},{8,56},{10... | collective-permute-start | bytes 786440 | tf_op jit(solution)/shard_map/ppermute | solution.py:317
  107.9 4.4 %collective-permute-start.12 = (f32[2,4,32,128]{3,2,1,0:T(8,128)S(1)}, f32[2,4,32,128]{3,2,1,0:T(8,128)S(1)}, u32[]{:S(2)}, u32[]{:S(2)}) collective-permute-start(f32[2,4,32,128]{3,2,1,0:T(8,128)S(1)} %get-tuple-element.62), channel_id=1, source_target_pairs={{8,2},{10,4},{12,6},{14,7},{15,5},{13,3},{11,1},{9,0},{0,9},{2,8},... | collective-permute-start | bytes 393224 | tf_op jit(solution)/shard_map/ppermute | solution.py:317
  108.2 15.9 %slice-start.2 = ((s8[11796480]{0:T(1024)(128)(4,1)}), s8[3407872]{0:T(1024)(128)(4,1)S(1)}, s32[]{:S(2)}) async-start(s8[11796480]{0:T(1024)(128)(4,1)} %bitcast), calls=%async_computation.4 | async-start | bytes 6815744
  108.2 4.0 %collective-permute-start.13 = (f32[2,4,32,128]{3,2,1,0:T(8,128)S(1)}, f32[2,4,32,128]{3,2,1,0:T(8,128)S(1)}, u32[]{:S(2)}, u32[]{:S(2)}) collective-permute-start(f32[2,4,32,128]{3,2,1,0:T(8,128)S(1)} %get-tuple-element.63), channel_id=1, source_target_pairs={{8,0},{10,2},{12,4},{14,6},{15,7},{13,5},{11,3},{9,1},{0,8},{2,10}... | collective-permute-start | bytes 393224 | tf_op jit(solution)/shard_map/ppermute | solution.py:317
  120.4 3.8 %collective-permute-start.17 = (f32[2,2,32,128]{3,2,1,0:T(8,128)S(1)}, f32[2,2,32,128]{3,2,1,0:T(8,128)S(1)}, u32[]{:S(2)}, u32[]{:S(2)}) collective-permute-start(f32[2,2,32,128]{3,2,1,0:T(8,128)S(1)} %get-tuple-element.70), channel_id=1, source_target_pairs={{8,2},{10,4},{12,6},{14,7},{15,5},{13,3},{11,1},{9,0},{0,9},{2,8},... | collective-permute-start | bytes 196616 | tf_op jit(solution)/shard_map/ppermute | solution.py:317
  120.5 3.7 %collective-permute-start.18 = (f32[2,2,32,128]{3,2,1,0:T(8,128)S(1)}, f32[2,2,32,128]{3,2,1,0:T(8,128)S(1)}, u32[]{:S(2)}, u32[]{:S(2)}) collective-permute-start(f32[2,2,32,128]{3,2,1,0:T(8,128)S(1)} %get-tuple-element.71), channel_id=1, source_target_pairs={{8,0},{10,2},{12,4},{14,6},{15,7},{13,5},{11,3},{9,1},{0,8},{2,10}... | collective-permute-start | bytes 196616 | tf_op jit(solution)/shard_map/ppermute | solution.py:317
  125.1 1.6 %collective-permute-start.19 = (f32[8,64,128]{2,1,0:T(8,128)S(1)}, f32[8,64,128]{2,1,0:T(8,128)S(1)}, u32[]{:S(2)}, u32[]{:S(2)}) collective-permute-start(f32[8,64,128]{2,1,0:T(8,128)S(1)} %get-tuple-element.74), channel_id=1, source_target_pairs={{8,0},{10,2},{12,4},{14,6},{15,7},{13,5},{11,3},{9,1},{0,8},{2,10}... | collective-permute-start | bytes 786440 | tf_op jit(solution)/shard_map/ppermute | solution.py:317

commit v9 on v8

--- a/solution.py
+++ b/solution.py
@@ -267,6 +267,14 @@
             outer[...] = even[:, pl.ds(4 * core, 4)]
 
 
+def choose_kernel(ours, across, low, high):
+    _, _, slab = position()
+    chip = slab // 2
+    stays = (chip < RING - 1) | (chip == CHIPS - 1)
+    low[...] = jnp.where(stays, ours[...], across[...])
+    high[...] = jnp.where(stays, across[...], ours[...])
+
+
 def share_kernel(*refs):
     *arrived, out, inner, outer = refs
     core, _, slab = position()
@@ -379,11 +387,7 @@
         body = functools.partial(leap_kernel, high is not None)
         return call(body, outs, [VMEM] * len(operands), (VMEM,) * len(outs), [field, field], 20, 2 + 3 * second)(*operands)
 
-    chip = lax.axis_index("chip")
-    across = sent(u, ACROSS, 0, 0)
-    stays = (chip < RING - 1) | (chip == CHIPS - 1)
-    low, high = jnp.where(stays, u, across), jnp.where(stays, across, u)
-
+    low, high = call(choose_kernel, (half, half), [VMEM] * 2, (VMEM,) * 2, [], 8)(u, sent(u, ACROSS, 0, 0))
     rim4, rim2 = shape(2, 4, NX, LAST), shape(2, 2, NX, LAST)
     a0 = along(low, 0)
     u1, u2 = leap(*exchanged(low, low, low))

time: 141 us -> 134 us (0.950)
  local copies, waits for them, and re-layouts: 8.69 us -> 0.01 us
    unnamed x12 -> x2, local copies, waits for them, and re-layouts: 8.69 us -> 0.01 us
where the time goes in v9:
time: 134 us; the launch traced here: 133 us
  blocking collectives  44.9 us (34%)
  waiting for transfers between devices  36.9 us (28%)
  Pallas kernels  34.4 us (26%)
  starting transfers between devices  17.1 us (13%)
    ppermute x20, waiting for transfers between devices, sent(): return lax.ppermute(value, AXES, pairs)  36.9 us
    all_to_all x1, blocking collectives, shards(): got = lax.all_to_all(packed, 'space', 0, 0, tiled=True)  31.8 us
    ppermute x20, starting transfers between devices, sent(): return lax.ppermute(value, AXES, pairs)  17.1 us
    pallas_call x4, Pallas kernels, leap(): call(body, outs, [VMEM] * len(operands), (VMEM,) * len(outs), [field, fie...  16.2 us
    pallas_call x1, Pallas kernels, shards(): call(relax_kernel, (pltpu.VMEM((HELD, 2 * PAIR, NX, LAST), F32), half, sh...  14.6 us
    all_to_all x1, blocking collectives, shards(): lax.all_to_all(jnp.concatenate([keep, swap(send)], axis=1), 'space', 0, 0...  13.1 us
  transfers between devices with their start and end apart: 20, of which 12 were waited for; matrix products, arithmetic and copies ran while one was open for 0% of the time, Pallas kernels for 12%

profile of v9, /device:TPU:4, one launch (start us, length us, event | category | flops | bytes accessed | tf_op | source)
XLA Modules:
  0.0 133.4 jit_solution(13460934266636361954)
XLA Ops:
  0.0 1.5 %shard_map.55 = f32[8,504,128]{2,1,0:T(8,128)S(1)} custom-call(f32[2,4,128,128]{3,2,1,0:T(8,128)} %startup.1, f32[1,2,4,128,128]{4,3,2,1,0:T(8,128)} %guess.1, f32[2,4,128,128]{3,2,1,0:T(8,128)} %conduct.1, f32[4,128,128]{2,1,0:T(8,128)} %couple.1), custom_call_target="tpu_custom_call" | custom-call | bytes 3145728 | tf_op jit(solution)/shard_map/pallas_call | solution.py:353
  1.5 31.8 %all_to_all.10.got = f32[8,504,128]{2,1,0:T(8,128)S(1)} all-to-all(f32[8,504,128]{2,1,0:T(8,128)S(1)} %shard_map.55), channel_id=1, replica_groups=mesh['chip'=8,'core'=2,'space'=8] {'space'}, dimensions={0} | all-to-all | bytes 4128768 | tf_op jit(solution)/shard_map/all_to_all | solution.py:366
  33.3 0.0 copy-start
  33.3 0.1 shard_map.56
  33.4 0.1 collective-permute-start
  33.5 2.4 %collective-permute-done.other = f32[3,18,32,128]{3,2,1,0:T(8,128)S(1)} collective-permute-done((f32[3,18,32,128]{3,2,1,0:T(8,128)S(1)}, f32[3,18,32,128]{3,2,1,0:T(8,128)S(1)}, u32[]{:S(2)}, u32[]{:S(2)}) %collective-permute-start) | collective-permute-done | bytes 884768 | tf_op jit(solution)/shard_map/ppermute | solution.py:325
  35.9 0.0 copy-done
  35.9 14.6 %shard_map.57 = (f32[40,18,32,128]{3,2,1,0:T(8,128)S(1)}, f32[2,8,32,128]{3,2,1,0:T(8,128)S(1)}, f32[4,8,32,128]{3,2,1,0:T(8,128)S(1)}, f32[2,8,32,128]{3,2,1,0:T(8,128)S(1)}) custom-call(f32[2,36,32,128]{3,2,1,0:T(8,128)S(1)} %get-tuple-element.42.begin, f32[3,18,32,128]{3,2,1,0:T(8,128)S(1)} %get-tuple-element.43.mine, ...), custom_call_target="tpu_custom_call" | custom-call | bytes 3145728 | tf_op jit(solution)/shard_map/pallas_call | solution.py:373
  50.5 0.2 collective-permute-start.1
  50.7 1.8 %collective-permute-done.1.taken = f32[4,8,32,128]{3,2,1,0:T(8,128)S(1)} collective-permute-done((f32[4,8,32,128]{3,2,1,0:T(8,128)S(1)}, f32[4,8,32,128]{3,2,1,0:T(8,128)S(1)}, u32[]{:S(2)}, u32[]{:S(2)}) %collective-permute-start.1) | collective-permute-done | bytes 524320 | tf_op jit(solution)/shard_map/ppermute | solution.py:325
  52.5 0.9 collective-permute-start.2
  53.4 9.1 %collective-permute-done.2.across = f32[2,8,32,128]{3,2,1,0:T(8,128)S(1)} collective-permute-done((f32[2,8,32,128]{3,2,1,0:T(8,128)S(1)}, f32[2,8,32,128]{3,2,1,0:T(8,128)S(1)}, u32[]{:S(2)}, u32[]{:S(2)}) %collective-permute-start.2) | collective-permute-done | bytes 262176 | tf_op jit(solution)/shard_map/ppermute | solution.py:325
  62.5 0.1 shard_map.58
  62.5 0.1 collective-permute-start.4
  62.6 0.7 collective-permute-start.3
  63.3 1.9 %collective-permute-start.7 = (f32[2,8,32,128]{3,2,1,0:T(8,128)S(1)}, f32[2,8,32,128]{3,2,1,0:T(8,128)S(1)}, u32[]{:S(2)}, u32[]{:S(2)}) collective-permute-start(f32[2,8,32,128]{3,2,1,0:T(8,128)S(1)} %get-tuple-element.47.own), channel_id=1, source_target_pairs={{0,16},{2,18},{4,20},{6,22},{7,23},{5,21},{3,19},{1,17},{8,24},{10... | collective-permute-start | bytes 786440 | tf_op jit(solution)/shard_map/ppermute | solution.py:325
  65.2 0.0 collective-permute-done.4.swapped
  65.2 3.3 %collective-permute-done.3.near = f32[2,8,32,128]{3,2,1,0:T(8,128)S(1)} collective-permute-done((f32[2,8,32,128]{3,2,1,0:T(8,128)S(1)}, f32[2,8,32,128]{3,2,1,0:T(8,128)S(1)}, u32[]{:S(2)}, u32[]{:S(2)}) %collective-permute-start.3) | collective-permute-done | bytes 262176 | tf_op jit(solution)/shard_map/ppermute | solution.py:325
  68.5 4.8 %shard_map.59 = (f32[2,8,32,128]{3,2,1,0:T(8,128)S(1)}, f32[2,8,32,128]{3,2,1,0:T(8,128)S(1)}) custom-call(f32[2,8,32,128]{3,2,1,0:T(8,128)S(1)} %get-tuple-element.47.own, f32[2,8,32,128]{3,2,1,0:T(8,128)S(1)} %collective-permute-done.3.near, f32[2,8,32,128]{3,2,1,0:T(8,128)S(1)} %collective-permute-done.4.swapped, f32[40,18,32,128]{3,2,1,0:T(8,128)S(1)} %get-tuple-element.50.w), custom_call_target="tpu_custom_call" | custom-call | bytes 15728640 | tf_op jit(solution)/shard_map/pallas_call | solution.py:388
  73.3 0.8 collective-permute-start.6
  74.1 0.2 collective-permute-start.5
  74.4 4.0 %collective-permute-start.11 = (f32[2,8,32,128]{3,2,1,0:T(8,128)S(1)}, f32[2,8,32,128]{3,2,1,0:T(8,128)S(1)}, u32[]{:S(2)}, u32[]{:S(2)}) collective-permute-start(f32[2,8,32,128]{3,2,1,0:T(8,128)S(1)} %get-tuple-element.53.own), channel_id=1, source_target_pairs={{0,48},{2,50},{4,52},{6,54},{7,55},{5,53},{3,51},{1,49},{8,56},{10... | collective-permute-start | bytes 786440 | tf_op jit(solution)/shard_map/ppermute | solution.py:325
  78.4 0.0 collective-permute-start.10
  78.4 0.0 collective-permute-done.7.refs_0_
  78.4 0.0 collective-permute-done.6.swapped
  78.4 1.5 %collective-permute-done.5.near = f32[2,8,32,128]{3,2,1,0:T(8,128)S(1)} collective-permute-done((f32[2,8,32,128]{3,2,1,0:T(8,128)S(1)}, f32[2,8,32,128]{3,2,1,0:T(8,128)S(1)}, u32[]{:S(2)}, u32[]{:S(2)}) %collective-permute-start.5) | collective-permute-done | bytes 262176 | tf_op jit(solution)/shard_map/ppermute | solution.py:325
  79.9 4.8 %shard_map.60 = (f32[2,8,32,128]{3,2,1,0:T(8,128)S(1)}, f32[2,8,32,128]{3,2,1,0:T(8,128)S(1)}) custom-call(f32[2,8,32,128]{3,2,1,0:T(8,128)S(1)} %get-tuple-element.53.own, f32[2,8,32,128]{3,2,1,0:T(8,128)S(1)} %collective-permute-done.5.near, f32[2,8,32,128]{3,2,1,0:T(8,128)S(1)} %collective-permute-done.6.swapped, ...), custom_call_target="tpu_custom_call" | custom-call | bytes 15728640 | tf_op jit(solution)/shard_map/pallas_call | solution.py:388
  84.7 0.5 collective-permute-start.9
  85.2 0.3 collective-permute-start.8
  85.5 1.9 %collective-permute-start.14 = (f32[2,8,32,128]{3,2,1,0:T(8,128)S(1)}, f32[2,8,32,128]{3,2,1,0:T(8,128)S(1)}, u32[]{:S(2)}, u32[]{:S(2)}) collective-permute-start(f32[2,8,32,128]{3,2,1,0:T(8,128)S(1)} %get-tuple-element.62.own), channel_id=1, source_target_pairs={{0,16},{2,18},{4,20},{6,22},{7,23},{5,21},{3,19},{1,17},{8,24},{10... | collective-permute-start | bytes 786440 | tf_op jit(solution)/shard_map/ppermute | solution.py:325
  87.4 0.6 collective-permute-done.10.refs_1_
  87.9 1.9 %collective-permute-done.11.refs_2_ = f32[2,8,32,128]{3,2,1,0:T(8,128)S(1)} collective-permute-done((f32[2,8,32,128]{3,2,1,0:T(8,128)S(1)}, f32[2,8,32,128]{3,2,1,0:T(8,128)S(1)}, u32[]{:S(2)}, u32[]{:S(2)}) %collective-permute-start.11) | collective-permute-done | bytes 262176 | tf_op jit(solution)/shard_map/ppermute | solution.py:325
  89.9 0.0 collective-permute-done.9.swapped
  89.9 1.1 collective-permute-done.8.near
  91.0 4.8 %shard_map.61 = (f32[2,8,32,128]{3,2,1,0:T(8,128)S(1)}, f32[2,8,32,128]{3,2,1,0:T(8,128)S(1)}, f32[2,4,32,128]{3,2,1,0:T(8,128)S(1)}, f32[2,4,32,128]{3,2,1,0:T(8,128)S(1)}) custom-call(f32[2,8,32,128]{3,2,1,0:T(8,128)S(1)} %get-tuple-element.62.own, f32[2,8,32,128]{3,2,1,0:T(8,128)S(1)} %collective-permute-done.8.near, ...), custom_call_target="tpu_custom_call" | custom-call | bytes 15728640 | tf_op jit(solution)/shard_map/pallas_call | solution.py:388
  95.8 4.0 %collective-permute-start.15 = (f32[2,8,32,128]{3,2,1,0:T(8,128)S(1)}, f32[2,8,32,128]{3,2,1,0:T(8,128)S(1)}, u32[]{:S(2)}, u32[]{:S(2)}) collective-permute-start(f32[2,8,32,128]{3,2,1,0:T(8,128)S(1)} %get-tuple-element.69), channel_id=1, source_target_pairs={{0,32},{2,34},{4,36},{6,38},{7,39},{5,37},{3,35},{1,33},{8,40},{10... | collective-permute-start | bytes 786440 | tf_op jit(solution)/shard_map/ppermute | solution.py:325
  99.8 0.7 collective-permute-start.16
  100.5 0.0 collective-permute-start.12
  100.5 0.3 collective-permute-start.13
  100.8 0.0 collective-permute-done.14.refs_4_
  100.8 4.0 %collective-permute-done.12.near = f32[2,4,32,128]{3,2,1,0:T(8,128)S(1)} collective-permute-done((f32[2,4,32,128]{3,2,1,0:T(8,128)S(1)}, f32[2,4,32,128]{3,2,1,0:T(8,128)S(1)}, u32[]{:S(2)}, u32[]{:S(2)}) %collective-permute-start.12) | collective-permute-done | bytes 131104 | tf_op jit(solution)/shard_map/ppermute | solution.py:325
  104.9 0.0 collective-permute-done.13.swapped
  104.9 1.8 %shard_map.62.refs_7_ = f32[2,8,32,128]{3,2,1,0:T(8,128)S(1)} custom-call(f32[2,8,32,128]{3,2,1,0:T(8,128)S(1)} %get-tuple-element.70.own, f32[2,4,32,128]{3,2,1,0:T(8,128)S(1)} %collective-permute-done.12.near, f32[2,4,32,128]{3,2,1,0:T(8,128)S(1)} %collective-permute-done.13.swapped, f32[40,18,32,128]{3,2,1,0:T(8,128)S(1)} %get-tuple-element.50.w), custom_call_target="tpu_custom_call" | custom-call | bytes 6291456 | tf_op jit(solution)/shard_map/pallas_call | solution.py:388
  106.7 0.0 collective-permute-done.15.refs_5_
  106.7 6.3 %collective-permute-done.16.refs_6_ = f32[2,8,32,128]{3,2,1,0:T(8,128)S(1)} collective-permute-done((f32[2,8,32,128]{3,2,1,0:T(8,128)S(1)}, f32[2,8,32,128]{3,2,1,0:T(8,128)S(1)}, u32[]{:S(2)}, u32[]{:S(2)}) %collective-permute-start.16) | collective-permute-done | bytes 262176 | tf_op jit(solution)/shard_map/ppermute | solution.py:325
  113.1 0.2 shard_map.63
  113.2 0.1 collective-permute-start.17
  113.3 0.3 collective-permute-start.18
  113.7 3.3 %collective-permute-done.17.near = f32[2,2,32,128]{3,2,1,0:T(8,128)S(1)} collective-permute-done((f32[2,2,32,128]{3,2,1,0:T(8,128)S(1)}, f32[2,2,32,128]{3,2,1,0:T(8,128)S(1)}, u32[]{:S(2)}, u32[]{:S(2)}) %collective-permute-start.17) | collective-permute-done | bytes 65568 | tf_op jit(solution)/shard_map/ppermute | solution.py:325
  117.0 0.0 collective-permute-done.18.swapped
  117.0 0.9 shard_map.64
  117.9 0.1 collective-permute-start.19
  118.0 1.5 %collective-permute-done.19 = f32[8,64,128]{2,1,0:T(8,128)S(1)} collective-permute-done((f32[8,64,128]{2,1,0:T(8,128)S(1)}, f32[8,64,128]{2,1,0:T(8,128)S(1)}, u32[]{:S(2)}, u32[]{:S(2)}) %collective-permute-start.19) | collective-permute-done | bytes 262176 | tf_op jit(solution)/shard_map/ppermute | solution.py:325
  119.5 13.1 %all_to_all.11.got = f32[8,128,128]{2,1,0:T(8,128)S(1)} all-to-all(f32[8,128,128]{2,1,0:T(8,128)S(1)} %pad_maximum_fusion), channel_id=1, replica_groups=mesh['chip'=8,'core'=2,'space'=8] {'space'}, dimensions={0} | all-to-all | bytes 1048576 | tf_op jit(solution)/shard_map/all_to_all | solution.py:410
  132.6 0.8 shard_map.65
  (2 shorter events, 0.1 us)
Async XLA Ops:
  33.3 2.7 %copy-start = (f32[128,128]{1,0:T(8,128)S(1)}, f32[128,128]{1,0:T(8,128)}, u32[]{:S(2)}) copy-start(f32[128,128]{1,0:T(8,128)} %inlet.1) | copy-start | bytes 196612
  33.4 2.5 %collective-permute-start = (f32[3,18,32,128]{3,2,1,0:T(8,128)S(1)}, f32[3,18,32,128]{3,2,1,0:T(8,128)S(1)}, u32[]{:S(2)}, u32[]{:S(2)}) collective-permute-start(f32[3,18,32,128]{3,2,1,0:T(8,128)S(1)} %get-tuple-element.43.mine), channel_id=1, source_target_pairs={{8,0},{10,2},{12,4},{14,6},{15,7},{13,5},{11,3},{9,1},{0,8},{2,10}... | collective-permute-start | bytes 2654216 | tf_op jit(solution)/shard_map/ppermute | solution.py:325
  50.5 2.0 %collective-permute-start.1 = (f32[4,8,32,128]{3,2,1,0:T(8,128)S(1)}, f32[4,8,32,128]{3,2,1,0:T(8,128)S(1)}, u32[]{:S(2)}, u32[]{:S(2)}) collective-permute-start(f32[4,8,32,128]{3,2,1,0:T(8,128)S(1)} %get-tuple-element.45), channel_id=1, source_target_pairs={{8,0},{10,2},{12,4},{14,6},{15,7},{13,5},{11,3},{9,1},{0,8},{2,10}... | collective-permute-start | bytes 1572872 | tf_op jit(solution)/shard_map/ppermute | solution.py:325
  52.5 9.9 %collective-permute-start.2 = (f32[2,8,32,128]{3,2,1,0:T(8,128)S(1)}, f32[2,8,32,128]{3,2,1,0:T(8,128)S(1)}, u32[]{:S(2)}, u32[]{:S(2)}) collective-permute-start(f32[2,8,32,128]{3,2,1,0:T(8,128)S(1)} %slice_add_fusion.ours), channel_id=1, source_target_pairs={{64,0},{66,2},{68,4},{70,6},{71,7},{69,5},{67,3},{65,1},{72,8},{74... | collective-permute-start | bytes 786440 | tf_op jit(solution)/shard_map/ppermute | solution.py:325
  62.5 2.7 %collective-permute-start.4 = (f32[2,8,32,128]{3,2,1,0:T(8,128)S(1)}, f32[2,8,32,128]{3,2,1,0:T(8,128)S(1)}, u32[]{:S(2)}, u32[]{:S(2)}) collective-permute-start(f32[2,8,32,128]{3,2,1,0:T(8,128)S(1)} %get-tuple-element.47.own), channel_id=1, source_target_pairs={{8,0},{10,2},{12,4},{14,6},{15,7},{13,5},{11,3},{9,1},{0,8},{2,10}... | collective-permute-start | bytes 786440 | tf_op jit(solution)/shard_map/ppermute | solution.py:325
  62.6 5.9 %collective-permute-start.3 = (f32[2,8,32,128]{3,2,1,0:T(8,128)S(1)}, f32[2,8,32,128]{3,2,1,0:T(8,128)S(1)}, u32[]{:S(2)}, u32[]{:S(2)}) collective-permute-start(f32[2,8,32,128]{3,2,1,0:T(8,128)S(1)} %get-tuple-element.47.own), channel_id=1, source_target_pairs={{8,2},{10,4},{12,6},{14,7},{15,5},{13,3},{11,1},{9,0},{0,9},{2,8},... | collective-permute-start | bytes 786440 | tf_op jit(solution)/shard_map/ppermute | solution.py:325
  63.3 15.1 %collective-permute-start.7 = (f32[2,8,32,128]{3,2,1,0:T(8,128)S(1)}, f32[2,8,32,128]{3,2,1,0:T(8,128)S(1)}, u32[]{:S(2)}, u32[]{:S(2)}) collective-permute-start(f32[2,8,32,128]{3,2,1,0:T(8,128)S(1)} %get-tuple-element.47.own), channel_id=1, source_target_pairs={{0,16},{2,18},{4,20},{6,22},{7,23},{5,21},{3,19},{1,17},{8,24},{10... | collective-permute-start | bytes 786440 | tf_op jit(solution)/shard_map/ppermute | solution.py:325
  73.3 5.1 %collective-permute-start.6 = (f32[2,8,32,128]{3,2,1,0:T(8,128)S(1)}, f32[2,8,32,128]{3,2,1,0:T(8,128)S(1)}, u32[]{:S(2)}, u32[]{:S(2)}) collective-permute-start(f32[2,8,32,128]{3,2,1,0:T(8,128)S(1)} %get-tuple-element.53.own), channel_id=1, source_target_pairs={{8,0},{10,2},{12,4},{14,6},{15,7},{13,5},{11,3},{9,1},{0,8},{2,10}... | collective-permute-start | bytes 786440 | tf_op jit(solution)/shard_map/ppermute | solution.py:325
  74.1 5.8 %collective-permute-start.5 = (f32[2,8,32,128]{3,2,1,0:T(8,128)S(1)}, f32[2,8,32,128]{3,2,1,0:T(8,128)S(1)}, u32[]{:S(2)}, u32[]{:S(2)}) collective-permute-start(f32[2,8,32,128]{3,2,1,0:T(8,128)S(1)} %get-tuple-element.53.own), channel_id=1, source_target_pairs={{8,2},{10,4},{12,6},{14,7},{15,5},{13,3},{11,1},{9,0},{0,9},{2,8},... | collective-permute-start | bytes 786440 | tf_op jit(solution)/shard_map/ppermute | solution.py:325
  74.4 15.5 %collective-permute-start.11 = (f32[2,8,32,128]{3,2,1,0:T(8,128)S(1)}, f32[2,8,32,128]{3,2,1,0:T(8,128)S(1)}, u32[]{:S(2)}, u32[]{:S(2)}) collective-permute-start(f32[2,8,32,128]{3,2,1,0:T(8,128)S(1)} %get-tuple-element.53.own), channel_id=1, source_target_pairs={{0,48},{2,50},{4,52},{6,54},{7,55},{5,53},{3,51},{1,49},{8,56},{10... | collective-permute-start | bytes 786440 | tf_op jit(solution)/shard_map/ppermute | solution.py:325
  78.4 9.5 %collective-permute-start.10 = (f32[2,8,32,128]{3,2,1,0:T(8,128)S(1)}, f32[2,8,32,128]{3,2,1,0:T(8,128)S(1)}, u32[]{:S(2)}, u32[]{:S(2)}) collective-permute-start(f32[2,8,32,128]{3,2,1,0:T(8,128)S(1)} %get-tuple-element.58), channel_id=1, source_target_pairs={{0,32},{2,34},{4,36},{6,38},{7,39},{5,37},{3,35},{1,33},{8,40},{10... | collective-permute-start | bytes 786440 | tf_op jit(solution)/shard_map/ppermute | solution.py:325
  84.7 5.1 %collective-permute-start.9 = (f32[2,8,32,128]{3,2,1,0:T(8,128)S(1)}, f32[2,8,32,128]{3,2,1,0:T(8,128)S(1)}, u32[]{:S(2)}, u32[]{:S(2)}) collective-permute-start(f32[2,8,32,128]{3,2,1,0:T(8,128)S(1)} %get-tuple-element.62.own), channel_id=1, source_target_pairs={{8,0},{10,2},{12,4},{14,6},{15,7},{13,5},{11,3},{9,1},{0,8},{2,10}... | collective-permute-start | bytes 786440 | tf_op jit(solution)/shard_map/ppermute | solution.py:325
  85.2 5.8 %collective-permute-start.8 = (f32[2,8,32,128]{3,2,1,0:T(8,128)S(1)}, f32[2,8,32,128]{3,2,1,0:T(8,128)S(1)}, u32[]{:S(2)}, u32[]{:S(2)}) collective-permute-start(f32[2,8,32,128]{3,2,1,0:T(8,128)S(1)} %get-tuple-element.62.own), channel_id=1, source_target_pairs={{8,2},{10,4},{12,6},{14,7},{15,5},{13,3},{11,1},{9,0},{0,9},{2,8},... | collective-permute-start | bytes 786440 | tf_op jit(solution)/shard_map/ppermute | solution.py:325
  85.5 15.4 %collective-permute-start.14 = (f32[2,8,32,128]{3,2,1,0:T(8,128)S(1)}, f32[2,8,32,128]{3,2,1,0:T(8,128)S(1)}, u32[]{:S(2)}, u32[]{:S(2)}) collective-permute-start(f32[2,8,32,128]{3,2,1,0:T(8,128)S(1)} %get-tuple-element.62.own), channel_id=1, source_target_pairs={{0,16},{2,18},{4,20},{6,22},{7,23},{5,21},{3,19},{1,17},{8,24},{10... | collective-permute-start | bytes 786440 | tf_op jit(solution)/shard_map/ppermute | solution.py:325
  95.8 10.9 %collective-permute-start.15 = (f32[2,8,32,128]{3,2,1,0:T(8,128)S(1)}, f32[2,8,32,128]{3,2,1,0:T(8,128)S(1)}, u32[]{:S(2)}, u32[]{:S(2)}) collective-permute-start(f32[2,8,32,128]{3,2,1,0:T(8,128)S(1)} %get-tuple-element.69), channel_id=1, source_target_pairs={{0,32},{2,34},{4,36},{6,38},{7,39},{5,37},{3,35},{1,33},{8,40},{10... | collective-permute-start | bytes 786440 | tf_op jit(solution)/shard_map/ppermute | solution.py:325
  99.8 13.3 %collective-permute-start.16 = (f32[2,8,32,128]{3,2,1,0:T(8,128)S(1)}, f32[2,8,32,128]{3,2,1,0:T(8,128)S(1)}, u32[]{:S(2)}, u32[]{:S(2)}) collective-permute-start(f32[2,8,32,128]{3,2,1,0:T(8,128)S(1)} %get-tuple-element.70.own), channel_id=1, source_target_pairs={{0,48},{2,50},{4,52},{6,54},{7,55},{5,53},{3,51},{1,49},{8,56},{10... | collective-permute-start | bytes 786440 | tf_op jit(solution)/shard_map/ppermute | solution.py:325
  100.5 4.4 %collective-permute-start.12 = (f32[2,4,32,128]{3,2,1,0:T(8,128)S(1)}, f32[2,4,32,128]{3,2,1,0:T(8,128)S(1)}, u32[]{:S(2)}, u32[]{:S(2)}) collective-permute-start(f32[2,4,32,128]{3,2,1,0:T(8,128)S(1)} %get-tuple-element.66), channel_id=1, source_target_pairs={{8,2},{10,4},{12,6},{14,7},{15,5},{13,3},{11,1},{9,0},{0,9},{2,8},... | collective-permute-start | bytes 393224 | tf_op jit(solution)/shard_map/ppermute | solution.py:325
  100.5 4.4 %collective-permute-start.13 = (f32[2,4,32,128]{3,2,1,0:T(8,128)S(1)}, f32[2,4,32,128]{3,2,1,0:T(8,128)S(1)}, u32[]{:S(2)}, u32[]{:S(2)}) collective-permute-start(f32[2,4,32,128]{3,2,1,0:T(8,128)S(1)} %get-tuple-element.67), channel_id=1, source_target_pairs={{8,0},{10,2},{12,4},{14,6},{15,7},{13,5},{11,3},{9,1},{0,8},{2,10}... | collective-permute-start | bytes 393224 | tf_op jit(solution)/shard_map/ppermute | solution.py:325
  113.2 3.8 %collective-permute-start.17 = (f32[2,2,32,128]{3,2,1,0:T(8,128)S(1)}, f32[2,2,32,128]{3,2,1,0:T(8,128)S(1)}, u32[]{:S(2)}, u32[]{:S(2)}) collective-permute-start(f32[2,2,32,128]{3,2,1,0:T(8,128)S(1)} %get-tuple-element.74), channel_id=1, source_target_pairs={{8,2},{10,4},{12,6},{14,7},{15,5},{13,3},{11,1},{9,0},{0,9},{2,8},... | collective-permute-start | bytes 196616 | tf_op jit(solution)/shard_map/ppermute | solution.py:325
  113.3 3.7 %collective-permute-start.18 = (f32[2,2,32,128]{3,2,1,0:T(8,128)S(1)}, f32[2,2,32,128]{3,2,1,0:T(8,128)S(1)}, u32[]{:S(2)}, u32[]{:S(2)}) collective-permute-start(f32[2,2,32,128]{3,2,1,0:T(8,128)S(1)} %get-tuple-element.75), channel_id=1, source_target_pairs={{8,0},{10,2},{12,4},{14,6},{15,7},{13,5},{11,3},{9,1},{0,8},{2,10}... | collective-permute-start | bytes 196616 | tf_op jit(solution)/shard_map/ppermute | solution.py:325
  117.9 1.6 %collective-permute-start.19 = (f32[8,64,128]{2,1,0:T(8,128)S(1)}, f32[8,64,128]{2,1,0:T(8,128)S(1)}, u32[]{:S(2)}, u32[]{:S(2)}) collective-permute-start(f32[8,64,128]{2,1,0:T(8,128)S(1)} %get-tuple-element.78), channel_id=1, source_target_pairs={{8,0},{10,2},{12,4},{14,6},{15,7},{13,5},{11,3},{9,1},{0,8},{2,10}... | collective-permute-start | bytes 786440 | tf_op jit(solution)/shard_map/ppermute | solution.py:325

commit v10 on v9

--- a/solution.py
+++ b/solution.py
@@ -19,7 +19,7 @@
 HALF = 8
 EDGE = 10
 ROWS = STRIP + 2 * EDGE
-HELD = ROWS + 4
+LONGEST = 12
 PART = ROWS // 2
 
 RATE_ALONG = 4.0
@@ -133,44 +133,50 @@
                     out[0, i, plane, pl.ds(first, HALF), :] = got[ORDER[b], pl.ds(at, HALF, stride=PLANES), :]
 
 
-def row_sweep(y, state, weights, earlier, step, source):
-    centre = (state[0, y], state[1, y])
-    out = []
-    for i in range(2):
-        v = centre[i]
-        w = lambda k: weights[y, PAIR * i + k]
-        along = w(0) * pltpu.roll(v, 1, 0) + w(1) * pltpu.roll(v, NX - 1, 0)
-        middle = w(2) * state[i, y - 1] + w(3) * state[i, y + 1]
-        across = w(4) * pltpu.roll(v, 1, 1) + w(5) * pltpu.roll(v, LAST - 1, 1)
-        begin = v if earlier is None else earlier[i, y]
-        if step == COARSE:
-            begin = (1.0 / COARSE_FACTOR) * begin
-        gain = (along + middle) + (across + (w(6) * centre[1 - i] + begin))
-        if i == 1 and source is not None:
-            gain = jnp.concatenate([gain[:8] + source[y], gain[8:]], axis=0)
-        out.append((1.0 - DAMPING) * v + w(step) * gain)
-    return out
-
-
-def sweep(state, weights, earlier, into, low, high, step, source=None, unroll=4):
-    def rows(k, carry):
-        for u in range(unroll):
-            y = low + unroll * k + u
-            new = row_sweep(y, state, weights, earlier, step, source)
-            into[0, y] = new[0]
-            into[1, y] = new[1]
-        return carry
-
-    lax.fori_loop(0, (high - low + unroll - 1) // unroll, rows, 0)
-
-
-def advances(count, e, v, weights, low, high, step, source=None):
-    def one(m, carry):
-        sweep(e, weights, None, v, low + 2 * m + 1, high - 2 * m - 1, step, source)
-        sweep(v, weights, e, e, low + 2 * m + 2, high - 2 * m - 2, step, source)
-        return carry
-
-    lax.fori_loop(0, count, one, 0)
+def sweep_rows(first, count, state, weights, earlier, into, step, source):
+    centres = [[state[i, first - 1 + k] for k in range(count + 2)] for i in range(2)]
+    for u in range(count):
+        y = first + u
+        for i in range(2):
+            v = centres[i][u + 1]
+            w = lambda k: weights[y, PAIR * i + k]
+            along = w(0) * pltpu.roll(v, 1, 0) + w(1) * pltpu.roll(v, NX - 1, 0)
+            middle = w(2) * centres[i][u] + w(3) * centres[i][u + 2]
+            across = w(4) * pltpu.roll(v, 1, 1) + w(5) * pltpu.roll(v, LAST - 1, 1)
+            begin = v if earlier is None else earlier[i, y]
+            if step == COARSE:
+                begin = (1.0 / COARSE_FACTOR) * begin
+            gain = (along + middle) + (across + (w(6) * centres[1 - i][u + 1] + begin))
+            if i == 1 and source is not None:
+                gain = jnp.concatenate([gain[:8] + source[y], gain[8:]], axis=0)
+            into[i, y] = (1.0 - DAMPING) * v + w(step) * gain
+
+
+def sweep(state, weights, earlier, into, low, count, step, source=None):
+    pieces = -(-count // LONGEST)
+    size = -(-count // pieces)
+    whole = count // size
+
+    def piece(first, rows):
+        sweep_rows(first, rows, state, weights, earlier, into, step, source)
+
+    if whole > 1:
+
+        def one(k, carry):
+            piece(low + k * size, size)
+            return carry
+
+        lax.fori_loop(0, whole, one, 0)
+    else:
+        piece(low, size)
+    if count > whole * size:
+        piece(low + whole * size, count - whole * size)
+
+
+def advances(many, e, v, weights, low, count, step, source=None):
+    for m in range(many):
+        sweep(e, weights, None, v, low + 2 * m + 1, count - 4 * m - 2, step, source)
+        sweep(v, weights, e, e, low + 2 * m + 2, count - 4 * m - 4, step, source)
 
 
 def relax_kernel(begin, mine, other, inlet, w, base, give, own, c, feed, e, v, e0):
@@ -184,7 +190,7 @@
     column = lax.broadcasted_iota(jnp.int32, (NX, LAST), 1)
     top = lax.broadcasted_iota(jnp.int32, (8, LAST), 0) == 0
 
-    def weigh(r, carry):
+    def weigh(r):
         y = strip * STRIP - EDGE + r
         lower = jnp.where(y == 0, 0.0, 1.0).astype(F32)
         upper = jnp.where(y == MIDDLE - 1, 0.0, 1.0).astype(F32)
@@ -221,17 +227,21 @@
             w[r, PAIR * i + COARSE] = (DAMPING * COARSE_FACTOR) / (1.0 + COARSE_FACTOR * outflow)
             if i == 1:
                 feed[r] = jnp.where(top, wxm[:8] * warmth, 0.0)
+
+    def weigh_two(k, carry):
+        weigh(1 + 2 * k)
+        weigh(2 + 2 * k)
         return carry
 
-    lax.fori_loop(1, ROWS - 1, weigh, 0)
-    sweep(e0, w, None, v, EDGE - 3, EDGE + STRIP + 3, COARSE)
-    sweep(v, w, e0, e0, EDGE - 2, EDGE + STRIP + 2, COARSE)
+    lax.fori_loop(0, (ROWS - 2) // 2, weigh_two, 0)
+    sweep(e0, w, None, v, EDGE - 3, STRIP + 6, COARSE)
+    sweep(v, w, e0, e0, EDGE - 2, STRIP + 4, COARSE)
     advances(4, e, v, w, 0, ROWS, FINE, feed)
     keep = jnp.where(slab == SLABS - 1, 0.0, 1.0).astype(F32)
     rows = pl.ds(EDGE - 2, STRIP + 4)
     e[:, rows] = e[:, rows] - keep * e0[:, rows]
-    sweep(e, w, None, v, EDGE - 1, EDGE + STRIP + 1, COARSE)
-    sweep(v, w, e, e0, EDGE, EDGE + STRIP, COARSE)
+    sweep(e, w, None, v, EDGE - 1, STRIP + 2, COARSE)
+    sweep(v, w, e, e0, EDGE, STRIP, COARSE)
     joined = jnp.where(slab == SLABS - 2, 0.0, 1.0).astype(F32)
     near, far = pl.ds(EDGE, HALF), pl.ds(EDGE + HALF, HALF)
     base[...] = jnp.where(core == 0, joined * e0[:, near], e[:, far])
@@ -255,11 +265,11 @@
     reach = HALF if more else HALF // 2
     e[:, rows] = own[...]
     place(core, e, middle, swapped, near)
-    advances(2, e, v, w, middle - reach, middle + HALF + reach, COARSE)
+    advances(2, e, v, w, middle - reach, HALF + 2 * reach, COARSE)
     odd[...] = e[:, rows]
     if more:
         even, *rims = more
-        advances(2, e, v, w, middle - 4, middle + HALF + 4, COARSE)
+        advances(2, e, v, w, middle - 4, HALF + 8, COARSE)
         even[...] = e[:, rows] + high[...] if joined else e[:, rows]
         if rims:
             inner, outer = rims
@@ -295,8 +305,8 @@
     rows = pl.ds(middle, HALF)
     r[:, rows] = own[...]
     place(core, r, middle, swapped, near)
-    sweep(r, w, None, v, middle - 1, middle + HALF + 1, COARSE)
-    sweep(v, w, r, e, middle, middle + HALF, COARSE)
+    sweep(r, w, None, v, middle - 1, HALF + 2, COARSE)
+    sweep(v, w, r, e, middle, HALF, COARSE)
     e[:, rows] = e[:, rows] + jnp.where(core == 0, g[...], taken[2:4])
     low = lax.broadcasted_iota(jnp.int32, (8, LAST), 0) < PLANES
     for out, other in ((keep, 0), (send, 1)):
@@ -369,13 +379,13 @@
     )(got)
     other = swap(mine)
 
-    field = pltpu.VMEM((2, HELD, NX, LAST), F32)
+    field = pltpu.VMEM((2, ROWS, NX, LAST), F32)
     weights, base, give, g = call(
         relax_kernel,
-        (pltpu.VMEM((HELD, 2 * PAIR, NX, LAST), F32), half, shape(4, HALF, NX, LAST), half),
+        (pltpu.VMEM((ROWS, 2 * PAIR, NX, LAST), F32), half, shape(4, HALF, NX, LAST), half),
         [VMEM] * 4,
         (VMEM,) * 4,
-        [pltpu.VMEM((3, ROWS, NX, LAST), F32), pltpu.VMEM((HELD, 8, LAST), F32), field, field, field],
+        [pltpu.VMEM((3, ROWS, NX, LAST), F32), pltpu.VMEM((ROWS, 8, LAST), F32), field, field, field],
         24,
     )(begin, mine, other, inlet)
     taken = swap(give)

time: 134 us -> 125 us (0.933)
  Pallas kernels: 34.4 us -> 24.4 us
    pallas_call x4, Pallas kernels: 16.2 us -> 11 us  [leap(): call(body, outs, [VMEM] * len(operands), (VMEM,) * len(outs), [field, fie...]
    pallas_call x1, Pallas kernels: 14.6 us -> 10.2 us  [shards(): call(relax_kernel, (pltpu.VMEM((ROWS, 2 * PAIR, NX, LAST), F32), half, sh...]
  transfers between devices with their start and end apart: 20 -> 20, of which waited for: 12 -> 12; matrix products, arithmetic and copies ran while one was open for 0% -> 0% of each run, Pallas kernels for 12% -> 9%
where the time goes in v10:
time: 125 us; the launch traced here: 124 us
  blocking collectives  44.9 us (36%)
  waiting for transfers between devices  37.1 us (30%)
  Pallas kernels  24.4 us (20%)
  starting transfers between devices  17.5 us (14%)
    ppermute x20, waiting for transfers between devices, sent(): return lax.ppermute(value, AXES, pairs)  37.1 us
    all_to_all x1, blocking collectives, shards(): got = lax.all_to_all(packed, 'space', 0, 0, tiled=True)  31.8 us
    ppermute x20, starting transfers between devices, sent(): return lax.ppermute(value, AXES, pairs)  17.5 us
    all_to_all x1, blocking collectives, shards(): lax.all_to_all(jnp.concatenate([keep, swap(send)], axis=1), 'space', 0, 0...  13.1 us
    pallas_call x4, Pallas kernels, leap(): call(body, outs, [VMEM] * len(operands), (VMEM,) * len(outs), [field, fie...  11 us
    pallas_call x1, Pallas kernels, shards(): call(relax_kernel, (pltpu.VMEM((ROWS, 2 * PAIR, NX, LAST), F32), half, sh...  10.2 us
  transfers between devices with their start and end apart: 20, of which 12 were waited for; matrix products, arithmetic and copies ran while one was open for 0% of the time, Pallas kernels for 9%

profile of v10, /device:TPU:4, one launch (start us, length us, event | category | flops | bytes accessed | tf_op | source)
XLA Modules:
  0.0 124.1 jit_solution(13420728440932898305)
XLA Ops:
  0.0 1.5 %shard_map.55 = f32[8,504,128]{2,1,0:T(8,128)S(1)} custom-call(f32[2,4,128,128]{3,2,1,0:T(8,128)} %startup.1, f32[1,2,4,128,128]{4,3,2,1,0:T(8,128)} %guess.1, f32[2,4,128,128]{3,2,1,0:T(8,128)} %conduct.1, f32[4,128,128]{2,1,0:T(8,128)} %couple.1), custom_call_target="tpu_custom_call" | custom-call | bytes 3145728 | tf_op jit(solution)/shard_map/pallas_call | solution.py:363
  1.5 31.8 %all_to_all.10.got = f32[8,504,128]{2,1,0:T(8,128)S(1)} all-to-all(f32[8,504,128]{2,1,0:T(8,128)S(1)} %shard_map.55), channel_id=1, replica_groups=mesh['chip'=8,'core'=2,'space'=8] {'space'}, dimensions={0} | all-to-all | bytes 4128768 | tf_op jit(solution)/shard_map/all_to_all | solution.py:376
  33.3 0.0 copy-start
  33.3 0.1 shard_map.56
  33.4 0.1 collective-permute-start
  33.5 2.4 %collective-permute-done.other = f32[3,18,32,128]{3,2,1,0:T(8,128)S(1)} collective-permute-done((f32[3,18,32,128]{3,2,1,0:T(8,128)S(1)}, f32[3,18,32,128]{3,2,1,0:T(8,128)S(1)}, u32[]{:S(2)}, u32[]{:S(2)}) %collective-permute-start) | collective-permute-done | bytes 884768 | tf_op jit(solution)/shard_map/ppermute | solution.py:335
  35.9 0.0 copy-done
  35.9 10.2 %shard_map.57 = (f32[36,18,32,128]{3,2,1,0:T(8,128)S(1)}, f32[2,8,32,128]{3,2,1,0:T(8,128)S(1)}, f32[4,8,32,128]{3,2,1,0:T(8,128)S(1)}, f32[2,8,32,128]{3,2,1,0:T(8,128)S(1)}) custom-call(f32[2,36,32,128]{3,2,1,0:T(8,128)S(1)} %get-tuple-element.42.begin, f32[3,18,32,128]{3,2,1,0:T(8,128)S(1)} %get-tuple-element.43.mine, ...), custom_call_target="tpu_custom_call" | custom-call | bytes 3145728 | tf_op jit(solution)/shard_map/pallas_call | solution.py:383
  46.1 0.2 collective-permute-start.1
  46.3 1.8 %collective-permute-done.1.taken = f32[4,8,32,128]{3,2,1,0:T(8,128)S(1)} collective-permute-done((f32[4,8,32,128]{3,2,1,0:T(8,128)S(1)}, f32[4,8,32,128]{3,2,1,0:T(8,128)S(1)}, u32[]{:S(2)}, u32[]{:S(2)}) %collective-permute-start.1) | collective-permute-done | bytes 524320 | tf_op jit(solution)/shard_map/ppermute | solution.py:335
  48.1 0.9 collective-permute-start.2
  49.0 9.1 %collective-permute-done.2.across = f32[2,8,32,128]{3,2,1,0:T(8,128)S(1)} collective-permute-done((f32[2,8,32,128]{3,2,1,0:T(8,128)S(1)}, f32[2,8,32,128]{3,2,1,0:T(8,128)S(1)}, u32[]{:S(2)}, u32[]{:S(2)}) %collective-permute-start.2) | collective-permute-done | bytes 262176 | tf_op jit(solution)/shard_map/ppermute | solution.py:335
  58.1 0.1 shard_map.58
  58.1 0.1 collective-permute-start.4
  58.2 0.7 collective-permute-start.3
  58.9 1.9 %collective-permute-start.7 = (f32[2,8,32,128]{3,2,1,0:T(8,128)S(1)}, f32[2,8,32,128]{3,2,1,0:T(8,128)S(1)}, u32[]{:S(2)}, u32[]{:S(2)}) collective-permute-start(f32[2,8,32,128]{3,2,1,0:T(8,128)S(1)} %get-tuple-element.47.own), channel_id=1, source_target_pairs={{0,16},{2,18},{4,20},{6,22},{7,23},{5,21},{3,19},{1,17},{8,24},{10... | collective-permute-start | bytes 786440 | tf_op jit(solution)/shard_map/ppermute | solution.py:335
  60.8 0.0 collective-permute-done.4.swapped
  60.8 3.3 %collective-permute-done.3.near = f32[2,8,32,128]{3,2,1,0:T(8,128)S(1)} collective-permute-done((f32[2,8,32,128]{3,2,1,0:T(8,128)S(1)}, f32[2,8,32,128]{3,2,1,0:T(8,128)S(1)}, u32[]{:S(2)}, u32[]{:S(2)}) %collective-permute-start.3) | collective-permute-done | bytes 262176 | tf_op jit(solution)/shard_map/ppermute | solution.py:335
  64.1 3.2 %shard_map.59 = (f32[2,8,32,128]{3,2,1,0:T(8,128)S(1)}, f32[2,8,32,128]{3,2,1,0:T(8,128)S(1)}) custom-call(f32[2,8,32,128]{3,2,1,0:T(8,128)S(1)} %get-tuple-element.47.own, f32[2,8,32,128]{3,2,1,0:T(8,128)S(1)} %collective-permute-done.3.near, f32[2,8,32,128]{3,2,1,0:T(8,128)S(1)} %collective-permute-done.4.swapped, f32[36,18,32,128]{3,2,1,0:T(8,128)S(1)} %get-tuple-element.50.w), custom_call_target="tpu_custom_call" | custom-call | bytes 15728640 | tf_op jit(solution)/shard_map/pallas_call | solution.py:398
  67.3 0.8 collective-permute-start.6
  68.1 0.2 collective-permute-start.5
  68.4 4.0 %collective-permute-start.11 = (f32[2,8,32,128]{3,2,1,0:T(8,128)S(1)}, f32[2,8,32,128]{3,2,1,0:T(8,128)S(1)}, u32[]{:S(2)}, u32[]{:S(2)}) collective-permute-start(f32[2,8,32,128]{3,2,1,0:T(8,128)S(1)} %get-tuple-element.53.own), channel_id=1, source_target_pairs={{0,48},{2,50},{4,52},{6,54},{7,55},{5,53},{3,51},{1,49},{8,56},{10... | collective-permute-start | bytes 786440 | tf_op jit(solution)/shard_map/ppermute | solution.py:335
  72.4 0.0 collective-permute-start.10
  72.4 0.0 collective-permute-done.7.refs_0_
  72.4 0.0 collective-permute-done.6.swapped
  72.4 1.5 %collective-permute-done.5.near = f32[2,8,32,128]{3,2,1,0:T(8,128)S(1)} collective-permute-done((f32[2,8,32,128]{3,2,1,0:T(8,128)S(1)}, f32[2,8,32,128]{3,2,1,0:T(8,128)S(1)}, u32[]{:S(2)}, u32[]{:S(2)}) %collective-permute-start.5) | collective-permute-done | bytes 262176 | tf_op jit(solution)/shard_map/ppermute | solution.py:335
  73.9 3.3 %shard_map.60 = (f32[2,8,32,128]{3,2,1,0:T(8,128)S(1)}, f32[2,8,32,128]{3,2,1,0:T(8,128)S(1)}) custom-call(f32[2,8,32,128]{3,2,1,0:T(8,128)S(1)} %get-tuple-element.53.own, f32[2,8,32,128]{3,2,1,0:T(8,128)S(1)} %collective-permute-done.5.near, f32[2,8,32,128]{3,2,1,0:T(8,128)S(1)} %collective-permute-done.6.swapped, ...), custom_call_target="tpu_custom_call" | custom-call | bytes 15728640 | tf_op jit(solution)/shard_map/pallas_call | solution.py:398
  77.2 0.5 collective-permute-start.9
  77.7 0.3 collective-permute-start.8
  77.9 1.9 %collective-permute-start.14 = (f32[2,8,32,128]{3,2,1,0:T(8,128)S(1)}, f32[2,8,32,128]{3,2,1,0:T(8,128)S(1)}, u32[]{:S(2)}, u32[]{:S(2)}) collective-permute-start(f32[2,8,32,128]{3,2,1,0:T(8,128)S(1)} %get-tuple-element.62.own), channel_id=1, source_target_pairs={{0,16},{2,18},{4,20},{6,22},{7,23},{5,21},{3,19},{1,17},{8,24},{10... | collective-permute-start | bytes 786440 | tf_op jit(solution)/shard_map/ppermute | solution.py:335
  79.9 2.1 %collective-permute-done.10.refs_1_ = f32[2,8,32,128]{3,2,1,0:T(8,128)S(1)} collective-permute-done((f32[2,8,32,128]{3,2,1,0:T(8,128)S(1)}, f32[2,8,32,128]{3,2,1,0:T(8,128)S(1)}, u32[]{:S(2)}, u32[]{:S(2)}) %collective-permute-start.10) | collective-permute-done | bytes 262176 | tf_op jit(solution)/shard_map/ppermute | solution.py:335
  82.0 1.9 %collective-permute-done.11.refs_2_ = f32[2,8,32,128]{3,2,1,0:T(8,128)S(1)} collective-permute-done((f32[2,8,32,128]{3,2,1,0:T(8,128)S(1)}, f32[2,8,32,128]{3,2,1,0:T(8,128)S(1)}, u32[]{:S(2)}, u32[]{:S(2)}) %collective-permute-start.11) | collective-permute-done | bytes 262176 | tf_op jit(solution)/shard_map/ppermute | solution.py:335
  83.9 0.0 collective-permute-done.9.swapped
  83.9 0.0 collective-permute-done.8.near
  83.9 3.3 %shard_map.61 = (f32[2,8,32,128]{3,2,1,0:T(8,128)S(1)}, f32[2,8,32,128]{3,2,1,0:T(8,128)S(1)}, f32[2,4,32,128]{3,2,1,0:T(8,128)S(1)}, f32[2,4,32,128]{3,2,1,0:T(8,128)S(1)}) custom-call(f32[2,8,32,128]{3,2,1,0:T(8,128)S(1)} %get-tuple-element.62.own, f32[2,8,32,128]{3,2,1,0:T(8,128)S(1)} %collective-permute-done.8.near, ...), custom_call_target="tpu_custom_call" | custom-call | bytes 15728640 | tf_op jit(solution)/shard_map/pallas_call | solution.py:398
  87.2 3.5 %collective-permute-start.15 = (f32[2,8,32,128]{3,2,1,0:T(8,128)S(1)}, f32[2,8,32,128]{3,2,1,0:T(8,128)S(1)}, u32[]{:S(2)}, u32[]{:S(2)}) collective-permute-start(f32[2,8,32,128]{3,2,1,0:T(8,128)S(1)} %get-tuple-element.69), channel_id=1, source_target_pairs={{0,32},{2,34},{4,36},{6,38},{7,39},{5,37},{3,35},{1,33},{8,40},{10... | collective-permute-start | bytes 786440 | tf_op jit(solution)/shard_map/ppermute | solution.py:335
  90.7 0.9 collective-permute-start.16
  91.7 0.3 collective-permute-start.12
  92.0 0.7 collective-permute-start.13
  92.6 0.0 collective-permute-done.14.refs_4_
  92.6 3.4 %collective-permute-done.12.near = f32[2,4,32,128]{3,2,1,0:T(8,128)S(1)} collective-permute-done((f32[2,4,32,128]{3,2,1,0:T(8,128)S(1)}, f32[2,4,32,128]{3,2,1,0:T(8,128)S(1)}, u32[]{:S(2)}, u32[]{:S(2)}) %collective-permute-start.12) | collective-permute-done | bytes 131104 | tf_op jit(solution)/shard_map/ppermute | solution.py:335
  96.0 0.0 collective-permute-done.13.swapped
  96.0 1.2 shard_map.62.refs_7_
  97.3 0.3 collective-permute-done.15.refs_5_
  97.6 6.4 %collective-permute-done.16.refs_6_ = f32[2,8,32,128]{3,2,1,0:T(8,128)S(1)} collective-permute-done((f32[2,8,32,128]{3,2,1,0:T(8,128)S(1)}, f32[2,8,32,128]{3,2,1,0:T(8,128)S(1)}, u32[]{:S(2)}, u32[]{:S(2)}) %collective-permute-start.16) | collective-permute-done | bytes 262176 | tf_op jit(solution)/shard_map/ppermute | solution.py:335
  104.0 0.2 shard_map.63
  104.1 0.1 collective-permute-start.17
  104.2 0.3 collective-permute-start.18
  104.6 3.3 %collective-permute-done.17.near = f32[2,2,32,128]{3,2,1,0:T(8,128)S(1)} collective-permute-done((f32[2,2,32,128]{3,2,1,0:T(8,128)S(1)}, f32[2,2,32,128]{3,2,1,0:T(8,128)S(1)}, u32[]{:S(2)}, u32[]{:S(2)}) %collective-permute-start.17) | collective-permute-done | bytes 65568 | tf_op jit(solution)/shard_map/ppermute | solution.py:335
  107.9 0.0 collective-permute-done.18.swapped
  107.9 0.6 shard_map.64
  108.5 0.1 collective-permute-start.19
  108.6 1.5 %collective-permute-done.19 = f32[8,64,128]{2,1,0:T(8,128)S(1)} collective-permute-done((f32[8,64,128]{2,1,0:T(8,128)S(1)}, f32[8,64,128]{2,1,0:T(8,128)S(1)}, u32[]{:S(2)}, u32[]{:S(2)}) %collective-permute-start.19) | collective-permute-done | bytes 262176 | tf_op jit(solution)/shard_map/ppermute | solution.py:335
  110.1 13.1 %all_to_all.11.got = f32[8,128,128]{2,1,0:T(8,128)S(1)} all-to-all(f32[8,128,128]{2,1,0:T(8,128)S(1)} %pad_maximum_fusion), channel_id=1, replica_groups=mesh['chip'=8,'core'=2,'space'=8] {'space'}, dimensions={0} | all-to-all | bytes 1048576 | tf_op jit(solution)/shard_map/all_to_all | solution.py:420
  123.2 0.8 shard_map.65
  (2 shorter events, 0.1 us)
Async XLA Ops:
  33.3 2.7 %copy-start = (f32[128,128]{1,0:T(8,128)S(1)}, f32[128,128]{1,0:T(8,128)}, u32[]{:S(2)}) copy-start(f32[128,128]{1,0:T(8,128)} %inlet.1) | copy-start | bytes 196612
  33.4 2.5 %collective-permute-start = (f32[3,18,32,128]{3,2,1,0:T(8,128)S(1)}, f32[3,18,32,128]{3,2,1,0:T(8,128)S(1)}, u32[]{:S(2)}, u32[]{:S(2)}) collective-permute-start(f32[3,18,32,128]{3,2,1,0:T(8,128)S(1)} %get-tuple-element.43.mine), channel_id=1, source_target_pairs={{8,0},{10,2},{12,4},{14,6},{15,7},{13,5},{11,3},{9,1},{0,8},{2,10}... | collective-permute-start | bytes 2654216 | tf_op jit(solution)/shard_map/ppermute | solution.py:335
  46.1 2.0 %collective-permute-start.1 = (f32[4,8,32,128]{3,2,1,0:T(8,128)S(1)}, f32[4,8,32,128]{3,2,1,0:T(8,128)S(1)}, u32[]{:S(2)}, u32[]{:S(2)}) collective-permute-start(f32[4,8,32,128]{3,2,1,0:T(8,128)S(1)} %get-tuple-element.45), channel_id=1, source_target_pairs={{8,0},{10,2},{12,4},{14,6},{15,7},{13,5},{11,3},{9,1},{0,8},{2,10}... | collective-permute-start | bytes 1572872 | tf_op jit(solution)/shard_map/ppermute | solution.py:335
  48.1 9.9 %collective-permute-start.2 = (f32[2,8,32,128]{3,2,1,0:T(8,128)S(1)}, f32[2,8,32,128]{3,2,1,0:T(8,128)S(1)}, u32[]{:S(2)}, u32[]{:S(2)}) collective-permute-start(f32[2,8,32,128]{3,2,1,0:T(8,128)S(1)} %slice_add_fusion.ours), channel_id=1, source_target_pairs={{64,0},{66,2},{68,4},{70,6},{71,7},{69,5},{67,3},{65,1},{72,8},{74... | collective-permute-start | bytes 786440 | tf_op jit(solution)/shard_map/ppermute | solution.py:335
  58.1 2.7 %collective-permute-start.4 = (f32[2,8,32,128]{3,2,1,0:T(8,128)S(1)}, f32[2,8,32,128]{3,2,1,0:T(8,128)S(1)}, u32[]{:S(2)}, u32[]{:S(2)}) collective-permute-start(f32[2,8,32,128]{3,2,1,0:T(8,128)S(1)} %get-tuple-element.47.own), channel_id=1, source_target_pairs={{8,0},{10,2},{12,4},{14,6},{15,7},{13,5},{11,3},{9,1},{0,8},{2,10}... | collective-permute-start | bytes 786440 | tf_op jit(solution)/shard_map/ppermute | solution.py:335
  58.2 5.9 %collective-permute-start.3 = (f32[2,8,32,128]{3,2,1,0:T(8,128)S(1)}, f32[2,8,32,128]{3,2,1,0:T(8,128)S(1)}, u32[]{:S(2)}, u32[]{:S(2)}) collective-permute-start(f32[2,8,32,128]{3,2,1,0:T(8,128)S(1)} %get-tuple-element.47.own), channel_id=1, source_target_pairs={{8,2},{10,4},{12,6},{14,7},{15,5},{13,3},{11,1},{9,0},{0,9},{2,8},... | collective-permute-start | bytes 786440 | tf_op jit(solution)/shard_map/ppermute | solution.py:335
  58.9 13.6 %collective-permute-start.7 = (f32[2,8,32,128]{3,2,1,0:T(8,128)S(1)}, f32[2,8,32,128]{3,2,1,0:T(8,128)S(1)}, u32[]{:S(2)}, u32[]{:S(2)}) collective-permute-start(f32[2,8,32,128]{3,2,1,0:T(8,128)S(1)} %get-tuple-element.47.own), channel_id=1, source_target_pairs={{0,16},{2,18},{4,20},{6,22},{7,23},{5,21},{3,19},{1,17},{8,24},{10... | collective-permute-start | bytes 786440 | tf_op jit(solution)/shard_map/ppermute | solution.py:335
  67.3 5.1 %collective-permute-start.6 = (f32[2,8,32,128]{3,2,1,0:T(8,128)S(1)}, f32[2,8,32,128]{3,2,1,0:T(8,128)S(1)}, u32[]{:S(2)}, u32[]{:S(2)}) collective-permute-start(f32[2,8,32,128]{3,2,1,0:T(8,128)S(1)} %get-tuple-element.53.own), channel_id=1, source_target_pairs={{8,0},{10,2},{12,4},{14,6},{15,7},{13,5},{11,3},{9,1},{0,8},{2,10}... | collective-permute-start | bytes 786440 | tf_op jit(solution)/shard_map/ppermute | solution.py:335
  68.1 5.8 %collective-permute-start.5 = (f32[2,8,32,128]{3,2,1,0:T(8,128)S(1)}, f32[2,8,32,128]{3,2,1,0:T(8,128)S(1)}, u32[]{:S(2)}, u32[]{:S(2)}) collective-permute-start(f32[2,8,32,128]{3,2,1,0:T(8,128)S(1)} %get-tuple-element.53.own), channel_id=1, source_target_pairs={{8,2},{10,4},{12,6},{14,7},{15,5},{13,3},{11,1},{9,0},{0,9},{2,8},... | collective-permute-start | bytes 786440 | tf_op jit(solution)/shard_map/ppermute | solution.py:335
  68.4 15.5 %collective-permute-start.11 = (f32[2,8,32,128]{3,2,1,0:T(8,128)S(1)}, f32[2,8,32,128]{3,2,1,0:T(8,128)S(1)}, u32[]{:S(2)}, u32[]{:S(2)}) collective-permute-start(f32[2,8,32,128]{3,2,1,0:T(8,128)S(1)} %get-tuple-element.53.own), channel_id=1, source_target_pairs={{0,48},{2,50},{4,52},{6,54},{7,55},{5,53},{3,51},{1,49},{8,56},{10... | collective-permute-start | bytes 786440 | tf_op jit(solution)/shard_map/ppermute | solution.py:335
  72.4 9.5 %collective-permute-start.10 = (f32[2,8,32,128]{3,2,1,0:T(8,128)S(1)}, f32[2,8,32,128]{3,2,1,0:T(8,128)S(1)}, u32[]{:S(2)}, u32[]{:S(2)}) collective-permute-start(f32[2,8,32,128]{3,2,1,0:T(8,128)S(1)} %get-tuple-element.58), channel_id=1, source_target_pairs={{0,32},{2,34},{4,36},{6,38},{7,39},{5,37},{3,35},{1,33},{8,40},{10... | collective-permute-start | bytes 786440 | tf_op jit(solution)/shard_map/ppermute | solution.py:335
  77.2 6.7 %collective-permute-start.9 = (f32[2,8,32,128]{3,2,1,0:T(8,128)S(1)}, f32[2,8,32,128]{3,2,1,0:T(8,128)S(1)}, u32[]{:S(2)}, u32[]{:S(2)}) collective-permute-start(f32[2,8,32,128]{3,2,1,0:T(8,128)S(1)} %get-tuple-element.62.own), channel_id=1, source_target_pairs={{8,0},{10,2},{12,4},{14,6},{15,7},{13,5},{11,3},{9,1},{0,8},{2,10}... | collective-permute-start | bytes 786440 | tf_op jit(solution)/shard_map/ppermute | solution.py:335
  77.7 6.2 %collective-permute-start.8 = (f32[2,8,32,128]{3,2,1,0:T(8,128)S(1)}, f32[2,8,32,128]{3,2,1,0:T(8,128)S(1)}, u32[]{:S(2)}, u32[]{:S(2)}) collective-permute-start(f32[2,8,32,128]{3,2,1,0:T(8,128)S(1)} %get-tuple-element.62.own), channel_id=1, source_target_pairs={{8,2},{10,4},{12,6},{14,7},{15,5},{13,3},{11,1},{9,0},{0,9},{2,8},... | collective-permute-start | bytes 786440 | tf_op jit(solution)/shard_map/ppermute | solution.py:335
  77.9 14.7 %collective-permute-start.14 = (f32[2,8,32,128]{3,2,1,0:T(8,128)S(1)}, f32[2,8,32,128]{3,2,1,0:T(8,128)S(1)}, u32[]{:S(2)}, u32[]{:S(2)}) collective-permute-start(f32[2,8,32,128]{3,2,1,0:T(8,128)S(1)} %get-tuple-element.62.own), channel_id=1, source_target_pairs={{0,16},{2,18},{4,20},{6,22},{7,23},{5,21},{3,19},{1,17},{8,24},{10... | collective-permute-start | bytes 786440 | tf_op jit(solution)/shard_map/ppermute | solution.py:335
  87.2 10.4 %collective-permute-start.15 = (f32[2,8,32,128]{3,2,1,0:T(8,128)S(1)}, f32[2,8,32,128]{3,2,1,0:T(8,128)S(1)}, u32[]{:S(2)}, u32[]{:S(2)}) collective-permute-start(f32[2,8,32,128]{3,2,1,0:T(8,128)S(1)} %get-tuple-element.69), channel_id=1, source_target_pairs={{0,32},{2,34},{4,36},{6,38},{7,39},{5,37},{3,35},{1,33},{8,40},{10... | collective-permute-start | bytes 786440 | tf_op jit(solution)/shard_map/ppermute | solution.py:335
  90.7 13.3 %collective-permute-start.16 = (f32[2,8,32,128]{3,2,1,0:T(8,128)S(1)}, f32[2,8,32,128]{3,2,1,0:T(8,128)S(1)}, u32[]{:S(2)}, u32[]{:S(2)}) collective-permute-start(f32[2,8,32,128]{3,2,1,0:T(8,128)S(1)} %get-tuple-element.70.own), channel_id=1, source_target_pairs={{0,48},{2,50},{4,52},{6,54},{7,55},{5,53},{3,51},{1,49},{8,56},{10... | collective-permute-start | bytes 786440 | tf_op jit(solution)/shard_map/ppermute | solution.py:335
  91.7 4.4 %collective-permute-start.12 = (f32[2,4,32,128]{3,2,1,0:T(8,128)S(1)}, f32[2,4,32,128]{3,2,1,0:T(8,128)S(1)}, u32[]{:S(2)}, u32[]{:S(2)}) collective-permute-start(f32[2,4,32,128]{3,2,1,0:T(8,128)S(1)} %get-tuple-element.66), channel_id=1, source_target_pairs={{8,2},{10,4},{12,6},{14,7},{15,5},{13,3},{11,1},{9,0},{0,9},{2,8},... | collective-permute-start | bytes 393224 | tf_op jit(solution)/shard_map/ppermute | solution.py:335
  92.0 4.1 %collective-permute-start.13 = (f32[2,4,32,128]{3,2,1,0:T(8,128)S(1)}, f32[2,4,32,128]{3,2,1,0:T(8,128)S(1)}, u32[]{:S(2)}, u32[]{:S(2)}) collective-permute-start(f32[2,4,32,128]{3,2,1,0:T(8,128)S(1)} %get-tuple-element.67), channel_id=1, source_target_pairs={{8,0},{10,2},{12,4},{14,6},{15,7},{13,5},{11,3},{9,1},{0,8},{2,10}... | collective-permute-start | bytes 393224 | tf_op jit(solution)/shard_map/ppermute | solution.py:335
  104.1 3.8 %collective-permute-start.17 = (f32[2,2,32,128]{3,2,1,0:T(8,128)S(1)}, f32[2,2,32,128]{3,2,1,0:T(8,128)S(1)}, u32[]{:S(2)}, u32[]{:S(2)}) collective-permute-start(f32[2,2,32,128]{3,2,1,0:T(8,128)S(1)} %get-tuple-element.74), channel_id=1, source_target_pairs={{8,2},{10,4},{12,6},{14,7},{15,5},{13,3},{11,1},{9,0},{0,9},{2,8},... | collective-permute-start | bytes 196616 | tf_op jit(solution)/shard_map/ppermute | solution.py:335
  104.2 3.7 %collective-permute-start.18 = (f32[2,2,32,128]{3,2,1,0:T(8,128)S(1)}, f32[2,2,32,128]{3,2,1,0:T(8,128)S(1)}, u32[]{:S(2)}, u32[]{:S(2)}) collective-permute-start(f32[2,2,32,128]{3,2,1,0:T(8,128)S(1)} %get-tuple-element.75), channel_id=1, source_target_pairs={{8,0},{10,2},{12,4},{14,6},{15,7},{13,5},{11,3},{9,1},{0,8},{2,10}... | collective-permute-start | bytes 196616 | tf_op jit(solution)/shard_map/ppermute | solution.py:335
  108.5 1.6 %collective-permute-start.19 = (f32[8,64,128]{2,1,0:T(8,128)S(1)}, f32[8,64,128]{2,1,0:T(8,128)S(1)}, u32[]{:S(2)}, u32[]{:S(2)}) collective-permute-start(f32[8,64,128]{2,1,0:T(8,128)S(1)} %get-tuple-element.78), channel_id=1, source_target_pairs={{8,0},{10,2},{12,4},{14,6},{15,7},{13,5},{11,3},{9,1},{0,8},{2,10}... | collective-permute-start | bytes 786440 | tf_op jit(solution)/shard_map/ppermute | solution.py:335

commit v11 on v10

--- a/solution.py
+++ b/solution.py
@@ -58,7 +58,11 @@
 def position():
     chip, core, space = (lax.axis_index(a) for a in AXES)
     y, odd = space // 2, space % 2
-    return core, jnp.where(odd == 0, y, BRICKS - 1 - y), chip * 2 + core
+    return core, placed(jnp.where(odd == 0, y, BRICKS - 1 - y), chip), chip * 2 + core
+
+
+def placed(place, chip):
+    return jnp.where(chip < RING, place, BRICKS - 1 - place)
 
 
 def pack_kernel(startup, guess, conduct, couple, out, padded, state, others, sems):
@@ -92,12 +96,12 @@
                 value = state[i, plane, first : first + 8] if i < 2 else others[i - 2, plane, first : first + 8]
                 padded[i, pl.ds((EDGE + first) * PLANES + plane, 8, stride=PLANES), :] = value
     tall, part = (STRIP + 2 * EDGE) * PLANES, PART * PLANES
-    for b in range(BRICKS):
-        s = ORDER[b]
-        start = (STRIP * b) * PLANES
+    for place in range(BRICKS):
+        s = ORDER[place]
+        start = pl.multiple_of(STRIP * PLANES * placed(place, slab // 2), 64)
         for i in range(2):
-            out[s, i * tall : (i + 1) * tall] = padded[i, start : start + tall]
-        start = pl.multiple_of(STRIP * b * PLANES + part * core, 32)
+            out[s, i * tall : (i + 1) * tall] = padded[i, pl.ds(start, tall)]
+        start = pl.multiple_of(start + part * core, 8)
         for i in range(3):
             at = 2 * tall + i * part
             out[s, at : at + part] = padded[2 + i, pl.ds(start, part)]
@@ -122,15 +126,15 @@
 
 
 def restore_kernel(got, out):
-    core, _, _ = position()
+    core, _, slab = position()
     for part in range(2):
         half = core if part == 0 else 1 - core
-        for b in range(BRICKS):
-            first = pl.multiple_of(STRIP * b + HALF * half, HALF)
+        for place in range(BRICKS):
+            first = pl.multiple_of(STRIP * placed(place, slab // 2) + HALF * half, HALF)
             for i in range(2):
                 for plane in range(PLANES):
                     at = (part * 2 + i) * HALF * PLANES + plane
-                    out[0, i, plane, pl.ds(first, HALF), :] = got[ORDER[b], pl.ds(at, HALF, stride=PLANES), :]
+                    out[0, i, plane, pl.ds(first, HALF), :] = got[ORDER[place], pl.ds(at, HALF, stride=PLANES), :]
 
 
 def sweep_rows(first, count, state, weights, earlier, into, step, source):
@@ -322,7 +326,7 @@
 
 
 def index(chip, core, strip):
-    return (chip * 2 + core) * BRICKS + ORDER[strip]
+    return (chip * 2 + core) * BRICKS + ORDER[strip if chip < RING else BRICKS - 1 - strip]
 
 
 def sent(value, chips, flip, shift):

time: 125 us -> 125 us (level)
  waiting for transfers between devices: 37.1 us -> 34.2 us
  starting transfers between devices: 17.5 us -> 19 us
  blocking collectives: 44.9 us -> 46.3 us
    ppermute x20, waiting for transfers between devices: 37.1 us -> 34.2 us  [sent(): return lax.ppermute(value, AXES, pairs)]
    ppermute x20, starting transfers between devices: 17.5 us -> 19 us  [sent(): return lax.ppermute(value, AXES, pairs)]
    all_to_all x1, blocking collectives: 13.1 us -> 14.5 us  [shards(): lax.all_to_all(jnp.concatenate([keep, swap(send)], axis=1), 'space', 0, 0...]
where the time goes in v11:
time: 125 us; the launch traced here: 124 us
  blocking collectives  46.3 us (37%)
  waiting for transfers between devices  34.2 us (27%)
  Pallas kernels  24.4 us (20%)
  starting transfers between devices  19 us (15%)
    ppermute x20, waiting for transfers between devices, sent(): return lax.ppermute(value, AXES, pairs)  34.2 us
    all_to_all x1, blocking collectives, shards(): got = lax.all_to_all(packed, 'space', 0, 0, tiled=True)  31.8 us
    ppermute x20, starting transfers between devices, sent(): return lax.ppermute(value, AXES, pairs)  19 us
    all_to_all x1, blocking collectives, shards(): lax.all_to_all(jnp.concatenate([keep, swap(send)], axis=1), 'space', 0, 0...  14.5 us
    pallas_call x4, Pallas kernels, leap(): call(body, outs, [VMEM] * len(operands), (VMEM,) * len(outs), [field, fie...  11 us
    pallas_call x1, Pallas kernels, shards(): call(relax_kernel, (pltpu.VMEM((ROWS, 2 * PAIR, NX, LAST), F32), half, sh...  10.2 us
  transfers between devices with their start and end apart: 20, of which 12 were waited for; matrix products, arithmetic and copies ran while one was open for 0% of the time, Pallas kernels for 9%

profile of v11, /device:TPU:4, one launch (start us, length us, event | category | flops | bytes accessed | tf_op | source)
XLA Modules:
  0.0 124.1 jit_solution(7095684516257622423)
XLA Ops:
  0.0 1.5 %shard_map.55 = f32[8,504,128]{2,1,0:T(8,128)S(1)} custom-call(f32[2,4,128,128]{3,2,1,0:T(8,128)} %startup.1, f32[1,2,4,128,128]{4,3,2,1,0:T(8,128)} %guess.1, f32[2,4,128,128]{3,2,1,0:T(8,128)} %conduct.1, f32[4,128,128]{2,1,0:T(8,128)} %couple.1), custom_call_target="tpu_custom_call" | custom-call | bytes 3145728 | tf_op jit(solution)/shard_map/pallas_call | solution.py:367
  1.5 31.8 %all_to_all.10.got = f32[8,504,128]{2,1,0:T(8,128)S(1)} all-to-all(f32[8,504,128]{2,1,0:T(8,128)S(1)} %shard_map.55), channel_id=1, replica_groups=mesh['chip'=8,'core'=2,'space'=8] {'space'}, dimensions={0} | all-to-all | bytes 4128768 | tf_op jit(solution)/shard_map/all_to_all | solution.py:380
  33.3 0.0 copy-start
  33.3 0.1 shard_map.56
  33.4 0.1 collective-permute-start
  33.5 2.4 %collective-permute-done.other = f32[3,18,32,128]{3,2,1,0:T(8,128)S(1)} collective-permute-done((f32[3,18,32,128]{3,2,1,0:T(8,128)S(1)}, f32[3,18,32,128]{3,2,1,0:T(8,128)S(1)}, u32[]{:S(2)}, u32[]{:S(2)}) %collective-permute-start) | collective-permute-done | bytes 884768 | tf_op jit(solution)/shard_map/ppermute | solution.py:339
  35.9 0.0 copy-done
  35.9 10.2 %shard_map.57 = (f32[36,18,32,128]{3,2,1,0:T(8,128)S(1)}, f32[2,8,32,128]{3,2,1,0:T(8,128)S(1)}, f32[4,8,32,128]{3,2,1,0:T(8,128)S(1)}, f32[2,8,32,128]{3,2,1,0:T(8,128)S(1)}) custom-call(f32[2,36,32,128]{3,2,1,0:T(8,128)S(1)} %get-tuple-element.42.begin, f32[3,18,32,128]{3,2,1,0:T(8,128)S(1)} %get-tuple-element.43.mine, ...), custom_call_target="tpu_custom_call" | custom-call | bytes 3145728 | tf_op jit(solution)/shard_map/pallas_call | solution.py:387
  46.1 0.2 collective-permute-start.1
  46.3 1.8 %collective-permute-done.1.taken = f32[4,8,32,128]{3,2,1,0:T(8,128)S(1)} collective-permute-done((f32[4,8,32,128]{3,2,1,0:T(8,128)S(1)}, f32[4,8,32,128]{3,2,1,0:T(8,128)S(1)}, u32[]{:S(2)}, u32[]{:S(2)}) %collective-permute-start.1) | collective-permute-done | bytes 524320 | tf_op jit(solution)/shard_map/ppermute | solution.py:339
  48.1 0.1 collective-permute-start.2
  48.2 8.3 %collective-permute-done.2.across = f32[2,8,32,128]{3,2,1,0:T(8,128)S(1)} collective-permute-done((f32[2,8,32,128]{3,2,1,0:T(8,128)S(1)}, f32[2,8,32,128]{3,2,1,0:T(8,128)S(1)}, u32[]{:S(2)}, u32[]{:S(2)}) %collective-permute-start.2) | collective-permute-done | bytes 262176 | tf_op jit(solution)/shard_map/ppermute | solution.py:339
  56.6 0.1 shard_map.58
  56.6 0.1 collective-permute-start.4
  56.7 0.3 collective-permute-start.3
  57.1 1.9 %collective-permute-start.7 = (f32[2,8,32,128]{3,2,1,0:T(8,128)S(1)}, f32[2,8,32,128]{3,2,1,0:T(8,128)S(1)}, u32[]{:S(2)}, u32[]{:S(2)}) collective-permute-start(f32[2,8,32,128]{3,2,1,0:T(8,128)S(1)} %get-tuple-element.47.own), channel_id=1, source_target_pairs={{0,16},{2,18},{4,20},{6,22},{7,23},{5,21},{3,19},{1,17},{8,24},{10... | collective-permute-start | bytes 786440 | tf_op jit(solution)/shard_map/ppermute | solution.py:339
  59.0 0.0 collective-permute-done.4.swapped
  59.0 3.6 %collective-permute-done.3.near = f32[2,8,32,128]{3,2,1,0:T(8,128)S(1)} collective-permute-done((f32[2,8,32,128]{3,2,1,0:T(8,128)S(1)}, f32[2,8,32,128]{3,2,1,0:T(8,128)S(1)}, u32[]{:S(2)}, u32[]{:S(2)}) %collective-permute-start.3) | collective-permute-done | bytes 262176 | tf_op jit(solution)/shard_map/ppermute | solution.py:339
  62.6 3.2 %shard_map.59 = (f32[2,8,32,128]{3,2,1,0:T(8,128)S(1)}, f32[2,8,32,128]{3,2,1,0:T(8,128)S(1)}) custom-call(f32[2,8,32,128]{3,2,1,0:T(8,128)S(1)} %get-tuple-element.47.own, f32[2,8,32,128]{3,2,1,0:T(8,128)S(1)} %collective-permute-done.3.near, f32[2,8,32,128]{3,2,1,0:T(8,128)S(1)} %collective-permute-done.4.swapped, f32[36,18,32,128]{3,2,1,0:T(8,128)S(1)} %get-tuple-element.50.w), custom_call_target="tpu_custom_call" | custom-call | bytes 15728640 | tf_op jit(solution)/shard_map/pallas_call | solution.py:402
  65.9 0.8 collective-permute-start.6
  66.6 0.0 collective-permute-start.5
  66.6 4.0 %collective-permute-start.11 = (f32[2,8,32,128]{3,2,1,0:T(8,128)S(1)}, f32[2,8,32,128]{3,2,1,0:T(8,128)S(1)}, u32[]{:S(2)}, u32[]{:S(2)}) collective-permute-start(f32[2,8,32,128]{3,2,1,0:T(8,128)S(1)} %get-tuple-element.53.own), channel_id=1, source_target_pairs={{0,48},{2,50},{4,52},{6,54},{7,55},{5,53},{3,51},{1,49},{8,56},{10... | collective-permute-start | bytes 786440 | tf_op jit(solution)/shard_map/ppermute | solution.py:339
  70.7 0.0 collective-permute-start.10
  70.7 0.0 collective-permute-done.7.refs_0_
  70.7 0.0 collective-permute-done.6.swapped
  70.7 1.7 %collective-permute-done.5.near = f32[2,8,32,128]{3,2,1,0:T(8,128)S(1)} collective-permute-done((f32[2,8,32,128]{3,2,1,0:T(8,128)S(1)}, f32[2,8,32,128]{3,2,1,0:T(8,128)S(1)}, u32[]{:S(2)}, u32[]{:S(2)}) %collective-permute-start.5) | collective-permute-done | bytes 262176 | tf_op jit(solution)/shard_map/ppermute | solution.py:339
  72.4 3.3 %shard_map.60 = (f32[2,8,32,128]{3,2,1,0:T(8,128)S(1)}, f32[2,8,32,128]{3,2,1,0:T(8,128)S(1)}) custom-call(f32[2,8,32,128]{3,2,1,0:T(8,128)S(1)} %get-tuple-element.53.own, f32[2,8,32,128]{3,2,1,0:T(8,128)S(1)} %collective-permute-done.5.near, f32[2,8,32,128]{3,2,1,0:T(8,128)S(1)} %collective-permute-done.6.swapped, ...), custom_call_target="tpu_custom_call" | custom-call | bytes 15728640 | tf_op jit(solution)/shard_map/pallas_call | solution.py:402
  75.7 0.5 collective-permute-start.9
  76.2 0.0 collective-permute-start.8
  76.2 1.9 %collective-permute-start.14 = (f32[2,8,32,128]{3,2,1,0:T(8,128)S(1)}, f32[2,8,32,128]{3,2,1,0:T(8,128)S(1)}, u32[]{:S(2)}, u32[]{:S(2)}) collective-permute-start(f32[2,8,32,128]{3,2,1,0:T(8,128)S(1)} %get-tuple-element.62.own), channel_id=1, source_target_pairs={{0,16},{2,18},{4,20},{6,22},{7,23},{5,21},{3,19},{1,17},{8,24},{10... | collective-permute-start | bytes 786440 | tf_op jit(solution)/shard_map/ppermute | solution.py:339
  78.1 2.7 %collective-permute-done.10.refs_1_ = f32[2,8,32,128]{3,2,1,0:T(8,128)S(1)} collective-permute-done((f32[2,8,32,128]{3,2,1,0:T(8,128)S(1)}, f32[2,8,32,128]{3,2,1,0:T(8,128)S(1)}, u32[]{:S(2)}, u32[]{:S(2)}) %collective-permute-start.10) | collective-permute-done | bytes 262176 | tf_op jit(solution)/shard_map/ppermute | solution.py:339
  80.8 1.3 %collective-permute-done.11.refs_2_ = f32[2,8,32,128]{3,2,1,0:T(8,128)S(1)} collective-permute-done((f32[2,8,32,128]{3,2,1,0:T(8,128)S(1)}, f32[2,8,32,128]{3,2,1,0:T(8,128)S(1)}, u32[]{:S(2)}, u32[]{:S(2)}) %collective-permute-start.11) | collective-permute-done | bytes 262176 | tf_op jit(solution)/shard_map/ppermute | solution.py:339
  82.1 0.0 collective-permute-done.9.swapped
  82.1 0.0 collective-permute-done.8.near
  82.1 3.3 %shard_map.61 = (f32[2,8,32,128]{3,2,1,0:T(8,128)S(1)}, f32[2,8,32,128]{3,2,1,0:T(8,128)S(1)}, f32[2,4,32,128]{3,2,1,0:T(8,128)S(1)}, f32[2,4,32,128]{3,2,1,0:T(8,128)S(1)}) custom-call(f32[2,8,32,128]{3,2,1,0:T(8,128)S(1)} %get-tuple-element.62.own, f32[2,8,32,128]{3,2,1,0:T(8,128)S(1)} %collective-permute-done.8.near, ...), custom_call_target="tpu_custom_call" | custom-call | bytes 15728640 | tf_op jit(solution)/shard_map/pallas_call | solution.py:402
  85.4 3.9 %collective-permute-start.15 = (f32[2,8,32,128]{3,2,1,0:T(8,128)S(1)}, f32[2,8,32,128]{3,2,1,0:T(8,128)S(1)}, u32[]{:S(2)}, u32[]{:S(2)}) collective-permute-start(f32[2,8,32,128]{3,2,1,0:T(8,128)S(1)} %get-tuple-element.69), channel_id=1, source_target_pairs={{0,32},{2,34},{4,36},{6,38},{7,39},{5,37},{3,35},{1,33},{8,40},{10... | collective-permute-start | bytes 786440 | tf_op jit(solution)/shard_map/ppermute | solution.py:339
  89.3 0.7 collective-permute-start.16
  90.0 0.5 collective-permute-start.12
  90.5 1.9 %collective-permute-start.13 = (f32[2,4,32,128]{3,2,1,0:T(8,128)S(1)}, f32[2,4,32,128]{3,2,1,0:T(8,128)S(1)}, u32[]{:S(2)}, u32[]{:S(2)}) collective-permute-start(f32[2,4,32,128]{3,2,1,0:T(8,128)S(1)} %get-tuple-element.67), channel_id=1, source_target_pairs={{8,0},{10,2},{12,4},{14,6},{15,7},{13,5},{11,3},{9,1},{0,8},{2,10}... | collective-permute-start | bytes 393224 | tf_op jit(solution)/shard_map/ppermute | solution.py:339
  92.3 0.0 collective-permute-done.14.refs_4_
  92.4 2.0 %collective-permute-done.12.near = f32[2,4,32,128]{3,2,1,0:T(8,128)S(1)} collective-permute-done((f32[2,4,32,128]{3,2,1,0:T(8,128)S(1)}, f32[2,4,32,128]{3,2,1,0:T(8,128)S(1)}, u32[]{:S(2)}, u32[]{:S(2)}) %collective-permute-start.12) | collective-permute-done | bytes 131104 | tf_op jit(solution)/shard_map/ppermute | solution.py:339
  94.3 0.0 collective-permute-done.13.swapped
  94.4 1.2 shard_map.62.refs_7_
  95.6 0.6 collective-permute-done.15.refs_5_
  96.2 6.4 %collective-permute-done.16.refs_6_ = f32[2,8,32,128]{3,2,1,0:T(8,128)S(1)} collective-permute-done((f32[2,8,32,128]{3,2,1,0:T(8,128)S(1)}, f32[2,8,32,128]{3,2,1,0:T(8,128)S(1)}, u32[]{:S(2)}, u32[]{:S(2)}) %collective-permute-start.16) | collective-permute-done | bytes 262176 | tf_op jit(solution)/shard_map/ppermute | solution.py:339
  102.6 0.2 shard_map.63
  102.7 0.1 collective-permute-start.17
  102.8 1.8 %collective-permute-start.18 = (f32[2,2,32,128]{3,2,1,0:T(8,128)S(1)}, f32[2,2,32,128]{3,2,1,0:T(8,128)S(1)}, u32[]{:S(2)}, u32[]{:S(2)}) collective-permute-start(f32[2,2,32,128]{3,2,1,0:T(8,128)S(1)} %get-tuple-element.75), channel_id=1, source_target_pairs={{8,0},{10,2},{12,4},{14,6},{15,7},{13,5},{11,3},{9,1},{0,8},{2,10}... | collective-permute-start | bytes 196616 | tf_op jit(solution)/shard_map/ppermute | solution.py:339
  104.6 1.9 %collective-permute-done.17.near = f32[2,2,32,128]{3,2,1,0:T(8,128)S(1)} collective-permute-done((f32[2,2,32,128]{3,2,1,0:T(8,128)S(1)}, f32[2,2,32,128]{3,2,1,0:T(8,128)S(1)}, u32[]{:S(2)}, u32[]{:S(2)}) %collective-permute-start.17) | collective-permute-done | bytes 65568 | tf_op jit(solution)/shard_map/ppermute | solution.py:339
  106.5 0.0 collective-permute-done.18.swapped
  106.5 0.6 shard_map.64
  107.1 0.2 collective-permute-start.19
  107.3 1.4 %collective-permute-done.19 = f32[8,64,128]{2,1,0:T(8,128)S(1)} collective-permute-done((f32[8,64,128]{2,1,0:T(8,128)S(1)}, f32[8,64,128]{2,1,0:T(8,128)S(1)}, u32[]{:S(2)}, u32[]{:S(2)}) %collective-permute-start.19) | collective-permute-done | bytes 262176 | tf_op jit(solution)/shard_map/ppermute | solution.py:339
  108.7 14.5 %all_to_all.11.got = f32[8,128,128]{2,1,0:T(8,128)S(1)} all-to-all(f32[8,128,128]{2,1,0:T(8,128)S(1)} %pad_maximum_fusion), channel_id=1, replica_groups=mesh['chip'=8,'core'=2,'space'=8] {'space'}, dimensions={0} | all-to-all | bytes 1048576 | tf_op jit(solution)/shard_map/all_to_all | solution.py:424
  123.2 0.9 shard_map.65
  (2 shorter events, 0.1 us)
Async XLA Ops:
  33.3 2.7 %copy-start = (f32[128,128]{1,0:T(8,128)S(1)}, f32[128,128]{1,0:T(8,128)}, u32[]{:S(2)}) copy-start(f32[128,128]{1,0:T(8,128)} %inlet.1) | copy-start | bytes 196612
  33.4 2.5 %collective-permute-start = (f32[3,18,32,128]{3,2,1,0:T(8,128)S(1)}, f32[3,18,32,128]{3,2,1,0:T(8,128)S(1)}, u32[]{:S(2)}, u32[]{:S(2)}) collective-permute-start(f32[3,18,32,128]{3,2,1,0:T(8,128)S(1)} %get-tuple-element.43.mine), channel_id=1, source_target_pairs={{8,0},{10,2},{12,4},{14,6},{15,7},{13,5},{11,3},{9,1},{0,8},{2,10}... | collective-permute-start | bytes 2654216 | tf_op jit(solution)/shard_map/ppermute | solution.py:339
  46.1 2.0 %collective-permute-start.1 = (f32[4,8,32,128]{3,2,1,0:T(8,128)S(1)}, f32[4,8,32,128]{3,2,1,0:T(8,128)S(1)}, u32[]{:S(2)}, u32[]{:S(2)}) collective-permute-start(f32[4,8,32,128]{3,2,1,0:T(8,128)S(1)} %get-tuple-element.45), channel_id=1, source_target_pairs={{8,0},{10,2},{12,4},{14,6},{15,7},{13,5},{11,3},{9,1},{0,8},{2,10}... | collective-permute-start | bytes 1572872 | tf_op jit(solution)/shard_map/ppermute | solution.py:339
  48.1 8.4 %collective-permute-start.2 = (f32[2,8,32,128]{3,2,1,0:T(8,128)S(1)}, f32[2,8,32,128]{3,2,1,0:T(8,128)S(1)}, u32[]{:S(2)}, u32[]{:S(2)}) collective-permute-start(f32[2,8,32,128]{3,2,1,0:T(8,128)S(1)} %slice_add_fusion.ours), channel_id=1, source_target_pairs={{65,0},{67,2},{69,4},{71,6},{70,7},{68,5},{66,3},{64,1},{73,8},{75... | collective-permute-start | bytes 786440 | tf_op jit(solution)/shard_map/ppermute | solution.py:339
  56.6 2.4 %collective-permute-start.4 = (f32[2,8,32,128]{3,2,1,0:T(8,128)S(1)}, f32[2,8,32,128]{3,2,1,0:T(8,128)S(1)}, u32[]{:S(2)}, u32[]{:S(2)}) collective-permute-start(f32[2,8,32,128]{3,2,1,0:T(8,128)S(1)} %get-tuple-element.47.own), channel_id=1, source_target_pairs={{8,0},{10,2},{12,4},{14,6},{15,7},{13,5},{11,3},{9,1},{0,8},{2,10}... | collective-permute-start | bytes 786440 | tf_op jit(solution)/shard_map/ppermute | solution.py:339
  56.7 5.9 %collective-permute-start.3 = (f32[2,8,32,128]{3,2,1,0:T(8,128)S(1)}, f32[2,8,32,128]{3,2,1,0:T(8,128)S(1)}, u32[]{:S(2)}, u32[]{:S(2)}) collective-permute-start(f32[2,8,32,128]{3,2,1,0:T(8,128)S(1)} %get-tuple-element.47.own), channel_id=1, source_target_pairs={{8,2},{10,4},{12,6},{14,7},{15,5},{13,3},{11,1},{9,0},{0,9},{2,8},... | collective-permute-start | bytes 786440 | tf_op jit(solution)/shard_map/ppermute | solution.py:339
  57.1 13.6 %collective-permute-start.7 = (f32[2,8,32,128]{3,2,1,0:T(8,128)S(1)}, f32[2,8,32,128]{3,2,1,0:T(8,128)S(1)}, u32[]{:S(2)}, u32[]{:S(2)}) collective-permute-start(f32[2,8,32,128]{3,2,1,0:T(8,128)S(1)} %get-tuple-element.47.own), channel_id=1, source_target_pairs={{0,16},{2,18},{4,20},{6,22},{7,23},{5,21},{3,19},{1,17},{8,24},{10... | collective-permute-start | bytes 786440 | tf_op jit(solution)/shard_map/ppermute | solution.py:339
  65.9 4.8 %collective-permute-start.6 = (f32[2,8,32,128]{3,2,1,0:T(8,128)S(1)}, f32[2,8,32,128]{3,2,1,0:T(8,128)S(1)}, u32[]{:S(2)}, u32[]{:S(2)}) collective-permute-start(f32[2,8,32,128]{3,2,1,0:T(8,128)S(1)} %get-tuple-element.53.own), channel_id=1, source_target_pairs={{8,0},{10,2},{12,4},{14,6},{15,7},{13,5},{11,3},{9,1},{0,8},{2,10}... | collective-permute-start | bytes 786440 | tf_op jit(solution)/shard_map/ppermute | solution.py:339
  66.6 5.8 %collective-permute-start.5 = (f32[2,8,32,128]{3,2,1,0:T(8,128)S(1)}, f32[2,8,32,128]{3,2,1,0:T(8,128)S(1)}, u32[]{:S(2)}, u32[]{:S(2)}) collective-permute-start(f32[2,8,32,128]{3,2,1,0:T(8,128)S(1)} %get-tuple-element.53.own), channel_id=1, source_target_pairs={{8,2},{10,4},{12,6},{14,7},{15,5},{13,3},{11,1},{9,0},{0,9},{2,8},... | collective-permute-start | bytes 786440 | tf_op jit(solution)/shard_map/ppermute | solution.py:339
  66.6 15.5 %collective-permute-start.11 = (f32[2,8,32,128]{3,2,1,0:T(8,128)S(1)}, f32[2,8,32,128]{3,2,1,0:T(8,128)S(1)}, u32[]{:S(2)}, u32[]{:S(2)}) collective-permute-start(f32[2,8,32,128]{3,2,1,0:T(8,128)S(1)} %get-tuple-element.53.own), channel_id=1, source_target_pairs={{0,48},{2,50},{4,52},{6,54},{7,55},{5,53},{3,51},{1,49},{8,56},{10... | collective-permute-start | bytes 786440 | tf_op jit(solution)/shard_map/ppermute | solution.py:339
  70.7 10.1 %collective-permute-start.10 = (f32[2,8,32,128]{3,2,1,0:T(8,128)S(1)}, f32[2,8,32,128]{3,2,1,0:T(8,128)S(1)}, u32[]{:S(2)}, u32[]{:S(2)}) collective-permute-start(f32[2,8,32,128]{3,2,1,0:T(8,128)S(1)} %get-tuple-element.58), channel_id=1, source_target_pairs={{0,32},{2,34},{4,36},{6,38},{7,39},{5,37},{3,35},{1,33},{8,40},{10... | collective-permute-start | bytes 786440 | tf_op jit(solution)/shard_map/ppermute | solution.py:339
  75.7 6.4 %collective-permute-start.9 = (f32[2,8,32,128]{3,2,1,0:T(8,128)S(1)}, f32[2,8,32,128]{3,2,1,0:T(8,128)S(1)}, u32[]{:S(2)}, u32[]{:S(2)}) collective-permute-start(f32[2,8,32,128]{3,2,1,0:T(8,128)S(1)} %get-tuple-element.62.own), channel_id=1, source_target_pairs={{8,0},{10,2},{12,4},{14,6},{15,7},{13,5},{11,3},{9,1},{0,8},{2,10}... | collective-permute-start | bytes 786440 | tf_op jit(solution)/shard_map/ppermute | solution.py:339
  76.2 5.9 %collective-permute-start.8 = (f32[2,8,32,128]{3,2,1,0:T(8,128)S(1)}, f32[2,8,32,128]{3,2,1,0:T(8,128)S(1)}, u32[]{:S(2)}, u32[]{:S(2)}) collective-permute-start(f32[2,8,32,128]{3,2,1,0:T(8,128)S(1)} %get-tuple-element.62.own), channel_id=1, source_target_pairs={{8,2},{10,4},{12,6},{14,7},{15,5},{13,3},{11,1},{9,0},{0,9},{2,8},... | collective-permute-start | bytes 786440 | tf_op jit(solution)/shard_map/ppermute | solution.py:339
  76.2 16.1 %collective-permute-start.14 = (f32[2,8,32,128]{3,2,1,0:T(8,128)S(1)}, f32[2,8,32,128]{3,2,1,0:T(8,128)S(1)}, u32[]{:S(2)}, u32[]{:S(2)}) collective-permute-start(f32[2,8,32,128]{3,2,1,0:T(8,128)S(1)} %get-tuple-element.62.own), channel_id=1, source_target_pairs={{0,16},{2,18},{4,20},{6,22},{7,23},{5,21},{3,19},{1,17},{8,24},{10... | collective-permute-start | bytes 786440 | tf_op jit(solution)/shard_map/ppermute | solution.py:339
  85.4 10.8 %collective-permute-start.15 = (f32[2,8,32,128]{3,2,1,0:T(8,128)S(1)}, f32[2,8,32,128]{3,2,1,0:T(8,128)S(1)}, u32[]{:S(2)}, u32[]{:S(2)}) collective-permute-start(f32[2,8,32,128]{3,2,1,0:T(8,128)S(1)} %get-tuple-element.69), channel_id=1, source_target_pairs={{0,32},{2,34},{4,36},{6,38},{7,39},{5,37},{3,35},{1,33},{8,40},{10... | collective-permute-start | bytes 786440 | tf_op jit(solution)/shard_map/ppermute | solution.py:339
  89.3 13.3 %collective-permute-start.16 = (f32[2,8,32,128]{3,2,1,0:T(8,128)S(1)}, f32[2,8,32,128]{3,2,1,0:T(8,128)S(1)}, u32[]{:S(2)}, u32[]{:S(2)}) collective-permute-start(f32[2,8,32,128]{3,2,1,0:T(8,128)S(1)} %get-tuple-element.70.own), channel_id=1, source_target_pairs={{0,48},{2,50},{4,52},{6,54},{7,55},{5,53},{3,51},{1,49},{8,56},{10... | collective-permute-start | bytes 786440 | tf_op jit(solution)/shard_map/ppermute | solution.py:339
  90.0 4.4 %collective-permute-start.12 = (f32[2,4,32,128]{3,2,1,0:T(8,128)S(1)}, f32[2,4,32,128]{3,2,1,0:T(8,128)S(1)}, u32[]{:S(2)}, u32[]{:S(2)}) collective-permute-start(f32[2,4,32,128]{3,2,1,0:T(8,128)S(1)} %get-tuple-element.66), channel_id=1, source_target_pairs={{8,2},{10,4},{12,6},{14,7},{15,5},{13,3},{11,1},{9,0},{0,9},{2,8},... | collective-permute-start | bytes 393224 | tf_op jit(solution)/shard_map/ppermute | solution.py:339
  90.5 3.9 %collective-permute-start.13 = (f32[2,4,32,128]{3,2,1,0:T(8,128)S(1)}, f32[2,4,32,128]{3,2,1,0:T(8,128)S(1)}, u32[]{:S(2)}, u32[]{:S(2)}) collective-permute-start(f32[2,4,32,128]{3,2,1,0:T(8,128)S(1)} %get-tuple-element.67), channel_id=1, source_target_pairs={{8,0},{10,2},{12,4},{14,6},{15,7},{13,5},{11,3},{9,1},{0,8},{2,10}... | collective-permute-start | bytes 393224 | tf_op jit(solution)/shard_map/ppermute | solution.py:339
  102.7 3.8 %collective-permute-start.17 = (f32[2,2,32,128]{3,2,1,0:T(8,128)S(1)}, f32[2,2,32,128]{3,2,1,0:T(8,128)S(1)}, u32[]{:S(2)}, u32[]{:S(2)}) collective-permute-start(f32[2,2,32,128]{3,2,1,0:T(8,128)S(1)} %get-tuple-element.74), channel_id=1, source_target_pairs={{8,2},{10,4},{12,6},{14,7},{15,5},{13,3},{11,1},{9,0},{0,9},{2,8},... | collective-permute-start | bytes 196616 | tf_op jit(solution)/shard_map/ppermute | solution.py:339
  102.8 3.7 %collective-permute-start.18 = (f32[2,2,32,128]{3,2,1,0:T(8,128)S(1)}, f32[2,2,32,128]{3,2,1,0:T(8,128)S(1)}, u32[]{:S(2)}, u32[]{:S(2)}) collective-permute-start(f32[2,2,32,128]{3,2,1,0:T(8,128)S(1)} %get-tuple-element.75), channel_id=1, source_target_pairs={{8,0},{10,2},{12,4},{14,6},{15,7},{13,5},{11,3},{9,1},{0,8},{2,10}... | collective-permute-start | bytes 196616 | tf_op jit(solution)/shard_map/ppermute | solution.py:339
  107.1 1.6 %collective-permute-start.19 = (f32[8,64,128]{2,1,0:T(8,128)S(1)}, f32[8,64,128]{2,1,0:T(8,128)S(1)}, u32[]{:S(2)}, u32[]{:S(2)}) collective-permute-start(f32[8,64,128]{2,1,0:T(8,128)S(1)} %get-tuple-element.78), channel_id=1, source_target_pairs={{8,0},{10,2},{12,4},{14,6},{15,7},{13,5},{11,3},{9,1},{0,8},{2,10}... | collective-permute-start | bytes 786440 | tf_op jit(solution)/shard_map/ppermute | solution.py:339

commit v12 on v11

--- a/solution.py
+++ b/solution.py
@@ -19,7 +19,7 @@
 HALF = 8
 EDGE = 10
 ROWS = STRIP + 2 * EDGE
-LONGEST = 12
+LONGEST = 22
 PART = ROWS // 2
 
 RATE_ALONG = 4.0
@@ -43,9 +43,10 @@
     return jax.ShapeDtypeStruct(dims, F32)
 
 
-def call(body, outs, in_specs, out_specs, scratch, limit, us=1):
+def call(body, outs, in_specs, out_specs, scratch, limit, us=1, aliases={}):
     return pl.pallas_call(
         body,
+        input_output_aliases=aliases,
         cost_estimate=pl.CostEstimate(flops=0, bytes_accessed=us * (3 << 20), transcendentals=0),
         out_shape=outs,
         in_specs=in_specs,
@@ -183,25 +184,21 @@
         sweep(v, weights, e, e, low + 2 * m + 2, count - 4 * m - 4, step, source)
 
 
-def relax_kernel(begin, mine, other, inlet, w, base, give, own, c, feed, e, v, e0):
-    core, strip, slab = position()
-    c[:, pl.ds(PART * core, PART)] = mine[...]
-    c[:, pl.ds(PART - PART * core, PART)] = other[...]
-    e[:, :ROWS] = begin[...]
-    e0[:, :ROWS] = begin[...]
-
+def weigh(first, count, c, offset, inlet, w, feed):
+    _, strip, _ = position()
     plane = lax.broadcasted_iota(jnp.int32, (NX, LAST), 0)
     column = lax.broadcasted_iota(jnp.int32, (NX, LAST), 1)
     top = lax.broadcasted_iota(jnp.int32, (8, LAST), 0) == 0
 
-    def weigh(r):
+    def row(r):
+        at = r - offset
         y = strip * STRIP - EDGE + r
         lower = jnp.where(y == 0, 0.0, 1.0).astype(F32)
         upper = jnp.where(y == MIDDLE - 1, 0.0, 1.0).astype(F32)
-        exchange = c[2, r]
+        exchange = c[2, at]
         warmth = inlet[pl.ds(jnp.clip(y, 0, MIDDLE - 1), 1), :]
         for i in range(2):
-            here = c[i, r]
+            here = c[i, at]
             xm = jnp.where(plane == 0, 0.0, pltpu.roll(here, 1, 0))
             xp = jnp.where(plane == NX - 1, 0.0, pltpu.roll(here, NX - 1, 0))
             zm = jnp.where(column == 0, 0.0, pltpu.roll(here, 1, 1))
@@ -211,8 +208,8 @@
             if i == 1:
                 wxm = wxm + ADVECTION
             wxp = half_along * (here + xp)
-            wym = half_across * (here + c[i, r - 1])
-            wyp = half_across * (here + c[i, r + 1])
+            wym = half_across * (here + c[i, at - 1])
+            wyp = half_across * (here + c[i, at + 1])
             wzm = half_across * (here + zm)
             wzp = half_across * (here + zp)
             outflow = wxm + wxp + wym + wyp + wzm + wzp + exchange
@@ -232,12 +229,29 @@
             if i == 1:
                 feed[r] = jnp.where(top, wxm[:8] * warmth, 0.0)
 
-    def weigh_two(k, carry):
-        weigh(1 + 2 * k)
-        weigh(2 + 2 * k)
+    def two(k, carry):
+        row(first + 2 * k)
+        row(first + 2 * k + 1)
         return carry
 
-    lax.fori_loop(0, (ROWS - 2) // 2, weigh_two, 0)
+    lax.fori_loop(0, count // 2, two, 0)
+
+
+def weigh_kernel(mine, inlet, w, feed):
+    core, _, _ = position()
+    weigh(PART * core + 1, PART - 2, mine, PART * core, inlet, w, feed)
+
+
+def relax_kernel(begin, mine, other, inlet, w_mine, feed_mine, w, base, give, own, beyond, c, feed, e, v, e0):
+    core, _, slab = position()
+    c[:, pl.ds(PART * core, PART)] = mine[...]
+    c[:, pl.ds(PART - PART * core, PART)] = other[...]
+    e[...] = begin[...]
+    e0[...] = begin[...]
+    ready = pl.ds(PART * core + 1, PART - 2)
+    feed[ready] = feed_mine[ready]
+    weigh(PART - 1 - (PART - 2) * core, PART, c, 0, inlet, w, feed)
+
     sweep(e0, w, None, v, EDGE - 3, STRIP + 6, COARSE)
     sweep(v, w, e0, e0, EDGE - 2, STRIP + 4, COARSE)
     advances(4, e, v, w, 0, ROWS, FINE, feed)
@@ -249,9 +263,9 @@
     joined = jnp.where(slab == SLABS - 2, 0.0, 1.0).astype(F32)
     near, far = pl.ds(EDGE, HALF), pl.ds(EDGE + HALF, HALF)
     base[...] = jnp.where(core == 0, joined * e0[:, near], e[:, far])
-    give[0:2] = jnp.where(core == 0, joined * e0[:, far], e[:, near])
-    give[2:4] = e[:, far]
+    give[...] = jnp.where(core == 0, joined * e0[:, far], e[:, near])
     own[...] = e[:, near]
+    beyond[...] = e[:, far]
 
 
 def place(core, state, middle, inward, outward):
@@ -311,7 +325,7 @@
     place(core, r, middle, swapped, near)
     sweep(r, w, None, v, middle - 1, HALF + 2, COARSE)
     sweep(v, w, r, e, middle, HALF, COARSE)
-    e[:, rows] = e[:, rows] + jnp.where(core == 0, g[...], taken[2:4])
+    e[:, rows] = e[:, rows] + jnp.where(core == 0, g[...], taken[...])
     low = lax.broadcasted_iota(jnp.int32, (8, LAST), 0) < PLANES
     for out, other in ((keep, 0), (send, 1)):
         pick = lambda *at: jnp.where(core == other, r[at], e[at])
@@ -384,16 +398,20 @@
     other = swap(mine)
 
     field = pltpu.VMEM((2, ROWS, NX, LAST), F32)
-    weights, base, give, g = call(
+    all_weights = pltpu.VMEM((ROWS, 2 * PAIR, NX, LAST), F32)
+    weights, feed = call(
+        weigh_kernel, (all_weights, shape(ROWS, 8, LAST)), [VMEM] * 2, (VMEM,) * 2, [], 16, 3
+    )(mine, inlet)
+    weights, base, give, g, beyond = call(
         relax_kernel,
-        (pltpu.VMEM((ROWS, 2 * PAIR, NX, LAST), F32), half, shape(4, HALF, NX, LAST), half),
-        [VMEM] * 4,
-        (VMEM,) * 4,
+        (all_weights, half, half, half, half),
+        [VMEM] * 6,
+        (VMEM,) * 5,
         [pltpu.VMEM((3, ROWS, NX, LAST), F32), pltpu.VMEM((ROWS, 8, LAST), F32), field, field, field],
         24,
-    )(begin, mine, other, inlet)
-    taken = swap(give)
-    u = base + taken[:2]
+        aliases={4: 0},
+    )(begin, mine, other, inlet, weights, feed)
+    u = base + swap(give)
 
     def leap(own, near, swapped, *rims, second=True, high=None):
         outs = (half,) * (1 + second) + rims
@@ -405,8 +423,8 @@
     rim4, rim2 = shape(2, 4, NX, LAST), shape(2, 2, NX, LAST)
     a0 = along(low, 0)
     u1, u2 = leap(*exchanged(low, low, low))
-    a1, a2 = along(u1, 1), along(u2, 2)
-    *operands, a0 = exchanged(u2, u2, u2, a0)
+    a1, a2, taken = along(u1, 1), along(u2, 2), swap(beyond)
+    *operands, a0, taken = exchanged(u2, u2, u2, a0, taken)
     u3, u4 = leap(*operands, high=high)
     a4 = along(u4, 4)
     *operands, a1, a2 = exchanged(u4, u4, u4, a1, a2)

time: 125 us -> 122 us (0.976)
  waiting for transfers between devices: 34.2 us -> 30.9 us
  starting transfers between devices: 19 us -> 20.7 us
    ppermute x20 -> x21, waiting for transfers between devices: 34.2 us -> 30.9 us  [sent(): return lax.ppermute(value, AXES, pairs)]
    ppermute x20 -> x21, starting transfers between devices: 19 us -> 20.7 us  [sent(): return lax.ppermute(value, AXES, pairs)]
    pallas_call x1 -> x2, Pallas kernels: 10.2 us -> 9.8 us  [the longest x1 8.81 us: shards(): call(relax_kernel, (all_weights, half, half, half, half), [VMEM] * 6, (VM...]
  transfers between devices with their start and end apart: 20 -> 21, of which waited for: 12 -> 12; matrix products, arithmetic and copies ran while one was open for 0% -> 0% of each run, Pallas kernels for 9% -> 9%
where the time goes in v12:
time: 122 us
  blocking collectives  46.3 us (38%)
  waiting for transfers between devices  30.9 us (25%)
  Pallas kernels  23.2 us (19%)
  starting transfers between devices  20.7 us (17%)
    all_to_all x1, blocking collectives, shards(): got = lax.all_to_all(packed, 'space', 0, 0, tiled=True)  31.8 us
    ppermute x21, waiting for transfers between devices, sent(): return lax.ppermute(value, AXES, pairs)  30.9 us
    ppermute x21, starting transfers between devices, sent(): return lax.ppermute(value, AXES, pairs)  20.7 us
    all_to_all x1, blocking collectives, shards(): lax.all_to_all(jnp.concatenate([keep, swap(send)], axis=1), 'space', 0, 0...  14.5 us
    pallas_call x4, Pallas kernels, leap(): call(body, outs, [VMEM] * len(operands), (VMEM,) * len(outs), [field, fie...  10.2 us
    pallas_call x1, Pallas kernels, shards(): call(relax_kernel, (all_weights, half, half, half, half), [VMEM] * 6, (VM...  8.81 us
  transfers between devices with their start and end apart: 21, of which 12 were waited for; matrix products, arithmetic and copies ran while one was open for 0% of the time, Pallas kernels for 9%

profile of v12, /device:TPU:4, one launch (start us, length us, event | category | flops | bytes accessed | tf_op | source)
XLA Modules:
  0.0 121.9 jit_solution(15089433773228667448)
XLA Ops:
  0.0 1.5 %shard_map.55 = f32[8,504,128]{2,1,0:T(8,128)S(1)} custom-call(f32[2,4,128,128]{3,2,1,0:T(8,128)} %startup.1, f32[1,2,4,128,128]{4,3,2,1,0:T(8,128)} %guess.1, f32[2,4,128,128]{3,2,1,0:T(8,128)} %conduct.1, f32[4,128,128]{2,1,0:T(8,128)} %couple.1), custom_call_target="tpu_custom_call" | custom-call | bytes 3145728 | tf_op jit(solution)/shard_map/pallas_call | solution.py:381
  1.5 31.8 %all_to_all.10.got = f32[8,504,128]{2,1,0:T(8,128)S(1)} all-to-all(f32[8,504,128]{2,1,0:T(8,128)S(1)} %shard_map.55), channel_id=1, replica_groups=mesh['chip'=8,'core'=2,'space'=8] {'space'}, dimensions={0} | all-to-all | bytes 4128768 | tf_op jit(solution)/shard_map/all_to_all | solution.py:394
  33.3 0.0 copy-start
  33.3 0.1 shard_map.56
  33.4 0.1 collective-permute-start
  33.5 0.6 copy-done
  34.1 1.0 shard_map.57
  35.1 0.8 collective-permute-done.other
  35.9 8.8 %shard_map.58 = (f32[36,18,32,128]{3,2,1,0:T(8,128)S(1)}, f32[2,8,32,128]{3,2,1,0:T(8,128)S(1)}, f32[2,8,32,128]{3,2,1,0:T(8,128)S(1)}, f32[2,8,32,128]{3,2,1,0:T(8,128)S(1)}, f32[2,8,32,128]{3,2,1,0:T(8,128)S(1)}) custom-call(f32[2,36,32,128]{3,2,1,0:T(8,128)S(1)} %get-tuple-element.46.begin, ...), custom_call_target="tpu_custom_call", output_to_operand_aliasing={{0}: (4, {})} | custom-call | bytes 3145728 | tf_op jit(solution)/shard_map/pallas_call | solution.py:405
  44.7 0.2 collective-permute-start.1
  45.0 1.4 %collective-permute-done.1 = f32[2,8,32,128]{3,2,1,0:T(8,128)S(1)} collective-permute-done((f32[2,8,32,128]{3,2,1,0:T(8,128)S(1)}, f32[2,8,32,128]{3,2,1,0:T(8,128)S(1)}, u32[]{:S(2)}, u32[]{:S(2)}) %collective-permute-start.1) | collective-permute-done | bytes 262176 | tf_op jit(solution)/shard_map/ppermute | solution.py:353
  46.4 0.1 collective-permute-start.2
  46.5 8.3 %collective-permute-done.2.across = f32[2,8,32,128]{3,2,1,0:T(8,128)S(1)} collective-permute-done((f32[2,8,32,128]{3,2,1,0:T(8,128)S(1)}, f32[2,8,32,128]{3,2,1,0:T(8,128)S(1)}, u32[]{:S(2)}, u32[]{:S(2)}) %collective-permute-start.2) | collective-permute-done | bytes 262176 | tf_op jit(solution)/shard_map/ppermute | solution.py:353
  54.8 0.1 shard_map.59
  54.9 0.1 collective-permute-start.4
  55.0 0.3 collective-permute-start.3
  55.3 1.6 %collective-permute-start.8 = (f32[2,8,32,128]{3,2,1,0:T(8,128)S(1)}, f32[2,8,32,128]{3,2,1,0:T(8,128)S(1)}, u32[]{:S(2)}, u32[]{:S(2)}) collective-permute-start(f32[2,8,32,128]{3,2,1,0:T(8,128)S(1)} %get-tuple-element.58), channel_id=1, source_target_pairs={{8,0},{10,2},{12,4},{14,6},{15,7},{13,5},{11,3},{9,1},{0,8},{2,10}... | collective-permute-start | bytes 786440 | tf_op jit(solution)/shard_map/ppermute | solution.py:353
  56.9 1.9 %collective-permute-start.7 = (f32[2,8,32,128]{3,2,1,0:T(8,128)S(1)}, f32[2,8,32,128]{3,2,1,0:T(8,128)S(1)}, u32[]{:S(2)}, u32[]{:S(2)}) collective-permute-start(f32[2,8,32,128]{3,2,1,0:T(8,128)S(1)} %get-tuple-element.53.own), channel_id=1, source_target_pairs={{0,16},{2,18},{4,20},{6,22},{7,23},{5,21},{3,19},{1,17},{8,24},{10... | collective-permute-start | bytes 786440 | tf_op jit(solution)/shard_map/ppermute | solution.py:353
  58.9 0.0 collective-permute-done.4.swapped
  58.9 2.0 %collective-permute-done.3.near = f32[2,8,32,128]{3,2,1,0:T(8,128)S(1)} collective-permute-done((f32[2,8,32,128]{3,2,1,0:T(8,128)S(1)}, f32[2,8,32,128]{3,2,1,0:T(8,128)S(1)}, u32[]{:S(2)}, u32[]{:S(2)}) %collective-permute-start.3) | collective-permute-done | bytes 262176 | tf_op jit(solution)/shard_map/ppermute | solution.py:353
  60.9 3.0 %shard_map.60 = (f32[2,8,32,128]{3,2,1,0:T(8,128)S(1)}, f32[2,8,32,128]{3,2,1,0:T(8,128)S(1)}) custom-call(f32[2,8,32,128]{3,2,1,0:T(8,128)S(1)} %get-tuple-element.53.own, f32[2,8,32,128]{3,2,1,0:T(8,128)S(1)} %collective-permute-done.3.near, f32[2,8,32,128]{3,2,1,0:T(8,128)S(1)} %collective-permute-done.4.swapped, f32[36,18,32,128]{3,2,1,0:T(8,128)S(1)} %get-tuple-element.56.w), custom_call_target="tpu_custom_call" | custom-call | bytes 15728640 | tf_op jit(solution)/shard_map/pallas_call | solution.py:420
  63.9 0.5 collective-permute-start.6
  64.4 0.0 collective-permute-start.5
  64.4 4.3 %collective-permute-start.12 = (f32[2,8,32,128]{3,2,1,0:T(8,128)S(1)}, f32[2,8,32,128]{3,2,1,0:T(8,128)S(1)}, u32[]{:S(2)}, u32[]{:S(2)}) collective-permute-start(f32[2,8,32,128]{3,2,1,0:T(8,128)S(1)} %get-tuple-element.60.own), channel_id=1, source_target_pairs={{0,48},{2,50},{4,52},{6,54},{7,55},{5,53},{3,51},{1,49},{8,56},{10... | collective-permute-start | bytes 786440 | tf_op jit(solution)/shard_map/ppermute | solution.py:353
  68.7 0.0 collective-permute-done.8.taken
  68.7 0.0 collective-permute-start.11
  68.7 0.0 collective-permute-done.7.refs_0_
  68.7 0.0 collective-permute-done.6.swapped
  68.7 1.4 %collective-permute-done.5.near = f32[2,8,32,128]{3,2,1,0:T(8,128)S(1)} collective-permute-done((f32[2,8,32,128]{3,2,1,0:T(8,128)S(1)}, f32[2,8,32,128]{3,2,1,0:T(8,128)S(1)}, u32[]{:S(2)}, u32[]{:S(2)}) %collective-permute-start.5) | collective-permute-done | bytes 262176 | tf_op jit(solution)/shard_map/ppermute | solution.py:353
  70.2 3.0 %shard_map.61 = (f32[2,8,32,128]{3,2,1,0:T(8,128)S(1)}, f32[2,8,32,128]{3,2,1,0:T(8,128)S(1)}) custom-call(f32[2,8,32,128]{3,2,1,0:T(8,128)S(1)} %get-tuple-element.60.own, f32[2,8,32,128]{3,2,1,0:T(8,128)S(1)} %collective-permute-done.5.near, f32[2,8,32,128]{3,2,1,0:T(8,128)S(1)} %collective-permute-done.6.swapped, ...), custom_call_target="tpu_custom_call" | custom-call | bytes 15728640 | tf_op jit(solution)/shard_map/pallas_call | solution.py:420
  73.2 0.8 collective-permute-start.10
  74.0 0.0 collective-permute-start.9
  74.0 1.9 %collective-permute-start.15 = (f32[2,8,32,128]{3,2,1,0:T(8,128)S(1)}, f32[2,8,32,128]{3,2,1,0:T(8,128)S(1)}, u32[]{:S(2)}, u32[]{:S(2)}) collective-permute-start(f32[2,8,32,128]{3,2,1,0:T(8,128)S(1)} %get-tuple-element.69.own), channel_id=1, source_target_pairs={{0,16},{2,18},{4,20},{6,22},{7,23},{5,21},{3,19},{1,17},{8,24},{10... | collective-permute-start | bytes 786440 | tf_op jit(solution)/shard_map/ppermute | solution.py:353
  75.9 2.9 %collective-permute-done.11.refs_1_ = f32[2,8,32,128]{3,2,1,0:T(8,128)S(1)} collective-permute-done((f32[2,8,32,128]{3,2,1,0:T(8,128)S(1)}, f32[2,8,32,128]{3,2,1,0:T(8,128)S(1)}, u32[]{:S(2)}, u32[]{:S(2)}) %collective-permute-start.11) | collective-permute-done | bytes 262176 | tf_op jit(solution)/shard_map/ppermute | solution.py:353
  78.8 1.3 %collective-permute-done.12.refs_2_ = f32[2,8,32,128]{3,2,1,0:T(8,128)S(1)} collective-permute-done((f32[2,8,32,128]{3,2,1,0:T(8,128)S(1)}, f32[2,8,32,128]{3,2,1,0:T(8,128)S(1)}, u32[]{:S(2)}, u32[]{:S(2)}) %collective-permute-start.12) | collective-permute-done | bytes 262176 | tf_op jit(solution)/shard_map/ppermute | solution.py:353
  80.1 0.0 collective-permute-done.10.swapped
  80.1 0.0 collective-permute-done.9.near
  80.1 3.0 %shard_map.62 = (f32[2,8,32,128]{3,2,1,0:T(8,128)S(1)}, f32[2,8,32,128]{3,2,1,0:T(8,128)S(1)}, f32[2,4,32,128]{3,2,1,0:T(8,128)S(1)}, f32[2,4,32,128]{3,2,1,0:T(8,128)S(1)}) custom-call(f32[2,8,32,128]{3,2,1,0:T(8,128)S(1)} %get-tuple-element.69.own, f32[2,8,32,128]{3,2,1,0:T(8,128)S(1)} %collective-permute-done.9.near, ...), custom_call_target="tpu_custom_call" | custom-call | bytes 15728640 | tf_op jit(solution)/shard_map/pallas_call | solution.py:420
  83.2 3.6 %collective-permute-start.16 = (f32[2,8,32,128]{3,2,1,0:T(8,128)S(1)}, f32[2,8,32,128]{3,2,1,0:T(8,128)S(1)}, u32[]{:S(2)}, u32[]{:S(2)}) collective-permute-start(f32[2,8,32,128]{3,2,1,0:T(8,128)S(1)} %get-tuple-element.76), channel_id=1, source_target_pairs={{0,32},{2,34},{4,36},{6,38},{7,39},{5,37},{3,35},{1,33},{8,40},{10... | collective-permute-start | bytes 786440 | tf_op jit(solution)/shard_map/ppermute | solution.py:353
  86.8 0.9 collective-permute-start.17
  87.6 0.6 collective-permute-start.13
  88.2 1.9 %collective-permute-start.14 = (f32[2,4,32,128]{3,2,1,0:T(8,128)S(1)}, f32[2,4,32,128]{3,2,1,0:T(8,128)S(1)}, u32[]{:S(2)}, u32[]{:S(2)}) collective-permute-start(f32[2,4,32,128]{3,2,1,0:T(8,128)S(1)} %get-tuple-element.74), channel_id=1, source_target_pairs={{8,0},{10,2},{12,4},{14,6},{15,7},{13,5},{11,3},{9,1},{0,8},{2,10}... | collective-permute-start | bytes 393224 | tf_op jit(solution)/shard_map/ppermute | solution.py:353
  90.1 0.0 collective-permute-done.15.refs_4_
  90.1 1.9 %collective-permute-done.13.near = f32[2,4,32,128]{3,2,1,0:T(8,128)S(1)} collective-permute-done((f32[2,4,32,128]{3,2,1,0:T(8,128)S(1)}, f32[2,4,32,128]{3,2,1,0:T(8,128)S(1)}, u32[]{:S(2)}, u32[]{:S(2)}) %collective-permute-start.13) | collective-permute-done | bytes 131104 | tf_op jit(solution)/shard_map/ppermute | solution.py:353
  92.0 0.0 collective-permute-done.14.swapped
  92.0 1.1 shard_map.63.refs_7_
  93.2 0.7 collective-permute-done.16.refs_5_
  93.9 6.5 %collective-permute-done.17.refs_6_ = f32[2,8,32,128]{3,2,1,0:T(8,128)S(1)} collective-permute-done((f32[2,8,32,128]{3,2,1,0:T(8,128)S(1)}, f32[2,8,32,128]{3,2,1,0:T(8,128)S(1)}, u32[]{:S(2)}, u32[]{:S(2)}) %collective-permute-start.17) | collective-permute-done | bytes 262176 | tf_op jit(solution)/shard_map/ppermute | solution.py:353
  100.4 0.2 shard_map.64
  100.5 0.1 collective-permute-start.18
  100.6 1.6 %collective-permute-start.19 = (f32[2,2,32,128]{3,2,1,0:T(8,128)S(1)}, f32[2,2,32,128]{3,2,1,0:T(8,128)S(1)}, u32[]{:S(2)}, u32[]{:S(2)}) collective-permute-start(f32[2,2,32,128]{3,2,1,0:T(8,128)S(1)} %get-tuple-element.82), channel_id=1, source_target_pairs={{8,0},{10,2},{12,4},{14,6},{15,7},{13,5},{11,3},{9,1},{0,8},{2,10}... | collective-permute-start | bytes 196616 | tf_op jit(solution)/shard_map/ppermute | solution.py:353
  102.2 2.1 %collective-permute-done.18.near = f32[2,2,32,128]{3,2,1,0:T(8,128)S(1)} collective-permute-done((f32[2,2,32,128]{3,2,1,0:T(8,128)S(1)}, f32[2,2,32,128]{3,2,1,0:T(8,128)S(1)}, u32[]{:S(2)}, u32[]{:S(2)}) %collective-permute-start.18) | collective-permute-done | bytes 65568 | tf_op jit(solution)/shard_map/ppermute | solution.py:353
  104.3 0.0 collective-permute-done.19.swapped
  104.3 0.6 shard_map.65
  104.9 0.2 collective-permute-start.20
  105.1 1.4 %collective-permute-done.20 = f32[8,64,128]{2,1,0:T(8,128)S(1)} collective-permute-done((f32[8,64,128]{2,1,0:T(8,128)S(1)}, f32[8,64,128]{2,1,0:T(8,128)S(1)}, u32[]{:S(2)}, u32[]{:S(2)}) %collective-permute-start.20) | collective-permute-done | bytes 262176 | tf_op jit(solution)/shard_map/ppermute | solution.py:353
  106.5 14.5 %all_to_all.11.got = f32[8,128,128]{2,1,0:T(8,128)S(1)} all-to-all(f32[8,128,128]{2,1,0:T(8,128)S(1)} %pad_maximum_fusion), channel_id=1, replica_groups=mesh['chip'=8,'core'=2,'space'=8] {'space'}, dimensions={0} | all-to-all | bytes 1048576 | tf_op jit(solution)/shard_map/all_to_all | solution.py:442
  121.0 0.9 shard_map.66
  (2 shorter events, 0.1 us)
Async XLA Ops:
  33.3 0.8 copy-start
  33.4 2.5 %collective-permute-start = (f32[3,18,32,128]{3,2,1,0:T(8,128)S(1)}, f32[3,18,32,128]{3,2,1,0:T(8,128)S(1)}, u32[]{:S(2)}, u32[]{:S(2)}) collective-permute-start(f32[3,18,32,128]{3,2,1,0:T(8,128)S(1)} %get-tuple-element.47.mine), channel_id=1, source_target_pairs={{8,0},{10,2},{12,4},{14,6},{15,7},{13,5},{11,3},{9,1},{0,8},{2,10}... | collective-permute-start | bytes 2654216 | tf_op jit(solution)/shard_map/ppermute | solution.py:353
  44.7 1.6 %collective-permute-start.1 = (f32[2,8,32,128]{3,2,1,0:T(8,128)S(1)}, f32[2,8,32,128]{3,2,1,0:T(8,128)S(1)}, u32[]{:S(2)}, u32[]{:S(2)}) collective-permute-start(f32[2,8,32,128]{3,2,1,0:T(8,128)S(1)} %get-tuple-element.51), channel_id=1, source_target_pairs={{8,0},{10,2},{12,4},{14,6},{15,7},{13,5},{11,3},{9,1},{0,8},{2,10}... | collective-permute-start | bytes 786440 | tf_op jit(solution)/shard_map/ppermute | solution.py:353
  46.4 8.4 %collective-permute-start.2 = (f32[2,8,32,128]{3,2,1,0:T(8,128)S(1)}, f32[2,8,32,128]{3,2,1,0:T(8,128)S(1)}, u32[]{:S(2)}, u32[]{:S(2)}) collective-permute-start(f32[2,8,32,128]{3,2,1,0:T(8,128)S(1)} %add.3.ours), channel_id=1, source_target_pairs={{65,0},{67,2},{69,4},{71,6},{70,7},{68,5},{66,3},{64,1},{73,8},{75... | collective-permute-start | bytes 786440 | tf_op jit(solution)/shard_map/ppermute | solution.py:353
  54.9 4.0 %collective-permute-start.4 = (f32[2,8,32,128]{3,2,1,0:T(8,128)S(1)}, f32[2,8,32,128]{3,2,1,0:T(8,128)S(1)}, u32[]{:S(2)}, u32[]{:S(2)}) collective-permute-start(f32[2,8,32,128]{3,2,1,0:T(8,128)S(1)} %get-tuple-element.53.own), channel_id=1, source_target_pairs={{8,0},{10,2},{12,4},{14,6},{15,7},{13,5},{11,3},{9,1},{0,8},{2,10}... | collective-permute-start | bytes 786440 | tf_op jit(solution)/shard_map/ppermute | solution.py:353
  55.0 5.9 %collective-permute-start.3 = (f32[2,8,32,128]{3,2,1,0:T(8,128)S(1)}, f32[2,8,32,128]{3,2,1,0:T(8,128)S(1)}, u32[]{:S(2)}, u32[]{:S(2)}) collective-permute-start(f32[2,8,32,128]{3,2,1,0:T(8,128)S(1)} %get-tuple-element.53.own), channel_id=1, source_target_pairs={{8,2},{10,4},{12,6},{14,7},{15,5},{13,3},{11,1},{9,0},{0,9},{2,8},... | collective-permute-start | bytes 786440 | tf_op jit(solution)/shard_map/ppermute | solution.py:353
  55.3 13.4 %collective-permute-start.8 = (f32[2,8,32,128]{3,2,1,0:T(8,128)S(1)}, f32[2,8,32,128]{3,2,1,0:T(8,128)S(1)}, u32[]{:S(2)}, u32[]{:S(2)}) collective-permute-start(f32[2,8,32,128]{3,2,1,0:T(8,128)S(1)} %get-tuple-element.58), channel_id=1, source_target_pairs={{8,0},{10,2},{12,4},{14,6},{15,7},{13,5},{11,3},{9,1},{0,8},{2,10}... | collective-permute-start | bytes 786440 | tf_op jit(solution)/shard_map/ppermute | solution.py:353
  56.9 11.8 %collective-permute-start.7 = (f32[2,8,32,128]{3,2,1,0:T(8,128)S(1)}, f32[2,8,32,128]{3,2,1,0:T(8,128)S(1)}, u32[]{:S(2)}, u32[]{:S(2)}) collective-permute-start(f32[2,8,32,128]{3,2,1,0:T(8,128)S(1)} %get-tuple-element.53.own), channel_id=1, source_target_pairs={{0,16},{2,18},{4,20},{6,22},{7,23},{5,21},{3,19},{1,17},{8,24},{10... | collective-permute-start | bytes 786440 | tf_op jit(solution)/shard_map/ppermute | solution.py:353
  63.9 4.8 %collective-permute-start.6 = (f32[2,8,32,128]{3,2,1,0:T(8,128)S(1)}, f32[2,8,32,128]{3,2,1,0:T(8,128)S(1)}, u32[]{:S(2)}, u32[]{:S(2)}) collective-permute-start(f32[2,8,32,128]{3,2,1,0:T(8,128)S(1)} %get-tuple-element.60.own), channel_id=1, source_target_pairs={{8,0},{10,2},{12,4},{14,6},{15,7},{13,5},{11,3},{9,1},{0,8},{2,10}... | collective-permute-start | bytes 786440 | tf_op jit(solution)/shard_map/ppermute | solution.py:353
  64.4 5.8 %collective-permute-start.5 = (f32[2,8,32,128]{3,2,1,0:T(8,128)S(1)}, f32[2,8,32,128]{3,2,1,0:T(8,128)S(1)}, u32[]{:S(2)}, u32[]{:S(2)}) collective-permute-start(f32[2,8,32,128]{3,2,1,0:T(8,128)S(1)} %get-tuple-element.60.own), channel_id=1, source_target_pairs={{8,2},{10,4},{12,6},{14,7},{15,5},{13,3},{11,1},{9,0},{0,9},{2,8},... | collective-permute-start | bytes 786440 | tf_op jit(solution)/shard_map/ppermute | solution.py:353
  64.4 15.8 %collective-permute-start.12 = (f32[2,8,32,128]{3,2,1,0:T(8,128)S(1)}, f32[2,8,32,128]{3,2,1,0:T(8,128)S(1)}, u32[]{:S(2)}, u32[]{:S(2)}) collective-permute-start(f32[2,8,32,128]{3,2,1,0:T(8,128)S(1)} %get-tuple-element.60.own), channel_id=1, source_target_pairs={{0,48},{2,50},{4,52},{6,54},{7,55},{5,53},{3,51},{1,49},{8,56},{10... | collective-permute-start | bytes 786440 | tf_op jit(solution)/shard_map/ppermute | solution.py:353
  68.7 10.1 %collective-permute-start.11 = (f32[2,8,32,128]{3,2,1,0:T(8,128)S(1)}, f32[2,8,32,128]{3,2,1,0:T(8,128)S(1)}, u32[]{:S(2)}, u32[]{:S(2)}) collective-permute-start(f32[2,8,32,128]{3,2,1,0:T(8,128)S(1)} %get-tuple-element.65), channel_id=1, source_target_pairs={{0,32},{2,34},{4,36},{6,38},{7,39},{5,37},{3,35},{1,33},{8,40},{10... | collective-permute-start | bytes 786440 | tf_op jit(solution)/shard_map/ppermute | solution.py:353
  73.2 7.0 %collective-permute-start.10 = (f32[2,8,32,128]{3,2,1,0:T(8,128)S(1)}, f32[2,8,32,128]{3,2,1,0:T(8,128)S(1)}, u32[]{:S(2)}, u32[]{:S(2)}) collective-permute-start(f32[2,8,32,128]{3,2,1,0:T(8,128)S(1)} %get-tuple-element.69.own), channel_id=1, source_target_pairs={{8,0},{10,2},{12,4},{14,6},{15,7},{13,5},{11,3},{9,1},{0,8},{2,10}... | collective-permute-start | bytes 786440 | tf_op jit(solution)/shard_map/ppermute | solution.py:353
  74.0 6.2 %collective-permute-start.9 = (f32[2,8,32,128]{3,2,1,0:T(8,128)S(1)}, f32[2,8,32,128]{3,2,1,0:T(8,128)S(1)}, u32[]{:S(2)}, u32[]{:S(2)}) collective-permute-start(f32[2,8,32,128]{3,2,1,0:T(8,128)S(1)} %get-tuple-element.69.own), channel_id=1, source_target_pairs={{8,2},{10,4},{12,6},{14,7},{15,5},{13,3},{11,1},{9,0},{0,9},{2,8},... | collective-permute-start | bytes 786440 | tf_op jit(solution)/shard_map/ppermute | solution.py:353
  74.0 16.2 %collective-permute-start.15 = (f32[2,8,32,128]{3,2,1,0:T(8,128)S(1)}, f32[2,8,32,128]{3,2,1,0:T(8,128)S(1)}, u32[]{:S(2)}, u32[]{:S(2)}) collective-permute-start(f32[2,8,32,128]{3,2,1,0:T(8,128)S(1)} %get-tuple-element.69.own), channel_id=1, source_target_pairs={{0,16},{2,18},{4,20},{6,22},{7,23},{5,21},{3,19},{1,17},{8,24},{10... | collective-permute-start | bytes 786440 | tf_op jit(solution)/shard_map/ppermute | solution.py:353
  83.2 10.7 %collective-permute-start.16 = (f32[2,8,32,128]{3,2,1,0:T(8,128)S(1)}, f32[2,8,32,128]{3,2,1,0:T(8,128)S(1)}, u32[]{:S(2)}, u32[]{:S(2)}) collective-permute-start(f32[2,8,32,128]{3,2,1,0:T(8,128)S(1)} %get-tuple-element.76), channel_id=1, source_target_pairs={{0,32},{2,34},{4,36},{6,38},{7,39},{5,37},{3,35},{1,33},{8,40},{10... | collective-permute-start | bytes 786440 | tf_op jit(solution)/shard_map/ppermute | solution.py:353
  86.8 13.6 %collective-permute-start.17 = (f32[2,8,32,128]{3,2,1,0:T(8,128)S(1)}, f32[2,8,32,128]{3,2,1,0:T(8,128)S(1)}, u32[]{:S(2)}, u32[]{:S(2)}) collective-permute-start(f32[2,8,32,128]{3,2,1,0:T(8,128)S(1)} %get-tuple-element.77.own), channel_id=1, source_target_pairs={{0,48},{2,50},{4,52},{6,54},{7,55},{5,53},{3,51},{1,49},{8,56},{10... | collective-permute-start | bytes 786440 | tf_op jit(solution)/shard_map/ppermute | solution.py:353
  87.6 4.4 %collective-permute-start.13 = (f32[2,4,32,128]{3,2,1,0:T(8,128)S(1)}, f32[2,4,32,128]{3,2,1,0:T(8,128)S(1)}, u32[]{:S(2)}, u32[]{:S(2)}) collective-permute-start(f32[2,4,32,128]{3,2,1,0:T(8,128)S(1)} %get-tuple-element.73), channel_id=1, source_target_pairs={{8,2},{10,4},{12,6},{14,7},{15,5},{13,3},{11,1},{9,0},{0,9},{2,8},... | collective-permute-start | bytes 393224 | tf_op jit(solution)/shard_map/ppermute | solution.py:353
  88.2 3.8 %collective-permute-start.14 = (f32[2,4,32,128]{3,2,1,0:T(8,128)S(1)}, f32[2,4,32,128]{3,2,1,0:T(8,128)S(1)}, u32[]{:S(2)}, u32[]{:S(2)}) collective-permute-start(f32[2,4,32,128]{3,2,1,0:T(8,128)S(1)} %get-tuple-element.74), channel_id=1, source_target_pairs={{8,0},{10,2},{12,4},{14,6},{15,7},{13,5},{11,3},{9,1},{0,8},{2,10}... | collective-permute-start | bytes 393224 | tf_op jit(solution)/shard_map/ppermute | solution.py:353
  100.5 3.8 %collective-permute-start.18 = (f32[2,2,32,128]{3,2,1,0:T(8,128)S(1)}, f32[2,2,32,128]{3,2,1,0:T(8,128)S(1)}, u32[]{:S(2)}, u32[]{:S(2)}) collective-permute-start(f32[2,2,32,128]{3,2,1,0:T(8,128)S(1)} %get-tuple-element.81), channel_id=1, source_target_pairs={{8,2},{10,4},{12,6},{14,7},{15,5},{13,3},{11,1},{9,0},{0,9},{2,8},... | collective-permute-start | bytes 196616 | tf_op jit(solution)/shard_map/ppermute | solution.py:353
  100.6 3.7 %collective-permute-start.19 = (f32[2,2,32,128]{3,2,1,0:T(8,128)S(1)}, f32[2,2,32,128]{3,2,1,0:T(8,128)S(1)}, u32[]{:S(2)}, u32[]{:S(2)}) collective-permute-start(f32[2,2,32,128]{3,2,1,0:T(8,128)S(1)} %get-tuple-element.82), channel_id=1, source_target_pairs={{8,0},{10,2},{12,4},{14,6},{15,7},{13,5},{11,3},{9,1},{0,8},{2,10}... | collective-permute-start | bytes 196616 | tf_op jit(solution)/shard_map/ppermute | solution.py:353
  104.9 1.6 %collective-permute-start.20 = (f32[8,64,128]{2,1,0:T(8,128)S(1)}, f32[8,64,128]{2,1,0:T(8,128)S(1)}, u32[]{:S(2)}, u32[]{:S(2)}) collective-permute-start(f32[8,64,128]{2,1,0:T(8,128)S(1)} %get-tuple-element.86), channel_id=1, source_target_pairs={{8,0},{10,2},{12,4},{14,6},{15,7},{13,5},{11,3},{9,1},{0,8},{2,10}... | collective-permute-start | bytes 786440 | tf_op jit(solution)/shard_map/ppermute | solution.py:353

commit v13 on v12

--- a/solution.py
+++ b/solution.py
@@ -286,13 +286,29 @@
     advances(2, e, v, w, middle - reach, HALF + 2 * reach, COARSE)
     odd[...] = e[:, rows]
     if more:
-        even, *rims = more
+        (even,) = more
         advances(2, e, v, w, middle - 4, HALF + 8, COARSE)
         even[...] = e[:, rows] + high[...] if joined else e[:, rows]
-        if rims:
-            inner, outer = rims
-            inner[...] = even[:, pl.ds(4 - 4 * core, 4)]
-            outer[...] = even[:, pl.ds(4 * core, 4)]
+
+
+def first_half_kernel(own, near, swapped, w, odd, state, e, v):
+    core, _, _ = position()
+    middle = EDGE + HALF * core
+    e[:, pl.ds(middle, HALF)] = own[...]
+    place(core, e, middle, swapped, near)
+    advances(2, e, v, w, middle - HALF, 3 * HALF, COARSE)
+    odd[...] = e[:, pl.ds(middle, HALF)]
+    state[...] = e[:, pl.ds(middle - 4, HALF + 8)]
+
+
+def second_half_kernel(state, w, even, inner, outer, e, v):
+    core, _, _ = position()
+    middle = EDGE + HALF * core
+    e[:, pl.ds(middle - 4, HALF + 8)] = state[...]
+    advances(2, e, v, w, middle - 4, HALF + 8, COARSE)
+    even[...] = e[:, pl.ds(middle, HALF)]
+    inner[...] = even[:, pl.ds(4 - 4 * core, 4)]
+    outer[...] = even[:, pl.ds(4 * core, 4)]
 
 
 def choose_kernel(ours, across, low, high):
@@ -413,8 +429,8 @@
     )(begin, mine, other, inlet, weights, feed)
     u = base + swap(give)
 
-    def leap(own, near, swapped, *rims, second=True, high=None):
-        outs = (half,) * (1 + second) + rims
+    def leap(own, near, swapped, second=True, high=None):
+        outs = (half,) * (1 + second)
         operands = [own, near, swapped, weights] + ([] if high is None else [high])
         body = functools.partial(leap_kernel, high is not None)
         return call(body, outs, [VMEM] * len(operands), (VMEM,) * len(outs), [field, field], 20, 2 + 3 * second)(*operands)
@@ -428,9 +444,15 @@
     u3, u4 = leap(*operands, high=high)
     a4 = along(u4, 4)
     *operands, a1, a2 = exchanged(u4, u4, u4, a1, a2)
-    u5, u6, inner, outer = leap(*operands, rim4, rim4)
-    a5, a6 = along(u5, 5), along(u6, 6)
-    *operands, a4 = exchanged(u6, inner, outer, a4)
+    u5, state = call(
+        first_half_kernel, (half, shape(2, 2 * HALF, NX, LAST)), [VMEM] * 4, (VMEM,) * 2, [field, field], 20, 2
+    )(*operands, weights)
+    a5 = along(u5, 5)
+    u6, inner, outer = call(
+        second_half_kernel, (half, rim4, rim4), [VMEM] * 2, (VMEM,) * 3, [field, field], 20, 2
+    )(state, weights)
+    a6 = along(u6, 6)
+    *operands, a4, a5 = exchanged(u6, inner, outer, a4, a5)
     (u7,) = leap(*operands, second=False)
     c, inner, outer = call(share_kernel, (half, rim2, rim2), [VMEM] * 8, (VMEM,) * 3, [], 16)(
         a0, a1, a2, u3, a4, a5, a6, u7

time: 122 us -> 121 us (level)
  waiting for transfers between devices: 30.9 us -> 29.4 us
    pallas_call x0 -> x2, Pallas kernels: none -> 3.07 us  [the longest x1 1.92 us: shards(): call(first_half_kernel, (half, shape(2, 2 * HALF, NX, LAST)), [VMEM] * 4,...]
    pallas_call x4 -> x3, Pallas kernels: 10.2 us -> 7.12 us  [leap(): call(body, outs, [VMEM] * len(operands), (VMEM,) * len(outs), [field, fie...]
    ppermute x21, waiting for transfers between devices: 30.9 us -> 29.4 us  [sent(): return lax.ppermute(value, AXES, pairs)]
where the time goes in v13:
time: 121 us
  blocking collectives  46.3 us (38%)
  waiting for transfers between devices  29.4 us (24%)
  Pallas kernels  23.3 us (19%)
  starting transfers between devices  21 us (17%)
    all_to_all x1, blocking collectives, shards(): got = lax.all_to_all(packed, 'space', 0, 0, tiled=True)  31.8 us
    ppermute x21, waiting for transfers between devices, sent(): return lax.ppermute(value, AXES, pairs)  29.4 us
    ppermute x21, starting transfers between devices, sent(): return lax.ppermute(value, AXES, pairs)  21 us
    all_to_all x1, blocking collectives, shards(): lax.all_to_all(jnp.concatenate([keep, swap(send)], axis=1), 'space', 0, 0...  14.5 us
    pallas_call x1, Pallas kernels, shards(): call(relax_kernel, (all_weights, half, half, half, half), [VMEM] * 6, (VM...  8.81 us
    pallas_call x3, Pallas kernels, leap(): call(body, outs, [VMEM] * len(operands), (VMEM,) * len(outs), [field, fie...  7.12 us
  transfers between devices with their start and end apart: 21, of which 12 were waited for; matrix products, arithmetic and copies ran while one was open for 0% of the time, Pallas kernels for 9%

profile of v13, /device:TPU:4, one launch (start us, length us, event | category | flops | bytes accessed | tf_op | source)
XLA Modules:
  0.0 120.8 jit_solution(14463727449253300958)
XLA Ops:
  0.0 1.5 %shard_map.55 = f32[8,504,128]{2,1,0:T(8,128)S(1)} custom-call(f32[2,4,128,128]{3,2,1,0:T(8,128)} %startup.1, f32[1,2,4,128,128]{4,3,2,1,0:T(8,128)} %guess.1, f32[2,4,128,128]{3,2,1,0:T(8,128)} %conduct.1, f32[4,128,128]{2,1,0:T(8,128)} %couple.1), custom_call_target="tpu_custom_call" | custom-call | bytes 3145728 | tf_op jit(solution)/shard_map/pallas_call | solution.py:397
  1.5 31.8 %all_to_all.10.got = f32[8,504,128]{2,1,0:T(8,128)S(1)} all-to-all(f32[8,504,128]{2,1,0:T(8,128)S(1)} %shard_map.55), channel_id=1, replica_groups=mesh['chip'=8,'core'=2,'space'=8] {'space'}, dimensions={0} | all-to-all | bytes 4128768 | tf_op jit(solution)/shard_map/all_to_all | solution.py:410
  33.3 0.0 copy-start
  33.3 0.1 shard_map.56
  33.4 0.1 collective-permute-start
  33.5 0.6 copy-done
  34.1 1.0 shard_map.57
  35.1 0.8 collective-permute-done.other
  35.9 8.8 %shard_map.58 = (f32[36,18,32,128]{3,2,1,0:T(8,128)S(1)}, f32[2,8,32,128]{3,2,1,0:T(8,128)S(1)}, f32[2,8,32,128]{3,2,1,0:T(8,128)S(1)}, f32[2,8,32,128]{3,2,1,0:T(8,128)S(1)}, f32[2,8,32,128]{3,2,1,0:T(8,128)S(1)}) custom-call(f32[2,36,32,128]{3,2,1,0:T(8,128)S(1)} %get-tuple-element.48.begin, ...), custom_call_target="tpu_custom_call", output_to_operand_aliasing={{0}: (4, {})} | custom-call | bytes 3145728 | tf_op jit(solution)/shard_map/pallas_call | solution.py:421
  44.7 0.2 collective-permute-start.1
  45.0 1.4 %collective-permute-done.1 = f32[2,8,32,128]{3,2,1,0:T(8,128)S(1)} collective-permute-done((f32[2,8,32,128]{3,2,1,0:T(8,128)S(1)}, f32[2,8,32,128]{3,2,1,0:T(8,128)S(1)}, u32[]{:S(2)}, u32[]{:S(2)}) %collective-permute-start.1) | collective-permute-done | bytes 262176 | tf_op jit(solution)/shard_map/ppermute | solution.py:369
  46.4 0.1 collective-permute-start.2
  46.5 8.3 %collective-permute-done.2.across = f32[2,8,32,128]{3,2,1,0:T(8,128)S(1)} collective-permute-done((f32[2,8,32,128]{3,2,1,0:T(8,128)S(1)}, f32[2,8,32,128]{3,2,1,0:T(8,128)S(1)}, u32[]{:S(2)}, u32[]{:S(2)}) %collective-permute-start.2) | collective-permute-done | bytes 262176 | tf_op jit(solution)/shard_map/ppermute | solution.py:369
  54.8 0.1 shard_map.59
  54.9 0.1 collective-permute-start.4
  55.0 0.3 collective-permute-start.3
  55.3 1.6 %collective-permute-start.8 = (f32[2,8,32,128]{3,2,1,0:T(8,128)S(1)}, f32[2,8,32,128]{3,2,1,0:T(8,128)S(1)}, u32[]{:S(2)}, u32[]{:S(2)}) collective-permute-start(f32[2,8,32,128]{3,2,1,0:T(8,128)S(1)} %get-tuple-element.60), channel_id=1, source_target_pairs={{8,0},{10,2},{12,4},{14,6},{15,7},{13,5},{11,3},{9,1},{0,8},{2,10}... | collective-permute-start | bytes 786440 | tf_op jit(solution)/shard_map/ppermute | solution.py:369
  56.9 1.9 %collective-permute-start.7 = (f32[2,8,32,128]{3,2,1,0:T(8,128)S(1)}, f32[2,8,32,128]{3,2,1,0:T(8,128)S(1)}, u32[]{:S(2)}, u32[]{:S(2)}) collective-permute-start(f32[2,8,32,128]{3,2,1,0:T(8,128)S(1)} %get-tuple-element.55.own), channel_id=1, source_target_pairs={{0,16},{2,18},{4,20},{6,22},{7,23},{5,21},{3,19},{1,17},{8,24},{10... | collective-permute-start | bytes 786440 | tf_op jit(solution)/shard_map/ppermute | solution.py:369
  58.9 0.0 collective-permute-done.4.swapped
  58.9 2.0 %collective-permute-done.3.near = f32[2,8,32,128]{3,2,1,0:T(8,128)S(1)} collective-permute-done((f32[2,8,32,128]{3,2,1,0:T(8,128)S(1)}, f32[2,8,32,128]{3,2,1,0:T(8,128)S(1)}, u32[]{:S(2)}, u32[]{:S(2)}) %collective-permute-start.3) | collective-permute-done | bytes 262176 | tf_op jit(solution)/shard_map/ppermute | solution.py:369
  60.9 3.0 %shard_map.60 = (f32[2,8,32,128]{3,2,1,0:T(8,128)S(1)}, f32[2,8,32,128]{3,2,1,0:T(8,128)S(1)}) custom-call(f32[2,8,32,128]{3,2,1,0:T(8,128)S(1)} %get-tuple-element.55.own, f32[2,8,32,128]{3,2,1,0:T(8,128)S(1)} %collective-permute-done.3.near, f32[2,8,32,128]{3,2,1,0:T(8,128)S(1)} %collective-permute-done.4.swapped, f32[36,18,32,128]{3,2,1,0:T(8,128)S(1)} %get-tuple-element.58.w), custom_call_target="tpu_custom_call" | custom-call | bytes 15728640 | tf_op jit(solution)/shard_map/pallas_call | solution.py:436
  63.9 0.5 collective-permute-start.6
  64.4 0.0 collective-permute-start.5
  64.4 4.3 %collective-permute-start.12 = (f32[2,8,32,128]{3,2,1,0:T(8,128)S(1)}, f32[2,8,32,128]{3,2,1,0:T(8,128)S(1)}, u32[]{:S(2)}, u32[]{:S(2)}) collective-permute-start(f32[2,8,32,128]{3,2,1,0:T(8,128)S(1)} %get-tuple-element.62.own), channel_id=1, source_target_pairs={{0,48},{2,50},{4,52},{6,54},{7,55},{5,53},{3,51},{1,49},{8,56},{10... | collective-permute-start | bytes 786440 | tf_op jit(solution)/shard_map/ppermute | solution.py:369
  68.7 0.0 collective-permute-done.8.taken
  68.7 0.0 collective-permute-start.11
  68.7 0.0 collective-permute-done.7.refs_0_
  68.7 0.0 collective-permute-done.6.swapped
  68.7 1.4 %collective-permute-done.5.near = f32[2,8,32,128]{3,2,1,0:T(8,128)S(1)} collective-permute-done((f32[2,8,32,128]{3,2,1,0:T(8,128)S(1)}, f32[2,8,32,128]{3,2,1,0:T(8,128)S(1)}, u32[]{:S(2)}, u32[]{:S(2)}) %collective-permute-start.5) | collective-permute-done | bytes 262176 | tf_op jit(solution)/shard_map/ppermute | solution.py:369
  70.2 3.0 %shard_map.61 = (f32[2,8,32,128]{3,2,1,0:T(8,128)S(1)}, f32[2,8,32,128]{3,2,1,0:T(8,128)S(1)}) custom-call(f32[2,8,32,128]{3,2,1,0:T(8,128)S(1)} %get-tuple-element.62.own, f32[2,8,32,128]{3,2,1,0:T(8,128)S(1)} %collective-permute-done.5.near, f32[2,8,32,128]{3,2,1,0:T(8,128)S(1)} %collective-permute-done.6.swapped, ...), custom_call_target="tpu_custom_call" | custom-call | bytes 15728640 | tf_op jit(solution)/shard_map/pallas_call | solution.py:436
  73.2 0.8 collective-permute-start.10
  74.0 0.0 collective-permute-start.9
  74.0 1.9 %collective-permute-start.15 = (f32[2,8,32,128]{3,2,1,0:T(8,128)S(1)}, f32[2,8,32,128]{3,2,1,0:T(8,128)S(1)}, u32[]{:S(2)}, u32[]{:S(2)}) collective-permute-start(f32[2,8,32,128]{3,2,1,0:T(8,128)S(1)} %get-tuple-element.71.own), channel_id=1, source_target_pairs={{0,16},{2,18},{4,20},{6,22},{7,23},{5,21},{3,19},{1,17},{8,24},{10... | collective-permute-start | bytes 786440 | tf_op jit(solution)/shard_map/ppermute | solution.py:369
  75.9 2.9 %collective-permute-done.11.refs_1_ = f32[2,8,32,128]{3,2,1,0:T(8,128)S(1)} collective-permute-done((f32[2,8,32,128]{3,2,1,0:T(8,128)S(1)}, f32[2,8,32,128]{3,2,1,0:T(8,128)S(1)}, u32[]{:S(2)}, u32[]{:S(2)}) %collective-permute-start.11) | collective-permute-done | bytes 262176 | tf_op jit(solution)/shard_map/ppermute | solution.py:369
  78.8 1.3 %collective-permute-done.12.refs_2_ = f32[2,8,32,128]{3,2,1,0:T(8,128)S(1)} collective-permute-done((f32[2,8,32,128]{3,2,1,0:T(8,128)S(1)}, f32[2,8,32,128]{3,2,1,0:T(8,128)S(1)}, u32[]{:S(2)}, u32[]{:S(2)}) %collective-permute-start.12) | collective-permute-done | bytes 262176 | tf_op jit(solution)/shard_map/ppermute | solution.py:369
  80.1 0.0 collective-permute-done.10.swapped
  80.1 0.0 collective-permute-done.9.near
  80.1 1.9 %shard_map.62 = (f32[2,8,32,128]{3,2,1,0:T(8,128)S(1)}, f32[2,16,32,128]{3,2,1,0:T(8,128)S(1)}) custom-call(f32[2,8,32,128]{3,2,1,0:T(8,128)S(1)} %get-tuple-element.71.own, f32[2,8,32,128]{3,2,1,0:T(8,128)S(1)} %collective-permute-done.9.near, f32[2,8,32,128]{3,2,1,0:T(8,128)S(1)} %collective-permute-done.10.swapped, ...), custom_call_target="tpu_custom_call" | custom-call | bytes 6291456 | tf_op jit(solution)/shard_map/pallas_call | solution.py:447
  82.1 3.6 %collective-permute-start.16 = (f32[2,8,32,128]{3,2,1,0:T(8,128)S(1)}, f32[2,8,32,128]{3,2,1,0:T(8,128)S(1)}, u32[]{:S(2)}, u32[]{:S(2)}) collective-permute-start(f32[2,8,32,128]{3,2,1,0:T(8,128)S(1)} %get-tuple-element.78), channel_id=1, source_target_pairs={{0,32},{2,34},{4,36},{6,38},{7,39},{5,37},{3,35},{1,33},{8,40},{10... | collective-permute-start | bytes 786440 | tf_op jit(solution)/shard_map/ppermute | solution.py:369
  85.7 1.2 shard_map.63
  86.8 1.2 collective-permute-start.17
  88.0 0.6 collective-permute-start.13
  88.6 1.9 %collective-permute-start.14 = (f32[2,4,32,128]{3,2,1,0:T(8,128)S(1)}, f32[2,4,32,128]{3,2,1,0:T(8,128)S(1)}, u32[]{:S(2)}, u32[]{:S(2)}) collective-permute-start(f32[2,4,32,128]{3,2,1,0:T(8,128)S(1)} %get-tuple-element.77), channel_id=1, source_target_pairs={{8,0},{10,2},{12,4},{14,6},{15,7},{13,5},{11,3},{9,1},{0,8},{2,10}... | collective-permute-start | bytes 393224 | tf_op jit(solution)/shard_map/ppermute | solution.py:369
  90.4 0.0 collective-permute-done.15.refs_4_
  90.4 1.9 %collective-permute-done.13.near = f32[2,4,32,128]{3,2,1,0:T(8,128)S(1)} collective-permute-done((f32[2,4,32,128]{3,2,1,0:T(8,128)S(1)}, f32[2,4,32,128]{3,2,1,0:T(8,128)S(1)}, u32[]{:S(2)}, u32[]{:S(2)}) %collective-permute-start.13) | collective-permute-done | bytes 131104 | tf_op jit(solution)/shard_map/ppermute | solution.py:369
  92.4 0.0 collective-permute-done.14.swapped
  92.4 0.4 collective-permute-done.16.refs_5_
  92.8 1.1 shard_map.64.refs_7_
  93.9 5.3 %collective-permute-done.17.refs_6_ = f32[2,8,32,128]{3,2,1,0:T(8,128)S(1)} collective-permute-done((f32[2,8,32,128]{3,2,1,0:T(8,128)S(1)}, f32[2,8,32,128]{3,2,1,0:T(8,128)S(1)}, u32[]{:S(2)}, u32[]{:S(2)}) %collective-permute-start.17) | collective-permute-done | bytes 262176 | tf_op jit(solution)/shard_map/ppermute | solution.py:369
  99.2 0.2 shard_map.65
  99.4 0.1 collective-permute-start.18
  99.5 1.6 %collective-permute-start.19 = (f32[2,2,32,128]{3,2,1,0:T(8,128)S(1)}, f32[2,2,32,128]{3,2,1,0:T(8,128)S(1)}, u32[]{:S(2)}, u32[]{:S(2)}) collective-permute-start(f32[2,2,32,128]{3,2,1,0:T(8,128)S(1)} %get-tuple-element.86), channel_id=1, source_target_pairs={{8,0},{10,2},{12,4},{14,6},{15,7},{13,5},{11,3},{9,1},{0,8},{2,10}... | collective-permute-start | bytes 196616 | tf_op jit(solution)/shard_map/ppermute | solution.py:369
  101.1 2.1 %collective-permute-done.18.near = f32[2,2,32,128]{3,2,1,0:T(8,128)S(1)} collective-permute-done((f32[2,2,32,128]{3,2,1,0:T(8,128)S(1)}, f32[2,2,32,128]{3,2,1,0:T(8,128)S(1)}, u32[]{:S(2)}, u32[]{:S(2)}) %collective-permute-start.18) | collective-permute-done | bytes 65568 | tf_op jit(solution)/shard_map/ppermute | solution.py:369
  103.2 0.0 collective-permute-done.19.swapped
  103.2 0.6 shard_map.66
  103.8 0.2 collective-permute-start.20
  103.9 1.4 %collective-permute-done.20 = f32[8,64,128]{2,1,0:T(8,128)S(1)} collective-permute-done((f32[8,64,128]{2,1,0:T(8,128)S(1)}, f32[8,64,128]{2,1,0:T(8,128)S(1)}, u32[]{:S(2)}, u32[]{:S(2)}) %collective-permute-start.20) | collective-permute-done | bytes 262176 | tf_op jit(solution)/shard_map/ppermute | solution.py:369
  105.4 14.5 %all_to_all.11.got = f32[8,128,128]{2,1,0:T(8,128)S(1)} all-to-all(f32[8,128,128]{2,1,0:T(8,128)S(1)} %pad_maximum_fusion), channel_id=1, replica_groups=mesh['chip'=8,'core'=2,'space'=8] {'space'}, dimensions={0} | all-to-all | bytes 1048576 | tf_op jit(solution)/shard_map/all_to_all | solution.py:464
  119.9 0.9 shard_map.67
  (2 shorter events, 0.1 us)
Async XLA Ops:
  33.3 0.8 copy-start
  33.4 2.5 %collective-permute-start = (f32[3,18,32,128]{3,2,1,0:T(8,128)S(1)}, f32[3,18,32,128]{3,2,1,0:T(8,128)S(1)}, u32[]{:S(2)}, u32[]{:S(2)}) collective-permute-start(f32[3,18,32,128]{3,2,1,0:T(8,128)S(1)} %get-tuple-element.49.mine), channel_id=1, source_target_pairs={{8,0},{10,2},{12,4},{14,6},{15,7},{13,5},{11,3},{9,1},{0,8},{2,10}... | collective-permute-start | bytes 2654216 | tf_op jit(solution)/shard_map/ppermute | solution.py:369
  44.7 1.6 %collective-permute-start.1 = (f32[2,8,32,128]{3,2,1,0:T(8,128)S(1)}, f32[2,8,32,128]{3,2,1,0:T(8,128)S(1)}, u32[]{:S(2)}, u32[]{:S(2)}) collective-permute-start(f32[2,8,32,128]{3,2,1,0:T(8,128)S(1)} %get-tuple-element.53), channel_id=1, source_target_pairs={{8,0},{10,2},{12,4},{14,6},{15,7},{13,5},{11,3},{9,1},{0,8},{2,10}... | collective-permute-start | bytes 786440 | tf_op jit(solution)/shard_map/ppermute | solution.py:369
  46.4 8.4 %collective-permute-start.2 = (f32[2,8,32,128]{3,2,1,0:T(8,128)S(1)}, f32[2,8,32,128]{3,2,1,0:T(8,128)S(1)}, u32[]{:S(2)}, u32[]{:S(2)}) collective-permute-start(f32[2,8,32,128]{3,2,1,0:T(8,128)S(1)} %add.3.ours), channel_id=1, source_target_pairs={{65,0},{67,2},{69,4},{71,6},{70,7},{68,5},{66,3},{64,1},{73,8},{75... | collective-permute-start | bytes 786440 | tf_op jit(solution)/shard_map/ppermute | solution.py:369
  54.9 4.0 %collective-permute-start.4 = (f32[2,8,32,128]{3,2,1,0:T(8,128)S(1)}, f32[2,8,32,128]{3,2,1,0:T(8,128)S(1)}, u32[]{:S(2)}, u32[]{:S(2)}) collective-permute-start(f32[2,8,32,128]{3,2,1,0:T(8,128)S(1)} %get-tuple-element.55.own), channel_id=1, source_target_pairs={{8,0},{10,2},{12,4},{14,6},{15,7},{13,5},{11,3},{9,1},{0,8},{2,10}... | collective-permute-start | bytes 786440 | tf_op jit(solution)/shard_map/ppermute | solution.py:369
  55.0 5.9 %collective-permute-start.3 = (f32[2,8,32,128]{3,2,1,0:T(8,128)S(1)}, f32[2,8,32,128]{3,2,1,0:T(8,128)S(1)}, u32[]{:S(2)}, u32[]{:S(2)}) collective-permute-start(f32[2,8,32,128]{3,2,1,0:T(8,128)S(1)} %get-tuple-element.55.own), channel_id=1, source_target_pairs={{8,2},{10,4},{12,6},{14,7},{15,5},{13,3},{11,1},{9,0},{0,9},{2,8},... | collective-permute-start | bytes 786440 | tf_op jit(solution)/shard_map/ppermute | solution.py:369
  55.3 13.4 %collective-permute-start.8 = (f32[2,8,32,128]{3,2,1,0:T(8,128)S(1)}, f32[2,8,32,128]{3,2,1,0:T(8,128)S(1)}, u32[]{:S(2)}, u32[]{:S(2)}) collective-permute-start(f32[2,8,32,128]{3,2,1,0:T(8,128)S(1)} %get-tuple-element.60), channel_id=1, source_target_pairs={{8,0},{10,2},{12,4},{14,6},{15,7},{13,5},{11,3},{9,1},{0,8},{2,10}... | collective-permute-start | bytes 786440 | tf_op jit(solution)/shard_map/ppermute | solution.py:369
  56.9 11.8 %collective-permute-start.7 = (f32[2,8,32,128]{3,2,1,0:T(8,128)S(1)}, f32[2,8,32,128]{3,2,1,0:T(8,128)S(1)}, u32[]{:S(2)}, u32[]{:S(2)}) collective-permute-start(f32[2,8,32,128]{3,2,1,0:T(8,128)S(1)} %get-tuple-element.55.own), channel_id=1, source_target_pairs={{0,16},{2,18},{4,20},{6,22},{7,23},{5,21},{3,19},{1,17},{8,24},{10... | collective-permute-start | bytes 786440 | tf_op jit(solution)/shard_map/ppermute | solution.py:369
  63.9 4.8 %collective-permute-start.6 = (f32[2,8,32,128]{3,2,1,0:T(8,128)S(1)}, f32[2,8,32,128]{3,2,1,0:T(8,128)S(1)}, u32[]{:S(2)}, u32[]{:S(2)}) collective-permute-start(f32[2,8,32,128]{3,2,1,0:T(8,128)S(1)} %get-tuple-element.62.own), channel_id=1, source_target_pairs={{8,0},{10,2},{12,4},{14,6},{15,7},{13,5},{11,3},{9,1},{0,8},{2,10}... | collective-permute-start | bytes 786440 | tf_op jit(solution)/shard_map/ppermute | solution.py:369
  64.4 5.8 %collective-permute-start.5 = (f32[2,8,32,128]{3,2,1,0:T(8,128)S(1)}, f32[2,8,32,128]{3,2,1,0:T(8,128)S(1)}, u32[]{:S(2)}, u32[]{:S(2)}) collective-permute-start(f32[2,8,32,128]{3,2,1,0:T(8,128)S(1)} %get-tuple-element.62.own), channel_id=1, source_target_pairs={{8,2},{10,4},{12,6},{14,7},{15,5},{13,3},{11,1},{9,0},{0,9},{2,8},... | collective-permute-start | bytes 786440 | tf_op jit(solution)/shard_map/ppermute | solution.py:369
  64.4 15.8 %collective-permute-start.12 = (f32[2,8,32,128]{3,2,1,0:T(8,128)S(1)}, f32[2,8,32,128]{3,2,1,0:T(8,128)S(1)}, u32[]{:S(2)}, u32[]{:S(2)}) collective-permute-start(f32[2,8,32,128]{3,2,1,0:T(8,128)S(1)} %get-tuple-element.62.own), channel_id=1, source_target_pairs={{0,48},{2,50},{4,52},{6,54},{7,55},{5,53},{3,51},{1,49},{8,56},{10... | collective-permute-start | bytes 786440 | tf_op jit(solution)/shard_map/ppermute | solution.py:369
  68.7 10.1 %collective-permute-start.11 = (f32[2,8,32,128]{3,2,1,0:T(8,128)S(1)}, f32[2,8,32,128]{3,2,1,0:T(8,128)S(1)}, u32[]{:S(2)}, u32[]{:S(2)}) collective-permute-start(f32[2,8,32,128]{3,2,1,0:T(8,128)S(1)} %get-tuple-element.67), channel_id=1, source_target_pairs={{0,32},{2,34},{4,36},{6,38},{7,39},{5,37},{3,35},{1,33},{8,40},{10... | collective-permute-start | bytes 786440 | tf_op jit(solution)/shard_map/ppermute | solution.py:369
  73.2 7.0 %collective-permute-start.10 = (f32[2,8,32,128]{3,2,1,0:T(8,128)S(1)}, f32[2,8,32,128]{3,2,1,0:T(8,128)S(1)}, u32[]{:S(2)}, u32[]{:S(2)}) collective-permute-start(f32[2,8,32,128]{3,2,1,0:T(8,128)S(1)} %get-tuple-element.71.own), channel_id=1, source_target_pairs={{8,0},{10,2},{12,4},{14,6},{15,7},{13,5},{11,3},{9,1},{0,8},{2,10}... | collective-permute-start | bytes 786440 | tf_op jit(solution)/shard_map/ppermute | solution.py:369
  74.0 6.2 %collective-permute-start.9 = (f32[2,8,32,128]{3,2,1,0:T(8,128)S(1)}, f32[2,8,32,128]{3,2,1,0:T(8,128)S(1)}, u32[]{:S(2)}, u32[]{:S(2)}) collective-permute-start(f32[2,8,32,128]{3,2,1,0:T(8,128)S(1)} %get-tuple-element.71.own), channel_id=1, source_target_pairs={{8,2},{10,4},{12,6},{14,7},{15,5},{13,3},{11,1},{9,0},{0,9},{2,8},... | collective-permute-start | bytes 786440 | tf_op jit(solution)/shard_map/ppermute | solution.py:369
  74.0 16.5 %collective-permute-start.15 = (f32[2,8,32,128]{3,2,1,0:T(8,128)S(1)}, f32[2,8,32,128]{3,2,1,0:T(8,128)S(1)}, u32[]{:S(2)}, u32[]{:S(2)}) collective-permute-start(f32[2,8,32,128]{3,2,1,0:T(8,128)S(1)} %get-tuple-element.71.own), channel_id=1, source_target_pairs={{0,16},{2,18},{4,20},{6,22},{7,23},{5,21},{3,19},{1,17},{8,24},{10... | collective-permute-start | bytes 786440 | tf_op jit(solution)/shard_map/ppermute | solution.py:369
  82.1 10.7 %collective-permute-start.16 = (f32[2,8,32,128]{3,2,1,0:T(8,128)S(1)}, f32[2,8,32,128]{3,2,1,0:T(8,128)S(1)}, u32[]{:S(2)}, u32[]{:S(2)}) collective-permute-start(f32[2,8,32,128]{3,2,1,0:T(8,128)S(1)} %get-tuple-element.78), channel_id=1, source_target_pairs={{0,32},{2,34},{4,36},{6,38},{7,39},{5,37},{3,35},{1,33},{8,40},{10... | collective-permute-start | bytes 786440 | tf_op jit(solution)/shard_map/ppermute | solution.py:369
  86.8 12.4 %collective-permute-start.17 = (f32[2,8,32,128]{3,2,1,0:T(8,128)S(1)}, f32[2,8,32,128]{3,2,1,0:T(8,128)S(1)}, u32[]{:S(2)}, u32[]{:S(2)}) collective-permute-start(f32[2,8,32,128]{3,2,1,0:T(8,128)S(1)} %get-tuple-element.81.own), channel_id=1, source_target_pairs={{0,48},{2,50},{4,52},{6,54},{7,55},{5,53},{3,51},{1,49},{8,56},{10... | collective-permute-start | bytes 786440 | tf_op jit(solution)/shard_map/ppermute | solution.py:369
  88.0 4.4 %collective-permute-start.13 = (f32[2,4,32,128]{3,2,1,0:T(8,128)S(1)}, f32[2,4,32,128]{3,2,1,0:T(8,128)S(1)}, u32[]{:S(2)}, u32[]{:S(2)}) collective-permute-start(f32[2,4,32,128]{3,2,1,0:T(8,128)S(1)} %get-tuple-element.76), channel_id=1, source_target_pairs={{8,2},{10,4},{12,6},{14,7},{15,5},{13,3},{11,1},{9,0},{0,9},{2,8},... | collective-permute-start | bytes 393224 | tf_op jit(solution)/shard_map/ppermute | solution.py:369
  88.6 3.8 %collective-permute-start.14 = (f32[2,4,32,128]{3,2,1,0:T(8,128)S(1)}, f32[2,4,32,128]{3,2,1,0:T(8,128)S(1)}, u32[]{:S(2)}, u32[]{:S(2)}) collective-permute-start(f32[2,4,32,128]{3,2,1,0:T(8,128)S(1)} %get-tuple-element.77), channel_id=1, source_target_pairs={{8,0},{10,2},{12,4},{14,6},{15,7},{13,5},{11,3},{9,1},{0,8},{2,10}... | collective-permute-start | bytes 393224 | tf_op jit(solution)/shard_map/ppermute | solution.py:369
  99.4 3.8 %collective-permute-start.18 = (f32[2,2,32,128]{3,2,1,0:T(8,128)S(1)}, f32[2,2,32,128]{3,2,1,0:T(8,128)S(1)}, u32[]{:S(2)}, u32[]{:S(2)}) collective-permute-start(f32[2,2,32,128]{3,2,1,0:T(8,128)S(1)} %get-tuple-element.85), channel_id=1, source_target_pairs={{8,2},{10,4},{12,6},{14,7},{15,5},{13,3},{11,1},{9,0},{0,9},{2,8},... | collective-permute-start | bytes 196616 | tf_op jit(solution)/shard_map/ppermute | solution.py:369
  99.5 3.7 %collective-permute-start.19 = (f32[2,2,32,128]{3,2,1,0:T(8,128)S(1)}, f32[2,2,32,128]{3,2,1,0:T(8,128)S(1)}, u32[]{:S(2)}, u32[]{:S(2)}) collective-permute-start(f32[2,2,32,128]{3,2,1,0:T(8,128)S(1)} %get-tuple-element.86), channel_id=1, source_target_pairs={{8,0},{10,2},{12,4},{14,6},{15,7},{13,5},{11,3},{9,1},{0,8},{2,10}... | collective-permute-start | bytes 196616 | tf_op jit(solution)/shard_map/ppermute | solution.py:369
  103.8 1.6 %collective-permute-start.20 = (f32[8,64,128]{2,1,0:T(8,128)S(1)}, f32[8,64,128]{2,1,0:T(8,128)S(1)}, u32[]{:S(2)}, u32[]{:S(2)}) collective-permute-start(f32[8,64,128]{2,1,0:T(8,128)S(1)} %get-tuple-element.90), channel_id=1, source_target_pairs={{8,0},{10,2},{12,4},{14,6},{15,7},{13,5},{11,3},{9,1},{0,8},{2,10}... | collective-permute-start | bytes 786440 | tf_op jit(solution)/shard_map/ppermute | solution.py:369

commit v14 on v13

--- a/solution.py
+++ b/solution.py
@@ -443,7 +443,7 @@
     *operands, a0, taken = exchanged(u2, u2, u2, a0, taken)
     u3, u4 = leap(*operands, high=high)
     a4 = along(u4, 4)
-    *operands, a1, a2 = exchanged(u4, u4, u4, a1, a2)
+    *operands, a1 = exchanged(u4, u4, u4, a1)
     u5, state = call(
         first_half_kernel, (half, shape(2, 2 * HALF, NX, LAST)), [VMEM] * 4, (VMEM,) * 2, [field, field], 20, 2
     )(*operands, weights)
@@ -452,7 +452,7 @@
         second_half_kernel, (half, rim4, rim4), [VMEM] * 2, (VMEM,) * 3, [field, field], 20, 2
     )(state, weights)
     a6 = along(u6, 6)
-    *operands, a4, a5 = exchanged(u6, inner, outer, a4, a5)
+    *operands, a2, a4, a5 = exchanged(u6, inner, outer, a2, a4, a5)
     (u7,) = leap(*operands, second=False)
     c, inner, outer = call(share_kernel, (half, rim2, rim2), [VMEM] * 8, (VMEM,) * 3, [], 16)(
         a0, a1, a2, u3, a4, a5, a6, u7

time: 121 us -> 121 us (level)
  waiting for transfers between devices: 29.4 us -> 27.2 us
  starting transfers between devices: 21 us -> 22.8 us
    ppermute x21, waiting for transfers between devices: 29.4 us -> 27.2 us  [sent(): return lax.ppermute(value, AXES, pairs)]
    ppermute x21, starting transfers between devices: 21 us -> 22.8 us  [sent(): return lax.ppermute(value, AXES, pairs)]
  transfers between devices with their start and end apart: 21 -> 21, of which waited for: 12 -> 10; matrix products, arithmetic and copies ran while one was open for 0% -> 0% of each run, Pallas kernels for 9% -> 9%
where the time goes in v14:
time: 121 us; the launch traced here: 120 us
  blocking collectives  45.7 us (38%)
  waiting for transfers between devices  27.2 us (22%)
  Pallas kernels  23.3 us (19%)
  starting transfers between devices  22.8 us (19%)
    all_to_all x1, blocking collectives, shards(): got = lax.all_to_all(packed, 'space', 0, 0, tiled=True)  31.8 us
    ppermute x21, waiting for transfers between devices, sent(): return lax.ppermute(value, AXES, pairs)  27.2 us
    ppermute x21, starting transfers between devices, sent(): return lax.ppermute(value, AXES, pairs)  22.8 us
    all_to_all x1, blocking collectives, shards(): lax.all_to_all(jnp.concatenate([keep, swap(send)], axis=1), 'space', 0, 0...  13.9 us
    pallas_call x1, Pallas kernels, shards(): call(relax_kernel, (all_weights, half, half, half, half), [VMEM] * 6, (VM...  8.81 us
    pallas_call x3, Pallas kernels, leap(): call(body, outs, [VMEM] * len(operands), (VMEM,) * len(outs), [field, fie...  7.12 us
  transfers between devices with their start and end apart: 21, of which 10 were waited for; matrix products, arithmetic and copies ran while one was open for 0% of the time, Pallas kernels for 9%

profile of v14, /device:TPU:4, one launch (start us, length us, event | category | flops | bytes accessed | tf_op | source)
XLA Modules:
  0.0 119.9 jit_solution(13678539154557583433)
XLA Ops:
  0.0 1.5 %shard_map.55 = f32[8,504,128]{2,1,0:T(8,128)S(1)} custom-call(f32[2,4,128,128]{3,2,1,0:T(8,128)} %startup.1, f32[1,2,4,128,128]{4,3,2,1,0:T(8,128)} %guess.1, f32[2,4,128,128]{3,2,1,0:T(8,128)} %conduct.1, f32[4,128,128]{2,1,0:T(8,128)} %couple.1), custom_call_target="tpu_custom_call" | custom-call | bytes 3145728 | tf_op jit(solution)/shard_map/pallas_call | solution.py:397
  1.5 31.8 %all_to_all.10.got = f32[8,504,128]{2,1,0:T(8,128)S(1)} all-to-all(f32[8,504,128]{2,1,0:T(8,128)S(1)} %shard_map.55), channel_id=1, replica_groups=mesh['chip'=8,'core'=2,'space'=8] {'space'}, dimensions={0} | all-to-all | bytes 4128768 | tf_op jit(solution)/shard_map/all_to_all | solution.py:410
  33.3 0.0 copy-start
  33.3 0.1 shard_map.56
  33.4 0.1 collective-permute-start
  33.5 0.6 copy-done
  34.1 1.0 shard_map.57
  35.1 0.8 collective-permute-done.other
  35.9 8.8 %shard_map.58 = (f32[36,18,32,128]{3,2,1,0:T(8,128)S(1)}, f32[2,8,32,128]{3,2,1,0:T(8,128)S(1)}, f32[2,8,32,128]{3,2,1,0:T(8,128)S(1)}, f32[2,8,32,128]{3,2,1,0:T(8,128)S(1)}, f32[2,8,32,128]{3,2,1,0:T(8,128)S(1)}) custom-call(f32[2,36,32,128]{3,2,1,0:T(8,128)S(1)} %get-tuple-element.48.begin, ...), custom_call_target="tpu_custom_call", output_to_operand_aliasing={{0}: (4, {})} | custom-call | bytes 3145728 | tf_op jit(solution)/shard_map/pallas_call | solution.py:421
  44.7 0.2 collective-permute-start.1
  45.0 1.4 %collective-permute-done.1 = f32[2,8,32,128]{3,2,1,0:T(8,128)S(1)} collective-permute-done((f32[2,8,32,128]{3,2,1,0:T(8,128)S(1)}, f32[2,8,32,128]{3,2,1,0:T(8,128)S(1)}, u32[]{:S(2)}, u32[]{:S(2)}) %collective-permute-start.1) | collective-permute-done | bytes 262176 | tf_op jit(solution)/shard_map/ppermute | solution.py:369
  46.4 0.1 collective-permute-start.2
  46.5 8.3 %collective-permute-done.2.across = f32[2,8,32,128]{3,2,1,0:T(8,128)S(1)} collective-permute-done((f32[2,8,32,128]{3,2,1,0:T(8,128)S(1)}, f32[2,8,32,128]{3,2,1,0:T(8,128)S(1)}, u32[]{:S(2)}, u32[]{:S(2)}) %collective-permute-start.2) | collective-permute-done | bytes 262176 | tf_op jit(solution)/shard_map/ppermute | solution.py:369
  54.8 0.1 shard_map.59
  54.9 0.1 collective-permute-start.4
  55.0 0.3 collective-permute-start.3
  55.3 1.6 %collective-permute-start.8 = (f32[2,8,32,128]{3,2,1,0:T(8,128)S(1)}, f32[2,8,32,128]{3,2,1,0:T(8,128)S(1)}, u32[]{:S(2)}, u32[]{:S(2)}) collective-permute-start(f32[2,8,32,128]{3,2,1,0:T(8,128)S(1)} %get-tuple-element.60), channel_id=1, source_target_pairs={{8,0},{10,2},{12,4},{14,6},{15,7},{13,5},{11,3},{9,1},{0,8},{2,10}... | collective-permute-start | bytes 786440 | tf_op jit(solution)/shard_map/ppermute | solution.py:369
  56.9 1.9 %collective-permute-start.7 = (f32[2,8,32,128]{3,2,1,0:T(8,128)S(1)}, f32[2,8,32,128]{3,2,1,0:T(8,128)S(1)}, u32[]{:S(2)}, u32[]{:S(2)}) collective-permute-start(f32[2,8,32,128]{3,2,1,0:T(8,128)S(1)} %get-tuple-element.55.own), channel_id=1, source_target_pairs={{0,16},{2,18},{4,20},{6,22},{7,23},{5,21},{3,19},{1,17},{8,24},{10... | collective-permute-start | bytes 786440 | tf_op jit(solution)/shard_map/ppermute | solution.py:369
  58.9 0.0 collective-permute-done.4.swapped
  58.9 2.0 %collective-permute-done.3.near = f32[2,8,32,128]{3,2,1,0:T(8,128)S(1)} collective-permute-done((f32[2,8,32,128]{3,2,1,0:T(8,128)S(1)}, f32[2,8,32,128]{3,2,1,0:T(8,128)S(1)}, u32[]{:S(2)}, u32[]{:S(2)}) %collective-permute-start.3) | collective-permute-done | bytes 262176 | tf_op jit(solution)/shard_map/ppermute | solution.py:369
  60.9 3.0 %shard_map.60 = (f32[2,8,32,128]{3,2,1,0:T(8,128)S(1)}, f32[2,8,32,128]{3,2,1,0:T(8,128)S(1)}) custom-call(f32[2,8,32,128]{3,2,1,0:T(8,128)S(1)} %get-tuple-element.55.own, f32[2,8,32,128]{3,2,1,0:T(8,128)S(1)} %collective-permute-done.3.near, f32[2,8,32,128]{3,2,1,0:T(8,128)S(1)} %collective-permute-done.4.swapped, f32[36,18,32,128]{3,2,1,0:T(8,128)S(1)} %get-tuple-element.58.w), custom_call_target="tpu_custom_call" | custom-call | bytes 15728640 | tf_op jit(solution)/shard_map/pallas_call | solution.py:436
  63.9 0.5 collective-permute-start.6
  64.4 0.0 collective-permute-start.5
  64.4 4.2 %collective-permute-start.11 = (f32[2,8,32,128]{3,2,1,0:T(8,128)S(1)}, f32[2,8,32,128]{3,2,1,0:T(8,128)S(1)}, u32[]{:S(2)}, u32[]{:S(2)}) collective-permute-start(f32[2,8,32,128]{3,2,1,0:T(8,128)S(1)} %get-tuple-element.67), channel_id=1, source_target_pairs={{0,32},{2,34},{4,36},{6,38},{7,39},{5,37},{3,35},{1,33},{8,40},{10... | collective-permute-start | bytes 786440 | tf_op jit(solution)/shard_map/ppermute | solution.py:369
  68.5 0.0 collective-permute-done.8.taken
  68.5 0.0 collective-permute-done.7.refs_0_
  68.5 0.0 collective-permute-done.6.swapped
  68.5 1.6 %collective-permute-done.5.near = f32[2,8,32,128]{3,2,1,0:T(8,128)S(1)} collective-permute-done((f32[2,8,32,128]{3,2,1,0:T(8,128)S(1)}, f32[2,8,32,128]{3,2,1,0:T(8,128)S(1)}, u32[]{:S(2)}, u32[]{:S(2)}) %collective-permute-start.5) | collective-permute-done | bytes 262176 | tf_op jit(solution)/shard_map/ppermute | solution.py:369
  70.2 3.0 %shard_map.61 = (f32[2,8,32,128]{3,2,1,0:T(8,128)S(1)}, f32[2,8,32,128]{3,2,1,0:T(8,128)S(1)}) custom-call(f32[2,8,32,128]{3,2,1,0:T(8,128)S(1)} %get-tuple-element.62.own, f32[2,8,32,128]{3,2,1,0:T(8,128)S(1)} %collective-permute-done.5.near, f32[2,8,32,128]{3,2,1,0:T(8,128)S(1)} %collective-permute-done.6.swapped, ...), custom_call_target="tpu_custom_call" | custom-call | bytes 15728640 | tf_op jit(solution)/shard_map/pallas_call | solution.py:436
  73.2 0.8 collective-permute-start.10
  74.0 0.0 collective-permute-start.9
  74.0 4.0 %collective-permute-start.14 = (f32[2,8,32,128]{3,2,1,0:T(8,128)S(1)}, f32[2,8,32,128]{3,2,1,0:T(8,128)S(1)}, u32[]{:S(2)}, u32[]{:S(2)}) collective-permute-start(f32[2,8,32,128]{3,2,1,0:T(8,128)S(1)} %get-tuple-element.62.own), channel_id=1, source_target_pairs={{0,48},{2,50},{4,52},{6,54},{7,55},{5,53},{3,51},{1,49},{8,56},{10... | collective-permute-start | bytes 786440 | tf_op jit(solution)/shard_map/ppermute | solution.py:369
  78.0 0.0 collective-permute-start.15
  78.0 0.0 collective-permute-done.11.refs_1_
  78.0 0.0 collective-permute-done.10.swapped
  78.0 1.7 %collective-permute-done.9.near = f32[2,8,32,128]{3,2,1,0:T(8,128)S(1)} collective-permute-done((f32[2,8,32,128]{3,2,1,0:T(8,128)S(1)}, f32[2,8,32,128]{3,2,1,0:T(8,128)S(1)}, u32[]{:S(2)}, u32[]{:S(2)}) %collective-permute-start.9) | collective-permute-done | bytes 262176 | tf_op jit(solution)/shard_map/ppermute | solution.py:369
  79.8 1.9 %shard_map.62 = (f32[2,8,32,128]{3,2,1,0:T(8,128)S(1)}, f32[2,16,32,128]{3,2,1,0:T(8,128)S(1)}) custom-call(f32[2,8,32,128]{3,2,1,0:T(8,128)S(1)} %get-tuple-element.69.own, f32[2,8,32,128]{3,2,1,0:T(8,128)S(1)} %collective-permute-done.9.near, f32[2,8,32,128]{3,2,1,0:T(8,128)S(1)} %collective-permute-done.10.swapped, ...), custom_call_target="tpu_custom_call" | custom-call | bytes 6291456 | tf_op jit(solution)/shard_map/pallas_call | solution.py:447
  81.7 4.0 %collective-permute-start.16 = (f32[2,8,32,128]{3,2,1,0:T(8,128)S(1)}, f32[2,8,32,128]{3,2,1,0:T(8,128)S(1)}, u32[]{:S(2)}, u32[]{:S(2)}) collective-permute-start(f32[2,8,32,128]{3,2,1,0:T(8,128)S(1)} %get-tuple-element.76), channel_id=1, source_target_pairs={{0,32},{2,34},{4,36},{6,38},{7,39},{5,37},{3,35},{1,33},{8,40},{10... | collective-permute-start | bytes 786440 | tf_op jit(solution)/shard_map/ppermute | solution.py:369
  85.7 1.2 shard_map.63
  86.8 1.0 collective-permute-start.17
  87.8 0.0 collective-permute-start.12
  87.8 0.0 collective-permute-done.14.refs_2_
  87.8 1.8 %collective-permute-start.13 = (f32[2,4,32,128]{3,2,1,0:T(8,128)S(1)}, f32[2,4,32,128]{3,2,1,0:T(8,128)S(1)}, u32[]{:S(2)}, u32[]{:S(2)}) collective-permute-start(f32[2,4,32,128]{3,2,1,0:T(8,128)S(1)} %get-tuple-element.75), channel_id=1, source_target_pairs={{8,0},{10,2},{12,4},{14,6},{15,7},{13,5},{11,3},{9,1},{0,8},{2,10}... | collective-permute-start | bytes 393224 | tf_op jit(solution)/shard_map/ppermute | solution.py:369
  89.6 3.9 %collective-permute-done.15.refs_4_ = f32[2,8,32,128]{3,2,1,0:T(8,128)S(1)} collective-permute-done((f32[2,8,32,128]{3,2,1,0:T(8,128)S(1)}, f32[2,8,32,128]{3,2,1,0:T(8,128)S(1)}, u32[]{:S(2)}, u32[]{:S(2)}) %collective-permute-start.15) | collective-permute-done | bytes 262176 | tf_op jit(solution)/shard_map/ppermute | solution.py:369
  93.5 0.0 collective-permute-done.12.near
  93.5 0.0 collective-permute-done.13.swapped
  93.5 0.0 collective-permute-done.16.refs_5_
  93.5 1.1 shard_map.64.refs_7_
  94.6 4.3 %collective-permute-done.17.refs_6_ = f32[2,8,32,128]{3,2,1,0:T(8,128)S(1)} collective-permute-done((f32[2,8,32,128]{3,2,1,0:T(8,128)S(1)}, f32[2,8,32,128]{3,2,1,0:T(8,128)S(1)}, u32[]{:S(2)}, u32[]{:S(2)}) %collective-permute-start.17) | collective-permute-done | bytes 262176 | tf_op jit(solution)/shard_map/ppermute | solution.py:369
  98.9 0.2 shard_map.65
  99.1 0.1 collective-permute-start.18
  99.1 1.9 %collective-permute-start.19 = (f32[2,2,32,128]{3,2,1,0:T(8,128)S(1)}, f32[2,2,32,128]{3,2,1,0:T(8,128)S(1)}, u32[]{:S(2)}, u32[]{:S(2)}) collective-permute-start(f32[2,2,32,128]{3,2,1,0:T(8,128)S(1)} %get-tuple-element.86), channel_id=1, source_target_pairs={{8,0},{10,2},{12,4},{14,6},{15,7},{13,5},{11,3},{9,1},{0,8},{2,10}... | collective-permute-start | bytes 196616 | tf_op jit(solution)/shard_map/ppermute | solution.py:369
  101.0 1.8 %collective-permute-done.18.near = f32[2,2,32,128]{3,2,1,0:T(8,128)S(1)} collective-permute-done((f32[2,2,32,128]{3,2,1,0:T(8,128)S(1)}, f32[2,2,32,128]{3,2,1,0:T(8,128)S(1)}, u32[]{:S(2)}, u32[]{:S(2)}) %collective-permute-start.18) | collective-permute-done | bytes 65568 | tf_op jit(solution)/shard_map/ppermute | solution.py:369
  102.8 0.0 collective-permute-done.19.swapped
  102.8 0.6 shard_map.66
  103.4 0.2 collective-permute-start.20
  103.6 1.4 %collective-permute-done.20 = f32[8,64,128]{2,1,0:T(8,128)S(1)} collective-permute-done((f32[8,64,128]{2,1,0:T(8,128)S(1)}, f32[8,64,128]{2,1,0:T(8,128)S(1)}, u32[]{:S(2)}, u32[]{:S(2)}) %collective-permute-start.20) | collective-permute-done | bytes 262176 | tf_op jit(solution)/shard_map/ppermute | solution.py:369
  105.1 13.9 %all_to_all.11.got = f32[8,128,128]{2,1,0:T(8,128)S(1)} all-to-all(f32[8,128,128]{2,1,0:T(8,128)S(1)} %pad_maximum_fusion), channel_id=1, replica_groups=mesh['chip'=8,'core'=2,'space'=8] {'space'}, dimensions={0} | all-to-all | bytes 1048576 | tf_op jit(solution)/shard_map/all_to_all | solution.py:464
  119.0 0.9 shard_map.67
  (2 shorter events, 0.1 us)
Async XLA Ops:
  33.3 0.8 copy-start
  33.4 2.5 %collective-permute-start = (f32[3,18,32,128]{3,2,1,0:T(8,128)S(1)}, f32[3,18,32,128]{3,2,1,0:T(8,128)S(1)}, u32[]{:S(2)}, u32[]{:S(2)}) collective-permute-start(f32[3,18,32,128]{3,2,1,0:T(8,128)S(1)} %get-tuple-element.49.mine), channel_id=1, source_target_pairs={{8,0},{10,2},{12,4},{14,6},{15,7},{13,5},{11,3},{9,1},{0,8},{2,10}... | collective-permute-start | bytes 2654216 | tf_op jit(solution)/shard_map/ppermute | solution.py:369
  44.7 1.6 %collective-permute-start.1 = (f32[2,8,32,128]{3,2,1,0:T(8,128)S(1)}, f32[2,8,32,128]{3,2,1,0:T(8,128)S(1)}, u32[]{:S(2)}, u32[]{:S(2)}) collective-permute-start(f32[2,8,32,128]{3,2,1,0:T(8,128)S(1)} %get-tuple-element.53), channel_id=1, source_target_pairs={{8,0},{10,2},{12,4},{14,6},{15,7},{13,5},{11,3},{9,1},{0,8},{2,10}... | collective-permute-start | bytes 786440 | tf_op jit(solution)/shard_map/ppermute | solution.py:369
  46.4 8.4 %collective-permute-start.2 = (f32[2,8,32,128]{3,2,1,0:T(8,128)S(1)}, f32[2,8,32,128]{3,2,1,0:T(8,128)S(1)}, u32[]{:S(2)}, u32[]{:S(2)}) collective-permute-start(f32[2,8,32,128]{3,2,1,0:T(8,128)S(1)} %add.3.ours), channel_id=1, source_target_pairs={{65,0},{67,2},{69,4},{71,6},{70,7},{68,5},{66,3},{64,1},{73,8},{75... | collective-permute-start | bytes 786440 | tf_op jit(solution)/shard_map/ppermute | solution.py:369
  54.9 4.0 %collective-permute-start.4 = (f32[2,8,32,128]{3,2,1,0:T(8,128)S(1)}, f32[2,8,32,128]{3,2,1,0:T(8,128)S(1)}, u32[]{:S(2)}, u32[]{:S(2)}) collective-permute-start(f32[2,8,32,128]{3,2,1,0:T(8,128)S(1)} %get-tuple-element.55.own), channel_id=1, source_target_pairs={{8,0},{10,2},{12,4},{14,6},{15,7},{13,5},{11,3},{9,1},{0,8},{2,10}... | collective-permute-start | bytes 786440 | tf_op jit(solution)/shard_map/ppermute | solution.py:369
  55.0 5.9 %collective-permute-start.3 = (f32[2,8,32,128]{3,2,1,0:T(8,128)S(1)}, f32[2,8,32,128]{3,2,1,0:T(8,128)S(1)}, u32[]{:S(2)}, u32[]{:S(2)}) collective-permute-start(f32[2,8,32,128]{3,2,1,0:T(8,128)S(1)} %get-tuple-element.55.own), channel_id=1, source_target_pairs={{8,2},{10,4},{12,6},{14,7},{15,5},{13,3},{11,1},{9,0},{0,9},{2,8},... | collective-permute-start | bytes 786440 | tf_op jit(solution)/shard_map/ppermute | solution.py:369
  55.3 13.2 %collective-permute-start.8 = (f32[2,8,32,128]{3,2,1,0:T(8,128)S(1)}, f32[2,8,32,128]{3,2,1,0:T(8,128)S(1)}, u32[]{:S(2)}, u32[]{:S(2)}) collective-permute-start(f32[2,8,32,128]{3,2,1,0:T(8,128)S(1)} %get-tuple-element.60), channel_id=1, source_target_pairs={{8,0},{10,2},{12,4},{14,6},{15,7},{13,5},{11,3},{9,1},{0,8},{2,10}... | collective-permute-start | bytes 786440 | tf_op jit(solution)/shard_map/ppermute | solution.py:369
  56.9 11.6 %collective-permute-start.7 = (f32[2,8,32,128]{3,2,1,0:T(8,128)S(1)}, f32[2,8,32,128]{3,2,1,0:T(8,128)S(1)}, u32[]{:S(2)}, u32[]{:S(2)}) collective-permute-start(f32[2,8,32,128]{3,2,1,0:T(8,128)S(1)} %get-tuple-element.55.own), channel_id=1, source_target_pairs={{0,16},{2,18},{4,20},{6,22},{7,23},{5,21},{3,19},{1,17},{8,24},{10... | collective-permute-start | bytes 786440 | tf_op jit(solution)/shard_map/ppermute | solution.py:369
  63.9 4.7 %collective-permute-start.6 = (f32[2,8,32,128]{3,2,1,0:T(8,128)S(1)}, f32[2,8,32,128]{3,2,1,0:T(8,128)S(1)}, u32[]{:S(2)}, u32[]{:S(2)}) collective-permute-start(f32[2,8,32,128]{3,2,1,0:T(8,128)S(1)} %get-tuple-element.62.own), channel_id=1, source_target_pairs={{8,0},{10,2},{12,4},{14,6},{15,7},{13,5},{11,3},{9,1},{0,8},{2,10}... | collective-permute-start | bytes 786440 | tf_op jit(solution)/shard_map/ppermute | solution.py:369
  64.4 5.8 %collective-permute-start.5 = (f32[2,8,32,128]{3,2,1,0:T(8,128)S(1)}, f32[2,8,32,128]{3,2,1,0:T(8,128)S(1)}, u32[]{:S(2)}, u32[]{:S(2)}) collective-permute-start(f32[2,8,32,128]{3,2,1,0:T(8,128)S(1)} %get-tuple-element.62.own), channel_id=1, source_target_pairs={{8,2},{10,4},{12,6},{14,7},{15,5},{13,3},{11,1},{9,0},{0,9},{2,8},... | collective-permute-start | bytes 786440 | tf_op jit(solution)/shard_map/ppermute | solution.py:369
  64.4 13.6 %collective-permute-start.11 = (f32[2,8,32,128]{3,2,1,0:T(8,128)S(1)}, f32[2,8,32,128]{3,2,1,0:T(8,128)S(1)}, u32[]{:S(2)}, u32[]{:S(2)}) collective-permute-start(f32[2,8,32,128]{3,2,1,0:T(8,128)S(1)} %get-tuple-element.67), channel_id=1, source_target_pairs={{0,32},{2,34},{4,36},{6,38},{7,39},{5,37},{3,35},{1,33},{8,40},{10... | collective-permute-start | bytes 786440 | tf_op jit(solution)/shard_map/ppermute | solution.py:369
  73.2 4.8 %collective-permute-start.10 = (f32[2,8,32,128]{3,2,1,0:T(8,128)S(1)}, f32[2,8,32,128]{3,2,1,0:T(8,128)S(1)}, u32[]{:S(2)}, u32[]{:S(2)}) collective-permute-start(f32[2,8,32,128]{3,2,1,0:T(8,128)S(1)} %get-tuple-element.69.own), channel_id=1, source_target_pairs={{8,0},{10,2},{12,4},{14,6},{15,7},{13,5},{11,3},{9,1},{0,8},{2,10}... | collective-permute-start | bytes 786440 | tf_op jit(solution)/shard_map/ppermute | solution.py:369
  74.0 5.8 %collective-permute-start.9 = (f32[2,8,32,128]{3,2,1,0:T(8,128)S(1)}, f32[2,8,32,128]{3,2,1,0:T(8,128)S(1)}, u32[]{:S(2)}, u32[]{:S(2)}) collective-permute-start(f32[2,8,32,128]{3,2,1,0:T(8,128)S(1)} %get-tuple-element.69.own), channel_id=1, source_target_pairs={{8,2},{10,4},{12,6},{14,7},{15,5},{13,3},{11,1},{9,0},{0,9},{2,8},... | collective-permute-start | bytes 786440 | tf_op jit(solution)/shard_map/ppermute | solution.py:369
  74.0 13.9 %collective-permute-start.14 = (f32[2,8,32,128]{3,2,1,0:T(8,128)S(1)}, f32[2,8,32,128]{3,2,1,0:T(8,128)S(1)}, u32[]{:S(2)}, u32[]{:S(2)}) collective-permute-start(f32[2,8,32,128]{3,2,1,0:T(8,128)S(1)} %get-tuple-element.62.own), channel_id=1, source_target_pairs={{0,48},{2,50},{4,52},{6,54},{7,55},{5,53},{3,51},{1,49},{8,56},{10... | collective-permute-start | bytes 786440 | tf_op jit(solution)/shard_map/ppermute | solution.py:369
  78.0 15.5 %collective-permute-start.15 = (f32[2,8,32,128]{3,2,1,0:T(8,128)S(1)}, f32[2,8,32,128]{3,2,1,0:T(8,128)S(1)}, u32[]{:S(2)}, u32[]{:S(2)}) collective-permute-start(f32[2,8,32,128]{3,2,1,0:T(8,128)S(1)} %get-tuple-element.69.own), channel_id=1, source_target_pairs={{0,16},{2,18},{4,20},{6,22},{7,23},{5,21},{3,19},{1,17},{8,24},{10... | collective-permute-start | bytes 786440 | tf_op jit(solution)/shard_map/ppermute | solution.py:369
  81.7 11.8 %collective-permute-start.16 = (f32[2,8,32,128]{3,2,1,0:T(8,128)S(1)}, f32[2,8,32,128]{3,2,1,0:T(8,128)S(1)}, u32[]{:S(2)}, u32[]{:S(2)}) collective-permute-start(f32[2,8,32,128]{3,2,1,0:T(8,128)S(1)} %get-tuple-element.76), channel_id=1, source_target_pairs={{0,32},{2,34},{4,36},{6,38},{7,39},{5,37},{3,35},{1,33},{8,40},{10... | collective-permute-start | bytes 786440 | tf_op jit(solution)/shard_map/ppermute | solution.py:369
  86.8 12.1 %collective-permute-start.17 = (f32[2,8,32,128]{3,2,1,0:T(8,128)S(1)}, f32[2,8,32,128]{3,2,1,0:T(8,128)S(1)}, u32[]{:S(2)}, u32[]{:S(2)}) collective-permute-start(f32[2,8,32,128]{3,2,1,0:T(8,128)S(1)} %get-tuple-element.81.own), channel_id=1, source_target_pairs={{0,48},{2,50},{4,52},{6,54},{7,55},{5,53},{3,51},{1,49},{8,56},{10... | collective-permute-start | bytes 786440 | tf_op jit(solution)/shard_map/ppermute | solution.py:369
  87.8 5.7 %collective-permute-start.12 = (f32[2,4,32,128]{3,2,1,0:T(8,128)S(1)}, f32[2,4,32,128]{3,2,1,0:T(8,128)S(1)}, u32[]{:S(2)}, u32[]{:S(2)}) collective-permute-start(f32[2,4,32,128]{3,2,1,0:T(8,128)S(1)} %get-tuple-element.74), channel_id=1, source_target_pairs={{8,2},{10,4},{12,6},{14,7},{15,5},{13,3},{11,1},{9,0},{0,9},{2,8},... | collective-permute-start | bytes 393224 | tf_op jit(solution)/shard_map/ppermute | solution.py:369
  87.8 5.7 %collective-permute-start.13 = (f32[2,4,32,128]{3,2,1,0:T(8,128)S(1)}, f32[2,4,32,128]{3,2,1,0:T(8,128)S(1)}, u32[]{:S(2)}, u32[]{:S(2)}) collective-permute-start(f32[2,4,32,128]{3,2,1,0:T(8,128)S(1)} %get-tuple-element.75), channel_id=1, source_target_pairs={{8,0},{10,2},{12,4},{14,6},{15,7},{13,5},{11,3},{9,1},{0,8},{2,10}... | collective-permute-start | bytes 393224 | tf_op jit(solution)/shard_map/ppermute | solution.py:369
  99.1 3.8 %collective-permute-start.18 = (f32[2,2,32,128]{3,2,1,0:T(8,128)S(1)}, f32[2,2,32,128]{3,2,1,0:T(8,128)S(1)}, u32[]{:S(2)}, u32[]{:S(2)}) collective-permute-start(f32[2,2,32,128]{3,2,1,0:T(8,128)S(1)} %get-tuple-element.85), channel_id=1, source_target_pairs={{8,2},{10,4},{12,6},{14,7},{15,5},{13,3},{11,1},{9,0},{0,9},{2,8},... | collective-permute-start | bytes 196616 | tf_op jit(solution)/shard_map/ppermute | solution.py:369
  99.1 3.7 %collective-permute-start.19 = (f32[2,2,32,128]{3,2,1,0:T(8,128)S(1)}, f32[2,2,32,128]{3,2,1,0:T(8,128)S(1)}, u32[]{:S(2)}, u32[]{:S(2)}) collective-permute-start(f32[2,2,32,128]{3,2,1,0:T(8,128)S(1)} %get-tuple-element.86), channel_id=1, source_target_pairs={{8,0},{10,2},{12,4},{14,6},{15,7},{13,5},{11,3},{9,1},{0,8},{2,10}... | collective-permute-start | bytes 196616 | tf_op jit(solution)/shard_map/ppermute | solution.py:369
  103.4 1.6 %collective-permute-start.20 = (f32[8,64,128]{2,1,0:T(8,128)S(1)}, f32[8,64,128]{2,1,0:T(8,128)S(1)}, u32[]{:S(2)}, u32[]{:S(2)}) collective-permute-start(f32[8,64,128]{2,1,0:T(8,128)S(1)} %get-tuple-element.90), channel_id=1, source_target_pairs={{8,0},{10,2},{12,4},{14,6},{15,7},{13,5},{11,3},{9,1},{0,8},{2,10}... | collective-permute-start | bytes 786440 | tf_op jit(solution)/shard_map/ppermute | solution.py:369
